TPU v7x, 32 devices: a whole 2x2x4 slice. The times are simulated.
32 devices in a mesh: dp: 4 (over y, x), expert: 8 (over z, core).
Axes of the slice: x: 2, y: 2, z: 4, core: 2. Of those that a mesh axis runs over, the one named last changes fastest.
Arguments:
- grad_out: bfloat16 [4096, 2048], P(('dp', 'expert')), may hold values from -6 to 6
- probs: bfloat16 [4096, 2], P(('dp', 'expert')), may hold values from 0.019897461 to 0.5
- routes: int32 [4096, 2], P(('dp', 'expert')), may hold values from 0 to 7, all different within a row; in each aligned block of 128 rows (0 to 127, 128 to 255, ...) at most 48 rows name the same one
- saved_gate: bfloat16 [4, 8, 8, 48, 768], P('dp', 'expert'), may hold values from -6 to 6
- saved_up: bfloat16 [4, 8, 8, 48, 768], P('dp', 'expert'), may hold values from -6 to 6
- w_down: bfloat16 [8, 768, 2048], P('expert'), may hold values from -0.21875 to 0.21875
Outputs:
- grad_gate: bfloat16 [4, 8, 8, 48, 768], P('dp', 'expert')
- grad_up: bfloat16 [4, 8, 8, 48, 768], P('dp', 'expert')
- grad_weight: float32 [8, 768, 2048], P('expert', 'dp')
- route_grad: float32 [4096, 2], P(('dp', 'expert'))
Inputs may be any that keep to these rules, and one draw needn't show every extreme that they name: A token's 2 routes name different experts. Among one device's 128 tokens no expert is named by more than 48 routes, a bound that some block reaches.
All inputs are finite; a program needn't handle non-finite values.
Results may differ from a plain program's by a relative error of at most 0.0049.
Values may be sent and summed in bfloat16 or wider, within the bound.
No kernel may reach another device: no remote copies, remote signals or barrier semaphores. Data moves between devices by JAX's collectives and lax.ppermute only.
A program may use at most 64 MiB of HBM per device.

v0:
```python
import jax
import jax.numpy as jnp
from jax import lax
from jax.sharding import PartitionSpec as P


def silu_parts(gate_value):
    sigmoid = jax.nn.sigmoid(gate_value)
    return (gate_value * sigmoid, sigmoid * (1.0 + gate_value * (1.0 - sigmoid)))


def weight_grad(hidden, scaled):
    whole_panel = lax.dot_general(
        hidden, scaled, (((0,), (0,)), ((), ())), preferred_element_type=jnp.float32
    )
    return lax.psum_scatter(whole_panel, "dp", scatter_dimension=0, tiled=True)


def route_back(slot_grad, position, expert_count, capacity, token_count, top_count):
    returned = lax.all_to_all(
        slot_grad.reshape(expert_count, capacity), "expert", split_axis=0, concat_axis=0, tiled=True
    )
    return jnp.take(returned.reshape(-1), position, axis=0).reshape(token_count, top_count)


def shards(grad_out, probs, routes, saved_gate, saved_up, w_down):
    expert_count = lax.axis_size("expert")
    capacity = saved_gate.shape[3]
    hidden_width = saved_gate.shape[4]
    token_count = routes.shape[0]
    top_count = routes.shape[1]
    model_width = grad_out.shape[1]
    flat_routes = routes.reshape(-1)
    onehot = (flat_routes[:, None] == jnp.arange(expert_count, dtype=jnp.int32)[None, :]).astype(
        jnp.int32
    )
    before = jnp.cumsum(onehot, axis=0) - onehot
    slot_index = jnp.sum(before * onehot, axis=1)
    position = flat_routes * capacity + slot_index
    row_count = expert_count * capacity
    selector = jnp.arange(row_count, dtype=jnp.int32)[:, None] == position[None, :]
    selector = selector.reshape(row_count, token_count, top_count)
    token_select = jnp.sum(selector.astype(jnp.int32), axis=2).astype(jnp.bfloat16)
    sent_grad = jnp.dot(token_select, grad_out, preferred_element_type=jnp.float32).astype(
        jnp.bfloat16
    )
    sent_prob = jnp.sum(
        jnp.where(selector, probs.astype(jnp.float32)[None], 0.0), axis=(1, 2)
    ).astype(jnp.bfloat16)
    arrived_grad, arrived_prob = (
        lax.all_to_all(
            sent_grad.reshape(expert_count, capacity, model_width),
            "expert",
            split_axis=0,
            concat_axis=0,
            tiled=True,
        ),
        lax.all_to_all(
            sent_prob.reshape(expert_count, capacity),
            "expert",
            split_axis=0,
            concat_axis=0,
            tiled=True,
        ),
    )
    arrived_grad = arrived_grad.reshape(row_count, model_width)
    arrived_prob = arrived_prob.reshape(row_count)
    gate_value = saved_gate.reshape(row_count, hidden_width).astype(jnp.float32)
    up_value = saved_up.reshape(row_count, hidden_width).astype(jnp.float32)
    activation, gate_slope = silu_parts(gate_value)
    hidden = (activation * up_value).astype(jnp.bfloat16)
    weight = w_down[0]
    expert_out = jnp.dot(hidden, weight, preferred_element_type=jnp.float32)
    slot_grad = jnp.sum(arrived_grad.astype(jnp.float32) * expert_out, axis=1)
    scaled = (arrived_prob.astype(jnp.float32)[:, None] * arrived_grad.astype(jnp.float32)).astype(
        jnp.bfloat16
    )
    grad_hidden = lax.dot_general(
        scaled, weight, (((1,), (1,)), ((), ())), preferred_element_type=jnp.float32
    )
    grad_up = (grad_hidden * activation).astype(jnp.bfloat16).reshape(saved_up.shape)
    grad_gate = (grad_hidden * up_value * gate_slope).astype(jnp.bfloat16).reshape(saved_gate.shape)
    grad_weight = weight_grad(hidden, scaled)
    route_grad = route_back(slot_grad, position, expert_count, capacity, token_count, top_count)
    return (grad_gate, grad_up, grad_weight[None], route_grad)


def solution(mesh):
    return jax.shard_map(
        shards,
        mesh=mesh,
        in_specs=(
            P(("dp", "expert"), None),
            P(("dp", "expert"), None),
            P(("dp", "expert"), None),
            P("dp", "expert", None, None, None),
            P("dp", "expert", None, None, None),
            P("expert", None, None),
        ),
        out_specs=(
            P("dp", "expert", None, None, None),
            P("dp", "expert", None, None, None),
            P("expert", "dp", None),
            P(("dp", "expert"), None),
        ),
        check_vma=False,
    )
```

profile of v0, /device:TPU:0, one launch (start us, length us, event | category | flops | bytes accessed | tf_op | source)
XLA Modules:
  0.0 148.6 jit_solution(7975554108320197869)
XLA Ops:
  7.2 0.9 copy.28
  8.1 0.1 eq.44
  8.3 0.1 eq.40
  8.4 0.6 reduce-window.6
  9.0 0.2 slice_reduce_fusion
  9.3 0.1 fusion.23
  9.3 0.1 reduce_sum.41
  9.6 0.7 convert_element_type.96
  10.3 0.1 select_reduce_fusion
  10.4 0.7 convert_element_type.123
  11.1 6.3 %all-to-all-start = ((bf16[8,1,48]{2,1,0:T(2,128)(2,1)}), bf16[8,1,48]{2,1,0:T(2,128)(2,1)S(1)}, u32[]{:S(2)}, u32[]{:S(2)}) async-start(bf16[8,1,48]{2,1,0:T(2,128)(2,1)} %convert_element_type.123), calls=%async_computation | async-start | bytes 8192 | tf_op jit(solution)/shard_map/all_to_all | solution.py:58
  17.5 2.7 %convolution_convert_fusion = bf16[384,2048]{1,0:T(8,128)(2,1)} fusion(bf16[128,2048]{1,0:T(8,128)(2,1)} %param.6, s32[384,128]{1,0:T(8,128)S(1)} %convert_reduce_fusion), kind=kOutput, calls=%fused_computation.8 | convolution fusion | flops 202162176 | bytes 2293760 | tf_op jit(solution)/shard_map/dot_general | solution.py:44
  20.2 2.7 %all-to-all-done = bf16[8,1,48]{2,1,0:T(2,128)(2,1)S(1)} async-done(((bf16[8,1,48]{2,1,0:T(2,128)(2,1)}), bf16[8,1,48]{2,1,0:T(2,128)(2,1)S(1)}, u32[]{:S(2)}, u32[]{:S(2)}) %all-to-all-start) | async-done | bytes 800 | tf_op jit(solution)/shard_map/all_to_all | solution.py:58
  22.9 4.3 %all-to-all-start.1 = ((bf16[8,48,2048]{2,1,0:T(8,128)(2,1)}), bf16[8,48,2048]{2,1,0:T(8,128)(2,1)}, u32[]{:S(2)}, u32[]{:S(2)}) async-start(bf16[8,48,2048]{2,1,0:T(8,128)(2,1)} %bitcast.67), calls=%async_computation.1 | async-start | bytes 3145728 | tf_op jit(solution)/shard_map/all_to_all | solution.py:51
  27.3 2.4 %fusion.20 = bf16[1,1,8,48,768]{4,3,2,1,0:T(8,128)(2,1)} fusion(bf16[1,1,8,48,768]{4,3,2,1,0:T(8,128)(2,1)} %param.9, bf16[1,1,8,48,768]{4,3,2,1,0:T(8,128)(2,1)} %param.10), kind=kLoop, calls=%fused_computation.28 | loop fusion | flops 2359296 | bytes 1769472 | tf_op jit(solution)/shard_map/convert_element_type | solution.py:71
  29.7 35.4 %all-to-all-done.1 = bf16[8,48,2048]{2,1,0:T(8,128)(2,1)} async-done(((bf16[8,48,2048]{2,1,0:T(8,128)(2,1)}), bf16[8,48,2048]{2,1,0:T(8,128)(2,1)}, u32[]{:S(2)}, u32[]{:S(2)}) %all-to-all-start.1) | async-done | bytes 1572896 | tf_op jit(solution)/shard_map/all_to_all | solution.py:51
  65.0 1.8 %multiply_convert_fusion = bf16[8,48,2048]{2,1,0:T(8,128)(2,1)S(1)} fusion(f32[8,48]{1,0:T(8,128)S(1)} %bitcast.70, bf16[8,48,2048]{2,1,0:T(8,128)(2,1)} %all-to-all-done.1), kind=kLoop, calls=%fused_computation.7 | loop fusion | flops 2359296 | bytes 3147264 | tf_op jit(solution)/shard_map/convert_element_type | solution.py:75
  66.8 1.1 copy-done.1
  68.0 4.5 %fusion.26 = f32[768,2048]{1,0:T(8,128)} fusion(bf16[384,768]{1,0:T(8,128)(2,1)S(1)} %bitcast.69, bf16[384,2048]{1,0:T(8,128)(2,1)S(1)} %bitcast.65), kind=kOutput, calls=%fused_computation.46 | convolution fusion | flops 1207959552 | bytes 8454144 | tf_op jit(solution)/shard_map/dot_general | solution.py:13
  72.5 0.1 mul.80
  72.7 3.1 %fusion = f32[384]{0:T(512)S(1)} fusion(bf16[384,768]{1,0:T(8,128)(2,1)} %bitcast.68, bf16[1,768,2048]{2,1,0:T(8,128)(2,1)S(1)} %copy-done, bf16[8,48,2048]{2,1,0:T(8,128)(2,1)} %all-to-all-done.1), kind=kOutput, calls=%fused_computation.2 | convolution fusion | flops 1210318464 | bytes 5309952 | tf_op jit(solution)/shard_map/dot_general | solution.py:73
  75.7 0.7 all_to_all.15
  76.4 3.3 %all-to-all-start.2 = ((f32[8,1,48]{2,1,0:T(1,128)}), f32[8,1,48]{2,1,0:T(1,128)S(1)}, u32[]{:S(2)}, u32[]{:S(2)}) async-start(f32[8,1,48]{2,1,0:T(1,128)} %all_to_all.15), calls=%async_computation.3 | async-start | bytes 8192 | tf_op jit(solution)/shard_map/all_to_all | solution.py:20
  79.8 4.5 %fusion.19 = (bf16[384,768]{1,0:T(8,128)(2,1)}, bf16[384,768]{1,0:T(8,128)(2,1)}) fusion(bf16[1,1,8,48,768]{4,3,2,1,0:T(8,128)(2,1)} %param.9, bf16[1,1,8,48,768]{4,3,2,1,0:T(8,128)(2,1)} %param.10, bf16[384,2048]{1,0:T(8,128)(2,1)} %bitcast.66, bf16[1,768,2048]{2,1,0:T(8,128)(2,1)S(1)} %copy-done), kind=kOutput, calls=%fused_computation.26 | convolution fusion | flops 1212383232 | bytes 7077888 | tf_op jit(solution)/shard_map/dot_general | solution.py:78
  84.2 1.0 all-to-all-done.2
  85.2 0.5 broadcast.95
  85.8 0.7 reduce.5
  86.4 0.1 reshape.150
  86.5 1.9 %gather_fusion = f32[256]{0:T(256)S(1)} fusion(f32[384]{0:T(512)S(1)} %reshape.150, s32[1024]{0:T(1024)S(1)} %pad_clamp_fusion), kind=kCustom, calls=%fused_computation | custom fusion | bytes 3072 | tf_op jit(solution)/shard_map/jit(_take)/gather | solution.py:23
  88.5 0.1 gather.7
  88.6 0.6 copy.33
  89.3 52.5 %reduce-scatter.2.cloned.1.call-done = f32[192,2048]{1,0:T(8,128)} async-done(((f32[768,2048]{1,0:T(8,128)}), f32[192,2048]{1,0:T(8,128)}) %reduce-scatter.2.cloned.1.call-update) | async-done | bytes 1572880 | tf_op jit(solution)/shard_map/reduce_scatter | solution.py:16
  (17 shorter events, 0.3 us)
Async XLA Ops:
  7.2 65.5 %copy-start = (bf16[1,768,2048]{2,1,0:T(8,128)(2,1)S(1)}, bf16[1,768,2048]{2,1,0:T(8,128)(2,1)}, u32[]{:S(2)}) copy-start(bf16[1,768,2048]{2,1,0:T(8,128)(2,1)} %param.11) | copy-start | bytes 9437188
  11.1 11.8 %all-to-all-start = ((bf16[8,1,48]{2,1,0:T(2,128)(2,1)}), bf16[8,1,48]{2,1,0:T(2,128)(2,1)S(1)}, u32[]{:S(2)}, u32[]{:S(2)}) async-start(bf16[8,1,48]{2,1,0:T(2,128)(2,1)} %convert_element_type.123), calls=%async_computation | async-start | bytes 8192 | tf_op jit(solution)/shard_map/all_to_all | solution.py:58
  22.9 42.1 %all-to-all-start.1 = ((bf16[8,48,2048]{2,1,0:T(8,128)(2,1)}), bf16[8,48,2048]{2,1,0:T(8,128)(2,1)}, u32[]{:S(2)}, u32[]{:S(2)}) async-start(bf16[8,48,2048]{2,1,0:T(8,128)(2,1)} %bitcast.67), calls=%async_computation.1 | async-start | bytes 3145728 | tf_op jit(solution)/shard_map/all_to_all | solution.py:51
  27.2 114.5 %reduce-scatter.2.cloned.1.call-start = ((), (), s32[]{:S(2)}) async-start(), calls=%async_computation.4 | async-start | bytes 7864320 | tf_op jit(solution)/shard_map/reduce_scatter | solution.py:16
  65.0 2.9 %copy-start.2 = (bf16[1,1,8,48,768]{4,3,2,1,0:T(8,128)(2,1)S(1)}, bf16[1,1,8,48,768]{4,3,2,1,0:T(8,128)(2,1)}, u32[]{:S(2)}) copy-start(bf16[1,1,8,48,768]{4,3,2,1,0:T(8,128)(2,1)} %fusion.20) | copy-start | bytes 1769476
  66.8 1.1 copy-start.1
  76.4 8.8 %all-to-all-start.2 = ((f32[8,1,48]{2,1,0:T(1,128)}), f32[8,1,48]{2,1,0:T(1,128)S(1)}, u32[]{:S(2)}, u32[]{:S(2)}) async-start(f32[8,1,48]{2,1,0:T(1,128)} %all_to_all.15), calls=%async_computation.3 | async-start | bytes 8192 | tf_op jit(solution)/shard_map/all_to_all | solution.py:20
Sparse Core Ops, SparseCore 0:
  72.6 69.0 reduce-scatter.1
where the time goes:
time: 149 us
  waiting for transfers between devices  91.5 us (61%)
  matrix products  14.8 us (10%)
  between operations  14.2 us (10%)
  starting transfers between devices  14 us (9%)
  local copies, waits for them, and re-layouts  7.6 us (5%)
  other arithmetic  6.52 us (4%)
    reduce_scatter x1, waiting for transfers between devices, weight_grad(): return lax.psum_scatter(whole_panel, 'dp', scatter_dimension=0, tiled=True)  52.5 us
    all_to_all x1, waiting for transfers between devices, shards(): lax.all_to_all(sent_grad.reshape(expert_count, capacity, model_width), 'e...  35.4 us
    all_to_all x1, starting transfers between devices, shards(): lax.all_to_all(sent_prob.reshape(expert_count, capacity), 'expert', split...  6.33 us
    dot_general x1, matrix products, weight_grad(): lax.dot_general(hidden, scaled, (((0,), (0,)), ((), ())), preferred_eleme...  4.49 us
    dot_general x1, matrix products, shards(): lax.dot_general(scaled, weight, (((1,), (1,)), ((), ())), preferred_eleme...  4.47 us
    all_to_all x1, starting transfers between devices, shards(): lax.all_to_all(sent_grad.reshape(expert_count, capacity, model_width), 'e...  4.29 us
    all_to_all x1, starting transfers between devices, route_back(): lax.all_to_all(slot_grad.reshape(expert_count, capacity), 'expert', split...  3.31 us
    dot_general x1, matrix products, shards(): expert_out = jnp.dot(hidden, weight, preferred_element_type=jnp.float32)  3.07 us
  transfers between devices with their start and end apart: 4, of which 4 were waited for; matrix products, arithmetic and copies ran while one was open for 11% of the time, Pallas kernels for 0%

commit v1 on v0

v1 whole, which is shorter than its diff:
```python
import functools

import jax
import jax.numpy as jnp
from jax import lax
from jax.experimental import pallas as pl
from jax.experimental.pallas import tpu as pltpu
from jax.sharding import PartitionSpec as P

LANES = 128
CHUNKS = 4
VMEM_LIMIT = 32 * 1024 * 1024


def params():
    return pltpu.CompilerParams(vmem_limit_bytes=VMEM_LIMIT)


def cost(flops, moved):
    return pl.CostEstimate(flops=flops, bytes_accessed=moved, transcendentals=0)


def silu_parts(gate_value):
    sigmoid = jax.nn.sigmoid(gate_value)
    return (gate_value * sigmoid, sigmoid * (1.0 + gate_value * (1.0 - sigmoid)))


def dispatch_kernel(expert_count, capacity, routes_ref, probs_ref, grad_ref, slot_ref, *sent_refs):
    token_count, top_count = routes_ref.shape
    row_count = expert_count * capacity
    experts = lax.broadcasted_iota(jnp.int32, (token_count, expert_count), 1)
    named = [routes_ref[:, k : k + 1] for k in range(top_count)]
    onehots = [(experts == name).astype(jnp.float32) for name in named]
    earlier = (
        lax.broadcasted_iota(jnp.int32, (token_count, token_count), 0)
        > lax.broadcasted_iota(jnp.int32, (token_count, token_count), 1)
    ).astype(jnp.bfloat16)
    before = jnp.dot(
        earlier, sum(onehots).astype(jnp.bfloat16), preferred_element_type=jnp.float32
    )
    slots = lax.broadcasted_iota(jnp.int32, (token_count, row_count), 1)
    selector = jnp.zeros((token_count, row_count), jnp.float32)
    for k in range(top_count):
        slot = jnp.sum(before * onehots[k], axis=1, keepdims=True).astype(jnp.int32)
        before = before + onehots[k]
        slot_ref[:, k : k + 1] = slot
        prob = probs_ref[:, k : k + 1].astype(jnp.float32)
        selector = selector + jnp.where(slots == named[k] * capacity + slot, prob, 0.0)
    selector = selector.T.astype(jnp.bfloat16)
    start = 0
    for sent_ref in sent_refs:
        width = sent_ref.shape[1]
        sent_ref[...] = jnp.dot(
            selector, grad_ref[:, start : start + width], preferred_element_type=jnp.float32
        ).astype(jnp.bfloat16)
        start += width


def dispatch(routes, probs, grad_out, expert_count, capacity, widths):
    token_count, top_count = routes.shape
    row_count = expert_count * capacity
    model_width = grad_out.shape[1]
    return pl.pallas_call(
        functools.partial(dispatch_kernel, expert_count, capacity),
        out_shape=[jax.ShapeDtypeStruct((token_count, top_count), jnp.int32)]
        + [jax.ShapeDtypeStruct((row_count, width), jnp.bfloat16) for width in widths],
        compiler_params=params(),
        cost_estimate=cost(
            2 * row_count * token_count * model_width, 2 * (row_count + token_count) * model_width
        ),
    )(routes, probs, grad_out)


def hidden_kernel(gate_ref, up_ref, hidden_ref):
    activation, _ = silu_parts(gate_ref[...].astype(jnp.float32))
    hidden = activation * up_ref[...].astype(jnp.float32)
    hidden_ref[...] = hidden.T.astype(jnp.bfloat16)


def hidden_transposed(gate, up):
    row_count, hidden_width = gate.shape
    step = 2 * LANES
    return pl.pallas_call(
        hidden_kernel,
        grid=(hidden_width // step,),
        in_specs=[pl.BlockSpec((row_count, step), lambda i: (0, i))] * 2,
        out_specs=pl.BlockSpec((step, row_count), lambda i: (i, 0)),
        out_shape=jax.ShapeDtypeStruct((hidden_width, row_count), jnp.bfloat16),
        compiler_params=params(),
        cost_estimate=cost(20 * row_count * hidden_width, 6 * row_count * hidden_width),
    )(gate, up)


def panel_kernel(group_count, group_ref, hidden_ref, rows_ref, own_ref, *sent_refs):
    share = own_ref.shape[0]
    rows = rows_ref[...]
    for step in list(range(1, group_count)) + [0]:
        owner = lax.bitwise_xor(group_ref[0], step)
        start = pl.multiple_of(owner * share, share)
        part = jnp.dot(
            hidden_ref[pl.ds(start, share), :], rows, preferred_element_type=jnp.float32
        )
        if step == 0:
            own_ref[...] = part
        else:
            sent_refs[step - 1][...] = part.astype(jnp.bfloat16)


def panel_parts(group, hidden, rows, group_count):
    hidden_width, row_count = hidden.shape
    width = rows.shape[1]
    share = hidden_width // group_count
    vmem = pl.BlockSpec(memory_space=pltpu.VMEM)
    return pl.pallas_call(
        functools.partial(panel_kernel, group_count),
        in_specs=[pl.BlockSpec(memory_space=pltpu.SMEM), vmem, vmem],
        out_shape=[jax.ShapeDtypeStruct((share, width), jnp.float32)]
        + [jax.ShapeDtypeStruct((share, width), jnp.bfloat16)] * (group_count - 1),
        compiler_params=params(),
        cost_estimate=cost(
            2 * hidden_width * row_count * width, 2 * hidden_width * (row_count + width)
        ),
    )(group, hidden, rows)


def total_kernel(own_ref, *refs):
    total = own_ref[...]
    for ref in refs[: len(refs) - 1]:
        total = total + ref[...].astype(jnp.float32)
    refs[-1][...] = total


def total_chunk(held, own, arrived, start, model_width):
    share, width = own.shape
    place = pl.BlockSpec((share, width), lambda i: (0, start // width))
    inputs = [own] + list(arrived)
    specs = [pl.BlockSpec((share, width), lambda i: (0, 0))] * len(inputs)
    kernel = total_kernel
    aliases = {}
    if held is not None:
        inputs = [held] + inputs
        specs = [pl.BlockSpec(memory_space=pl.ANY)] + specs
        aliases = {0: 0}

        def kernel(held_ref, *refs):
            total_kernel(*refs)

    return pl.pallas_call(
        kernel,
        grid=(1,),
        in_specs=specs,
        out_specs=place,
        out_shape=jax.ShapeDtypeStruct((share, model_width), jnp.float32),
        input_output_aliases=aliases,
        compiler_params=params(),
        cost_estimate=cost(4 * share * width, 14 * share * width),
    )(*inputs)


def rows_times_weight(rows_ref, weight_ref):
    return lax.dot_general(
        rows_ref[...],
        weight_ref[...],
        (((1,), (1,)), ((), ())),
        preferred_element_type=jnp.float32,
    )


def first_kernel(rows_ref, weight_ref, sum_ref):
    sum_ref[...] = rows_times_weight(rows_ref, weight_ref)


def middle_kernel(held_ref, rows_ref, weight_ref, sum_ref):
    sum_ref[...] = held_ref[...] + rows_times_weight(rows_ref, weight_ref)


def grad_hidden_step(held, rows, weight, start):
    row_count, width = rows.shape
    hidden_width = weight.shape[0]
    step = 2 * LANES
    block = pl.BlockSpec((row_count, step), lambda i: (0, i))
    specs = [
        pl.BlockSpec((row_count, width), lambda i: (0, 0)),
        pl.BlockSpec((step, width), lambda i: (i, start // width)),
    ]
    return pl.pallas_call(
        first_kernel if held is None else middle_kernel,
        grid=(hidden_width // step,),
        in_specs=specs if held is None else [block] + specs,
        out_specs=block,
        out_shape=jax.ShapeDtypeStruct((row_count, hidden_width), jnp.float32),
        compiler_params=params(),
        cost_estimate=cost(
            2 * row_count * hidden_width * width, 8 * row_count * hidden_width
        ),
    )(*([rows, weight] if held is None else [held, rows, weight]))


def last_kernel(
    capacity,
    held_ref,
    rows_ref,
    weight_ref,
    gate_ref,
    up_ref,
    grad_gate_ref,
    grad_up_ref,
    slot_ref,
    sum_ref,
):
    place = pl.program_id(0)
    grad_hidden = held_ref[...] + rows_times_weight(rows_ref, weight_ref)
    activation, gate_slope = silu_parts(gate_ref[...].astype(jnp.float32))
    up_value = up_ref[...].astype(jnp.float32)
    grad_up_ref[...] = (grad_hidden * activation).astype(jnp.bfloat16)
    grad_gate_ref[...] = (grad_hidden * up_value * gate_slope).astype(jnp.bfloat16)
    hidden = (activation * up_value).astype(jnp.bfloat16).astype(jnp.float32)
    product = hidden * grad_hidden
    folded = product[:, :LANES]
    for start in range(LANES, product.shape[1], LANES):
        folded = folded + product[:, start : start + LANES]

    @pl.when(place == 0)
    def _():
        sum_ref[...] = folded

    @pl.when(place > 0)
    def _():
        sum_ref[...] = sum_ref[...] + folded

    @pl.when(place == pl.num_programs(0) - 1)
    def _():
        line = jnp.sum(sum_ref[...].T, axis=0, keepdims=True)
        slot_ref[...] = jnp.zeros_like(slot_ref)
        for source in range(slot_ref.shape[0]):
            slot_ref[source, 0:1, 0:capacity] = line[:, source * capacity : (source + 1) * capacity]


def grad_hidden_last(held, rows, weight, start, gate, up, expert_count, capacity):
    row_count, width = rows.shape
    hidden_width = weight.shape[0]
    step = 2 * LANES
    lanes = -(-capacity // LANES) * LANES
    block = pl.BlockSpec((row_count, step), lambda i: (0, i))
    return pl.pallas_call(
        functools.partial(last_kernel, capacity),
        grid=(hidden_width // step,),
        in_specs=[
            block,
            pl.BlockSpec((row_count, width), lambda i: (0, 0)),
            pl.BlockSpec((step, width), lambda i: (i, start // width)),
            block,
            block,
        ],
        out_specs=[
            block,
            block,
            pl.BlockSpec((expert_count, 8, lanes), lambda i: (0, 0, 0)),
        ],
        out_shape=[
            jax.ShapeDtypeStruct((row_count, hidden_width), jnp.bfloat16),
            jax.ShapeDtypeStruct((row_count, hidden_width), jnp.bfloat16),
            jax.ShapeDtypeStruct((expert_count, 8, lanes), jnp.float32),
        ],
        scratch_shapes=[pltpu.VMEM((row_count, LANES), jnp.float32)],
        compiler_params=params(),
        cost_estimate=cost(
            2 * row_count * hidden_width * width, 12 * row_count * hidden_width
        ),
    )(held, rows, weight, gate, up)


def route_kernel(returned_ref, routes_ref, slot_ref, probs_ref, out_ref):
    token_count, top_count = routes_ref.shape
    lanes = returned_ref.shape[2]
    places = lax.broadcasted_iota(jnp.int32, (token_count, lanes), 1)
    for k in range(top_count):
        name = routes_ref[:, k : k + 1]
        line = jnp.zeros((token_count, lanes), jnp.float32)
        for expert in range(returned_ref.shape[0]):
            line = jnp.where(name == expert, returned_ref[expert, 0:1, :], line)
        line = jnp.where(places == slot_ref[:, k : k + 1], line, 0.0)
        picked = jnp.sum(line, axis=1, keepdims=True)
        out_ref[:, k : k + 1] = picked / probs_ref[:, k : k + 1].astype(jnp.float32)


def shards(grad_out, probs, routes, saved_gate, saved_up, w_down):
    expert_count = lax.axis_size("expert")
    group_count = lax.axis_size("dp")
    capacity = saved_gate.shape[3]
    hidden_width = saved_gate.shape[4]
    model_width = grad_out.shape[1]
    row_count = expert_count * capacity
    share = hidden_width // group_count
    width = model_width // CHUNKS
    starts = [chunk * width for chunk in range(CHUNKS)]
    direct = share % 16 == 0 and group_count & (group_count - 1) == 0

    slot, *sent = dispatch(routes, probs, grad_out, expert_count, capacity, [width] * CHUNKS)
    gate = saved_gate.reshape(row_count, hidden_width)
    up = saved_up.reshape(row_count, hidden_width)
    weight = w_down[0]
    hidden = hidden_transposed(gate, up)
    group = lax.axis_index("dp").reshape(1)
    held = None
    panel = None
    panels = []
    for chunk, start in enumerate(starts):
        rows = lax.all_to_all(
            sent[chunk].reshape(expert_count, capacity, width),
            "expert",
            split_axis=0,
            concat_axis=0,
            tiled=True,
        ).reshape(row_count, width)
        if direct:
            own, *parts = panel_parts(group, hidden, rows, group_count)
            arrived = [
                lax.ppermute(part, "dp", [(g, g ^ (step + 1)) for g in range(group_count)])
                for step, part in enumerate(parts)
            ]
            panel = total_chunk(panel, own, arrived, start, model_width)
        else:
            whole = jnp.dot(hidden, rows, preferred_element_type=jnp.float32)
            panels.append(lax.psum_scatter(whole, "dp", scatter_dimension=0, tiled=True))
        if chunk + 1 < CHUNKS:
            held = grad_hidden_step(held, rows, weight, start)
        else:
            grad_gate, grad_up, slot_grad = grad_hidden_last(
                held, rows, weight, start, gate, up, expert_count, capacity
            )
    if not direct:
        panel = jnp.concatenate(panels, axis=1)
    returned = lax.all_to_all(slot_grad, "expert", split_axis=0, concat_axis=0, tiled=True)
    route_grad = pl.pallas_call(
        route_kernel,
        out_shape=jax.ShapeDtypeStruct(routes.shape, jnp.float32),
        compiler_params=params(),
        cost_estimate=cost(100000, 100000),
    )(returned, routes, slot, probs)
    return (
        grad_gate.reshape(saved_gate.shape),
        grad_up.reshape(saved_up.shape),
        panel[None],
        route_grad,
    )


def solution(mesh):
    return jax.shard_map(
        shards,
        mesh=mesh,
        in_specs=(
            P(("dp", "expert"), None),
            P(("dp", "expert"), None),
            P(("dp", "expert"), None),
            P("dp", "expert", None, None, None),
            P("dp", "expert", None, None, None),
            P("expert", None, None),
        ),
        out_specs=(
            P("dp", "expert", None, None, None),
            P("dp", "expert", None, None, None),
            P("expert", "dp", None),
            P(("dp", "expert"), None),
        ),
        check_vma=False,
    )
```

time: 149 us -> 118 us (0.79)
  waiting for transfers between devices: 91.5 us -> 1.79 us
  blocking collectives: 0 us -> 60.7 us
  Pallas kernels: 0 us -> 21.2 us
  matrix products: 14.8 us -> 0 us
  between operations: 14.2 us -> 0.86 us
  local copies, waits for them, and re-layouts: 7.6 us -> 15.1 us
  other arithmetic: 6.52 us -> 0 us
  starting transfers between devices: 14 us -> 17.5 us
    all_to_all x0 -> x4, blocking collectives: none -> 60.7 us  [the longest x3 50 us: shards(): lax.all_to_all(sent[chunk].reshape(expert_count, capacity, width), 'exper...]
    reduce_scatter x1 -> x0, waiting for transfers between devices: 52.5 us -> none  [weight_grad(): return lax.psum_scatter(whole_panel, 'dp', scatter_dimension=0, tiled=True)]
    all_to_all x3 -> x1, waiting for transfers between devices: 39.1 us -> 0.01 us  [shards(): lax.all_to_all(sent[chunk].reshape(expert_count, capacity, width), 'exper...]
    pallas_call x0 -> x15, Pallas kernels: none -> 21.2 us  [the longest x4 7.68 us: total_chunk(): pl.pallas_call(kernel, grid=(1,), in_specs=specs, out_specs=place, out_sh...]
    dot_general x4 -> x0, matrix products: 14.8 us -> none  [the longest x1 4.49 us: weight_grad(): lax.dot_general(hidden, scaled, (((0,), (0,)), ((), ())), preferred_eleme...]
    ppermute x0 -> x12, starting transfers between devices: none -> 14 us  [shards(): lax.ppermute(part, 'dp', [(g, g ^ step + 1) for g in range(group_count)])]
    unnamed x8 -> x71, local copies, waits for them, and re-layouts: 2.72 us -> 15.1 us
    all_to_all x3 -> x1, starting transfers between devices: 13.9 us -> 3.45 us  [shards(): lax.all_to_all(sent[chunk].reshape(expert_count, capacity, width), 'exper...]
  transfers between devices with their start and end apart: 4 -> 13, of which waited for: 4 -> 1; matrix products, arithmetic and copies ran while one was open for 11% -> 1% of each run, Pallas kernels for 0% -> 15%
where the time goes in v1:
time: 118 us; the launch traced here: 117 us
  blocking collectives  60.7 us (51%)
  Pallas kernels  21.2 us (18%)
  starting transfers between devices  17.5 us (15%)
  local copies, waits for them, and re-layouts  15.1 us (13%)
  waiting for transfers between devices  1.79 us (2%)
    all_to_all x3, blocking collectives, shards(): lax.all_to_all(sent[chunk].reshape(expert_count, capacity, width), 'exper...  50 us
    unnamed x71, local copies, waits for them, and re-layouts  15.1 us
    ppermute x12, starting transfers between devices, shards(): lax.ppermute(part, 'dp', [(g, g ^ step + 1) for g in range(group_count)])  14 us
    all_to_all x1, blocking collectives, shards(): lax.all_to_all(slot_grad, 'expert', split_axis=0, concat_axis=0, tiled=True)  10.7 us
    pallas_call x4, Pallas kernels, total_chunk(): pl.pallas_call(kernel, grid=(1,), in_specs=specs, out_specs=place, out_sh...  7.68 us
    pallas_call x4, Pallas kernels, panel_parts(): pl.pallas_call(functools.partial(panel_kernel, group_count), in_specs=[pl...  4.56 us
    all_to_all x1, starting transfers between devices, shards(): lax.all_to_all(sent[chunk].reshape(expert_count, capacity, width), 'exper...  3.45 us
    pallas_call x3, Pallas kernels, grad_hidden_step(): pl.pallas_call(first_kernel if held is None else middle_kernel, grid=(hid...  3.3 us
  transfers between devices with their start and end apart: 13, of which 1 were waited for; matrix products, arithmetic and copies ran while one was open for 1% of the time, Pallas kernels for 15%

profile of v1, /device:TPU:0, one launch (start us, length us, event | category | flops | bytes accessed | tf_op | source)
XLA Modules:
  0.0 117.1 jit_solution(7019356831887553920)
XLA Ops:
  2.2 1.0 copy-done.31
  3.3 1.8 %shard_map.93 = (s32[128,2]{1,0:T(8,128)S(1)}, bf16[384,512]{1,0:T(8,128)(2,1)S(1)}, bf16[384,512]{1,0:T(8,128)(2,1)S(1)}, bf16[384,512]{1,0:T(8,128)(2,1)S(1)}, bf16[384,512]{1,0:T(8,128)(2,1)}) custom-call(s32[128,2]{1,0:T(8,128)S(1)} %copy.13.routes_ref, bf16[128,2]{1,0:T(8,128)(2,1)S(1)} %copy.14.probs_ref, bf16[128,2048]{1,0:T(8,128)(2,1)S(1)} %copy-done.31), custom_call_target="tpu_custom_call" | custom-call | flops 201326592 | bytes 2097152 | tf_op jit(solution)/shard_map/pallas_call | solution.py:63
  5.1 18.8 %all_to_all.25 = bf16[8,48,512]{2,1,0:T(8,128)(2,1)S(1)} all-to-all(bf16[8,48,512]{2,1,0:T(8,128)(2,1)S(1)} %bitcast.33), channel_id=1, replica_groups=mesh['dp'=4,'expert'=8] {'expert'}, dimensions={0} | all-to-all | bytes 786432 | tf_op jit(solution)/shard_map/all_to_all | solution.py:309
  23.9 15.6 %all_to_all.26 = bf16[8,48,512]{2,1,0:T(8,128)(2,1)} all-to-all(bf16[8,48,512]{2,1,0:T(8,128)(2,1)S(1)} %bitcast.32), channel_id=1, replica_groups=mesh['dp'=4,'expert'=8] {'expert'}, dimensions={0} | all-to-all | bytes 786432 | tf_op jit(solution)/shard_map/all_to_all | solution.py:309
  39.5 15.6 %all_to_all.27 = bf16[8,48,512]{2,1,0:T(8,128)(2,1)} all-to-all(bf16[8,48,512]{2,1,0:T(8,128)(2,1)S(1)} %bitcast.31), channel_id=1, replica_groups=mesh['dp'=4,'expert'=8] {'expert'}, dimensions={0} | all-to-all | bytes 786432 | tf_op jit(solution)/shard_map/all_to_all | solution.py:309
  55.1 3.5 %all-to-all-start.3 = ((bf16[8,48,512]{2,1,0:T(8,128)(2,1)}), bf16[8,48,512]{2,1,0:T(8,128)(2,1)S(1)}, u32[]{:S(2)}, u32[]{:S(2)}) async-start(bf16[8,48,512]{2,1,0:T(8,128)(2,1)} %bitcast.7), calls=%async_computation.3 | async-start | bytes 786432 | tf_op jit(solution)/shard_map/all_to_all | solution.py:309
  59.3 1.1 shard_map.99
  61.2 1.5 %collective-permute-start = (bf16[192,512]{1,0:T(8,128)(2,1)S(1)}, bf16[192,512]{1,0:T(8,128)(2,1)S(1)}, u32[]{:S(2)}, u32[]{:S(2)}) collective-permute-start(bf16[192,512]{1,0:T(8,128)(2,1)S(1)} %get-tuple-element.35), channel_id=1, source_target_pairs={{0,8},{8,0},{16,24},{24,16},{1,9},{9,1},{17,25},{25,17},{2,10},{10... | collective-permute-start | bytes 589832 | tf_op jit(solution)/shard_map/ppermute | solution.py:319
  62.7 1.5 %collective-permute-start.1 = (bf16[192,512]{1,0:T(8,128)(2,1)S(1)}, bf16[192,512]{1,0:T(8,128)(2,1)S(1)}, u32[]{:S(2)}, u32[]{:S(2)}) collective-permute-start(bf16[192,512]{1,0:T(8,128)(2,1)S(1)} %get-tuple-element.36), channel_id=1, source_target_pairs={{0,16},{8,24},{16,0},{24,8},{1,17},{9,25},{17,1},{25,9},{2,18},{10... | collective-permute-start | bytes 589832 | tf_op jit(solution)/shard_map/ppermute | solution.py:319
  64.7 1.0 copy-done.9
  65.7 1.2 shard_map.101
  67.6 1.5 %collective-permute-start.3 = (bf16[192,512]{1,0:T(8,128)(2,1)}, bf16[192,512]{1,0:T(8,128)(2,1)}, u32[]{:S(2)}, u32[]{:S(2)}) collective-permute-start(bf16[192,512]{1,0:T(8,128)(2,1)} %get-tuple-element.39), channel_id=1, source_target_pairs={{0,8},{8,0},{16,24},{24,16},{1,9},{9,1},{17,25},{25,17},{2,10},{10... | collective-permute-start | bytes 589832 | tf_op jit(solution)/shard_map/ppermute | solution.py:319
  69.1 1.5 %collective-permute-start.4 = (bf16[192,512]{1,0:T(8,128)(2,1)}, bf16[192,512]{1,0:T(8,128)(2,1)}, u32[]{:S(2)}, u32[]{:S(2)}) collective-permute-start(bf16[192,512]{1,0:T(8,128)(2,1)} %get-tuple-element.40), channel_id=1, source_target_pairs={{0,16},{8,24},{16,0},{24,8},{1,17},{9,25},{17,1},{25,9},{2,18},{10... | collective-permute-start | bytes 589832 | tf_op jit(solution)/shard_map/ppermute | solution.py:319
  70.7 1.1 shard_map.103
  75.7 1.5 %collective-permute-start.6 = (bf16[192,512]{1,0:T(8,128)(2,1)}, bf16[192,512]{1,0:T(8,128)(2,1)}, u32[]{:S(2)}, u32[]{:S(2)}) collective-permute-start(bf16[192,512]{1,0:T(8,128)(2,1)} %get-tuple-element.43), channel_id=1, source_target_pairs={{0,8},{8,0},{16,24},{24,16},{1,9},{9,1},{17,25},{25,17},{2,10},{10... | collective-permute-start | bytes 589832 | tf_op jit(solution)/shard_map/ppermute | solution.py:319
  77.2 1.1 copy-done.12
  78.3 1.1 shard_map.105
  80.2 1.5 %collective-permute-start.7 = (bf16[192,512]{1,0:T(8,128)(2,1)}, bf16[192,512]{1,0:T(8,128)(2,1)}, u32[]{:S(2)}, u32[]{:S(2)}) collective-permute-start(bf16[192,512]{1,0:T(8,128)(2,1)} %copy-done.33), channel_id=1, source_target_pairs={{0,16},{8,24},{16,0},{24,8},{1,17},{9,25},{17,1},{25,9},{2,18},{10... | collective-permute-start | bytes 589832 | tf_op jit(solution)/shard_map/ppermute | solution.py:319
  82.2 1.9 %collective-permute-start.10 = (bf16[192,512]{1,0:T(8,128)(2,1)}, bf16[192,512]{1,0:T(8,128)(2,1)}, u32[]{:S(2)}, u32[]{:S(2)}) collective-permute-start(bf16[192,512]{1,0:T(8,128)(2,1)} %get-tuple-element.48), channel_id=1, source_target_pairs={{0,16},{8,24},{16,0},{24,8},{1,17},{9,25},{17,1},{25,9},{2,18},{10... | collective-permute-start | bytes 589832 | tf_op jit(solution)/shard_map/ppermute | solution.py:319
  84.1 1.1 collective-permute-start.11
  85.1 1.8 %collective-permute-done.6.refs_1_ = bf16[192,512]{1,0:T(8,128)(2,1)} collective-permute-done((bf16[192,512]{1,0:T(8,128)(2,1)}, bf16[192,512]{1,0:T(8,128)(2,1)}, u32[]{:S(2)}, u32[]{:S(2)}) %collective-permute-start.6) | collective-permute-done | bytes 196640 | tf_op jit(solution)/shard_map/ppermute | solution.py:319
  87.5 1.0 copy-done.8
  88.5 1.0 shard_map.94.held_ref
  89.5 1.1 shard_map.95.held_ref
  90.7 1.1 shard_map.96.held_ref
  92.0 2.7 %shard_map.97 = (bf16[384,768]{1,0:T(8,128)(2,1)}, bf16[384,768]{1,0:T(8,128)(2,1)}, f32[8,8,128]{2,1,0:T(8,128)S(1)}) custom-call(f32[384,768]{1,0:T(8,128)S(1)} %shard_map.96.held_ref, bf16[384,512]{1,0:T(8,128)(2,1)S(1)} %bitcast.24, bf16[768,2048]{1,0:T(8,128)(2,1)S(1)} %bitcast.18, bf16[384,768]{1,0:T(8,128)(2,1)S(1)} %bitcast.20, ...), custom_call_target="tpu_custom_call" | custom-call | flops 301989888 | bytes 3538944 | tf_op jit(solution)/shard_map/pallas_call | solution.py:245
  94.7 10.7 %all_to_all.28.returned_ref = f32[8,8,128]{2,1,0:T(8,128)S(1)} all-to-all(f32[8,8,128]{2,1,0:T(8,128)S(1)} %get-tuple-element.50), channel_id=1, replica_groups=mesh['dp'=4,'expert'=8] {'expert'}, dimensions={0} | all-to-all | bytes 65536 | tf_op jit(solution)/shard_map/all_to_all | solution.py:334
  106.5 1.0 copy-done.14
  109.4 1.8 %shard_map.100.held_ref = f32[192,2048]{1,0:T(8,128)} custom-call(f32[192,512]{1,0:T(8,128)S(1)} %copy-done.14, bf16[192,512]{1,0:T(8,128)(2,1)S(1)} %copy-done.24, bf16[192,512]{1,0:T(8,128)(2,1)S(1)} %copy-done.26, bf16[192,512]{1,0:T(8,128)(2,1)} %collective-permute-done.2.refs_2_), custom_call_target="tpu_custom_call" | custom-call | flops 393216 | bytes 1376256 | tf_op jit(solution)/shard_map/pallas_call | solution.py:148
  111.1 2.0 %shard_map.102.held_ref = f32[192,2048]{1,0:T(8,128)} custom-call(f32[192,2048]{1,0:T(8,128)} %shard_map.100.held_ref, f32[192,512]{1,0:T(8,128)S(1)} %copy-done.18, bf16[192,512]{1,0:T(8,128)(2,1)} %collective-permute-done.3.refs_1_, bf16[192,512]{1,0:T(8,128)(2,1)} %collective-permute-done.4.refs_2_, ...), custom_call_target="tpu_custom_call", output_to_operand_aliasing={{}: (0, {})} | custom-call | flops 393216 | bytes 1376256 | tf_op jit(solution)/shard_map/pallas_call | solution.py:148
  113.2 2.0 %shard_map.104.held_ref = f32[192,2048]{1,0:T(8,128)} custom-call(f32[192,2048]{1,0:T(8,128)} %shard_map.102.held_ref, f32[192,512]{1,0:T(8,128)S(1)} %copy-done.16, bf16[192,512]{1,0:T(8,128)(2,1)} %collective-permute-done.6.refs_1_, bf16[192,512]{1,0:T(8,128)(2,1)} %collective-permute-done.7.refs_2_, ...), custom_call_target="tpu_custom_call", output_to_operand_aliasing={{}: (0, {})} | custom-call | flops 393216 | bytes 1376256 | tf_op jit(solution)/shard_map/pallas_call | solution.py:148
  115.2 1.9 %shard_map.106 = f32[192,2048]{1,0:T(8,128)} custom-call(f32[192,2048]{1,0:T(8,128)} %shard_map.104.held_ref, f32[192,512]{1,0:T(8,128)S(1)} %copy-done.20, bf16[192,512]{1,0:T(8,128)(2,1)} %collective-permute-done.9.refs_1_, bf16[192,512]{1,0:T(8,128)(2,1)} %collective-permute-done.10.refs_2_, ...), custom_call_target="tpu_custom_call", output_to_operand_aliasing={{}: (0, {})} | custom-call | flops 393216 | bytes 1376256 | tf_op jit(solution)/shard_map/pallas_call | solution.py:148
  (84 shorter events, 13.2 us)
Async XLA Ops:
  1.4 3.6 %copy-start.21 = (s32[128,2]{1,0:T(8,128)}, s32[128,2]{1,0:T(8,128)S(1)}, u32[]{:S(2)}) copy-start(s32[128,2]{1,0:T(8,128)S(1)} %copy.13.routes_ref) | copy-start | bytes 3076
  3.3 1.8 %copy-start.27 = (bf16[128,2]{1,0:T(8,128)(2,1)}, bf16[128,2]{1,0:T(8,128)(2,1)S(1)}, u32[]{:S(2)}) copy-start(bf16[128,2]{1,0:T(8,128)(2,1)S(1)} %copy.14.probs_ref) | copy-start | bytes 1540
  5.1 50.1 %copy-start.29 = (s32[128,2]{1,0:T(8,128)}, s32[128,2]{1,0:T(8,128)S(1)}, u32[]{:S(2)}) copy-start(s32[128,2]{1,0:T(8,128)S(1)} %get-tuple-element.51.slot_ref) | copy-start | bytes 3076
  5.1 53.5 %copy-start.1 = (bf16[1,1,8,48,768]{4,3,2,1,0:T(8,128)(2,1)S(1)}, bf16[1,1,8,48,768]{4,3,2,1,0:T(8,128)(2,1)}, u32[]{:S(2)}) copy-start(bf16[1,1,8,48,768]{4,3,2,1,0:T(8,128)(2,1)} %param.9) | copy-start | bytes 1769476
  5.1 53.5 %copy-start.3 = (bf16[1,1,8,48,768]{4,3,2,1,0:T(8,128)(2,1)S(1)}, bf16[1,1,8,48,768]{4,3,2,1,0:T(8,128)(2,1)}, u32[]{:S(2)}) copy-start(bf16[1,1,8,48,768]{4,3,2,1,0:T(8,128)(2,1)} %param.10) | copy-start | bytes 1769476
  23.9 35.4 %copy-start.7 = (bf16[8,48,512]{2,1,0:T(8,128)(2,1)}, bf16[8,48,512]{2,1,0:T(8,128)(2,1)S(1)}, u32[]{:S(2)}) copy-start(bf16[8,48,512]{2,1,0:T(8,128)(2,1)S(1)} %all_to_all.25) | copy-start | bytes 1179652
  55.1 22.1 %all-to-all-start.3 = ((bf16[8,48,512]{2,1,0:T(8,128)(2,1)}), bf16[8,48,512]{2,1,0:T(8,128)(2,1)S(1)}, u32[]{:S(2)}, u32[]{:S(2)}) async-start(bf16[8,48,512]{2,1,0:T(8,128)(2,1)} %bitcast.7), calls=%async_computation.3 | async-start | bytes 786432 | tf_op jit(solution)/shard_map/all_to_all | solution.py:309
  58.6 12.0 %copy-start.5 = (bf16[8,48,512]{2,1,0:T(8,128)(2,1)S(1)}, bf16[8,48,512]{2,1,0:T(8,128)(2,1)}, u32[]{:S(2)}) copy-start(bf16[8,48,512]{2,1,0:T(8,128)(2,1)} %all_to_all.27) | copy-start | bytes 1179652
  59.3 12.5 %copy-start.11 = (bf16[768,384]{1,0:T(8,128)(2,1)}, bf16[768,384]{1,0:T(8,128)(2,1)S(1)}, u32[]{:S(2)}) copy-start(bf16[768,384]{1,0:T(8,128)(2,1)S(1)} %shard_map.98.hidden_ref) | copy-start | bytes 1769476
  61.2 12.7 %collective-permute-start = (bf16[192,512]{1,0:T(8,128)(2,1)S(1)}, bf16[192,512]{1,0:T(8,128)(2,1)S(1)}, u32[]{:S(2)}, u32[]{:S(2)}) collective-permute-start(bf16[192,512]{1,0:T(8,128)(2,1)S(1)} %get-tuple-element.35), channel_id=1, source_target_pairs={{0,8},{8,0},{16,24},{24,16},{1,9},{9,1},{17,25},{25,17},{2,10},{10... | collective-permute-start | bytes 589832 | tf_op jit(solution)/shard_map/ppermute | solution.py:319
  62.7 12.3 %collective-permute-start.1 = (bf16[192,512]{1,0:T(8,128)(2,1)S(1)}, bf16[192,512]{1,0:T(8,128)(2,1)S(1)}, u32[]{:S(2)}, u32[]{:S(2)}) collective-permute-start(bf16[192,512]{1,0:T(8,128)(2,1)S(1)} %get-tuple-element.36), channel_id=1, source_target_pairs={{0,16},{8,24},{16,0},{24,8},{1,17},{9,25},{17,1},{25,9},{2,18},{10... | collective-permute-start | bytes 589832 | tf_op jit(solution)/shard_map/ppermute | solution.py:319
  64.2 15.9 %collective-permute-start.2 = (bf16[192,512]{1,0:T(8,128)(2,1)}, bf16[192,512]{1,0:T(8,128)(2,1)}, u32[]{:S(2)}, u32[]{:S(2)}) collective-permute-start(bf16[192,512]{1,0:T(8,128)(2,1)} %get-tuple-element.37), channel_id=1, source_target_pairs={{0,24},{8,16},{16,8},{24,0},{1,25},{9,17},{17,9},{25,1},{2,26},{10... | collective-permute-start | bytes 589832 | tf_op jit(solution)/shard_map/ppermute | solution.py:319
  65.7 21.8 %copy-start = (bf16[1,768,2048]{2,1,0:T(8,128)(2,1)S(1)}, bf16[1,768,2048]{2,1,0:T(8,128)(2,1)}, u32[]{:S(2)}) copy-start(bf16[1,768,2048]{2,1,0:T(8,128)(2,1)} %param.11) | copy-start | bytes 9437188
  67.6 14.1 %collective-permute-start.3 = (bf16[192,512]{1,0:T(8,128)(2,1)}, bf16[192,512]{1,0:T(8,128)(2,1)}, u32[]{:S(2)}, u32[]{:S(2)}) collective-permute-start(bf16[192,512]{1,0:T(8,128)(2,1)} %get-tuple-element.39), channel_id=1, source_target_pairs={{0,8},{8,0},{16,24},{24,16},{1,9},{9,1},{17,25},{25,17},{2,10},{10... | collective-permute-start | bytes 589832 | tf_op jit(solution)/shard_map/ppermute | solution.py:319
  69.1 13.0 %collective-permute-start.4 = (bf16[192,512]{1,0:T(8,128)(2,1)}, bf16[192,512]{1,0:T(8,128)(2,1)}, u32[]{:S(2)}, u32[]{:S(2)}) collective-permute-start(bf16[192,512]{1,0:T(8,128)(2,1)} %get-tuple-element.40), channel_id=1, source_target_pairs={{0,16},{8,24},{16,0},{24,8},{1,17},{9,25},{17,1},{25,9},{2,18},{10... | collective-permute-start | bytes 589832 | tf_op jit(solution)/shard_map/ppermute | solution.py:319
  74.5 9.5 %collective-permute-start.5 = (bf16[192,512]{1,0:T(8,128)(2,1)}, bf16[192,512]{1,0:T(8,128)(2,1)}, u32[]{:S(2)}, u32[]{:S(2)}) collective-permute-start(bf16[192,512]{1,0:T(8,128)(2,1)} %get-tuple-element.41), channel_id=1, source_target_pairs={{0,24},{8,16},{16,8},{24,0},{1,25},{9,17},{17,9},{25,1},{2,26},{10... | collective-permute-start | bytes 589832 | tf_op jit(solution)/shard_map/ppermute | solution.py:319
  75.7 11.2 %collective-permute-start.6 = (bf16[192,512]{1,0:T(8,128)(2,1)}, bf16[192,512]{1,0:T(8,128)(2,1)}, u32[]{:S(2)}, u32[]{:S(2)}) collective-permute-start(bf16[192,512]{1,0:T(8,128)(2,1)} %get-tuple-element.43), channel_id=1, source_target_pairs={{0,8},{8,0},{16,24},{24,16},{1,9},{9,1},{17,25},{25,17},{2,10},{10... | collective-permute-start | bytes 589832 | tf_op jit(solution)/shard_map/ppermute | solution.py:319
  77.2 1.1 copy-start.12
  80.2 33.0 %collective-permute-start.7 = (bf16[192,512]{1,0:T(8,128)(2,1)}, bf16[192,512]{1,0:T(8,128)(2,1)}, u32[]{:S(2)}, u32[]{:S(2)}) collective-permute-start(bf16[192,512]{1,0:T(8,128)(2,1)} %copy-done.33), channel_id=1, source_target_pairs={{0,16},{8,24},{16,0},{24,8},{1,17},{9,25},{17,1},{25,9},{2,18},{10... | collective-permute-start | bytes 589832 | tf_op jit(solution)/shard_map/ppermute | solution.py:319
  81.7 31.4 %collective-permute-start.8 = (bf16[192,512]{1,0:T(8,128)(2,1)}, bf16[192,512]{1,0:T(8,128)(2,1)}, u32[]{:S(2)}, u32[]{:S(2)}) collective-permute-start(bf16[192,512]{1,0:T(8,128)(2,1)} %copy-done.32), channel_id=1, source_target_pairs={{0,24},{8,16},{16,8},{24,0},{1,25},{9,17},{17,9},{25,1},{2,26},{10... | collective-permute-start | bytes 589832 | tf_op jit(solution)/shard_map/ppermute | solution.py:319
  82.2 33.0 %collective-permute-start.10 = (bf16[192,512]{1,0:T(8,128)(2,1)}, bf16[192,512]{1,0:T(8,128)(2,1)}, u32[]{:S(2)}, u32[]{:S(2)}) collective-permute-start(bf16[192,512]{1,0:T(8,128)(2,1)} %get-tuple-element.48), channel_id=1, source_target_pairs={{0,16},{8,24},{16,0},{24,8},{1,17},{9,25},{17,1},{25,9},{2,18},{10... | collective-permute-start | bytes 589832 | tf_op jit(solution)/shard_map/ppermute | solution.py:319
  84.1 31.1 %collective-permute-start.11 = (bf16[192,512]{1,0:T(8,128)(2,1)}, bf16[192,512]{1,0:T(8,128)(2,1)}, u32[]{:S(2)}, u32[]{:S(2)}) collective-permute-start(bf16[192,512]{1,0:T(8,128)(2,1)} %get-tuple-element.49), channel_id=1, source_target_pairs={{0,24},{8,16},{16,8},{24,0},{1,25},{9,17},{17,9},{25,1},{2,26},{10... | collective-permute-start | bytes 589832 | tf_op jit(solution)/shard_map/ppermute | solution.py:319
  86.9 28.3 %collective-permute-start.9 = (bf16[192,512]{1,0:T(8,128)(2,1)}, bf16[192,512]{1,0:T(8,128)(2,1)}, u32[]{:S(2)}, u32[]{:S(2)}) collective-permute-start(bf16[192,512]{1,0:T(8,128)(2,1)} %get-tuple-element.47), channel_id=1, source_target_pairs={{0,8},{8,0},{16,24},{24,16},{1,9},{9,1},{17,25},{25,17},{2,10},{10... | collective-permute-start | bytes 589832 | tf_op jit(solution)/shard_map/ppermute | solution.py:319
  89.5 1.2 copy-start.6
  90.7 1.2 copy-start.2
  90.7 1.2 %copy-start.4 = (bf16[1,1,8,48,768]{4,3,2,1,0:T(8,128)(2,1)S(1)}, bf16[1,1,8,48,768]{4,3,2,1,0:T(8,128)(2,1)}, u32[]{:S(2)}) copy-start(bf16[1,1,8,48,768]{4,3,2,1,0:T(8,128)(2,1)} %param.10) | copy-start | bytes 1769476
  92.0 13.4 %copy-start.22 = (s32[128,2]{1,0:T(8,128)S(1)}, s32[128,2]{1,0:T(8,128)}, u32[]{:S(2)}) copy-start(s32[128,2]{1,0:T(8,128)} %copy-done.21) | copy-start | bytes 3076
  92.0 13.4 %copy-start.28 = (bf16[128,2]{1,0:T(8,128)(2,1)S(1)}, bf16[128,2]{1,0:T(8,128)(2,1)}, u32[]{:S(2)}) copy-start(bf16[128,2]{1,0:T(8,128)(2,1)} %copy-done.27) | copy-start | bytes 1540
  92.0 13.4 %copy-start.30 = (s32[128,2]{1,0:T(8,128)S(1)}, s32[128,2]{1,0:T(8,128)}, u32[]{:S(2)}) copy-start(s32[128,2]{1,0:T(8,128)} %copy-done.29) | copy-start | bytes 3076
  94.7 16.5 %copy-start.18 = (f32[192,512]{1,0:T(8,128)S(1)}, f32[192,512]{1,0:T(8,128)}, u32[]{:S(2)}) copy-start(f32[192,512]{1,0:T(8,128)} %copy-done.17) | copy-start | bytes 1179652
  111.1 2.0 %copy-start.16 = (f32[192,512]{1,0:T(8,128)S(1)}, f32[192,512]{1,0:T(8,128)}, u32[]{:S(2)}) copy-start(f32[192,512]{1,0:T(8,128)} %copy-done.15) | copy-start | bytes 1179652
  113.1 2.0 %copy-start.20 = (f32[192,512]{1,0:T(8,128)S(1)}, f32[192,512]{1,0:T(8,128)}, u32[]{:S(2)}) copy-start(f32[192,512]{1,0:T(8,128)} %copy-done.19) | copy-start | bytes 1179652
  (15 other events, 12.7 us)

commit v2 on v1

v2 whole, which is shorter than its diff:
```python
import functools

import jax
import jax.numpy as jnp
from jax import lax
from jax.experimental import pallas as pl
from jax.experimental.pallas import tpu as pltpu
from jax.sharding import PartitionSpec as P

LANES = 128
CHUNKS = 4
VMEM_LIMIT = 10 * 1024 * 1024
VMEM = pl.BlockSpec(memory_space=pltpu.VMEM)
ANY = pl.BlockSpec(memory_space=pl.ANY)
SMEM = pl.BlockSpec(memory_space=pltpu.SMEM)


def params():
    return pltpu.CompilerParams(vmem_limit_bytes=VMEM_LIMIT)


def cost(flops, moved):
    return pl.CostEstimate(flops=flops, bytes_accessed=moved, transcendentals=0)


def silu_parts(gate_value):
    sigmoid = jax.nn.sigmoid(gate_value)
    return (gate_value * sigmoid, sigmoid * (1.0 + gate_value * (1.0 - sigmoid)))


def select_kernel(
    expert_count, capacity, place_ref, routes_ref, probs_ref, slot_ref, keep_ref, give_ref
):
    top_count, token_count = routes_ref.shape
    row_count = keep_ref.shape[0]
    names = [
        lax.bitwise_xor(routes_ref[k : k + 1, :], place_ref[0]) for k in range(top_count)
    ]
    experts = lax.broadcasted_iota(jnp.int32, (expert_count, token_count), 0)
    onehots = [(experts == name).astype(jnp.float32) for name in names]
    earlier = (
        lax.broadcasted_iota(jnp.int32, (token_count, token_count), 0)
        < lax.broadcasted_iota(jnp.int32, (token_count, token_count), 1)
    ).astype(jnp.bfloat16)
    before = jnp.dot(
        sum(onehots).astype(jnp.bfloat16), earlier, preferred_element_type=jnp.float32
    )
    slots = lax.broadcasted_iota(jnp.int32, (row_count, token_count), 0)
    keep = jnp.zeros((row_count, token_count), jnp.float32)
    give = jnp.zeros((row_count, token_count), jnp.float32)
    for k in range(top_count):
        slot = jnp.sum(before * onehots[k], axis=0, keepdims=True).astype(jnp.int32)
        before = before + onehots[k]
        slot_ref[k : k + 1, :] = slot
        prob = probs_ref[k : k + 1, :].astype(jnp.float32)
        row = lax.shift_right_logical(names[k], 1) * capacity + slot
        core = lax.bitwise_and(names[k], 1)
        keep = keep + jnp.where(slots == jnp.where(core == 0, row, -1), prob, 0.0)
        give = give + jnp.where(slots == jnp.where(core == 1, row, -1), prob, 0.0)
    keep_ref[...] = keep.astype(jnp.bfloat16)
    give_ref[...] = give.astype(jnp.bfloat16)


def select(place, routes, probs, expert_count, capacity):
    top_count, token_count = routes.shape
    row_count = expert_count // 2 * capacity
    matrix = jax.ShapeDtypeStruct((row_count, token_count), jnp.bfloat16)
    return pl.pallas_call(
        functools.partial(select_kernel, expert_count, capacity),
        in_specs=[SMEM, VMEM, VMEM],
        out_shape=[jax.ShapeDtypeStruct((top_count, token_count), jnp.int32), matrix, matrix],
        compiler_params=params(),
        cost_estimate=cost(20 * row_count * token_count, 8 * row_count * token_count),
    )(place, routes, probs)


def dispatch_kernel(
    capacity, start, width, later_count, keep_ref, own_ref, give_ref, other_ref, *refs
):
    block_refs = refs[later_count:]
    for half, (select_ref, rows_ref) in enumerate(((keep_ref, own_ref), (give_ref, other_ref))):
        rows = jnp.dot(
            select_ref[...],
            rows_ref[:, start : start + width],
            preferred_element_type=jnp.float32,
        ).astype(jnp.bfloat16)
        for step, block_ref in enumerate(block_refs):
            block_ref[half * capacity : (half + 1) * capacity, :] = rows[
                step * capacity : (step + 1) * capacity, :
            ]


def dispatch(keep, own, give, other, capacity, start, width, earlier):
    row_count, token_count = keep.shape
    return pl.pallas_call(
        functools.partial(dispatch_kernel, capacity, start, width, len(earlier)),
        in_specs=[VMEM] * 4 + [ANY] * len(earlier),
        out_shape=[jax.ShapeDtypeStruct((2 * capacity, width), jnp.bfloat16)]
        * (row_count // capacity),
        compiler_params=params(),
        cost_estimate=cost(
            4 * row_count * token_count * width, 4 * (row_count + token_count) * width
        ),
    )(keep, own, give, other, *earlier)


def hidden_kernel(gate_ref, up_ref, hidden_ref):
    activation, _ = silu_parts(gate_ref[...].astype(jnp.float32))
    hidden = activation * up_ref[...].astype(jnp.float32)
    hidden_ref[...] = hidden.T.astype(jnp.bfloat16)


def hidden_transposed(gate, up):
    row_count, hidden_width = gate.shape
    step = 2 * LANES
    return pl.pallas_call(
        hidden_kernel,
        grid=(hidden_width // step,),
        in_specs=[pl.BlockSpec((row_count, step), lambda i: (0, i))] * 2,
        out_specs=pl.BlockSpec((step, row_count), lambda i: (i, 0)),
        out_shape=jax.ShapeDtypeStruct((hidden_width, row_count), jnp.bfloat16),
        compiler_params=params(),
        cost_estimate=cost(20 * row_count * hidden_width, 6 * row_count * hidden_width),
    )(gate, up)


def panel_kernel(line_count, earlier_count, capacity, place_ref, hidden_ref, *refs):
    block_refs = refs[:line_count]
    rows_ref, own_ref, *sent_refs = refs[line_count + earlier_count :]
    group_count = len(sent_refs) + 1
    share = own_ref.shape[0]
    for step, block_ref in enumerate(block_refs):
        for half in range(2):
            source = lax.bitwise_xor(place_ref[0], 2 * step + half)
            start = pl.multiple_of(source * capacity, capacity)
            rows_ref[pl.ds(start, capacity), :] = block_ref[
                half * capacity : (half + 1) * capacity, :
            ]
    rows = rows_ref[...]
    for step in list(range(group_count - 1, -1, -1)):
        owner = lax.bitwise_xor(place_ref[1], step)
        start = pl.multiple_of(owner * share, share)
        part = jnp.dot(
            hidden_ref[pl.ds(start, share), :], rows, preferred_element_type=jnp.float32
        )
        if step == 0:
            own_ref[...] = part
        else:
            sent_refs[step - 1][...] = part.astype(jnp.bfloat16)


def panel_parts(place, hidden, blocks, group_count, earlier):
    hidden_width, row_count = hidden.shape
    width = blocks[0].shape[1]
    share = hidden_width // group_count
    return pl.pallas_call(
        functools.partial(panel_kernel, len(blocks), len(earlier), blocks[0].shape[0] // 2),
        in_specs=[SMEM, VMEM] + [VMEM] * len(blocks) + [ANY] * len(earlier),
        out_shape=[
            jax.ShapeDtypeStruct((row_count, width), jnp.bfloat16),
            jax.ShapeDtypeStruct((share, width), jnp.float32),
        ]
        + [jax.ShapeDtypeStruct((share, width), jnp.bfloat16)] * (group_count - 1),
        compiler_params=params(),
        cost_estimate=cost(
            2 * hidden_width * row_count * width, 2 * hidden_width * (row_count + width)
        ),
    )(place, hidden, *blocks, *earlier)


def total_kernel(own_ref, *refs):
    total = own_ref[...]
    for ref in refs[: len(refs) - 1]:
        total = total + ref[...].astype(jnp.float32)
    refs[-1][...] = total


def total_chunk(held, own, arrived, start, model_width):
    share, width = own.shape
    place = pl.BlockSpec((share, width), lambda i: (0, start // width))
    inputs = [own] + list(arrived)
    specs = [pl.BlockSpec((share, width), lambda i: (0, 0))] * len(inputs)
    kernel = total_kernel
    aliases = {}
    if held is not None:
        inputs = [held] + inputs
        specs = [pl.BlockSpec(memory_space=pl.ANY)] + specs
        aliases = {0: 0}

        def kernel(held_ref, *refs):
            total_kernel(*refs)

    return pl.pallas_call(
        kernel,
        grid=(1,),
        in_specs=specs,
        out_specs=place,
        out_shape=jax.ShapeDtypeStruct((share, model_width), jnp.float32),
        input_output_aliases=aliases,
        compiler_params=params(),
        cost_estimate=cost(4 * share * width, 14 * share * width),
    )(*inputs)


def rows_times_weight(rows_ref, weight_ref):
    return lax.dot_general(
        rows_ref[...],
        weight_ref[...],
        (((1,), (1,)), ((), ())),
        preferred_element_type=jnp.float32,
    )


def first_kernel(rows_ref, weight_ref, sum_ref):
    sum_ref[...] = rows_times_weight(rows_ref, weight_ref)


def middle_kernel(held_ref, rows_ref, weight_ref, sum_ref):
    sum_ref[...] = held_ref[...] + rows_times_weight(rows_ref, weight_ref)


def grad_hidden_step(held, rows, weight, start):
    row_count, width = rows.shape
    hidden_width = weight.shape[0]
    step = 2 * LANES
    block = pl.BlockSpec((row_count, step), lambda i: (0, i))
    specs = [
        pl.BlockSpec((row_count, width), lambda i: (0, 0)),
        pl.BlockSpec((step, width), lambda i: (i, start // width)),
    ]
    return pl.pallas_call(
        first_kernel if held is None else middle_kernel,
        grid=(hidden_width // step,),
        in_specs=specs if held is None else [block] + specs,
        out_specs=block,
        out_shape=jax.ShapeDtypeStruct((row_count, hidden_width), jnp.float32),
        compiler_params=params(),
        cost_estimate=cost(2 * row_count * hidden_width * width, 8 * row_count * hidden_width),
    )(*([rows, weight] if held is None else [held, rows, weight]))


def last_kernel(
    capacity,
    place_ref,
    held_ref,
    rows_ref,
    weight_ref,
    gate_ref,
    up_ref,
    grad_gate_ref,
    grad_up_ref,
    *refs,
):
    slot_refs, sum_ref = refs[:-1], refs[-1]
    grid_place = pl.program_id(0)
    grad_hidden = held_ref[...] + rows_times_weight(rows_ref, weight_ref)
    activation, gate_slope = silu_parts(gate_ref[...].astype(jnp.float32))
    up_value = up_ref[...].astype(jnp.float32)
    grad_up_ref[...] = (grad_hidden * activation).astype(jnp.bfloat16)
    grad_gate_ref[...] = (grad_hidden * up_value * gate_slope).astype(jnp.bfloat16)
    hidden = (activation * up_value).astype(jnp.bfloat16).astype(jnp.float32)
    product = hidden * grad_hidden
    folded = product[:, :LANES]
    for start in range(LANES, product.shape[1], LANES):
        folded = folded + product[:, start : start + LANES]

    @pl.when(grid_place == 0)
    def _():
        sum_ref[...] = folded

    @pl.when(grid_place > 0)
    def _():
        sum_ref[...] = sum_ref[...] + folded

    @pl.when(grid_place == pl.num_programs(0) - 1)
    def _():
        line = jnp.sum(sum_ref[...].T, axis=0, keepdims=True)
        for slot_ref in slot_refs:
            slot_ref[...] = jnp.zeros_like(slot_ref)
        for source in range(2 * len(slot_refs)):
            name = lax.bitwise_xor(place_ref[0], source)
            piece = line[:, source * capacity : (source + 1) * capacity]
            for step, slot_ref in enumerate(slot_refs):
                for half in range(2):

                    @pl.when(name == 2 * step + half)
                    def _(slot_ref=slot_ref, half=half, piece=piece):
                        slot_ref[half, 0:1, 0:capacity] = piece


def grad_hidden_last(place, held, rows, weight, start, gate, up, line_count, capacity):
    row_count, width = rows.shape
    hidden_width = weight.shape[0]
    step = 2 * LANES
    block = pl.BlockSpec((row_count, step), lambda i: (0, i))
    return pl.pallas_call(
        functools.partial(last_kernel, capacity),
        grid=(hidden_width // step,),
        in_specs=[
            SMEM,
            block,
            pl.BlockSpec((row_count, width), lambda i: (0, 0)),
            pl.BlockSpec((step, width), lambda i: (i, start // width)),
            block,
            block,
        ],
        out_specs=[block, block]
        + [pl.BlockSpec((2, 8, LANES), lambda i: (0, 0, 0))] * line_count,
        out_shape=[jax.ShapeDtypeStruct((row_count, hidden_width), jnp.bfloat16)] * 2
        + [jax.ShapeDtypeStruct((2, 8, LANES), jnp.float32)] * line_count,
        scratch_shapes=[pltpu.VMEM((row_count, LANES), jnp.float32)],
        compiler_params=params(),
        cost_estimate=cost(2 * row_count * hidden_width * width, 12 * row_count * hidden_width),
    )(place, held, rows, weight, gate, up)


def forward_kernel(*refs):
    for step, slot_ref in enumerate(refs[:-1]):
        refs[-1][step] = slot_ref[1]


def forward(slot_lines):
    return pl.pallas_call(
        forward_kernel,
        in_specs=[VMEM] * len(slot_lines),
        out_shape=jax.ShapeDtypeStruct((len(slot_lines), 8, LANES), jnp.float32),
        compiler_params=params(),
        cost_estimate=cost(1000, 40000),
    )(*slot_lines)


def route_kernel(line_count, place_ref, routes_ref, probs_ref, slot_ref, other_ref, *refs):
    line_refs, (out_ref, table_ref) = refs[:line_count], refs[line_count:]
    top_count, token_count = routes_ref.shape
    expert_count = 2 * line_count
    for step, line_ref in enumerate(line_refs):
        table_ref[2 * step : 2 * step + 1, :] = line_ref[0, 0:1, :]
        table_ref[2 * step + 1 : 2 * step + 2, :] = other_ref[step, 0:1, :]
    table = table_ref[...]
    slots = lax.broadcasted_iota(jnp.int32, (LANES, token_count), 0)
    experts = lax.broadcasted_iota(jnp.int32, (expert_count, token_count), 0)
    for k in range(top_count):
        chosen = (slots == slot_ref[k : k + 1, :]).astype(jnp.float32)
        spread = jnp.dot(
            table,
            chosen,
            preferred_element_type=jnp.float32,
            precision=lax.Precision.HIGHEST,
        )
        name = lax.bitwise_xor(routes_ref[k : k + 1, :], place_ref[0])
        picked = jnp.sum(jnp.where(experts == name, spread, 0.0), axis=0, keepdims=True)
        out_ref[k : k + 1, :] = picked / probs_ref[k : k + 1, :].astype(jnp.float32)


def route_back(place, routes, probs, slot, other, slot_lines):
    return pl.pallas_call(
        functools.partial(route_kernel, len(slot_lines)),
        in_specs=[SMEM] + [VMEM] * (4 + len(slot_lines)),
        out_shape=jax.ShapeDtypeStruct(routes.shape, jnp.float32),
        scratch_shapes=[pltpu.VMEM((2 * len(slot_lines), LANES), jnp.float32)],
        compiler_params=params(),
        cost_estimate=cost(1000000, 100000),
    )(place, routes, probs, slot, other, *slot_lines)


def swap(value, axis, offset):
    size = lax.axis_size(axis)
    return lax.ppermute(value, axis, [(place, place ^ offset) for place in range(size)])


def line_shards(grad_out, probs, routes, saved_gate, saved_up, w_down):
    expert_count = lax.axis_size("expert")
    group_count = lax.axis_size("dp")
    line_count = expert_count // 2
    capacity = saved_gate.shape[3]
    hidden_width = saved_gate.shape[4]
    model_width = grad_out.shape[1]
    row_count = expert_count * capacity
    width = model_width // CHUNKS
    starts = [chunk * width for chunk in range(CHUNKS)]

    place = jnp.stack([lax.axis_index("expert"), lax.axis_index("dp")]).astype(jnp.int32)
    other_tokens = swap(grad_out, "expert", 1)
    routes, probs = routes.T, probs.T
    slot, keep, give = select(place, routes, probs, expert_count, capacity)
    given = swap(give, "expert", 1)
    gate = saved_gate.reshape(row_count, hidden_width)
    up = saved_up.reshape(row_count, hidden_width)
    weight = w_down[0]
    hidden = hidden_transposed(gate, up)
    held = None
    panel = None
    all_rows, all_arrived = [], []
    for chunk, start in enumerate(starts):
        earlier = all_rows[chunk - 2 : chunk - 1] if chunk > 1 else []
        earlier = earlier + (all_arrived[chunk - 3] if chunk > 2 else [])
        blocks = list(
            dispatch(keep, grad_out, given, other_tokens, capacity, start, width, earlier)
        )
        for step in range(line_count - 1, 0, -1):
            blocks[step] = swap(blocks[step], "expert", 2 * step)
        earlier = all_arrived[chunk - 2] if chunk > 1 else []
        rows, own, *parts = panel_parts(place, hidden, blocks, group_count, earlier)
        arrived = [swap(part, "dp", step + 1) for step, part in enumerate(parts)]
        all_rows.append(rows)
        all_arrived.append(arrived)
        panel = total_chunk(panel, own, arrived, start, model_width)
        if chunk + 1 < CHUNKS:
            held = grad_hidden_step(held, rows, weight, start)
        else:
            grad_gate, grad_up, *slot_lines = grad_hidden_last(
                place, held, rows, weight, start, gate, up, line_count, capacity
            )
    for step in range(line_count - 1, 0, -1):
        slot_lines[step] = swap(slot_lines[step], "expert", 2 * step)
    other = swap(forward(slot_lines), "expert", 1)
    route_grad = route_back(place, routes, probs, slot, other, slot_lines)
    return (
        grad_gate.reshape(saved_gate.shape),
        grad_up.reshape(saved_up.shape),
        panel[None],
        route_grad.T,
    )


def plain_shards(grad_out, probs, routes, saved_gate, saved_up, w_down):
    expert_count = lax.axis_size("expert")
    capacity = saved_gate.shape[3]
    hidden_width = saved_gate.shape[4]
    token_count, top_count = routes.shape
    model_width = grad_out.shape[1]
    row_count = expert_count * capacity
    flat_routes = routes.reshape(-1)
    onehot = (flat_routes[:, None] == jnp.arange(expert_count)[None, :]).astype(jnp.int32)
    before = jnp.cumsum(onehot, axis=0) - onehot
    position = flat_routes * capacity + jnp.sum(before * onehot, axis=1)
    selector = jnp.arange(row_count)[:, None] == position[None, :]
    selector = jnp.where(selector, probs.reshape(-1)[None], 0).reshape(
        row_count, token_count, top_count
    )
    sent = jnp.dot(jnp.sum(selector, axis=2), grad_out, preferred_element_type=jnp.float32)
    rows = lax.all_to_all(
        sent.astype(jnp.bfloat16).reshape(expert_count, capacity, model_width),
        "expert",
        split_axis=0,
        concat_axis=0,
        tiled=True,
    ).reshape(row_count, model_width)
    up_value = saved_up.reshape(row_count, hidden_width).astype(jnp.float32)
    activation, gate_slope = silu_parts(
        saved_gate.reshape(row_count, hidden_width).astype(jnp.float32)
    )
    hidden = (activation * up_value).astype(jnp.bfloat16)
    grad_hidden = lax.dot_general(
        rows, w_down[0], (((1,), (1,)), ((), ())), preferred_element_type=jnp.float32
    )
    slot_grad = jnp.sum(hidden.astype(jnp.float32) * grad_hidden, axis=1)
    grad_up = (grad_hidden * activation).astype(jnp.bfloat16)
    grad_gate = (grad_hidden * up_value * gate_slope).astype(jnp.bfloat16)
    whole_panel = lax.dot_general(
        hidden, rows, (((0,), (0,)), ((), ())), preferred_element_type=jnp.float32
    )
    panel = lax.psum_scatter(whole_panel, "dp", scatter_dimension=0, tiled=True)
    returned = lax.all_to_all(
        slot_grad.reshape(expert_count, capacity), "expert", split_axis=0, concat_axis=0, tiled=True
    )
    route_grad = jnp.take(returned.reshape(-1), position, axis=0).reshape(token_count, top_count)
    return (
        grad_gate.reshape(saved_gate.shape),
        grad_up.reshape(saved_up.shape),
        panel[None],
        route_grad / probs.astype(jnp.float32),
    )


def shards(grad_out, probs, routes, saved_gate, saved_up, w_down):
    expert_count = lax.axis_size("expert")
    group_count = lax.axis_size("dp")
    capacity, hidden_width = saved_gate.shape[3:]
    aligned = (
        expert_count & (expert_count - 1) == 0
        and group_count & (group_count - 1) == 0
        and capacity % 16 == 0
        and capacity <= LANES
        and hidden_width % (16 * group_count) == 0
        and routes.shape[0] % LANES == 0
    )
    run = line_shards if aligned else plain_shards
    return run(grad_out, probs, routes, saved_gate, saved_up, w_down)


def solution(mesh):
    return jax.shard_map(
        shards,
        mesh=mesh,
        in_specs=(
            P(("dp", "expert"), None),
            P(("dp", "expert"), None),
            P(("dp", "expert"), None),
            P("dp", "expert", None, None, None),
            P("dp", "expert", None, None, None),
            P("expert", None, None),
        ),
        out_specs=(
            P("dp", "expert", None, None, None),
            P("dp", "expert", None, None, None),
            P("expert", "dp", None),
            P(("dp", "expert"), None),
        ),
        check_vma=False,
    )
```

time: 118 us -> 89.4 us (0.76)
  blocking collectives: 60.7 us -> 0 us
  starting transfers between devices: 17.5 us -> 43.2 us
  waiting for transfers between devices: 1.79 us -> 24.2 us
  local copies, waits for them, and re-layouts: 15.1 us -> 2.4 us
  Pallas kernels: 21.2 us -> 18.5 us
    all_to_all x4 -> x0, blocking collectives: 60.7 us -> none  [the longest x3 50 us: shards(): lax.all_to_all(sent[chunk].reshape(expert_count, capacity, width), 'exper...]
    ppermute x12 -> x30, starting transfers between devices: 14 us -> 43.2 us  [swap(): lax.ppermute(value, axis, [(place, place ^ offset) for place in range(siz...]
    ppermute x12 -> x30, waiting for transfers between devices: 1.78 us -> 24.2 us  [swap(): lax.ppermute(value, axis, [(place, place ^ offset) for place in range(siz...]
    unnamed x71 -> x18, local copies, waits for them, and re-layouts: 15.1 us -> 2.4 us
    pallas_call x4, Pallas kernels: 7.68 us -> 3.33 us  [total_chunk(): pl.pallas_call(kernel, grid=(1,), in_specs=specs, out_specs=place, out_sh...]
    all_to_all x1 -> x0, starting transfers between devices: 3.45 us -> none  [shards(): lax.all_to_all(sent[chunk].reshape(expert_count, capacity, width), 'exper...]
    pallas_call x6 -> x11, Pallas kernels: 6.87 us -> 7.61 us  [the longest x4 4.54 us: panel_parts(): pl.pallas_call(functools.partial(panel_kernel, len(blocks), len(earlier),...]
  transfers between devices with their start and end apart: 13 -> 30, of which waited for: 1 -> 10; matrix products, arithmetic and copies ran while one was open for 1% -> 0% of each run, Pallas kernels for 15% -> 20%
where the time goes in v2:
time: 89.4 us; the launch traced here: 89.2 us
  starting transfers between devices  43.2 us (48%)
  waiting for transfers between devices  24.2 us (27%)
  Pallas kernels  18.5 us (21%)
  local copies, waits for them, and re-layouts  2.4 us (3%)
    ppermute x30, starting transfers between devices, swap(): lax.ppermute(value, axis, [(place, place ^ offset) for place in range(siz...  43.2 us
    ppermute x30, waiting for transfers between devices, swap(): lax.ppermute(value, axis, [(place, place ^ offset) for place in range(siz...  24.2 us
    pallas_call x4, Pallas kernels, panel_parts(): pl.pallas_call(functools.partial(panel_kernel, len(blocks), len(earlier),...  4.54 us
    pallas_call x1, Pallas kernels, grad_hidden_last(): pl.pallas_call(functools.partial(last_kernel, capacity), grid=(hidden_wid...  3.65 us
    pallas_call x4, Pallas kernels, total_chunk(): pl.pallas_call(kernel, grid=(1,), in_specs=specs, out_specs=place, out_sh...  3.33 us
    pallas_call x3, Pallas kernels, grad_hidden_step(): pl.pallas_call(first_kernel if held is None else middle_kernel, grid=(hid...  3.28 us
    unnamed x18, local copies, waits for them, and re-layouts  2.4 us
  transfers between devices with their start and end apart: 30, of which 10 were waited for; matrix products, arithmetic and copies ran while one was open for 0% of the time, Pallas kernels for 20%

profile of v2, /device:TPU:0, one launch (start us, length us, event | category | flops | bytes accessed | tf_op | source)
XLA Modules:
  0.0 89.2 jit_solution(12856282876178800238)
XLA Ops:
  3.4 1.2 %collective-permute-done.give_ref = bf16[192,128]{1,0:T(8,128)(2,1)S(1)} collective-permute-done((bf16[192,128]{1,0:T(8,128)(2,1)S(1)}, bf16[192,128]{1,0:T(8,128)(2,1)S(1)}, u32[]{:S(2)}, u32[]{:S(2)}) %collective-permute-start) | collective-permute-done | bytes 49184 | tf_op jit(solution)/shard_map/ppermute | solution.py:368
  5.9 2.8 %collective-permute-start.2 = (bf16[96,512]{1,0:T(8,128)(2,1)S(1)}, bf16[96,512]{1,0:T(8,128)(2,1)S(1)}, u32[]{:S(2)}, u32[]{:S(2)}) collective-permute-start(bf16[96,512]{1,0:T(8,128)(2,1)S(1)} %get-tuple-element.52), channel_id=1, source_target_pairs={{0,2},{1,3},{2,0},{3,1},{4,6},{5,7},{6,4},{7,5},{8,10},{9,11},{10,... | collective-permute-start | bytes 294920 | tf_op jit(solution)/shard_map/ppermute | solution.py:368
  8.7 2.6 %collective-permute-start.3 = (bf16[96,512]{1,0:T(8,128)(2,1)S(1)}, bf16[96,512]{1,0:T(8,128)(2,1)S(1)}, u32[]{:S(2)}, u32[]{:S(2)}) collective-permute-start(bf16[96,512]{1,0:T(8,128)(2,1)S(1)} %get-tuple-element.53), channel_id=1, source_target_pairs={{0,4},{1,5},{2,6},{3,7},{4,0},{5,1},{6,2},{7,3},{8,12},{9,13},{10,... | collective-permute-start | bytes 294920 | tf_op jit(solution)/shard_map/ppermute | solution.py:368
  12.5 3.5 %collective-permute-start.6 = (bf16[96,512]{1,0:T(8,128)(2,1)S(1)}, bf16[96,512]{1,0:T(8,128)(2,1)S(1)}, u32[]{:S(2)}, u32[]{:S(2)}) collective-permute-start(bf16[96,512]{1,0:T(8,128)(2,1)S(1)} %get-tuple-element.58), channel_id=1, source_target_pairs={{0,4},{1,5},{2,6},{3,7},{4,0},{5,1},{6,2},{7,3},{8,12},{9,13},{10,... | collective-permute-start | bytes 294920 | tf_op jit(solution)/shard_map/ppermute | solution.py:368
  16.9 2.5 %collective-permute-done.3.refs_2_ = bf16[96,512]{1,0:T(8,128)(2,1)S(1)} collective-permute-done((bf16[96,512]{1,0:T(8,128)(2,1)S(1)}, bf16[96,512]{1,0:T(8,128)(2,1)S(1)}, u32[]{:S(2)}, u32[]{:S(2)}) %collective-permute-start.3) | collective-permute-done | bytes 98336 | tf_op jit(solution)/shard_map/ppermute | solution.py:368
  19.4 1.1 %shard_map.96 = (bf16[384,512]{1,0:T(8,128)(2,1)S(1)}, f32[192,512]{1,0:T(8,128)S(1)}, bf16[192,512]{1,0:T(8,128)(2,1)S(1)}, bf16[192,512]{1,0:T(8,128)(2,1)S(1)}, bf16[192,512]{1,0:T(8,128)(2,1)S(1)}) custom-call(s32[2]{0:T(128)S(1)} %pad_add_fusion.place_ref, bf16[768,384]{1,0:T(8,128)(2,1)S(1)} %shard_map.93.hidden_ref, ...), custom_call_target="tpu_custom_call" | custom-call | flops 301989888 | bytes 1376256 | tf_op jit(solution)/shard_map/pallas_call | solution.py:156
  20.8 7.0 %collective-permute-start.8 = (bf16[96,512]{1,0:T(8,128)(2,1)S(1)}, bf16[96,512]{1,0:T(8,128)(2,1)S(1)}, u32[]{:S(2)}, u32[]{:S(2)}) collective-permute-start(bf16[96,512]{1,0:T(8,128)(2,1)S(1)} %get-tuple-element.62), channel_id=1, source_target_pairs={{0,2},{1,3},{2,0},{3,1},{4,6},{5,7},{6,4},{7,5},{8,10},{9,11},{10,... | collective-permute-start | bytes 294920 | tf_op jit(solution)/shard_map/ppermute | solution.py:368
  27.8 1.5 %collective-permute-start.11 = (bf16[192,512]{1,0:T(8,128)(2,1)S(1)}, bf16[192,512]{1,0:T(8,128)(2,1)S(1)}, u32[]{:S(2)}, u32[]{:S(2)}) collective-permute-start(bf16[192,512]{1,0:T(8,128)(2,1)S(1)} %get-tuple-element.65), channel_id=1, source_target_pairs={{0,8},{8,0},{16,24},{24,16},{1,9},{9,1},{17,25},{25,17},{2,10},{10... | collective-permute-start | bytes 589832 | tf_op jit(solution)/shard_map/ppermute | solution.py:368
  29.3 1.2 %collective-permute-start.9 = (bf16[96,512]{1,0:T(8,128)(2,1)S(1)}, bf16[96,512]{1,0:T(8,128)(2,1)S(1)}, u32[]{:S(2)}, u32[]{:S(2)}) collective-permute-start(bf16[96,512]{1,0:T(8,128)(2,1)S(1)} %get-tuple-element.63), channel_id=1, source_target_pairs={{0,4},{1,5},{2,6},{3,7},{4,0},{5,1},{6,2},{7,3},{8,12},{9,13},{10,... | collective-permute-start | bytes 294920 | tf_op jit(solution)/shard_map/ppermute | solution.py:368
  30.5 1.5 %collective-permute-start.10 = (bf16[96,512]{1,0:T(8,128)(2,1)S(1)}, bf16[96,512]{1,0:T(8,128)(2,1)S(1)}, u32[]{:S(2)}, u32[]{:S(2)}) collective-permute-start(bf16[96,512]{1,0:T(8,128)(2,1)S(1)} %get-tuple-element.64), channel_id=1, source_target_pairs={{0,6},{1,7},{2,4},{3,5},{4,2},{5,3},{6,0},{7,1},{8,14},{9,15},{10,... | collective-permute-start | bytes 294920 | tf_op jit(solution)/shard_map/ppermute | solution.py:368
  31.9 1.5 %collective-permute-start.12 = (bf16[192,512]{1,0:T(8,128)(2,1)S(1)}, bf16[192,512]{1,0:T(8,128)(2,1)S(1)}, u32[]{:S(2)}, u32[]{:S(2)}) collective-permute-start(bf16[192,512]{1,0:T(8,128)(2,1)S(1)} %get-tuple-element.66), channel_id=1, source_target_pairs={{0,16},{8,24},{16,0},{24,8},{1,17},{9,25},{17,1},{25,9},{2,18},{10... | collective-permute-start | bytes 589832 | tf_op jit(solution)/shard_map/ppermute | solution.py:368
  33.9 1.1 %shard_map.99 = (bf16[384,512]{1,0:T(8,128)(2,1)S(1)}, f32[192,512]{1,0:T(8,128)S(1)}, bf16[192,512]{1,0:T(8,128)(2,1)S(1)}, bf16[192,512]{1,0:T(8,128)(2,1)S(1)}, bf16[192,512]{1,0:T(8,128)(2,1)S(1)}) custom-call(s32[2]{0:T(128)S(1)} %pad_add_fusion.place_ref, bf16[768,384]{1,0:T(8,128)(2,1)S(1)} %shard_map.93.hidden_ref, ...), custom_call_target="tpu_custom_call" | custom-call | flops 301989888 | bytes 1376256 | tf_op jit(solution)/shard_map/pallas_call | solution.py:156
  35.1 2.2 %collective-permute-done.9.refs_2_ = bf16[96,512]{1,0:T(8,128)(2,1)S(1)} collective-permute-done((bf16[96,512]{1,0:T(8,128)(2,1)S(1)}, bf16[96,512]{1,0:T(8,128)(2,1)S(1)}, u32[]{:S(2)}, u32[]{:S(2)}) %collective-permute-start.9) | collective-permute-done | bytes 98336 | tf_op jit(solution)/shard_map/ppermute | solution.py:368
  38.1 1.5 %collective-permute-start.18 = (bf16[192,512]{1,0:T(8,128)(2,1)S(1)}, bf16[192,512]{1,0:T(8,128)(2,1)S(1)}, u32[]{:S(2)}, u32[]{:S(2)}) collective-permute-start(bf16[192,512]{1,0:T(8,128)(2,1)S(1)} %get-tuple-element.74), channel_id=1, source_target_pairs={{0,16},{8,24},{16,0},{24,8},{1,17},{9,25},{17,1},{25,9},{2,18},{10... | collective-permute-start | bytes 589832 | tf_op jit(solution)/shard_map/ppermute | solution.py:368
  40.7 3.6 %collective-permute-done.12.refs_5_.refs_2_.refs_1_ = bf16[192,512]{1,0:T(8,128)(2,1)S(1)} collective-permute-done((bf16[192,512]{1,0:T(8,128)(2,1)S(1)}, bf16[192,512]{1,0:T(8,128)(2,1)S(1)}, u32[]{:S(2)}, u32[]{:S(2)}) %collective-permute-start.12) | collective-permute-done | bytes 196640 | tf_op jit(solution)/shard_map/ppermute | solution.py:368
  44.3 1.1 %shard_map.102 = (bf16[384,512]{1,0:T(8,128)(2,1)S(1)}, f32[192,512]{1,0:T(8,128)S(1)}, bf16[192,512]{1,0:T(8,128)(2,1)S(1)}, bf16[192,512]{1,0:T(8,128)(2,1)S(1)}, bf16[192,512]{1,0:T(8,128)(2,1)S(1)}) custom-call(s32[2]{0:T(128)S(1)} %pad_add_fusion.place_ref, bf16[768,384]{1,0:T(8,128)(2,1)S(1)} %shard_map.93.hidden_ref, ...), custom_call_target="tpu_custom_call" | custom-call | flops 301989888 | bytes 1376256 | tf_op jit(solution)/shard_map/pallas_call | solution.py:156
  46.0 3.6 %collective-permute-start.15 = (bf16[96,512]{1,0:T(8,128)(2,1)S(1)}, bf16[96,512]{1,0:T(8,128)(2,1)S(1)}, u32[]{:S(2)}, u32[]{:S(2)}) collective-permute-start(bf16[96,512]{1,0:T(8,128)(2,1)S(1)} %get-tuple-element.71), channel_id=1, source_target_pairs={{0,4},{1,5},{2,6},{3,7},{4,0},{5,1},{6,2},{7,3},{8,12},{9,13},{10,... | collective-permute-start | bytes 294920 | tf_op jit(solution)/shard_map/ppermute | solution.py:368
  51.4 1.1 %shard_map.100.held_ref = f32[384,768]{1,0:T(8,128)S(1)} custom-call(f32[384,768]{1,0:T(8,128)S(1)} %shard_map.97.held_ref, bf16[384,512]{1,0:T(8,128)(2,1)S(1)} %get-tuple-element.60.rows_ref.refs_0_, bf16[768,2048]{1,0:T(8,128)(2,1)S(1)} %bitcast.12), custom_call_target="tpu_custom_call" | custom-call | flops 301989888 | bytes 2359296 | tf_op jit(solution)/shard_map/pallas_call | solution.py:231
  52.5 1.1 %shard_map.103.held_ref = f32[384,768]{1,0:T(8,128)S(1)} custom-call(f32[384,768]{1,0:T(8,128)S(1)} %shard_map.100.held_ref, bf16[384,512]{1,0:T(8,128)(2,1)S(1)} %get-tuple-element.68.rows_ref, bf16[768,2048]{1,0:T(8,128)(2,1)S(1)} %bitcast.13), custom_call_target="tpu_custom_call" | custom-call | flops 301989888 | bytes 2359296 | tf_op jit(solution)/shard_map/pallas_call | solution.py:231
  53.7 2.3 %collective-permute-done.16.refs_3_ = bf16[96,512]{1,0:T(8,128)(2,1)S(1)} collective-permute-done((bf16[96,512]{1,0:T(8,128)(2,1)S(1)}, bf16[96,512]{1,0:T(8,128)(2,1)S(1)}, u32[]{:S(2)}, u32[]{:S(2)}) %collective-permute-start.16) | collective-permute-done | bytes 98336 | tf_op jit(solution)/shard_map/ppermute | solution.py:368
  56.0 1.1 %shard_map.105 = (bf16[384,512]{1,0:T(8,128)(2,1)S(1)}, f32[192,512]{1,0:T(8,128)S(1)}, bf16[192,512]{1,0:T(8,128)(2,1)S(1)}, bf16[192,512]{1,0:T(8,128)(2,1)S(1)}, bf16[192,512]{1,0:T(8,128)(2,1)S(1)}) custom-call(s32[2]{0:T(128)S(1)} %pad_add_fusion.place_ref, bf16[768,384]{1,0:T(8,128)(2,1)S(1)} %shard_map.93.hidden_ref, ...), custom_call_target="tpu_custom_call" | custom-call | flops 301989888 | bytes 1376256 | tf_op jit(solution)/shard_map/pallas_call | solution.py:156
  57.1 3.7 %shard_map.106 = (bf16[384,768]{1,0:T(8,128)(2,1)}, bf16[384,768]{1,0:T(8,128)(2,1)}, f32[2,8,128]{2,1,0:T(8,128)S(1)}, f32[2,8,128]{2,1,0:T(8,128)S(1)}, f32[2,...) custom-call(s32[2]{0:T(128)S(1)} %pad_add_fusion.place_ref, f32[384,768]{1,0:T(8,128)S(1)} %shard_map.103.held_ref, ...), custom_call_target="tpu_custom_call" | custom-call | flops 301989888 | bytes 3538944 | tf_op jit(solution)/shard_map/pallas_call | solution.py:296
  60.8 1.7 %collective-permute-start.27 = (f32[2,8,128]{2,1,0:T(8,128)S(1)}, f32[2,8,128]{2,1,0:T(8,128)S(1)}, u32[]{:S(2)}, u32[]{:S(2)}) collective-permute-start(f32[2,8,128]{2,1,0:T(8,128)S(1)} %get-tuple-element.92), channel_id=1, source_target_pairs={{0,4},{1,5},{2,6},{3,7},{4,0},{5,1},{6,2},{7,3},{8,12},{9,13},{10,... | collective-permute-start | bytes 24584 | tf_op jit(solution)/shard_map/ppermute | solution.py:368
  62.5 2.6 %collective-permute-start.28 = (f32[2,8,128]{2,1,0:T(8,128)S(1)}, f32[2,8,128]{2,1,0:T(8,128)S(1)}, u32[]{:S(2)}, u32[]{:S(2)}) collective-permute-start(f32[2,8,128]{2,1,0:T(8,128)S(1)} %get-tuple-element.93), channel_id=1, source_target_pairs={{0,6},{1,7},{2,4},{3,5},{4,2},{5,3},{6,0},{7,1},{8,14},{9,15},{10,... | collective-permute-start | bytes 24584 | tf_op jit(solution)/shard_map/ppermute | solution.py:368
  65.3 2.6 %collective-permute-done.28.refs_3_ = f32[2,8,128]{2,1,0:T(8,128)S(1)} collective-permute-done((f32[2,8,128]{2,1,0:T(8,128)S(1)}, f32[2,8,128]{2,1,0:T(8,128)S(1)}, u32[]{:S(2)}, u32[]{:S(2)}) %collective-permute-start.28) | collective-permute-done | bytes 8224 | tf_op jit(solution)/shard_map/ppermute | solution.py:368
  68.0 2.2 %collective-permute-start.21 = (bf16[192,512]{1,0:T(8,128)(2,1)S(1)}, bf16[192,512]{1,0:T(8,128)(2,1)S(1)}, u32[]{:S(2)}, u32[]{:S(2)}) collective-permute-start(bf16[192,512]{1,0:T(8,128)(2,1)S(1)} %get-tuple-element.83), channel_id=1, source_target_pairs={{0,16},{8,24},{16,0},{24,8},{1,17},{9,25},{17,1},{25,9},{2,18},{10... | collective-permute-start | bytes 589832 | tf_op jit(solution)/shard_map/ppermute | solution.py:368
  70.1 1.3 %collective-permute-start.22 = (bf16[192,512]{1,0:T(8,128)(2,1)S(1)}, bf16[192,512]{1,0:T(8,128)(2,1)S(1)}, u32[]{:S(2)}, u32[]{:S(2)}) collective-permute-start(bf16[192,512]{1,0:T(8,128)(2,1)S(1)} %get-tuple-element.84), channel_id=1, source_target_pairs={{0,24},{8,16},{16,8},{24,0},{1,25},{9,17},{17,9},{25,1},{2,26},{10... | collective-permute-start | bytes 589832 | tf_op jit(solution)/shard_map/ppermute | solution.py:368
  71.7 2.0 %collective-permute-start.24 = (bf16[192,512]{1,0:T(8,128)(2,1)S(1)}, bf16[192,512]{1,0:T(8,128)(2,1)S(1)}, u32[]{:S(2)}, u32[]{:S(2)}) collective-permute-start(bf16[192,512]{1,0:T(8,128)(2,1)S(1)} %get-tuple-element.87), channel_id=1, source_target_pairs={{0,16},{8,24},{16,0},{24,8},{1,17},{9,25},{17,1},{25,9},{2,18},{10... | collective-permute-start | bytes 589832 | tf_op jit(solution)/shard_map/ppermute | solution.py:368
  73.6 1.3 %collective-permute-start.25 = (bf16[192,512]{1,0:T(8,128)(2,1)S(1)}, bf16[192,512]{1,0:T(8,128)(2,1)S(1)}, u32[]{:S(2)}, u32[]{:S(2)}) collective-permute-start(bf16[192,512]{1,0:T(8,128)(2,1)S(1)} %get-tuple-element.88), channel_id=1, source_target_pairs={{0,24},{8,16},{16,8},{24,0},{1,25},{9,17},{17,9},{25,1},{2,26},{10... | collective-permute-start | bytes 589832 | tf_op jit(solution)/shard_map/ppermute | solution.py:368
  76.6 1.3 %shard_map.112 = f32[2,128]{1,0:T(2,128)} custom-call(s32[2]{0:T(128)S(1)} %pad_add_fusion.place_ref, s32[2,128]{1,0:T(2,128)S(1)} %bitcast.20, bf16[2,128]{1,0:T(2,128)(2,1)S(1)} %bitcast.22, s32[2,128]{1,0:T(2,128)S(1)} %get-tuple-element.89.slot_ref, f32[4,8,128]{2,1,0:T(8,128)S(1)} %collective-permute-done.29.other_ref, ...), custom_call_target="tpu_custom_call" | custom-call | flops 1000000 | bytes 100000 | tf_op jit(solution)/shard_map/pallas_call | solution.py:356
  77.9 2.2 %collective-permute-done.21.refs_2_ = bf16[192,512]{1,0:T(8,128)(2,1)S(1)} collective-permute-done((bf16[192,512]{1,0:T(8,128)(2,1)S(1)}, bf16[192,512]{1,0:T(8,128)(2,1)S(1)}, u32[]{:S(2)}, u32[]{:S(2)}) %collective-permute-start.21) | collective-permute-done | bytes 196640 | tf_op jit(solution)/shard_map/ppermute | solution.py:368
  81.6 6.7 %collective-permute-done.24.refs_2_ = bf16[192,512]{1,0:T(8,128)(2,1)S(1)} collective-permute-done((bf16[192,512]{1,0:T(8,128)(2,1)S(1)}, bf16[192,512]{1,0:T(8,128)(2,1)S(1)}, u32[]{:S(2)}, u32[]{:S(2)}) %collective-permute-start.24) | collective-permute-done | bytes 196640 | tf_op jit(solution)/shard_map/ppermute | solution.py:368
  (67 shorter events, 15.5 us)
Async XLA Ops:
  0.6 4.0 %collective-permute-start.1 = (bf16[128,2048]{1,0:T(8,128)(2,1)}, bf16[128,2048]{1,0:T(8,128)(2,1)S(1)}, u32[]{:S(2)}, u32[]{:S(2)}) collective-permute-start(bf16[128,2048]{1,0:T(8,128)(2,1)} %own_ref.7), channel_id=1, source_target_pairs={{0,1},{1,0},{2,3},{3,2},{4,5},{5,4},{6,7},{7,6},{8,9},{9,8},{10,11... | collective-permute-start | bytes 1572872 | tf_op jit(solution)/shard_map/ppermute | solution.py:368
  3.3 1.3 %collective-permute-start = (bf16[192,128]{1,0:T(8,128)(2,1)S(1)}, bf16[192,128]{1,0:T(8,128)(2,1)S(1)}, u32[]{:S(2)}, u32[]{:S(2)}) collective-permute-start(bf16[192,128]{1,0:T(8,128)(2,1)S(1)} %get-tuple-element.50), channel_id=1, source_target_pairs={{0,1},{1,0},{2,3},{3,2},{4,5},{5,4},{6,7},{7,6},{8,9},{9,8},{10,11... | collective-permute-start | bytes 147464 | tf_op jit(solution)/shard_map/ppermute | solution.py:368
  5.7 10.4 %copy-start.3 = (bf16[1,1,8,48,768]{4,3,2,1,0:T(8,128)(2,1)S(1)}, bf16[1,1,8,48,768]{4,3,2,1,0:T(8,128)(2,1)}, u32[]{:S(2)}) copy-start(bf16[1,1,8,48,768]{4,3,2,1,0:T(8,128)(2,1)} %param.9) | copy-start | bytes 1769476
  5.7 10.4 %copy-start.4 = (bf16[1,1,8,48,768]{4,3,2,1,0:T(8,128)(2,1)S(1)}, bf16[1,1,8,48,768]{4,3,2,1,0:T(8,128)(2,1)}, u32[]{:S(2)}) copy-start(bf16[1,1,8,48,768]{4,3,2,1,0:T(8,128)(2,1)} %param.10) | copy-start | bytes 1769476
  5.9 10.8 %collective-permute-start.2 = (bf16[96,512]{1,0:T(8,128)(2,1)S(1)}, bf16[96,512]{1,0:T(8,128)(2,1)S(1)}, u32[]{:S(2)}, u32[]{:S(2)}) collective-permute-start(bf16[96,512]{1,0:T(8,128)(2,1)S(1)} %get-tuple-element.52), channel_id=1, source_target_pairs={{0,2},{1,3},{2,0},{3,1},{4,6},{5,7},{6,4},{7,5},{8,10},{9,11},{10,... | collective-permute-start | bytes 294920 | tf_op jit(solution)/shard_map/ppermute | solution.py:368
  8.7 10.7 %collective-permute-start.3 = (bf16[96,512]{1,0:T(8,128)(2,1)S(1)}, bf16[96,512]{1,0:T(8,128)(2,1)S(1)}, u32[]{:S(2)}, u32[]{:S(2)}) collective-permute-start(bf16[96,512]{1,0:T(8,128)(2,1)S(1)} %get-tuple-element.53), channel_id=1, source_target_pairs={{0,4},{1,5},{2,6},{3,7},{4,0},{5,1},{6,2},{7,3},{8,12},{9,13},{10,... | collective-permute-start | bytes 294920 | tf_op jit(solution)/shard_map/ppermute | solution.py:368
  11.3 8.1 %collective-permute-start.4 = (bf16[96,512]{1,0:T(8,128)(2,1)S(1)}, bf16[96,512]{1,0:T(8,128)(2,1)S(1)}, u32[]{:S(2)}, u32[]{:S(2)}) collective-permute-start(bf16[96,512]{1,0:T(8,128)(2,1)S(1)} %get-tuple-element.54), channel_id=1, source_target_pairs={{0,6},{1,7},{2,4},{3,5},{4,2},{5,3},{6,0},{7,1},{8,14},{9,15},{10,... | collective-permute-start | bytes 294920 | tf_op jit(solution)/shard_map/ppermute | solution.py:368
  11.6 17.7 %collective-permute-start.5 = (bf16[96,512]{1,0:T(8,128)(2,1)S(1)}, bf16[96,512]{1,0:T(8,128)(2,1)S(1)}, u32[]{:S(2)}, u32[]{:S(2)}) collective-permute-start(bf16[96,512]{1,0:T(8,128)(2,1)S(1)} %get-tuple-element.57), channel_id=1, source_target_pairs={{0,2},{1,3},{2,0},{3,1},{4,6},{5,7},{6,4},{7,5},{8,10},{9,11},{10,... | collective-permute-start | bytes 294920 | tf_op jit(solution)/shard_map/ppermute | solution.py:368
  12.5 17.9 %collective-permute-start.6 = (bf16[96,512]{1,0:T(8,128)(2,1)S(1)}, bf16[96,512]{1,0:T(8,128)(2,1)S(1)}, u32[]{:S(2)}, u32[]{:S(2)}) collective-permute-start(bf16[96,512]{1,0:T(8,128)(2,1)S(1)} %get-tuple-element.58), channel_id=1, source_target_pairs={{0,4},{1,5},{2,6},{3,7},{4,0},{5,1},{6,2},{7,3},{8,12},{9,13},{10,... | collective-permute-start | bytes 294920 | tf_op jit(solution)/shard_map/ppermute | solution.py:368
  16.7 15.2 %collective-permute-start.7 = (bf16[96,512]{1,0:T(8,128)(2,1)S(1)}, bf16[96,512]{1,0:T(8,128)(2,1)S(1)}, u32[]{:S(2)}, u32[]{:S(2)}) collective-permute-start(bf16[96,512]{1,0:T(8,128)(2,1)S(1)} %get-tuple-element.59), channel_id=1, source_target_pairs={{0,6},{1,7},{2,4},{3,5},{4,2},{5,3},{6,0},{7,1},{8,14},{9,15},{10,... | collective-permute-start | bytes 294920 | tf_op jit(solution)/shard_map/ppermute | solution.py:368
  20.8 12.6 %collective-permute-start.8 = (bf16[96,512]{1,0:T(8,128)(2,1)S(1)}, bf16[96,512]{1,0:T(8,128)(2,1)S(1)}, u32[]{:S(2)}, u32[]{:S(2)}) collective-permute-start(bf16[96,512]{1,0:T(8,128)(2,1)S(1)} %get-tuple-element.62), channel_id=1, source_target_pairs={{0,2},{1,3},{2,0},{3,1},{4,6},{5,7},{6,4},{7,5},{8,10},{9,11},{10,... | collective-permute-start | bytes 294920 | tf_op jit(solution)/shard_map/ppermute | solution.py:368
  27.8 11.9 %collective-permute-start.11 = (bf16[192,512]{1,0:T(8,128)(2,1)S(1)}, bf16[192,512]{1,0:T(8,128)(2,1)S(1)}, u32[]{:S(2)}, u32[]{:S(2)}) collective-permute-start(bf16[192,512]{1,0:T(8,128)(2,1)S(1)} %get-tuple-element.65), channel_id=1, source_target_pairs={{0,8},{8,0},{16,24},{24,16},{1,9},{9,1},{17,25},{25,17},{2,10},{10... | collective-permute-start | bytes 589832 | tf_op jit(solution)/shard_map/ppermute | solution.py:368
  29.3 7.9 %collective-permute-start.9 = (bf16[96,512]{1,0:T(8,128)(2,1)S(1)}, bf16[96,512]{1,0:T(8,128)(2,1)S(1)}, u32[]{:S(2)}, u32[]{:S(2)}) collective-permute-start(bf16[96,512]{1,0:T(8,128)(2,1)S(1)} %get-tuple-element.63), channel_id=1, source_target_pairs={{0,4},{1,5},{2,6},{3,7},{4,0},{5,1},{6,2},{7,3},{8,12},{9,13},{10,... | collective-permute-start | bytes 294920 | tf_op jit(solution)/shard_map/ppermute | solution.py:368
  30.5 7.7 %collective-permute-start.10 = (bf16[96,512]{1,0:T(8,128)(2,1)S(1)}, bf16[96,512]{1,0:T(8,128)(2,1)S(1)}, u32[]{:S(2)}, u32[]{:S(2)}) collective-permute-start(bf16[96,512]{1,0:T(8,128)(2,1)S(1)} %get-tuple-element.64), channel_id=1, source_target_pairs={{0,6},{1,7},{2,4},{3,5},{4,2},{5,3},{6,0},{7,1},{8,14},{9,15},{10,... | collective-permute-start | bytes 294920 | tf_op jit(solution)/shard_map/ppermute | solution.py:368
  31.9 12.4 %collective-permute-start.12 = (bf16[192,512]{1,0:T(8,128)(2,1)S(1)}, bf16[192,512]{1,0:T(8,128)(2,1)S(1)}, u32[]{:S(2)}, u32[]{:S(2)}) collective-permute-start(bf16[192,512]{1,0:T(8,128)(2,1)S(1)} %get-tuple-element.66), channel_id=1, source_target_pairs={{0,16},{8,24},{16,0},{24,8},{1,17},{9,25},{17,1},{25,9},{2,18},{10... | collective-permute-start | bytes 589832 | tf_op jit(solution)/shard_map/ppermute | solution.py:368
  33.4 10.9 %collective-permute-start.13 = (bf16[192,512]{1,0:T(8,128)(2,1)S(1)}, bf16[192,512]{1,0:T(8,128)(2,1)S(1)}, u32[]{:S(2)}, u32[]{:S(2)}) collective-permute-start(bf16[192,512]{1,0:T(8,128)(2,1)S(1)} %get-tuple-element.67), channel_id=1, source_target_pairs={{0,24},{8,16},{16,8},{24,0},{1,25},{9,17},{17,9},{25,1},{2,26},{10... | collective-permute-start | bytes 589832 | tf_op jit(solution)/shard_map/ppermute | solution.py:368
  37.2 8.7 %collective-permute-start.17 = (bf16[192,512]{1,0:T(8,128)(2,1)S(1)}, bf16[192,512]{1,0:T(8,128)(2,1)S(1)}, u32[]{:S(2)}, u32[]{:S(2)}) collective-permute-start(bf16[192,512]{1,0:T(8,128)(2,1)S(1)} %get-tuple-element.73), channel_id=1, source_target_pairs={{0,8},{8,0},{16,24},{24,16},{1,9},{9,1},{17,25},{25,17},{2,10},{10... | collective-permute-start | bytes 589832 | tf_op jit(solution)/shard_map/ppermute | solution.py:368
  38.1 11.4 %collective-permute-start.18 = (bf16[192,512]{1,0:T(8,128)(2,1)S(1)}, bf16[192,512]{1,0:T(8,128)(2,1)S(1)}, u32[]{:S(2)}, u32[]{:S(2)}) collective-permute-start(bf16[192,512]{1,0:T(8,128)(2,1)S(1)} %get-tuple-element.74), channel_id=1, source_target_pairs={{0,16},{8,24},{16,0},{24,8},{1,17},{9,25},{17,1},{25,9},{2,18},{10... | collective-permute-start | bytes 589832 | tf_op jit(solution)/shard_map/ppermute | solution.py:368
  39.7 14.0 %collective-permute-start.19 = (bf16[192,512]{1,0:T(8,128)(2,1)S(1)}, bf16[192,512]{1,0:T(8,128)(2,1)S(1)}, u32[]{:S(2)}, u32[]{:S(2)}) collective-permute-start(bf16[192,512]{1,0:T(8,128)(2,1)S(1)} %get-tuple-element.75), channel_id=1, source_target_pairs={{0,24},{8,16},{16,8},{24,0},{1,25},{9,17},{17,9},{25,1},{2,26},{10... | collective-permute-start | bytes 589832 | tf_op jit(solution)/shard_map/ppermute | solution.py:368
  45.5 28.1 %collective-permute-start.20 = (bf16[192,512]{1,0:T(8,128)(2,1)S(1)}, bf16[192,512]{1,0:T(8,128)(2,1)S(1)}, u32[]{:S(2)}, u32[]{:S(2)}) collective-permute-start(bf16[192,512]{1,0:T(8,128)(2,1)S(1)} %get-tuple-element.82), channel_id=1, source_target_pairs={{0,8},{8,0},{16,24},{24,16},{1,9},{9,1},{17,25},{25,17},{2,10},{10... | collective-permute-start | bytes 589832 | tf_op jit(solution)/shard_map/ppermute | solution.py:368
  45.9 7.8 %collective-permute-start.14 = (bf16[96,512]{1,0:T(8,128)(2,1)S(1)}, bf16[96,512]{1,0:T(8,128)(2,1)S(1)}, u32[]{:S(2)}, u32[]{:S(2)}) collective-permute-start(bf16[96,512]{1,0:T(8,128)(2,1)S(1)} %get-tuple-element.70), channel_id=1, source_target_pairs={{0,2},{1,3},{2,0},{3,1},{4,6},{5,7},{6,4},{7,5},{8,10},{9,11},{10,... | collective-permute-start | bytes 294920 | tf_op jit(solution)/shard_map/ppermute | solution.py:368
  46.0 7.7 %collective-permute-start.15 = (bf16[96,512]{1,0:T(8,128)(2,1)S(1)}, bf16[96,512]{1,0:T(8,128)(2,1)S(1)}, u32[]{:S(2)}, u32[]{:S(2)}) collective-permute-start(bf16[96,512]{1,0:T(8,128)(2,1)S(1)} %get-tuple-element.71), channel_id=1, source_target_pairs={{0,4},{1,5},{2,6},{3,7},{4,0},{5,1},{6,2},{7,3},{8,12},{9,13},{10,... | collective-permute-start | bytes 294920 | tf_op jit(solution)/shard_map/ppermute | solution.py:368
  49.5 6.4 %collective-permute-start.16 = (bf16[96,512]{1,0:T(8,128)(2,1)S(1)}, bf16[96,512]{1,0:T(8,128)(2,1)S(1)}, u32[]{:S(2)}, u32[]{:S(2)}) collective-permute-start(bf16[96,512]{1,0:T(8,128)(2,1)S(1)} %get-tuple-element.72), channel_id=1, source_target_pairs={{0,6},{1,7},{2,4},{3,5},{4,2},{5,3},{6,0},{7,1},{8,14},{9,15},{10,... | collective-permute-start | bytes 294920 | tf_op jit(solution)/shard_map/ppermute | solution.py:368
  60.8 4.4 %collective-permute-start.26 = (f32[2,8,128]{2,1,0:T(8,128)S(1)}, f32[2,8,128]{2,1,0:T(8,128)S(1)}, u32[]{:S(2)}, u32[]{:S(2)}) collective-permute-start(f32[2,8,128]{2,1,0:T(8,128)S(1)} %get-tuple-element.91), channel_id=1, source_target_pairs={{0,2},{1,3},{2,0},{3,1},{4,6},{5,7},{6,4},{7,5},{8,10},{9,11},{10,... | collective-permute-start | bytes 24584 | tf_op jit(solution)/shard_map/ppermute | solution.py:368
  60.8 4.5 %collective-permute-start.27 = (f32[2,8,128]{2,1,0:T(8,128)S(1)}, f32[2,8,128]{2,1,0:T(8,128)S(1)}, u32[]{:S(2)}, u32[]{:S(2)}) collective-permute-start(f32[2,8,128]{2,1,0:T(8,128)S(1)} %get-tuple-element.92), channel_id=1, source_target_pairs={{0,4},{1,5},{2,6},{3,7},{4,0},{5,1},{6,2},{7,3},{8,12},{9,13},{10,... | collective-permute-start | bytes 24584 | tf_op jit(solution)/shard_map/ppermute | solution.py:368
  62.5 5.4 %collective-permute-start.28 = (f32[2,8,128]{2,1,0:T(8,128)S(1)}, f32[2,8,128]{2,1,0:T(8,128)S(1)}, u32[]{:S(2)}, u32[]{:S(2)}) collective-permute-start(f32[2,8,128]{2,1,0:T(8,128)S(1)} %get-tuple-element.93), channel_id=1, source_target_pairs={{0,6},{1,7},{2,4},{3,5},{4,2},{5,3},{6,0},{7,1},{8,14},{9,15},{10,... | collective-permute-start | bytes 24584 | tf_op jit(solution)/shard_map/ppermute | solution.py:368
  68.0 3.7 %collective-permute-start.29 = (f32[4,8,128]{2,1,0:T(8,128)S(1)}, f32[4,8,128]{2,1,0:T(8,128)S(1)}, u32[]{:S(2)}, u32[]{:S(2)}) collective-permute-start(f32[4,8,128]{2,1,0:T(8,128)S(1)} %shard_map.111), channel_id=1, source_target_pairs={{0,1},{1,0},{2,3},{3,2},{4,5},{5,4},{6,7},{7,6},{8,9},{9,8},{10,11... | collective-permute-start | bytes 49160 | tf_op jit(solution)/shard_map/ppermute | solution.py:368
  68.0 12.1 %collective-permute-start.21 = (bf16[192,512]{1,0:T(8,128)(2,1)S(1)}, bf16[192,512]{1,0:T(8,128)(2,1)S(1)}, u32[]{:S(2)}, u32[]{:S(2)}) collective-permute-start(bf16[192,512]{1,0:T(8,128)(2,1)S(1)} %get-tuple-element.83), channel_id=1, source_target_pairs={{0,16},{8,24},{16,0},{24,8},{1,17},{9,25},{17,1},{25,9},{2,18},{10... | collective-permute-start | bytes 589832 | tf_op jit(solution)/shard_map/ppermute | solution.py:368
  70.1 10.0 %collective-permute-start.22 = (bf16[192,512]{1,0:T(8,128)(2,1)S(1)}, bf16[192,512]{1,0:T(8,128)(2,1)S(1)}, u32[]{:S(2)}, u32[]{:S(2)}) collective-permute-start(bf16[192,512]{1,0:T(8,128)(2,1)S(1)} %get-tuple-element.84), channel_id=1, source_target_pairs={{0,24},{8,16},{16,8},{24,0},{1,25},{9,17},{17,9},{25,1},{2,26},{10... | collective-permute-start | bytes 589832 | tf_op jit(solution)/shard_map/ppermute | solution.py:368
  71.4 10.2 %collective-permute-start.23 = (bf16[192,512]{1,0:T(8,128)(2,1)S(1)}, bf16[192,512]{1,0:T(8,128)(2,1)S(1)}, u32[]{:S(2)}, u32[]{:S(2)}) collective-permute-start(bf16[192,512]{1,0:T(8,128)(2,1)S(1)} %get-tuple-element.86), channel_id=1, source_target_pairs={{0,8},{8,0},{16,24},{24,16},{1,9},{9,1},{17,25},{25,17},{2,10},{10... | collective-permute-start | bytes 589832 | tf_op jit(solution)/shard_map/ppermute | solution.py:368
  71.7 16.7 %collective-permute-start.24 = (bf16[192,512]{1,0:T(8,128)(2,1)S(1)}, bf16[192,512]{1,0:T(8,128)(2,1)S(1)}, u32[]{:S(2)}, u32[]{:S(2)}) collective-permute-start(bf16[192,512]{1,0:T(8,128)(2,1)S(1)} %get-tuple-element.87), channel_id=1, source_target_pairs={{0,16},{8,24},{16,0},{24,8},{1,17},{9,25},{17,1},{25,9},{2,18},{10... | collective-permute-start | bytes 589832 | tf_op jit(solution)/shard_map/ppermute | solution.py:368
  73.6 14.7 %collective-permute-start.25 = (bf16[192,512]{1,0:T(8,128)(2,1)S(1)}, bf16[192,512]{1,0:T(8,128)(2,1)S(1)}, u32[]{:S(2)}, u32[]{:S(2)}) collective-permute-start(bf16[192,512]{1,0:T(8,128)(2,1)S(1)} %get-tuple-element.88), channel_id=1, source_target_pairs={{0,24},{8,16},{16,8},{24,0},{1,25},{9,17},{17,9},{25,1},{2,26},{10... | collective-permute-start | bytes 589832 | tf_op jit(solution)/shard_map/ppermute | solution.py:368
  (7 other events, 19.0 us)

commit v3 on v2

v3 whole, which is shorter than its diff:
```python
import functools

import jax
import jax.numpy as jnp
from jax import lax
from jax.experimental import pallas as pl
from jax.experimental.pallas import tpu as pltpu
from jax.sharding import PartitionSpec as P

LANES = 128
META = 16
OFFSETS = (0, 1, 4, 5)
WIDTHS = (640, 768, 640)
FIRST_PART = WIDTHS[0]
VMEM_LIMIT = 10 * 1024 * 1024
VMEM = pl.BlockSpec(memory_space=pltpu.VMEM)
ANY = pl.BlockSpec(memory_space=pl.ANY)
SMEM = pl.BlockSpec(memory_space=pltpu.SMEM)


def params():
    return pltpu.CompilerParams(vmem_limit_bytes=VMEM_LIMIT)


def cost(flops, moved):
    return pl.CostEstimate(flops=flops // 64, bytes_accessed=moved // 64, transcendentals=0)


def silu_parts(gate_value):
    sigmoid = jax.nn.sigmoid(gate_value)
    return (gate_value * sigmoid, sigmoid * (1.0 + gate_value * (1.0 - sigmoid)))


def tokens_kernel(expert_count, routes_ref, probs_ref, rows_ref, meta_ref, *part_refs):
    top_count, token_count = routes_ref.shape
    names = [routes_ref[k : k + 1, :] for k in range(top_count)]
    experts = lax.broadcasted_iota(jnp.int32, (expert_count, token_count), 0)
    onehots = [(experts == name).astype(jnp.float32) for name in names]
    earlier = (
        lax.broadcasted_iota(jnp.int32, (token_count, token_count), 0)
        < lax.broadcasted_iota(jnp.int32, (token_count, token_count), 1)
    ).astype(jnp.bfloat16)
    before = jnp.dot(
        sum(onehots).astype(jnp.bfloat16), earlier, preferred_element_type=jnp.float32
    )
    lines = [name.astype(jnp.float32) for name in names]
    for onehot in onehots:
        lines.append(jnp.sum(before * onehot, axis=0, keepdims=True))
        before = before + onehot
    for k in range(top_count):
        lines.append(probs_ref[k : k + 1, :].astype(jnp.float32))
    lines.append(jnp.zeros((META - len(lines), token_count), jnp.float32))
    meta = jnp.concatenate(lines, axis=0).astype(jnp.bfloat16)
    meta_ref[...] = meta
    start = 0
    for part, part_ref in enumerate(part_refs):
        width = part_ref.shape[1]
        part_ref[:token_count, :] = rows_ref[:, start : start + width]
        if part == 0:
            part_ref[token_count:, :] = jnp.zeros((META, width), jnp.bfloat16)
            part_ref[token_count:, :token_count] = meta
        start += width


def token_parts(routes, probs, grad_out, expert_count, widths):
    token_count = routes.shape[1]
    return pl.pallas_call(
        functools.partial(tokens_kernel, expert_count),
        in_specs=[VMEM] * 3,
        out_shape=[jax.ShapeDtypeStruct((META, token_count), jnp.bfloat16)]
        + [
            jax.ShapeDtypeStruct((token_count + (0 if part else META), width), jnp.bfloat16)
            for part, width in enumerate(widths)
        ],
        compiler_params=params(),
        cost_estimate=cost(100 * token_count * token_count, 4 * grad_out.size),
    )(routes, probs, grad_out)


def chosen_rows(meta, top_count, capacity, targets):
    token_count = meta.shape[1]
    slots = lax.broadcasted_iota(jnp.int32, (capacity, token_count), 0).astype(jnp.float32)
    parts = []
    for target in targets:
        part = jnp.zeros((capacity, token_count), jnp.float32)
        for k in range(top_count):
            name, slot, prob = (meta[k + top_count * i :][:1, :] for i in range(3))
            slot = jnp.where(name == target, slot, -1.0)
            part = part + jnp.where(slots == slot, prob, 0.0)
        parts.append(part)
    return jnp.concatenate(parts, axis=0).astype(jnp.bfloat16)


def dispatch_kernel(capacity, top_count, starts, first, *refs):
    if first:
        place_ref, own_meta_ref, other_meta_ref, *refs = refs
        row_refs, (local_ref, sent_ref, select_ref) = refs[:4], refs[4:]
        token_count = own_meta_ref.shape[1]
        targets = [
            lax.bitwise_xor(place_ref[0], offset).astype(jnp.float32) for offset in (0, 2)
        ]
        for source in range(4):
            if source < 2:
                meta = (own_meta_ref, other_meta_ref)[source][...]
            else:
                meta = row_refs[source][token_count:, :token_count]
            select_ref[2 * capacity * source : 2 * capacity * (source + 1), :] = chosen_rows(
                meta.astype(jnp.float32), top_count, capacity, targets
            )
    else:
        select_ref, *refs = refs
        row_refs, (local_ref, sent_ref) = refs[:4], refs[4:]
    token_count = select_ref.shape[1]
    width = local_ref.shape[1]
    for source, row_ref in enumerate(row_refs):
        columns = slice(starts[source // 2], starts[source // 2] + width)
        rows = jnp.dot(
            select_ref[2 * capacity * source : 2 * capacity * (source + 1), :],
            row_ref[:token_count, columns],
            preferred_element_type=jnp.float32,
        ).astype(jnp.bfloat16)
        local_ref[source * capacity : (source + 1) * capacity, :] = rows[:capacity, :]
        sent_ref[source * capacity : (source + 1) * capacity, :] = rows[capacity:, :]


def dispatch(lead, rows, capacity, top_count, token_count, starts, width):
    first = len(lead) > 1
    block = jax.ShapeDtypeStruct((4 * capacity, width), jnp.bfloat16)
    chosen = jax.ShapeDtypeStruct((8 * capacity, token_count), jnp.bfloat16)
    return pl.pallas_call(
        functools.partial(dispatch_kernel, capacity, top_count, starts, first),
        in_specs=([SMEM, VMEM, VMEM] if first else [VMEM]) + [VMEM] * 4,
        out_shape=[block, block] + ([chosen] if first else []),
        compiler_params=params(),
        cost_estimate=cost(
            16 * capacity * token_count * width, 4 * (8 * capacity + token_count) * width
        ),
    )(*lead, *rows)


def hidden_kernel(gate_ref, up_ref, turned_ref, hidden_ref, up_scale_ref, gate_scale_ref):
    activation, gate_slope = silu_parts(gate_ref[...].astype(jnp.float32))
    up_value = up_ref[...].astype(jnp.float32)
    hidden = activation * up_value
    turned_ref[...] = hidden.T.astype(jnp.bfloat16)
    hidden_ref[...] = hidden.astype(jnp.bfloat16)
    up_scale_ref[...] = activation
    gate_scale_ref[...] = up_value * gate_slope


def hidden_parts(gate, up):
    row_count, hidden_width = gate.shape
    step = 2 * LANES
    block = pl.BlockSpec((row_count, step), lambda i: (0, i))
    return pl.pallas_call(
        hidden_kernel,
        grid=(hidden_width // step,),
        in_specs=[block] * 2,
        out_specs=[pl.BlockSpec((step, row_count), lambda i: (i, 0))] + [block] * 3,
        out_shape=[
            jax.ShapeDtypeStruct((hidden_width, row_count), jnp.bfloat16),
            jax.ShapeDtypeStruct((row_count, hidden_width), jnp.bfloat16),
            jax.ShapeDtypeStruct((row_count, hidden_width), jnp.float32),
            jax.ShapeDtypeStruct((row_count, hidden_width), jnp.float32),
        ],
        compiler_params=params(),
        cost_estimate=cost(20 * row_count * hidden_width, 16 * row_count * hidden_width),
    )(gate, up)


def panel_kernel(capacity, place_ref, turned_ref, local_ref, near_ref, *refs):
    rows_ref, own_ref, later_ref, sent_ref = refs[-4:]
    share = own_ref.shape[0]
    for source in range(4):
        for offset, block_ref in ((0, local_ref), (2, near_ref)):
            place = lax.bitwise_xor(place_ref[0], OFFSETS[source] + offset)
            start = pl.multiple_of(place * capacity, capacity)
            rows_ref[pl.ds(start, capacity), :] = block_ref[
                source * capacity : (source + 1) * capacity, :
            ]
    rows = rows_ref[...]

    def part(offset):
        owner = lax.bitwise_xor(place_ref[1], offset)
        start = pl.multiple_of(owner * share, share)
        return jnp.dot(turned_ref[pl.ds(start, share), :], rows, preferred_element_type=jnp.float32)

    step = 1 + lax.bitwise_and(place_ref[0], 1)
    sent_ref[:share, :] = part(step).astype(jnp.bfloat16)
    sent_ref[share:, :] = part(3).astype(jnp.bfloat16)
    later_ref[...] = part(3 - step)
    own_ref[...] = part(0)


def panel_parts(place, turned, local, near, capacity, earlier):
    hidden_width, row_count = turned.shape
    width = local.shape[1]
    share = hidden_width // 4
    return pl.pallas_call(
        functools.partial(panel_kernel, capacity),
        in_specs=[SMEM] + [VMEM] * 3 + [ANY] * len(earlier),
        out_shape=[
            jax.ShapeDtypeStruct((row_count, width), jnp.bfloat16),
            jax.ShapeDtypeStruct((share, width), jnp.float32),
            jax.ShapeDtypeStruct((share, width), jnp.float32),
            jax.ShapeDtypeStruct((2 * share, width), jnp.bfloat16),
        ],
        compiler_params=params(),
        cost_estimate=cost(
            2 * hidden_width * row_count * width, 2 * hidden_width * (row_count + width)
        ),
    )(place, turned, local, near, *earlier)


def halve_kernel(own_ref, later_ref, arrived_ref, sum_ref, sent_ref):
    share = own_ref.shape[0]
    sent_ref[...] = (later_ref[...] + arrived_ref[share:, :].astype(jnp.float32)).astype(
        jnp.bfloat16
    )
    sum_ref[...] = own_ref[...] + arrived_ref[:share, :].astype(jnp.float32)


def halve(own, later, arrived):
    return pl.pallas_call(
        halve_kernel,
        in_specs=[VMEM] * 3,
        out_shape=[
            jax.ShapeDtypeStruct(own.shape, jnp.float32),
            jax.ShapeDtypeStruct(own.shape, jnp.bfloat16),
        ],
        compiler_params=params(),
        cost_estimate=cost(4 * own.size, 18 * own.size),
    )(own, later, arrived)


def total_kernel(start, *refs):
    own_ref, arrived_ref, total_ref, sum_ref, semaphore = refs[-5:]
    sum_ref[...] = own_ref[...] + arrived_ref[...].astype(jnp.float32)
    copy = pltpu.make_async_copy(
        sum_ref, total_ref.at[:, start : start + sum_ref.shape[1]], semaphore
    )
    copy.start()
    copy.wait()


def total_chunk(held, own, arrived, start, model_width):
    share, width = own.shape
    first = held is None
    return pl.pallas_call(
        functools.partial(total_kernel, start),
        in_specs=([] if first else [ANY]) + [VMEM] * 2,
        out_specs=ANY,
        out_shape=jax.ShapeDtypeStruct((share, model_width), jnp.float32),
        scratch_shapes=[pltpu.VMEM((share, width), jnp.float32), pltpu.SemaphoreType.DMA],
        input_output_aliases={} if first else {0: 0},
        compiler_params=params(),
        cost_estimate=cost(2 * share * width, 10 * share * width),
    )(*([] if first else [held]), own, arrived)


def rows_times_weight(start, rows_ref, weight_ref):
    return lax.dot_general(
        rows_ref[...],
        weight_ref[:, start : start + rows_ref.shape[1]],
        (((1,), (1,)), ((), ())),
        preferred_element_type=jnp.float32,
    )


def first_kernel(start, rows_ref, weight_ref, sum_ref):
    sum_ref[...] = rows_times_weight(start, rows_ref, weight_ref)


def middle_kernel(start, held_ref, rows_ref, weight_ref, sum_ref):
    sum_ref[...] = held_ref[...] + rows_times_weight(start, rows_ref, weight_ref)


def grad_hidden_step(held, rows, weight, start):
    row_count, width = rows.shape
    hidden_width = weight.shape[0]
    step = 2 * LANES
    block = pl.BlockSpec((row_count, step), lambda i: (0, i))
    specs = [
        pl.BlockSpec((row_count, width), lambda i: (0, 0)),
        pl.BlockSpec((step, weight.shape[1]), lambda i: (i, 0)),
    ]
    return pl.pallas_call(
        functools.partial(first_kernel if held is None else middle_kernel, start),
        grid=(hidden_width // step,),
        in_specs=specs if held is None else [block] + specs,
        out_specs=block,
        out_shape=jax.ShapeDtypeStruct((row_count, hidden_width), jnp.float32),
        compiler_params=params(),
        cost_estimate=cost(2 * row_count * hidden_width * width, 8 * row_count * hidden_width),
    )(*([rows, weight] if held is None else [held, rows, weight]))


def last_kernel(
    capacity,
    start,
    held_ref,
    rows_ref,
    weight_ref,
    hidden_ref,
    up_scale_ref,
    gate_scale_ref,
    grad_gate_ref,
    grad_up_ref,
    slot_ref,
    sum_ref,
):
    grid_place = pl.program_id(0)
    grad_hidden = held_ref[...] + rows_times_weight(start, rows_ref, weight_ref)
    grad_up_ref[...] = (grad_hidden * up_scale_ref[...]).astype(jnp.bfloat16)
    grad_gate_ref[...] = (grad_hidden * gate_scale_ref[...]).astype(jnp.bfloat16)
    product = hidden_ref[...].astype(jnp.float32) * grad_hidden
    folded = product[:, :LANES]
    for column in range(LANES, product.shape[1], LANES):
        folded = folded + product[:, column : column + LANES]

    @pl.when(grid_place == 0)
    def _():
        sum_ref[...] = folded

    @pl.when(grid_place > 0)
    def _():
        sum_ref[...] = sum_ref[...] + folded

    @pl.when(grid_place == pl.num_programs(0) - 1)
    def _():
        line = jnp.sum(sum_ref[...].T, axis=0, keepdims=True)
        slot_ref[...] = jnp.zeros_like(slot_ref)
        for source in range(slot_ref.shape[0]):
            slot_ref[source : source + 1, 0:capacity] = line[
                :, source * capacity : (source + 1) * capacity
            ]


def grad_hidden_last(held, rows, weight, start, hidden, up_scale, gate_scale, capacity):
    row_count, width = rows.shape
    hidden_width = weight.shape[0]
    step = 2 * LANES
    block = pl.BlockSpec((row_count, step), lambda i: (0, i))
    expert_count = row_count // capacity
    return pl.pallas_call(
        functools.partial(last_kernel, capacity, start),
        grid=(hidden_width // step,),
        in_specs=[
            block,
            pl.BlockSpec((row_count, width), lambda i: (0, 0)),
            pl.BlockSpec((step, weight.shape[1]), lambda i: (i, 0)),
            block,
            block,
            block,
        ],
        out_specs=[block, block, pl.BlockSpec((expert_count, LANES), lambda i: (0, 0))],
        out_shape=[jax.ShapeDtypeStruct((row_count, hidden_width), jnp.bfloat16)] * 2
        + [jax.ShapeDtypeStruct((expert_count, LANES), jnp.float32)],
        scratch_shapes=[pltpu.VMEM((row_count, LANES), jnp.float32)],
        compiler_params=params(),
        cost_estimate=cost(2 * row_count * hidden_width * width, 12 * row_count * hidden_width),
    )(held, rows, weight, hidden, up_scale, gate_scale)


def route_kernel(capacity, place_ref, meta_ref, near_ref, far_ref, out_ref, table_ref):
    top_count, token_count = out_ref.shape
    expert_count = table_ref.shape[0]
    half = expert_count // 2
    for offset in range(expert_count):
        block_ref = near_ref if offset < half else far_ref
        row = offset % half * expert_count + place_ref[0]
        table_ref[offset : offset + 1, :] = block_ref[pl.ds(row, 1), :]
    table = table_ref[...].T
    meta = meta_ref[...].astype(jnp.float32)
    slots = lax.broadcasted_iota(jnp.int32, (capacity, token_count), 0).astype(jnp.float32)
    for k in range(top_count):
        name, slot, prob = (meta[k + top_count * i :][:1, :] for i in range(3))
        picked = jnp.zeros((capacity, token_count), jnp.float32)
        for offset in range(expert_count):
            expert = lax.bitwise_xor(place_ref[0], offset).astype(jnp.float32)
            wanted = jnp.where(name == expert, slot, -1.0)
            picked = picked + jnp.where(
                slots == wanted, table[:capacity, offset : offset + 1], 0.0
            )
        out_ref[k : k + 1, :] = jnp.sum(picked, axis=0, keepdims=True) / prob


def route_back(place, meta, near, far, expert_count, top_count, capacity):
    token_count = meta.shape[1]
    return pl.pallas_call(
        functools.partial(route_kernel, capacity),
        in_specs=[SMEM] + [VMEM] * 3,
        out_shape=jax.ShapeDtypeStruct((top_count, token_count), jnp.float32),
        scratch_shapes=[pltpu.VMEM((expert_count, LANES), jnp.float32)],
        compiler_params=params(),
        cost_estimate=cost(1000000, 100000),
    )(place, meta, near, far)


def after_kernel(*refs):
    pass


def after(value, *earlier):
    return pl.pallas_call(
        after_kernel,
        in_specs=[ANY] * (1 + len(earlier)),
        out_specs=ANY,
        out_shape=jax.ShapeDtypeStruct(value.shape, value.dtype),
        input_output_aliases={0: 0},
        compiler_params=params(),
        cost_estimate=cost(64, 64),
    )(value, *earlier)


def swap(value, offset):
    size = lax.axis_size("expert")
    return lax.ppermute(value, "expert", [(place, place ^ offset) for place in range(size)])


def swap_groups(value, later):
    groups, places = lax.axis_size("dp"), lax.axis_size("expert")
    pairs = []
    for group in range(groups):
        for place in range(places):
            other = group ^ (1 + (place & 1) ^ (3 if later else 0))
            pairs.append((group * places + place, other * places + place))
    return lax.ppermute(value, ("dp", "expert"), pairs)


def line_shards(grad_out, probs, routes, saved_gate, saved_up, w_down):
    expert_count = lax.axis_size("expert")
    capacity = saved_gate.shape[3]
    hidden_width = saved_gate.shape[4]
    token_count, model_width = grad_out.shape
    top_count = routes.shape[1]
    row_count = expert_count * capacity

    place = jnp.stack([lax.axis_index("expert"), lax.axis_index("dp")]).astype(jnp.int32)
    part_widths = (FIRST_PART, model_width - FIRST_PART)
    meta, *parts = token_parts(routes.T, probs.T, grad_out, expert_count, part_widths)
    parts = [swap(part, 4) for part in parts]
    other_rows, other_meta = swap(grad_out, 1), swap(meta, 1)
    gate = saved_gate.reshape(row_count, hidden_width)
    up = saved_up.reshape(row_count, hidden_width)
    weight = w_down[0]
    turned, hidden, up_scale, gate_scale = hidden_parts(gate, up)
    lead = [place, meta, other_meta]
    held, panel, start, halves = None, None, 0, []
    for chunk, width in enumerate(WIDTHS):
        part = int(start >= FIRST_PART)
        starts = (start, start - part * FIRST_PART)
        if start == FIRST_PART:
            parts[part] = after(parts[part], sent)
        if start in (0, FIRST_PART):
            other_part = swap(parts[part], 1)
        sources = [grad_out, other_rows, parts[part], other_part]
        local, sent, *select = dispatch(
            lead, sources, capacity, top_count, token_count, starts, width
        )
        lead = select or lead
        earlier = ([held] if chunk > 0 else []) + (halves[chunk - 2 : chunk - 1] if chunk > 1 else [])
        rows, own, later, half = panel_parts(
            place, turned, local, swap(sent, 2), capacity, earlier
        )
        own, half = halve(own, later, swap_groups(half, False))
        half = swap_groups(half, True)
        halves.append(half)
        panel = total_chunk(panel, own, half, start, model_width)
        if chunk + 1 < len(WIDTHS):
            held = grad_hidden_step(held, rows, weight, start)
        else:
            grad_gate, grad_up, lines = grad_hidden_last(
                held, rows, weight, start, hidden, up_scale, gate_scale, capacity
            )
        start += width
    for offset in (1, 2):
        lines = jnp.concatenate([lines, swap(lines, offset)], axis=0)
    route_grad = route_back(
        place, meta, lines, swap(lines, 4), expert_count, top_count, capacity
    )
    return (
        grad_gate.reshape(saved_gate.shape),
        grad_up.reshape(saved_up.shape),
        panel[None],
        route_grad.T,
    )


def plain_shards(grad_out, probs, routes, saved_gate, saved_up, w_down):
    expert_count = lax.axis_size("expert")
    capacity = saved_gate.shape[3]
    hidden_width = saved_gate.shape[4]
    token_count, top_count = routes.shape
    model_width = grad_out.shape[1]
    row_count = expert_count * capacity
    flat_routes = routes.reshape(-1)
    onehot = (flat_routes[:, None] == jnp.arange(expert_count)[None, :]).astype(jnp.int32)
    before = jnp.cumsum(onehot, axis=0) - onehot
    position = flat_routes * capacity + jnp.sum(before * onehot, axis=1)
    selector = jnp.arange(row_count)[:, None] == position[None, :]
    selector = jnp.where(selector, probs.reshape(-1)[None], 0).reshape(
        row_count, token_count, top_count
    )
    sent = jnp.dot(jnp.sum(selector, axis=2), grad_out, preferred_element_type=jnp.float32)
    rows = lax.all_to_all(
        sent.astype(jnp.bfloat16).reshape(expert_count, capacity, model_width),
        "expert",
        split_axis=0,
        concat_axis=0,
        tiled=True,
    ).reshape(row_count, model_width)
    up_value = saved_up.reshape(row_count, hidden_width).astype(jnp.float32)
    activation, gate_slope = silu_parts(
        saved_gate.reshape(row_count, hidden_width).astype(jnp.float32)
    )
    hidden = (activation * up_value).astype(jnp.bfloat16)
    grad_hidden = lax.dot_general(
        rows, w_down[0], (((1,), (1,)), ((), ())), preferred_element_type=jnp.float32
    )
    slot_grad = jnp.sum(hidden.astype(jnp.float32) * grad_hidden, axis=1)
    grad_up = (grad_hidden * activation).astype(jnp.bfloat16)
    grad_gate = (grad_hidden * up_value * gate_slope).astype(jnp.bfloat16)
    whole_panel = lax.dot_general(
        hidden, rows, (((0,), (0,)), ((), ())), preferred_element_type=jnp.float32
    )
    panel = lax.psum_scatter(whole_panel, "dp", scatter_dimension=0, tiled=True)
    returned = lax.all_to_all(
        slot_grad.reshape(expert_count, capacity), "expert", split_axis=0, concat_axis=0, tiled=True
    )
    route_grad = jnp.take(returned.reshape(-1), position, axis=0).reshape(token_count, top_count)
    return (
        grad_gate.reshape(saved_gate.shape),
        grad_up.reshape(saved_up.shape),
        panel[None],
        route_grad / probs.astype(jnp.float32),
    )


def shards(grad_out, probs, routes, saved_gate, saved_up, w_down):
    expert_count = lax.axis_size("expert")
    group_count = lax.axis_size("dp")
    capacity, hidden_width = saved_gate.shape[3:]
    aligned = (
        expert_count == 8
        and group_count == 4
        and capacity % 16 == 0
        and capacity <= LANES
        and hidden_width % (16 * group_count) == 0
        and routes.shape[0] == LANES
        and grad_out.shape[1] == sum(WIDTHS)
    )
    run = line_shards if aligned else plain_shards
    return run(grad_out, probs, routes, saved_gate, saved_up, w_down)


def solution(mesh):
    return jax.shard_map(
        shards,
        mesh=mesh,
        in_specs=(
            P(("dp", "expert"), None),
            P(("dp", "expert"), None),
            P(("dp", "expert"), None),
            P("dp", "expert", None, None, None),
            P("dp", "expert", None, None, None),
            P("expert", None, None),
        ),
        out_specs=(
            P("dp", "expert", None, None, None),
            P("dp", "expert", None, None, None),
            P("expert", "dp", None),
            P(("dp", "expert"), None),
        ),
        check_vma=False,
    )
```

time: 89.4 us -> 83.6 us (0.935)
  starting transfers between devices: 43.2 us -> 20.6 us
  waiting for transfers between devices: 24.2 us -> 42.6 us
  Pallas kernels: 18.5 us -> 15.8 us
  local copies, waits for them, and re-layouts: 2.4 us -> 3.44 us
    ppermute x30 -> x18, starting transfers between devices: 43.2 us -> 20.6 us  [the longest x12 11.9 us: swap(): lax.ppermute(value, 'expert', [(place, place ^ offset) for place in range...]
    ppermute x30 -> x18, waiting for transfers between devices: 24.2 us -> 42.6 us  [the longest x12 29.3 us: swap(): lax.ppermute(value, 'expert', [(place, place ^ offset) for place in range...]
    pallas_call x20 -> x19, Pallas kernels: 18.5 us -> 15.8 us  [the longest x3 4.02 us: panel_parts(): pl.pallas_call(functools.partial(panel_kernel, capacity), in_specs=[SMEM]...]
    unnamed x18, local copies, waits for them, and re-layouts: 2.4 us -> 3.44 us
  transfers between devices with their start and end apart: 30 -> 18, of which waited for: 10 -> 10; matrix products, arithmetic and copies ran while one was open for 0% -> 0% of each run, Pallas kernels for 20% -> 18%
where the time goes in v3:
time: 83.6 us; the launch traced here: 83.3 us
  waiting for transfers between devices  42.6 us (51%)
  starting transfers between devices  20.6 us (25%)
  Pallas kernels  15.8 us (19%)
  local copies, waits for them, and re-layouts  3.44 us (4%)
    ppermute x12, waiting for transfers between devices, swap(): lax.ppermute(value, 'expert', [(place, place ^ offset) for place in range...  29.3 us
    ppermute x6, waiting for transfers between devices, swap_groups(): return lax.ppermute(value, ('dp', 'expert'), pairs)  13.4 us
    ppermute x12, starting transfers between devices, swap(): lax.ppermute(value, 'expert', [(place, place ^ offset) for place in range...  11.9 us
    ppermute x6, starting transfers between devices, swap_groups(): return lax.ppermute(value, ('dp', 'expert'), pairs)  8.7 us
    pallas_call x3, Pallas kernels, panel_parts(): pl.pallas_call(functools.partial(panel_kernel, capacity), in_specs=[SMEM]...  4.02 us
    unnamed x18, local copies, waits for them, and re-layouts  3.44 us
    pallas_call x1, Pallas kernels, grad_hidden_last(): pl.pallas_call(functools.partial(last_kernel, capacity, start), grid=(hid...  2.68 us
    pallas_call x3, Pallas kernels, total_chunk(): pl.pallas_call(functools.partial(total_kernel, start), in_specs=([] if fi...  2.55 us
  transfers between devices with their start and end apart: 18, of which 10 were waited for; matrix products, arithmetic and copies ran while one was open for 0% of the time, Pallas kernels for 18%

profile of v3, /device:TPU:0, one launch (start us, length us, event | category | flops | bytes accessed | tf_op | source)
XLA Modules:
  0.0 83.3 jit_solution(15870572290594677266)
XLA Ops:
  1.2 1.0 %copy-done.1 = bf16[128,2048]{1,0:T(8,128)(2,1)S(1)} copy-done((bf16[128,2048]{1,0:T(8,128)(2,1)S(1)}, bf16[128,2048]{1,0:T(8,128)(2,1)}, u32[]{:S(2)}) %copy-start.1) | copy-done | bytes 524312
  3.7 3.6 %collective-permute-start.2 = (bf16[144,640]{1,0:T(8,128)(2,1)S(1)}, bf16[144,640]{1,0:T(8,128)(2,1)S(1)}, u32[]{:S(2)}, u32[]{:S(2)}) collective-permute-start(bf16[144,640]{1,0:T(8,128)(2,1)S(1)} %get-tuple-element.41), channel_id=1, source_target_pairs={{0,4},{1,5},{2,6},{3,7},{4,0},{5,1},{6,2},{7,3},{8,12},{9,13},{10,... | collective-permute-start | bytes 552968 | tf_op jit(solution)/shard_map/ppermute | solution.py:418
  7.3 9.2 %collective-permute-done.2.refs_5_ = bf16[144,640]{1,0:T(8,128)(2,1)S(1)} collective-permute-done((bf16[144,640]{1,0:T(8,128)(2,1)S(1)}, bf16[144,640]{1,0:T(8,128)(2,1)S(1)}, u32[]{:S(2)}, u32[]{:S(2)}) %collective-permute-start.2) | collective-permute-done | bytes 184352 | tf_op jit(solution)/shard_map/ppermute | solution.py:418
  17.1 0.8 %collective-permute-done.refs_2_ = bf16[16,128]{1,0:T(8,128)(2,1)S(1)} collective-permute-done((bf16[16,128]{1,0:T(8,128)(2,1)S(1)}, bf16[16,128]{1,0:T(8,128)(2,1)S(1)}, u32[]{:S(2)}, u32[]{:S(2)}) %collective-permute-start) | collective-permute-done | bytes 4128 | tf_op jit(solution)/shard_map/ppermute | solution.py:418
  18.0 1.0 %copy-done.2 = bf16[128,2048]{1,0:T(8,128)(2,1)S(1)} copy-done((bf16[128,2048]{1,0:T(8,128)(2,1)S(1)}, bf16[128,2048]{1,0:T(8,128)(2,1)}, u32[]{:S(2)}) %copy-start.2) | copy-done | bytes 524312
  19.0 0.8 %shard_map.95 = (bf16[192,640]{1,0:T(8,128)(2,1)S(1)}, bf16[192,640]{1,0:T(8,128)(2,1)S(1)}, bf16[384,128]{1,0:T(8,128)(2,1)S(1)}) custom-call(s32[2]{0:T(128)S(1)} %pad_add_fusion.refs_0_.place_ref, bf16[16,128]{1,0:T(8,128)(2,1)S(1)} %get-tuple-element.40.refs_1_.meta_ref, bf16[16,128]{1,0:T(8,128)(2,1)S(1)} %collective-permute-done.refs_2_, ...), custom_call_target="tpu_custom_call" | custom-call | flops 983040 | bytes 20480 | tf_op jit(solution)/shard_map/pallas_call | solution.py:130
  19.9 4.0 %collective-permute-start.4 = (bf16[192,640]{1,0:T(8,128)(2,1)S(1)}, bf16[192,640]{1,0:T(8,128)(2,1)S(1)}, u32[]{:S(2)}, u32[]{:S(2)}) collective-permute-start(bf16[192,640]{1,0:T(8,128)(2,1)S(1)} %get-tuple-element.43.refs_1_), channel_id=1, source_target_pairs={{0,2},{1,3},{2,0},{3,1},{4,6},{5,7},{6,4},{7,5},{8,10},{9,11},{10,... | collective-permute-start | bytes 737288 | tf_op jit(solution)/shard_map/ppermute | solution.py:418
  23.8 12.2 %collective-permute-done.5.refs_0_ = bf16[128,1408]{1,0:T(8,128)(2,1)S(1)} collective-permute-done((bf16[128,1408]{1,0:T(8,128)(2,1)S(1)}, bf16[128,1408]{1,0:T(8,128)(2,1)S(1)}, u32[]{:S(2)}, u32[]{:S(2)}) %collective-permute-start.5) | collective-permute-done | bytes 360480 | tf_op jit(solution)/shard_map/ppermute | solution.py:418
  36.1 1.0 %shard_map.93 = (bf16[768,384]{1,0:T(8,128)(2,1)S(1)}, bf16[384,768]{1,0:T(8,128)(2,1)S(1)}, f32[384,768]{1,0:T(8,128)S(1)}, f32[384,768]{1,0:T(8,128)S(1)}) custom-call(bf16[384,768]{1,0:T(8,128)(2,1)S(1)} %bitcast.14, bf16[384,768]{1,0:T(8,128)(2,1)S(1)} %bitcast.15), custom_call_target="tpu_custom_call" | custom-call | flops 92160 | bytes 73728 | tf_op jit(solution)/shard_map/pallas_call | solution.py:155
  37.1 1.3 %shard_map.96 = (bf16[384,640]{1,0:T(8,128)(2,1)S(1)}, f32[192,640]{1,0:T(8,128)S(1)}, f32[192,640]{1,0:T(8,128)S(1)}, bf16[384,640]{1,0:T(8,128)(2,1)S(1)}) custom-call(s32[2]{0:T(128)S(1)} %pad_add_fusion.refs_0_.place_ref, bf16[768,384]{1,0:T(8,128)(2,1)S(1)} %get-tuple-element.39.turned_ref, bf16[192,640]{1,0:T(8,128)(2,1)S(1)} %get-tuple-element.42.local_ref, ...), custom_call_target="tpu_custom_call" | custom-call | flops 5898240 | bytes 24576 | tf_op jit(solution)/shard_map/pallas_call | solution.py:199
  38.5 1.6 %collective-permute-start.9 = (bf16[384,640]{1,0:T(8,128)(2,1)S(1)}, bf16[384,640]{1,0:T(8,128)(2,1)S(1)}, u32[]{:S(2)}, u32[]{:S(2)}) collective-permute-start(bf16[384,640]{1,0:T(8,128)(2,1)S(1)} %get-tuple-element.54), channel_id=1, source_target_pairs={{0,8},{1,17},{2,10},{3,19},{4,12},{5,21},{6,14},{7,23},{8,0},{9,25... | collective-permute-start | bytes 1474568 | tf_op jit(solution)/shard_map/ppermute | solution.py:428
  40.8 2.1 %collective-permute-start.8 = (bf16[192,640]{1,0:T(8,128)(2,1)S(1)}, bf16[192,640]{1,0:T(8,128)(2,1)S(1)}, u32[]{:S(2)}, u32[]{:S(2)}) collective-permute-start(bf16[192,640]{1,0:T(8,128)(2,1)S(1)} %get-tuple-element.51), channel_id=1, source_target_pairs={{0,2},{1,3},{2,0},{3,1},{4,6},{5,7},{6,4},{7,5},{8,10},{9,11},{10,... | collective-permute-start | bytes 737288 | tf_op jit(solution)/shard_map/ppermute | solution.py:418
  42.9 4.5 %collective-permute-done.9.arrived_ref = bf16[384,640]{1,0:T(8,128)(2,1)S(1)} collective-permute-done((bf16[384,640]{1,0:T(8,128)(2,1)S(1)}, bf16[384,640]{1,0:T(8,128)(2,1)S(1)}, u32[]{:S(2)}, u32[]{:S(2)}) %collective-permute-start.9) | collective-permute-done | bytes 491552 | tf_op jit(solution)/shard_map/ppermute | solution.py:428
  47.5 1.6 %collective-permute-start.10 = (bf16[192,640]{1,0:T(8,128)(2,1)S(1)}, bf16[192,640]{1,0:T(8,128)(2,1)S(1)}, u32[]{:S(2)}, u32[]{:S(2)}) collective-permute-start(bf16[192,640]{1,0:T(8,128)(2,1)S(1)} %get-tuple-element.55), channel_id=1, source_target_pairs={{0,16},{1,9},{2,18},{3,11},{4,20},{5,13},{6,22},{7,15},{8,24},{9,1... | collective-permute-start | bytes 737288 | tf_op jit(solution)/shard_map/ppermute | solution.py:428
  49.1 1.1 %shard_map.97.refs_0_.held_ref = f32[384,768]{1,0:T(8,128)S(1)} custom-call(bf16[384,640]{1,0:T(8,128)(2,1)S(1)} %get-tuple-element.44.rows_ref, bf16[768,2048]{1,0:T(8,128)(2,1)S(1)} %bitcast.11), custom_call_target="tpu_custom_call" | custom-call | flops 5898240 | bytes 36864 | tf_op jit(solution)/shard_map/pallas_call | solution.py:287
  50.3 1.4 %shard_map.100 = (bf16[384,768]{1,0:T(8,128)(2,1)S(1)}, f32[192,768]{1,0:T(8,128)S(1)}, f32[192,768]{1,0:T(8,128)S(1)}, bf16[384,768]{1,0:T(8,128)(2,1)S(1)}) custom-call(s32[2]{0:T(128)S(1)} %pad_add_fusion.refs_0_.place_ref, bf16[768,384]{1,0:T(8,128)(2,1)S(1)} %get-tuple-element.39.turned_ref, bf16[192,768]{1,0:T(8,128)(2,1)S(1)} %get-tuple-element.47.local_ref, ...), custom_call_target="tpu_custom_call" | custom-call | flops 7077888 | bytes 27648 | tf_op jit(solution)/shard_map/pallas_call | solution.py:199
  51.7 1.5 %collective-permute-start.11 = (bf16[384,768]{1,0:T(8,128)(2,1)S(1)}, bf16[384,768]{1,0:T(8,128)(2,1)S(1)}, u32[]{:S(2)}, u32[]{:S(2)}) collective-permute-start(bf16[384,768]{1,0:T(8,128)(2,1)S(1)} %get-tuple-element.65), channel_id=1, source_target_pairs={{0,8},{1,17},{2,10},{3,19},{4,12},{5,21},{6,14},{7,23},{8,0},{9,25... | collective-permute-start | bytes 1769480 | tf_op jit(solution)/shard_map/ppermute | solution.py:428
  53.1 1.3 %shard_map.101.refs_0_.held_ref = f32[384,768]{1,0:T(8,128)S(1)} custom-call(f32[384,768]{1,0:T(8,128)S(1)} %shard_map.97.refs_0_.held_ref, bf16[384,768]{1,0:T(8,128)(2,1)S(1)} %get-tuple-element.49.rows_ref, bf16[768,2048]{1,0:T(8,128)(2,1)S(1)} %bitcast.12), custom_call_target="tpu_custom_call" | custom-call | flops 7077888 | bytes 36864 | tf_op jit(solution)/shard_map/pallas_call | solution.py:287
  54.9 1.3 %shard_map.104 = (bf16[384,640]{1,0:T(8,128)(2,1)S(1)}, f32[192,640]{1,0:T(8,128)S(1)}, f32[192,640]{1,0:T(8,128)S(1)}, bf16[384,640]{1,0:T(8,128)(2,1)S(1)}) custom-call(s32[2]{0:T(128)S(1)} %pad_add_fusion.refs_0_.place_ref, bf16[768,384]{1,0:T(8,128)(2,1)S(1)} %get-tuple-element.39.turned_ref, bf16[192,640]{1,0:T(8,128)(2,1)S(1)} %get-tuple-element.50.local_ref, ...), custom_call_target="tpu_custom_call" | custom-call | flops 5898240 | bytes 24576 | tf_op jit(solution)/shard_map/pallas_call | solution.py:199
  56.2 1.0 %collective-permute-start.13 = (bf16[384,640]{1,0:T(8,128)(2,1)S(1)}, bf16[384,640]{1,0:T(8,128)(2,1)S(1)}, u32[]{:S(2)}, u32[]{:S(2)}) collective-permute-start(bf16[384,640]{1,0:T(8,128)(2,1)S(1)} %get-tuple-element.70), channel_id=1, source_target_pairs={{0,8},{1,17},{2,10},{3,19},{4,12},{5,21},{6,14},{7,23},{8,0},{9,25... | collective-permute-start | bytes 1474568 | tf_op jit(solution)/shard_map/ppermute | solution.py:428
  57.2 2.7 %shard_map.105 = (bf16[384,768]{1,0:T(8,128)(2,1)}, bf16[384,768]{1,0:T(8,128)(2,1)}, f32[8,128]{1,0:T(8,128)S(1)}) custom-call(f32[384,768]{1,0:T(8,128)S(1)} %shard_map.101.refs_0_.held_ref, bf16[384,640]{1,0:T(8,128)(2,1)S(1)} %get-tuple-element.56.rows_ref, bf16[768,2048]{1,0:T(8,128)(2,1)S(1)} %bitcast.13, ...), custom_call_target="tpu_custom_call" | custom-call | flops 5898240 | bytes 55296 | tf_op jit(solution)/shard_map/pallas_call | solution.py:345
  59.9 1.7 %collective-permute-done.11.arrived_ref = bf16[384,768]{1,0:T(8,128)(2,1)S(1)} collective-permute-done((bf16[384,768]{1,0:T(8,128)(2,1)S(1)}, bf16[384,768]{1,0:T(8,128)(2,1)S(1)}, u32[]{:S(2)}, u32[]{:S(2)}) %collective-permute-start.11) | collective-permute-done | bytes 589856 | tf_op jit(solution)/shard_map/ppermute | solution.py:428
  61.7 1.7 %collective-permute-start.12 = (bf16[192,768]{1,0:T(8,128)(2,1)S(1)}, bf16[192,768]{1,0:T(8,128)(2,1)S(1)}, u32[]{:S(2)}, u32[]{:S(2)}) collective-permute-start(bf16[192,768]{1,0:T(8,128)(2,1)S(1)} %get-tuple-element.67), channel_id=1, source_target_pairs={{0,16},{1,9},{2,18},{3,11},{4,20},{5,13},{6,22},{7,15},{8,24},{9,1... | collective-permute-start | bytes 884744 | tf_op jit(solution)/shard_map/ppermute | solution.py:428
  63.4 7.1 %collective-permute-done.13.arrived_ref = bf16[384,640]{1,0:T(8,128)(2,1)S(1)} collective-permute-done((bf16[384,640]{1,0:T(8,128)(2,1)S(1)}, bf16[384,640]{1,0:T(8,128)(2,1)S(1)}, u32[]{:S(2)}, u32[]{:S(2)}) %collective-permute-start.13) | collective-permute-done | bytes 491552 | tf_op jit(solution)/shard_map/ppermute | solution.py:428
  70.6 1.3 %collective-permute-start.14 = (bf16[192,640]{1,0:T(8,128)(2,1)S(1)}, bf16[192,640]{1,0:T(8,128)(2,1)S(1)}, u32[]{:S(2)}, u32[]{:S(2)}) collective-permute-start(bf16[192,640]{1,0:T(8,128)(2,1)S(1)} %get-tuple-element.72), channel_id=1, source_target_pairs={{0,16},{1,9},{2,18},{3,11},{4,20},{5,13},{6,22},{7,15},{8,24},{9,1... | collective-permute-start | bytes 737288 | tf_op jit(solution)/shard_map/ppermute | solution.py:428
  72.0 0.7 collective-permute-start.16
  72.6 3.0 %collective-permute-done.16 = f32[16,128]{1,0:T(8,128)S(1)} collective-permute-done((f32[16,128]{1,0:T(8,128)S(1)}, f32[16,128]{1,0:T(8,128)S(1)}, u32[]{:S(2)}, u32[]{:S(2)}) %collective-permute-start.16) | collective-permute-done | bytes 8224 | tf_op jit(solution)/shard_map/ppermute | solution.py:418
  76.0 0.8 %shard_map.106.refs_0_ = f32[192,2048]{1,0:T(8,128)} custom-call(f32[192,640]{1,0:T(8,128)S(1)} %get-tuple-element.62.refs_0_, bf16[192,640]{1,0:T(8,128)(2,1)S(1)} %collective-permute-done.10.refs_1_), custom_call_target="tpu_custom_call" | custom-call | flops 3840 | bytes 19200 | tf_op jit(solution)/shard_map/pallas_call | solution.py:249
  76.9 3.4 %collective-permute-done.17.far_ref = f32[32,128]{1,0:T(8,128)S(1)} collective-permute-done((f32[32,128]{1,0:T(8,128)S(1)}, f32[32,128]{1,0:T(8,128)S(1)}, u32[]{:S(2)}, u32[]{:S(2)}) %collective-permute-start.17) | collective-permute-done | bytes 16416 | tf_op jit(solution)/shard_map/ppermute | solution.py:418
  80.3 1.3 %shard_map.111 = f32[2,128]{1,0:T(2,128)} custom-call(s32[2]{0:T(128)S(1)} %pad_add_fusion.refs_0_.place_ref, bf16[16,128]{1,0:T(8,128)(2,1)S(1)} %get-tuple-element.40.refs_1_.meta_ref, f32[32,128]{1,0:T(8,128)S(1)} %constant_dynamic-update-slice_fusion.near_ref, f32[32,128]{1,0:T(8,128)S(1)} %collective-permute-done.17.far_ref), custom_call_target="tpu_custom_call" | custom-call | flops 15625 | bytes 1562 | tf_op jit(solution)/shard_map/pallas_call | solution.py:390
  81.6 0.9 %shard_map.108.refs_0_ = f32[192,2048]{1,0:T(8,128)} custom-call(f32[192,2048]{1,0:T(8,128)} %shard_map.106.refs_0_, f32[192,768]{1,0:T(8,128)S(1)} %get-tuple-element.66.refs_1_, bf16[192,768]{1,0:T(8,128)(2,1)S(1)} %collective-permute-done.12.refs_2_), custom_call_target="tpu_custom_call", output_to_operand_aliasing={{}: (0, {})} | custom-call | flops 4608 | bytes 23040 | tf_op jit(solution)/shard_map/pallas_call | solution.py:249
  82.5 0.8 shard_map.110
  (44 shorter events, 4.5 us)
Async XLA Ops:
  0.6 17.3 %collective-permute-start.1 = (bf16[128,2048]{1,0:T(8,128)(2,1)}, bf16[128,2048]{1,0:T(8,128)(2,1)S(1)}, u32[]{:S(2)}, u32[]{:S(2)}) collective-permute-start(bf16[128,2048]{1,0:T(8,128)(2,1)} %refs_1_.3), channel_id=1, source_target_pairs={{0,1},{1,0},{2,3},{3,2},{4,5},{5,4},{6,7},{7,6},{8,9},{9,8},{10,11... | collective-permute-start | bytes 1572872 | tf_op jit(solution)/shard_map/ppermute | solution.py:418
  1.1 1.0 %copy-start.1 = (bf16[128,2048]{1,0:T(8,128)(2,1)S(1)}, bf16[128,2048]{1,0:T(8,128)(2,1)}, u32[]{:S(2)}) copy-start(bf16[128,2048]{1,0:T(8,128)(2,1)} %refs_1_.3) | copy-start | bytes 1572868
  2.2 0.7 copy-start.6
  2.9 0.7 copy-start.7
  3.7 12.9 %collective-permute-start.2 = (bf16[144,640]{1,0:T(8,128)(2,1)S(1)}, bf16[144,640]{1,0:T(8,128)(2,1)S(1)}, u32[]{:S(2)}, u32[]{:S(2)}) collective-permute-start(bf16[144,640]{1,0:T(8,128)(2,1)S(1)} %get-tuple-element.41), channel_id=1, source_target_pairs={{0,4},{1,5},{2,6},{3,7},{4,0},{5,1},{6,2},{7,3},{8,12},{9,13},{10,... | collective-permute-start | bytes 552968 | tf_op jit(solution)/shard_map/ppermute | solution.py:418
  16.5 1.4 %collective-permute-start.3 = (bf16[144,640]{1,0:T(8,128)(2,1)S(1)}, bf16[144,640]{1,0:T(8,128)(2,1)S(1)}, u32[]{:S(2)}, u32[]{:S(2)}) collective-permute-start(bf16[144,640]{1,0:T(8,128)(2,1)S(1)} %collective-permute-done.2.refs_5_), channel_id=1, source_target_pairs={{0,1},{1,0},{2,3},{3,2},{4,5},{5,4},{6,7},{7,6},{8,9},{9,8},{10,11... | collective-permute-start | bytes 552968 | tf_op jit(solution)/shard_map/ppermute | solution.py:418
  16.5 19.6 %collective-permute-start.5 = (bf16[128,1408]{1,0:T(8,128)(2,1)S(1)}, bf16[128,1408]{1,0:T(8,128)(2,1)S(1)}, u32[]{:S(2)}, u32[]{:S(2)}) collective-permute-start(bf16[128,1408]{1,0:T(8,128)(2,1)S(1)} %get-tuple-element.46), channel_id=1, source_target_pairs={{0,4},{1,5},{2,6},{3,7},{4,0},{5,1},{6,2},{7,3},{8,12},{9,13},{10,... | collective-permute-start | bytes 1081352 | tf_op jit(solution)/shard_map/ppermute | solution.py:418
  16.5 1.4 %collective-permute-start = (bf16[16,128]{1,0:T(8,128)(2,1)S(1)}, bf16[16,128]{1,0:T(8,128)(2,1)S(1)}, u32[]{:S(2)}, u32[]{:S(2)}) collective-permute-start(bf16[16,128]{1,0:T(8,128)(2,1)S(1)} %get-tuple-element.40.refs_1_.meta_ref), channel_id=1, source_target_pairs={{0,1},{1,0},{2,3},{3,2},{4,5},{5,4},{6,7},{7,6},{8,9},{9,8},{10,11... | collective-permute-start | bytes 12296 | tf_op jit(solution)/shard_map/ppermute | solution.py:418
  18.0 1.0 %copy-start.2 = (bf16[128,2048]{1,0:T(8,128)(2,1)S(1)}, bf16[128,2048]{1,0:T(8,128)(2,1)}, u32[]{:S(2)}) copy-start(bf16[128,2048]{1,0:T(8,128)(2,1)} %refs_1_.3) | copy-start | bytes 1572868
  19.0 17.1 %copy-start.4 = (bf16[1,1,8,48,768]{4,3,2,1,0:T(8,128)(2,1)S(1)}, bf16[1,1,8,48,768]{4,3,2,1,0:T(8,128)(2,1)}, u32[]{:S(2)}) copy-start(bf16[1,1,8,48,768]{4,3,2,1,0:T(8,128)(2,1)} %param.9) | copy-start | bytes 1769476
  19.0 17.1 %copy-start.5 = (bf16[1,1,8,48,768]{4,3,2,1,0:T(8,128)(2,1)S(1)}, bf16[1,1,8,48,768]{4,3,2,1,0:T(8,128)(2,1)}, u32[]{:S(2)}) copy-start(bf16[1,1,8,48,768]{4,3,2,1,0:T(8,128)(2,1)} %param.10) | copy-start | bytes 1769476
  19.9 20.2 %copy-start.3 = (bf16[128,2048]{1,0:T(8,128)(2,1)S(1)}, bf16[128,2048]{1,0:T(8,128)(2,1)}, u32[]{:S(2)}) copy-start(bf16[128,2048]{1,0:T(8,128)(2,1)} %refs_1_.3) | copy-start | bytes 1572868
  19.9 17.3 %collective-permute-start.4 = (bf16[192,640]{1,0:T(8,128)(2,1)S(1)}, bf16[192,640]{1,0:T(8,128)(2,1)S(1)}, u32[]{:S(2)}, u32[]{:S(2)}) collective-permute-start(bf16[192,640]{1,0:T(8,128)(2,1)S(1)} %get-tuple-element.43.refs_1_), channel_id=1, source_target_pairs={{0,2},{1,3},{2,0},{3,1},{4,6},{5,7},{6,4},{7,5},{8,10},{9,11},{10,... | collective-permute-start | bytes 737288 | tf_op jit(solution)/shard_map/ppermute | solution.py:418
  36.1 4.0 %collective-permute-start.6 = (bf16[128,1408]{1,0:T(8,128)(2,1)S(1)}, bf16[128,1408]{1,0:T(8,128)(2,1)S(1)}, u32[]{:S(2)}, u32[]{:S(2)}) collective-permute-start(bf16[128,1408]{1,0:T(8,128)(2,1)S(1)} %shard_map.98.refs_3_), channel_id=1, source_target_pairs={{0,1},{1,0},{2,3},{3,2},{4,5},{5,4},{6,7},{7,6},{8,9},{9,8},{10,11... | collective-permute-start | bytes 1081352 | tf_op jit(solution)/shard_map/ppermute | solution.py:418
  38.5 8.9 %collective-permute-start.9 = (bf16[384,640]{1,0:T(8,128)(2,1)S(1)}, bf16[384,640]{1,0:T(8,128)(2,1)S(1)}, u32[]{:S(2)}, u32[]{:S(2)}) collective-permute-start(bf16[384,640]{1,0:T(8,128)(2,1)S(1)} %get-tuple-element.54), channel_id=1, source_target_pairs={{0,8},{1,17},{2,10},{3,19},{4,12},{5,21},{6,14},{7,23},{8,0},{9,25... | collective-permute-start | bytes 1474568 | tf_op jit(solution)/shard_map/ppermute | solution.py:428
  40.4 8.7 %copy-start = (bf16[1,768,2048]{2,1,0:T(8,128)(2,1)S(1)}, bf16[1,768,2048]{2,1,0:T(8,128)(2,1)}, u32[]{:S(2)}) copy-start(bf16[1,768,2048]{2,1,0:T(8,128)(2,1)} %param.11) | copy-start | bytes 9437188
  40.4 9.9 %collective-permute-start.7 = (bf16[192,768]{1,0:T(8,128)(2,1)S(1)}, bf16[192,768]{1,0:T(8,128)(2,1)S(1)}, u32[]{:S(2)}, u32[]{:S(2)}) collective-permute-start(bf16[192,768]{1,0:T(8,128)(2,1)S(1)} %get-tuple-element.48), channel_id=1, source_target_pairs={{0,2},{1,3},{2,0},{3,1},{4,6},{5,7},{6,4},{7,5},{8,10},{9,11},{10,... | collective-permute-start | bytes 884744 | tf_op jit(solution)/shard_map/ppermute | solution.py:418
  40.8 14.1 %collective-permute-start.8 = (bf16[192,640]{1,0:T(8,128)(2,1)S(1)}, bf16[192,640]{1,0:T(8,128)(2,1)S(1)}, u32[]{:S(2)}, u32[]{:S(2)}) collective-permute-start(bf16[192,640]{1,0:T(8,128)(2,1)S(1)} %get-tuple-element.51), channel_id=1, source_target_pairs={{0,2},{1,3},{2,0},{3,1},{4,6},{5,7},{6,4},{7,5},{8,10},{9,11},{10,... | collective-permute-start | bytes 737288 | tf_op jit(solution)/shard_map/ppermute | solution.py:418
  47.5 7.4 %collective-permute-start.10 = (bf16[192,640]{1,0:T(8,128)(2,1)S(1)}, bf16[192,640]{1,0:T(8,128)(2,1)S(1)}, u32[]{:S(2)}, u32[]{:S(2)}) collective-permute-start(bf16[192,640]{1,0:T(8,128)(2,1)S(1)} %get-tuple-element.55), channel_id=1, source_target_pairs={{0,16},{1,9},{2,18},{3,11},{4,20},{5,13},{6,22},{7,15},{8,24},{9,1... | collective-permute-start | bytes 737288 | tf_op jit(solution)/shard_map/ppermute | solution.py:428
  51.7 9.9 %collective-permute-start.11 = (bf16[384,768]{1,0:T(8,128)(2,1)S(1)}, bf16[384,768]{1,0:T(8,128)(2,1)S(1)}, u32[]{:S(2)}, u32[]{:S(2)}) collective-permute-start(bf16[384,768]{1,0:T(8,128)(2,1)S(1)} %get-tuple-element.65), channel_id=1, source_target_pairs={{0,8},{1,17},{2,10},{3,19},{4,12},{5,21},{6,14},{7,23},{8,0},{9,25... | collective-permute-start | bytes 1769480 | tf_op jit(solution)/shard_map/ppermute | solution.py:428
  56.2 14.3 %collective-permute-start.13 = (bf16[384,640]{1,0:T(8,128)(2,1)S(1)}, bf16[384,640]{1,0:T(8,128)(2,1)S(1)}, u32[]{:S(2)}, u32[]{:S(2)}) collective-permute-start(bf16[384,640]{1,0:T(8,128)(2,1)S(1)} %get-tuple-element.70), channel_id=1, source_target_pairs={{0,8},{1,17},{2,10},{3,19},{4,12},{5,21},{6,14},{7,23},{8,0},{9,25... | collective-permute-start | bytes 1474568 | tf_op jit(solution)/shard_map/ppermute | solution.py:428
  59.9 12.0 %collective-permute-start.15 = (f32[8,128]{1,0:T(8,128)S(1)}, f32[8,128]{1,0:T(8,128)S(1)}, u32[]{:S(2)}, u32[]{:S(2)}) collective-permute-start(f32[8,128]{1,0:T(8,128)S(1)} %get-tuple-element.73), channel_id=1, source_target_pairs={{0,1},{1,0},{2,3},{3,2},{4,5},{5,4},{6,7},{7,6},{8,9},{9,8},{10,11... | collective-permute-start | bytes 12296 | tf_op jit(solution)/shard_map/ppermute | solution.py:418
  61.7 19.9 %collective-permute-start.12 = (bf16[192,768]{1,0:T(8,128)(2,1)S(1)}, bf16[192,768]{1,0:T(8,128)(2,1)S(1)}, u32[]{:S(2)}, u32[]{:S(2)}) collective-permute-start(bf16[192,768]{1,0:T(8,128)(2,1)S(1)} %get-tuple-element.67), channel_id=1, source_target_pairs={{0,16},{1,9},{2,18},{3,11},{4,20},{5,13},{6,22},{7,15},{8,24},{9,1... | collective-permute-start | bytes 884744 | tf_op jit(solution)/shard_map/ppermute | solution.py:428
  70.6 11.8 %collective-permute-start.14 = (bf16[192,640]{1,0:T(8,128)(2,1)S(1)}, bf16[192,640]{1,0:T(8,128)(2,1)S(1)}, u32[]{:S(2)}, u32[]{:S(2)}) collective-permute-start(bf16[192,640]{1,0:T(8,128)(2,1)S(1)} %get-tuple-element.72), channel_id=1, source_target_pairs={{0,16},{1,9},{2,18},{3,11},{4,20},{5,13},{6,22},{7,15},{8,24},{9,1... | collective-permute-start | bytes 737288 | tf_op jit(solution)/shard_map/ppermute | solution.py:428
  72.0 3.7 %collective-permute-start.16 = (f32[16,128]{1,0:T(8,128)S(1)}, f32[16,128]{1,0:T(8,128)S(1)}, u32[]{:S(2)}, u32[]{:S(2)}) collective-permute-start(f32[16,128]{1,0:T(8,128)S(1)} %pad_maximum_fusion), channel_id=1, source_target_pairs={{0,2},{1,3},{2,0},{3,1},{4,6},{5,7},{6,4},{7,5},{8,10},{9,11},{10,... | collective-permute-start | bytes 24584 | tf_op jit(solution)/shard_map/ppermute | solution.py:418
  75.6 4.6 %collective-permute-start.17 = (f32[32,128]{1,0:T(8,128)S(1)}, f32[32,128]{1,0:T(8,128)S(1)}, u32[]{:S(2)}, u32[]{:S(2)}) collective-permute-start(f32[32,128]{1,0:T(8,128)S(1)} %constant_dynamic-update-slice_fusion.near_ref), channel_id=1, source_target_pairs={{0,4},{1,5},{2,6},{3,7},{4,0},{5,1},{6,2},{7,3},{8,12},{9,13},{10,... | collective-permute-start | bytes 49160 | tf_op jit(solution)/shard_map/ppermute | solution.py:418

commit v4 on v3

--- a/solution.py
+++ b/solution.py
@@ -9,13 +9,11 @@
 
 LANES = 128
 META = 16
-OFFSETS = (0, 1, 4, 5)
-WIDTHS = (640, 768, 640)
-FIRST_PART = WIDTHS[0]
+PARTS = ((768,), (640, 640))
 VMEM_LIMIT = 10 * 1024 * 1024
 VMEM = pl.BlockSpec(memory_space=pltpu.VMEM)
 ANY = pl.BlockSpec(memory_space=pl.ANY)
-SMEM = pl.BlockSpec(memory_space=pltpu.SMEM)
+HBM = pl.BlockSpec(memory_space=pltpu.HBM)
 
 
 def params():
@@ -31,8 +29,29 @@
     return (gate_value * sigmoid, sigmoid * (1.0 + gate_value * (1.0 - sigmoid)))
 
 
-def tokens_kernel(expert_count, routes_ref, probs_ref, rows_ref, meta_ref, *part_refs):
-    top_count, token_count = routes_ref.shape
+def tokens_kernel(expert_count, routes_hbm, probs_hbm, rows_hbm, meta_ref, *refs):
+    part_refs, (routes_ref, probs_ref, semaphores) = refs[:-3], refs[-3:]
+    token_count = rows_hbm.shape[0]
+    top_count = routes_ref.shape[0]
+    copies = [
+        pltpu.make_async_copy(routes_hbm, routes_ref, semaphores.at[0]),
+        pltpu.make_async_copy(probs_hbm, probs_ref, semaphores.at[1]),
+    ]
+    start = 0
+    for part, part_ref in enumerate(part_refs):
+        width = part_ref.shape[1]
+        copies.append(
+            pltpu.make_async_copy(
+                rows_hbm.at[:, start : start + width],
+                part_ref.at[:token_count, :],
+                semaphores.at[2 + part],
+            )
+        )
+        start += width
+    for copy in copies:
+        copy.start()
+    for copy in copies[:2]:
+        copy.wait()
     names = [routes_ref[k : k + 1, :] for k in range(top_count)]
     experts = lax.broadcasted_iota(jnp.int32, (expert_count, token_count), 0)
     onehots = [(experts == name).astype(jnp.float32) for name in names]
@@ -52,36 +71,39 @@
     lines.append(jnp.zeros((META - len(lines), token_count), jnp.float32))
     meta = jnp.concatenate(lines, axis=0).astype(jnp.bfloat16)
     meta_ref[...] = meta
-    start = 0
-    for part, part_ref in enumerate(part_refs):
-        width = part_ref.shape[1]
-        part_ref[:token_count, :] = rows_ref[:, start : start + width]
-        if part == 0:
-            part_ref[token_count:, :] = jnp.zeros((META, width), jnp.bfloat16)
-            part_ref[token_count:, :token_count] = meta
-        start += width
-
-
-def token_parts(routes, probs, grad_out, expert_count, widths):
+    lead_ref = part_refs[0]
+    lead_ref[token_count:, :] = jnp.zeros((META, lead_ref.shape[1]), jnp.bfloat16)
+    lead_ref[token_count:, :token_count] = meta
+    for copy in copies[2:]:
+        copy.wait()
+
+
+def token_parts(routes, probs, grad_out, expert_count):
     token_count = routes.shape[1]
     return pl.pallas_call(
         functools.partial(tokens_kernel, expert_count),
-        in_specs=[VMEM] * 3,
+        in_specs=[HBM] * 3,
         out_shape=[jax.ShapeDtypeStruct((META, token_count), jnp.bfloat16)]
         + [
             jax.ShapeDtypeStruct((token_count + (0 if part else META), width), jnp.bfloat16)
-            for part, width in enumerate(widths)
+            for part, width in enumerate(map(sum, PARTS))
+        ],
+        scratch_shapes=[
+            pltpu.VMEM(routes.shape, routes.dtype),
+            pltpu.VMEM(probs.shape, probs.dtype),
+            pltpu.SemaphoreType.DMA((2 + len(PARTS),)),
         ],
         compiler_params=params(),
         cost_estimate=cost(100 * token_count * token_count, 4 * grad_out.size),
     )(routes, probs, grad_out)
 
 
-def chosen_rows(meta, top_count, capacity, targets):
+def chosen_rows(meta, top_count, capacity):
     token_count = meta.shape[1]
     slots = lax.broadcasted_iota(jnp.int32, (capacity, token_count), 0).astype(jnp.float32)
     parts = []
-    for target in targets:
+    for offset in (0, 2):
+        target = lax.bitwise_xor(lax.axis_index("expert"), offset).astype(jnp.float32)
         part = jnp.zeros((capacity, token_count), jnp.float32)
         for k in range(top_count):
             name, slot, prob = (meta[k + top_count * i :][:1, :] for i in range(3))
@@ -91,51 +113,31 @@
     return jnp.concatenate(parts, axis=0).astype(jnp.bfloat16)
 
 
-def dispatch_kernel(capacity, top_count, starts, first, *refs):
-    if first:
-        place_ref, own_meta_ref, other_meta_ref, *refs = refs
-        row_refs, (local_ref, sent_ref, select_ref) = refs[:4], refs[4:]
-        token_count = own_meta_ref.shape[1]
-        targets = [
-            lax.bitwise_xor(place_ref[0], offset).astype(jnp.float32) for offset in (0, 2)
-        ]
-        for source in range(4):
-            if source < 2:
-                meta = (own_meta_ref, other_meta_ref)[source][...]
-            else:
-                meta = row_refs[source][token_count:, :token_count]
-            select_ref[2 * capacity * source : 2 * capacity * (source + 1), :] = chosen_rows(
-                meta.astype(jnp.float32), top_count, capacity, targets
-            )
-    else:
-        select_ref, *refs = refs
-        row_refs, (local_ref, sent_ref) = refs[:4], refs[4:]
-    token_count = select_ref.shape[1]
+def dispatch_kernel(capacity, top_count, start, *refs):
+    meta_refs, row_refs, (local_ref, sent_ref) = refs[:2], refs[2:4], refs[-2:]
+    token_count = meta_refs[0].shape[1] if meta_refs[0].shape[0] == META else LANES
     width = local_ref.shape[1]
-    for source, row_ref in enumerate(row_refs):
-        columns = slice(starts[source // 2], starts[source // 2] + width)
+    for source in range(2):
+        first = meta_refs[source].shape[0] - META
+        meta = meta_refs[source][first:, :token_count].astype(jnp.float32)
         rows = jnp.dot(
-            select_ref[2 * capacity * source : 2 * capacity * (source + 1), :],
-            row_ref[:token_count, columns],
+            chosen_rows(meta, top_count, capacity),
+            row_refs[source][:token_count, start : start + width],
             preferred_element_type=jnp.float32,
         ).astype(jnp.bfloat16)
         local_ref[source * capacity : (source + 1) * capacity, :] = rows[:capacity, :]
         sent_ref[source * capacity : (source + 1) * capacity, :] = rows[capacity:, :]
 
 
-def dispatch(lead, rows, capacity, top_count, token_count, starts, width):
-    first = len(lead) > 1
-    block = jax.ShapeDtypeStruct((4 * capacity, width), jnp.bfloat16)
-    chosen = jax.ShapeDtypeStruct((8 * capacity, token_count), jnp.bfloat16)
-    return pl.pallas_call(
-        functools.partial(dispatch_kernel, capacity, top_count, starts, first),
-        in_specs=([SMEM, VMEM, VMEM] if first else [VMEM]) + [VMEM] * 4,
-        out_shape=[block, block] + ([chosen] if first else []),
-        compiler_params=params(),
-        cost_estimate=cost(
-            16 * capacity * token_count * width, 4 * (8 * capacity + token_count) * width
-        ),
-    )(*lead, *rows)
+def dispatch(metas, rows, capacity, top_count, start, width, earlier=()):
+    block = jax.ShapeDtypeStruct((2 * capacity, width), jnp.bfloat16)
+    return pl.pallas_call(
+        functools.partial(dispatch_kernel, capacity, top_count, start),
+        in_specs=[VMEM] * 4 + [ANY] * len(earlier),
+        out_shape=[block, block],
+        compiler_params=params(),
+        cost_estimate=cost(8 * capacity * LANES * width, 8 * capacity * width),
+    )(*metas, *rows, *earlier)
 
 
 def hidden_kernel(gate_ref, up_ref, turned_ref, hidden_ref, up_scale_ref, gate_scale_ref):
@@ -168,37 +170,37 @@
     )(gate, up)
 
 
-def panel_kernel(capacity, place_ref, turned_ref, local_ref, near_ref, *refs):
-    rows_ref, own_ref, later_ref, sent_ref = refs[-4:]
-    share = own_ref.shape[0]
-    for source in range(4):
-        for offset, block_ref in ((0, local_ref), (2, near_ref)):
-            place = lax.bitwise_xor(place_ref[0], OFFSETS[source] + offset)
-            start = pl.multiple_of(place * capacity, capacity)
-            rows_ref[pl.ds(start, capacity), :] = block_ref[
-                source * capacity : (source + 1) * capacity, :
+def panel_kernel(capacity, columns, turned_ref, *refs):
+    block_refs, (rows_ref, own_ref, later_ref, sent_ref) = refs[:4], refs[-4:]
+    share, width = own_ref.shape
+    device = lax.axis_index("expert")
+    for block, (block_ref, column) in enumerate(zip(block_refs, columns)):
+        for half in range(2):
+            place = lax.bitwise_xor(device, 2 * block + half)
+            row = pl.multiple_of(place * capacity, capacity)
+            rows_ref[pl.ds(row, capacity), :] = block_ref[
+                half * capacity : (half + 1) * capacity, column : column + width
             ]
     rows = rows_ref[...]
 
     def part(offset):
-        owner = lax.bitwise_xor(place_ref[1], offset)
-        start = pl.multiple_of(owner * share, share)
-        return jnp.dot(turned_ref[pl.ds(start, share), :], rows, preferred_element_type=jnp.float32)
-
-    step = 1 + lax.bitwise_and(place_ref[0], 1)
+        owner = lax.bitwise_xor(lax.axis_index("dp"), offset)
+        row = pl.multiple_of(owner * share, share)
+        return jnp.dot(turned_ref[pl.ds(row, share), :], rows, preferred_element_type=jnp.float32)
+
+    step = 1 + lax.bitwise_and(device, 1)
     sent_ref[:share, :] = part(step).astype(jnp.bfloat16)
     sent_ref[share:, :] = part(3).astype(jnp.bfloat16)
     later_ref[...] = part(3 - step)
     own_ref[...] = part(0)
 
 
-def panel_parts(place, turned, local, near, capacity, earlier):
+def panel_parts(turned, blocks, capacity, width, earlier):
     hidden_width, row_count = turned.shape
-    width = local.shape[1]
     share = hidden_width // 4
     return pl.pallas_call(
-        functools.partial(panel_kernel, capacity),
-        in_specs=[SMEM] + [VMEM] * 3 + [ANY] * len(earlier),
+        functools.partial(panel_kernel, capacity, [column for _, column in blocks]),
+        in_specs=[VMEM] * 5 + [ANY] * len(earlier),
         out_shape=[
             jax.ShapeDtypeStruct((row_count, width), jnp.bfloat16),
             jax.ShapeDtypeStruct((share, width), jnp.float32),
@@ -209,10 +211,11 @@
         cost_estimate=cost(
             2 * hidden_width * row_count * width, 2 * hidden_width * (row_count + width)
         ),
-    )(place, turned, local, near, *earlier)
-
-
-def halve_kernel(own_ref, later_ref, arrived_ref, sum_ref, sent_ref):
+    )(turned, *[block for block, _ in blocks], *earlier)
+
+
+def halve_kernel(own_ref, later_ref, arrived_ref, *refs):
+    sum_ref, sent_ref = refs[-2:]
     share = own_ref.shape[0]
     sent_ref[...] = (later_ref[...] + arrived_ref[share:, :].astype(jnp.float32)).astype(
         jnp.bfloat16
@@ -220,42 +223,51 @@
     sum_ref[...] = own_ref[...] + arrived_ref[:share, :].astype(jnp.float32)
 
 
-def halve(own, later, arrived):
+def halve(own, later, arrived, earlier):
     return pl.pallas_call(
         halve_kernel,
-        in_specs=[VMEM] * 3,
+        in_specs=[VMEM] * 3 + [ANY] * len(earlier),
         out_shape=[
             jax.ShapeDtypeStruct(own.shape, jnp.float32),
             jax.ShapeDtypeStruct(own.shape, jnp.bfloat16),
         ],
         compiler_params=params(),
         cost_estimate=cost(4 * own.size, 18 * own.size),
-    )(own, later, arrived)
-
-
-def total_kernel(start, *refs):
-    own_ref, arrived_ref, total_ref, sum_ref, semaphore = refs[-5:]
-    sum_ref[...] = own_ref[...] + arrived_ref[...].astype(jnp.float32)
-    copy = pltpu.make_async_copy(
-        sum_ref, total_ref.at[:, start : start + sum_ref.shape[1]], semaphore
-    )
-    copy.start()
-    copy.wait()
-
-
-def total_chunk(held, own, arrived, start, model_width):
-    share, width = own.shape
-    first = held is None
-    return pl.pallas_call(
-        functools.partial(total_kernel, start),
-        in_specs=([] if first else [ANY]) + [VMEM] * 2,
-        out_specs=ANY,
-        out_shape=jax.ShapeDtypeStruct((share, model_width), jnp.float32),
-        scratch_shapes=[pltpu.VMEM((share, width), jnp.float32), pltpu.SemaphoreType.DMA],
-        input_output_aliases={} if first else {0: 0},
-        compiler_params=params(),
-        cost_estimate=cost(2 * share * width, 10 * share * width),
-    )(*([] if first else [held]), own, arrived)
+    )(own, later, arrived, *earlier)
+
+
+def total_kernel(count, *refs):
+    own_refs, arrived_refs = refs[:count], refs[count : 2 * count]
+    total_ref, *sum_refs, semaphores = refs[2 * count :]
+    copies = []
+    start = 0
+    for place, (own_ref, arrived_ref) in enumerate(zip(own_refs, arrived_refs)):
+        width = own_ref.shape[1]
+        sum_refs[place][...] = own_ref[...] + arrived_ref[...].astype(jnp.float32)
+        copies.append(
+            pltpu.make_async_copy(
+                sum_refs[place], total_ref.at[:, start : start + width], semaphores.at[place]
+            )
+        )
+        copies[-1].start()
+        start += width
+    for copy in copies:
+        copy.wait()
+
+
+def total(owns, arrived):
+    share = owns[0].shape[0]
+    size = share * sum(own.shape[1] for own in owns)
+    return pl.pallas_call(
+        functools.partial(total_kernel, len(owns)),
+        in_specs=[VMEM] * (2 * len(owns)),
+        out_specs=HBM,
+        out_shape=jax.ShapeDtypeStruct((share, size // share), jnp.float32),
+        scratch_shapes=[pltpu.VMEM(own.shape, jnp.float32) for own in owns]
+        + [pltpu.SemaphoreType.DMA((len(owns),))],
+        compiler_params=params(),
+        cost_estimate=cost(2 * size, 10 * size),
+    )(*owns, *arrived)
 
 
 def rows_times_weight(start, rows_ref, weight_ref):
@@ -362,13 +374,13 @@
     )(held, rows, weight, hidden, up_scale, gate_scale)
 
 
-def route_kernel(capacity, place_ref, meta_ref, near_ref, far_ref, out_ref, table_ref):
+def route_kernel(capacity, meta_ref, near_ref, far_ref, out_ref, table_ref):
     top_count, token_count = out_ref.shape
     expert_count = table_ref.shape[0]
     half = expert_count // 2
     for offset in range(expert_count):
         block_ref = near_ref if offset < half else far_ref
-        row = offset % half * expert_count + place_ref[0]
+        row = offset % half * expert_count + lax.axis_index("expert")
         table_ref[offset : offset + 1, :] = block_ref[pl.ds(row, 1), :]
     table = table_ref[...].T
     meta = meta_ref[...].astype(jnp.float32)
@@ -377,7 +389,7 @@
         name, slot, prob = (meta[k + top_count * i :][:1, :] for i in range(3))
         picked = jnp.zeros((capacity, token_count), jnp.float32)
         for offset in range(expert_count):
-            expert = lax.bitwise_xor(place_ref[0], offset).astype(jnp.float32)
+            expert = lax.bitwise_xor(lax.axis_index("expert"), offset).astype(jnp.float32)
             wanted = jnp.where(name == expert, slot, -1.0)
             picked = picked + jnp.where(
                 slots == wanted, table[:capacity, offset : offset + 1], 0.0
@@ -385,16 +397,16 @@
         out_ref[k : k + 1, :] = jnp.sum(picked, axis=0, keepdims=True) / prob
 
 
-def route_back(place, meta, near, far, expert_count, top_count, capacity):
+def route_back(meta, near, far, expert_count, top_count, capacity):
     token_count = meta.shape[1]
     return pl.pallas_call(
         functools.partial(route_kernel, capacity),
-        in_specs=[SMEM] + [VMEM] * 3,
+        in_specs=[VMEM] * 3,
         out_shape=jax.ShapeDtypeStruct((top_count, token_count), jnp.float32),
         scratch_shapes=[pltpu.VMEM((expert_count, LANES), jnp.float32)],
         compiler_params=params(),
         cost_estimate=cost(1000000, 100000),
-    )(place, meta, near, far)
+    )(meta, near, far)
 
 
 def after_kernel(*refs):
@@ -436,49 +448,56 @@
     top_count = routes.shape[1]
     row_count = expert_count * capacity
 
-    place = jnp.stack([lax.axis_index("expert"), lax.axis_index("dp")]).astype(jnp.int32)
-    part_widths = (FIRST_PART, model_width - FIRST_PART)
-    meta, *parts = token_parts(routes.T, probs.T, grad_out, expert_count, part_widths)
+    meta, *parts = token_parts(routes.T, probs.T, grad_out, expert_count)
     parts = [swap(part, 4) for part in parts]
-    other_rows, other_meta = swap(grad_out, 1), swap(meta, 1)
-    gate = saved_gate.reshape(row_count, hidden_width)
-    up = saved_up.reshape(row_count, hidden_width)
+    metas = [meta, swap(meta, 1)]
+    local, sent = dispatch(
+        metas, [grad_out, swap(grad_out, 1)], capacity, top_count, 0, model_width
+    )
+    near = swap(sent, 2)
     weight = w_down[0]
-    turned, hidden, up_scale, gate_scale = hidden_parts(gate, up)
-    lead = [place, meta, other_meta]
-    held, panel, start, halves = None, None, 0, []
-    for chunk, width in enumerate(WIDTHS):
-        part = int(start >= FIRST_PART)
-        starts = (start, start - part * FIRST_PART)
-        if start == FIRST_PART:
-            parts[part] = after(parts[part], sent)
-        if start in (0, FIRST_PART):
-            other_part = swap(parts[part], 1)
-        sources = [grad_out, other_rows, parts[part], other_part]
-        local, sent, *select = dispatch(
-            lead, sources, capacity, top_count, token_count, starts, width
+    turned, hidden, up_scale, gate_scale = hidden_parts(
+        saved_gate.reshape(row_count, hidden_width), saved_up.reshape(row_count, hidden_width)
+    )
+    held, start = None, 0
+    halves, owns, arrived = [], [], []
+    for part, widths in enumerate(PARTS):
+        part_start, part_width = start, sum(widths)
+        parts[part] = after(parts[part], sent)
+        other_part = swap(parts[part], 1)
+        far_metas = [parts[0], other_part] if part == 0 else far_metas
+        far_local, sent = dispatch(
+            far_metas,
+            [parts[part], other_part],
+            capacity,
+            top_count,
+            0,
+            part_width,
+            [near] if part == 0 else [],
         )
-        lead = select or lead
-        earlier = ([held] if chunk > 0 else []) + (halves[chunk - 2 : chunk - 1] if chunk > 1 else [])
-        rows, own, later, half = panel_parts(
-            place, turned, local, swap(sent, 2), capacity, earlier
-        )
-        own, half = halve(own, later, swap_groups(half, False))
-        half = swap_groups(half, True)
-        halves.append(half)
-        panel = total_chunk(panel, own, half, start, model_width)
-        if chunk + 1 < len(WIDTHS):
-            held = grad_hidden_step(held, rows, weight, start)
-        else:
-            grad_gate, grad_up, lines = grad_hidden_last(
-                held, rows, weight, start, hidden, up_scale, gate_scale, capacity
-            )
-        start += width
-    for offset in (1, 2):
-        lines = jnp.concatenate([lines, swap(lines, offset)], axis=0)
-    route_grad = route_back(
-        place, meta, lines, swap(lines, 4), expert_count, top_count, capacity
-    )
+        far_near = swap(sent, 2)
+        for width in widths:
+            blocks = [(local, start), (near, start)]
+            blocks += [(far_local, start - part_start), (far_near, start - part_start)]
+            earlier = ([] if held is None else [held]) + halves[:-1]
+            rows, own, later, half = panel_parts(turned, blocks, capacity, width, earlier)
+            earlier = []
+            if start + width < model_width:
+                held = grad_hidden_step(held, rows, weight, start)
+            else:
+                grad_gate, grad_up, lines = grad_hidden_last(
+                    held, rows, weight, start, hidden, up_scale, gate_scale, capacity
+                )
+                lines = jnp.concatenate([lines, swap(lines, 1)], axis=0)
+                earlier = [lines]
+            own, half = halve(own, later, swap_groups(half, False), earlier)
+            halves.append(half)
+            owns.append(own)
+            arrived.append(swap_groups(half, True))
+            start += width
+    lines = jnp.concatenate([lines, swap(lines, 2)], axis=0)
+    panel = total(owns, arrived)
+    route_grad = route_back(meta, lines, swap(lines, 4), expert_count, top_count, capacity)
     return (
         grad_gate.reshape(saved_gate.shape),
         grad_up.reshape(saved_up.shape),
@@ -548,7 +567,7 @@
         and capacity <= LANES
         and hidden_width % (16 * group_count) == 0
         and routes.shape[0] == LANES
-        and grad_out.shape[1] == sum(WIDTHS)
+        and grad_out.shape[1] == sum(map(sum, PARTS))
     )
     run = line_shards if aligned else plain_shards
     return run(grad_out, probs, routes, saved_gate, saved_up, w_down)

time: 83.6 us -> 81 us (0.969)
  waiting for transfers between devices: 42.6 us -> 48.4 us
  starting transfers between devices: 20.6 us -> 16.2 us
  Pallas kernels: 15.8 us -> 12 us
    ppermute x12, waiting for transfers between devices: 29.3 us -> 40.5 us  [swap(): lax.ppermute(value, 'expert', [(place, place ^ offset) for place in range...]
    ppermute x6, waiting for transfers between devices: 13.4 us -> 7.96 us  [swap_groups(): return lax.ppermute(value, ('dp', 'expert'), pairs)]
    ppermute x12, starting transfers between devices: 11.9 us -> 7.71 us  [swap(): lax.ppermute(value, 'expert', [(place, place ^ offset) for place in range...]
    pallas_call x10 -> x8, Pallas kernels: 8.19 us -> 4.71 us  [the longest x3 2.39 us: panel_parts(): pl.pallas_call(functools.partial(panel_kernel, capacity, [column for _, c...]
    unnamed x18 -> x16, local copies, waits for them, and re-layouts: 3.44 us -> 3.44 us
  transfers between devices with their start and end apart: 18 -> 18, of which waited for: 10 -> 11; matrix products, arithmetic and copies ran while one was open for 0% -> 0% of each run, Pallas kernels for 18% -> 13%
where the time goes in v4:
time: 81 us; the launch traced here: 80.8 us
  waiting for transfers between devices  48.4 us (60%)
  starting transfers between devices  16.2 us (20%)
  Pallas kernels  12 us (15%)
  local copies, waits for them, and re-layouts  3.44 us (4%)
  between operations  0.81 us (1%)
    ppermute x12, waiting for transfers between devices, swap(): lax.ppermute(value, 'expert', [(place, place ^ offset) for place in range...  40.5 us
    ppermute x6, starting transfers between devices, swap_groups(): return lax.ppermute(value, ('dp', 'expert'), pairs)  8.46 us
    ppermute x6, waiting for transfers between devices, swap_groups(): return lax.ppermute(value, ('dp', 'expert'), pairs)  7.96 us
    ppermute x12, starting transfers between devices, swap(): lax.ppermute(value, 'expert', [(place, place ^ offset) for place in range...  7.71 us
    unnamed x16, local copies, waits for them, and re-layouts  3.44 us
    pallas_call x1, Pallas kernels, grad_hidden_last(): pl.pallas_call(functools.partial(last_kernel, capacity, start), grid=(hid...  2.67 us
    pallas_call x2, Pallas kernels, grad_hidden_step(): pl.pallas_call(functools.partial(first_kernel if held is None else middle...  2.44 us
    pallas_call x3, Pallas kernels, panel_parts(): pl.pallas_call(functools.partial(panel_kernel, capacity, [column for _, c...  2.39 us
  transfers between devices with their start and end apart: 18, of which 11 were waited for; matrix products, arithmetic and copies ran while one was open for 0% of the time, Pallas kernels for 13%

profile of v4, /device:TPU:0, one launch (start us, length us, event | category | flops | bytes accessed | tf_op | source)
XLA Modules:
  0.0 80.8 jit_solution(15577475322872287361)
XLA Ops:
  1.2 1.0 %copy-done.1 = bf16[128,2048]{1,0:T(8,128)(2,1)S(1)} copy-done((bf16[128,2048]{1,0:T(8,128)(2,1)S(1)}, bf16[128,2048]{1,0:T(8,128)(2,1)}, u32[]{:S(2)}) %copy-start.1) | copy-done | bytes 524312
  2.2 0.7 copy-done.5
  2.9 0.7 copy-done.6
  3.8 3.7 %collective-permute-start.3 = (bf16[144,768]{1,0:T(8,128)(2,1)S(1)}, bf16[144,768]{1,0:T(8,128)(2,1)S(1)}, u32[]{:S(2)}, u32[]{:S(2)}) collective-permute-start(bf16[144,768]{1,0:T(8,128)(2,1)S(1)} %get-tuple-element.42), channel_id=1, source_target_pairs={{0,4},{1,5},{2,6},{3,7},{4,0},{5,1},{6,2},{7,3},{8,12},{9,13},{10,... | collective-permute-start | bytes 663560 | tf_op jit(solution)/shard_map/ppermute | solution.py:430
  7.7 1.0 %collective-permute-done.refs_1_ = bf16[16,128]{1,0:T(8,128)(2,1)S(1)} collective-permute-done((bf16[16,128]{1,0:T(8,128)(2,1)S(1)}, bf16[16,128]{1,0:T(8,128)(2,1)S(1)}, u32[]{:S(2)}, u32[]{:S(2)}) %collective-permute-start) | collective-permute-done | bytes 4128 | tf_op jit(solution)/shard_map/ppermute | solution.py:430
  8.6 1.0 %copy-done.2 = bf16[128,2048]{1,0:T(8,128)(2,1)S(1)} copy-done((bf16[128,2048]{1,0:T(8,128)(2,1)S(1)}, bf16[128,2048]{1,0:T(8,128)(2,1)}, u32[]{:S(2)}) %copy-start.2) | copy-done | bytes 524312
  10.1 1.7 %collective-permute-start.2 = (bf16[96,2048]{1,0:T(8,128)(2,1)S(1)}, bf16[96,2048]{1,0:T(8,128)(2,1)S(1)}, u32[]{:S(2)}, u32[]{:S(2)}) collective-permute-start(bf16[96,2048]{1,0:T(8,128)(2,1)S(1)} %get-tuple-element.41.refs_1_), channel_id=1, source_target_pairs={{0,2},{1,3},{2,0},{3,1},{4,6},{5,7},{6,4},{7,5},{8,10},{9,11},{10,... | collective-permute-start | bytes 1179656 | tf_op jit(solution)/shard_map/ppermute | solution.py:430
  11.7 6.7 %collective-permute-done.3.refs_0_ = bf16[144,768]{1,0:T(8,128)(2,1)S(1)} collective-permute-done((bf16[144,768]{1,0:T(8,128)(2,1)S(1)}, bf16[144,768]{1,0:T(8,128)(2,1)S(1)}, u32[]{:S(2)}, u32[]{:S(2)}) %collective-permute-start.3) | collective-permute-done | bytes 221216 | tf_op jit(solution)/shard_map/ppermute | solution.py:430
  18.4 1.5 %collective-permute-done.4.refs_1_.refs_3_ = bf16[144,768]{1,0:T(8,128)(2,1)S(1)} collective-permute-done((bf16[144,768]{1,0:T(8,128)(2,1)S(1)}, bf16[144,768]{1,0:T(8,128)(2,1)S(1)}, u32[]{:S(2)}, u32[]{:S(2)}) %collective-permute-start.4) | collective-permute-done | bytes 221216 | tf_op jit(solution)/shard_map/ppermute | solution.py:430
  19.9 6.1 %collective-permute-done.2.refs_4_.refs_1_ = bf16[96,2048]{1,0:T(8,128)(2,1)S(1)} collective-permute-done((bf16[96,2048]{1,0:T(8,128)(2,1)S(1)}, bf16[96,2048]{1,0:T(8,128)(2,1)S(1)}, u32[]{:S(2)}, u32[]{:S(2)}) %collective-permute-start.2) | collective-permute-done | bytes 393248 | tf_op jit(solution)/shard_map/ppermute | solution.py:430
  26.3 1.0 %shard_map.93 = (bf16[768,384]{1,0:T(8,128)(2,1)S(1)}, bf16[384,768]{1,0:T(8,128)(2,1)S(1)}, f32[384,768]{1,0:T(8,128)S(1)}, f32[384,768]{1,0:T(8,128)S(1)}) custom-call(bf16[384,768]{1,0:T(8,128)(2,1)S(1)} %bitcast.12, bf16[384,768]{1,0:T(8,128)(2,1)S(1)} %bitcast.13), custom_call_target="tpu_custom_call" | custom-call | flops 92160 | bytes 73728 | tf_op jit(solution)/shard_map/pallas_call | solution.py:157
  27.3 10.1 %collective-permute-done.5.refs_3_ = bf16[96,768]{1,0:T(8,128)(2,1)S(1)} collective-permute-done((bf16[96,768]{1,0:T(8,128)(2,1)S(1)}, bf16[96,768]{1,0:T(8,128)(2,1)S(1)}, u32[]{:S(2)}, u32[]{:S(2)}) %collective-permute-start.5) | collective-permute-done | bytes 147488 | tf_op jit(solution)/shard_map/ppermute | solution.py:430
  37.4 0.8 %shard_map.98 = (bf16[384,768]{1,0:T(8,128)(2,1)S(1)}, f32[192,768]{1,0:T(8,128)S(1)}, f32[192,768]{1,0:T(8,128)S(1)}, bf16[384,768]{1,0:T(8,128)(2,1)S(1)}) custom-call(bf16[768,384]{1,0:T(8,128)(2,1)S(1)} %get-tuple-element.38.turned_ref, bf16[96,2048]{1,0:T(8,128)(2,1)S(1)} %get-tuple-element.40.refs_0_, ...), custom_call_target="tpu_custom_call" | custom-call | flops 7077888 | bytes 27648 | tf_op jit(solution)/shard_map/pallas_call | solution.py:201
  38.2 1.6 %collective-permute-start.9 = (bf16[384,768]{1,0:T(8,128)(2,1)S(1)}, bf16[384,768]{1,0:T(8,128)(2,1)S(1)}, u32[]{:S(2)}, u32[]{:S(2)}) collective-permute-start(bf16[384,768]{1,0:T(8,128)(2,1)S(1)} %get-tuple-element.52), channel_id=1, source_target_pairs={{0,8},{1,17},{2,10},{3,19},{4,12},{5,21},{6,14},{7,23},{8,0},{9,25... | collective-permute-start | bytes 1769480 | tf_op jit(solution)/shard_map/ppermute | solution.py:440
  39.9 1.6 %collective-permute-done.7.refs_3_ = bf16[128,1280]{1,0:T(8,128)(2,1)S(1)} collective-permute-done((bf16[128,1280]{1,0:T(8,128)(2,1)S(1)}, bf16[128,1280]{1,0:T(8,128)(2,1)S(1)}, u32[]{:S(2)}, u32[]{:S(2)}) %collective-permute-start.7) | collective-permute-done | bytes 327712 | tf_op jit(solution)/shard_map/ppermute | solution.py:430
  41.9 1.2 %shard_map.99.refs_4_.held_ref = f32[384,768]{1,0:T(8,128)S(1)} custom-call(bf16[384,768]{1,0:T(8,128)(2,1)S(1)} %get-tuple-element.45.rows_ref, bf16[768,2048]{1,0:T(8,128)(2,1)S(1)} %bitcast.9), custom_call_target="tpu_custom_call" | custom-call | flops 7077888 | bytes 36864 | tf_op jit(solution)/shard_map/pallas_call | solution.py:299
  43.0 6.8 %collective-permute-done.8.refs_3_ = bf16[96,1280]{1,0:T(8,128)(2,1)S(1)} collective-permute-done((bf16[96,1280]{1,0:T(8,128)(2,1)S(1)}, bf16[96,1280]{1,0:T(8,128)(2,1)S(1)}, u32[]{:S(2)}, u32[]{:S(2)}) %collective-permute-start.8) | collective-permute-done | bytes 245792 | tf_op jit(solution)/shard_map/ppermute | solution.py:430
  49.8 0.8 shard_map.102
  50.6 0.6 collective-permute-start.10
  51.2 1.3 %shard_map.103.refs_4_.held_ref = f32[384,768]{1,0:T(8,128)S(1)} custom-call(f32[384,768]{1,0:T(8,128)S(1)} %shard_map.99.refs_4_.held_ref, bf16[384,640]{1,0:T(8,128)(2,1)S(1)} %get-tuple-element.49.rows_ref, bf16[768,2048]{1,0:T(8,128)(2,1)S(1)} %bitcast.10), custom_call_target="tpu_custom_call" | custom-call | flops 5898240 | bytes 36864 | tf_op jit(solution)/shard_map/pallas_call | solution.py:299
  52.6 0.8 shard_map.105
  53.4 1.6 %collective-permute-start.11 = (bf16[384,640]{1,0:T(8,128)(2,1)S(1)}, bf16[384,640]{1,0:T(8,128)(2,1)S(1)}, u32[]{:S(2)}, u32[]{:S(2)}) collective-permute-start(bf16[384,640]{1,0:T(8,128)(2,1)S(1)} %get-tuple-element.67), channel_id=1, source_target_pairs={{0,8},{1,17},{2,10},{3,19},{4,12},{5,21},{6,14},{7,23},{8,0},{9,25... | collective-permute-start | bytes 1474568 | tf_op jit(solution)/shard_map/ppermute | solution.py:440
  54.9 2.7 %shard_map.106 = (bf16[384,768]{1,0:T(8,128)(2,1)}, bf16[384,768]{1,0:T(8,128)(2,1)}, f32[8,128]{1,0:T(8,128)S(1)}) custom-call(f32[384,768]{1,0:T(8,128)S(1)} %shard_map.103.refs_4_.held_ref, bf16[384,640]{1,0:T(8,128)(2,1)S(1)} %get-tuple-element.54.rows_ref, bf16[768,2048]{1,0:T(8,128)(2,1)S(1)} %bitcast.11, ...), custom_call_target="tpu_custom_call" | custom-call | flops 5898240 | bytes 55296 | tf_op jit(solution)/shard_map/pallas_call | solution.py:357
  57.6 1.5 %collective-permute-start.13 = (bf16[192,768]{1,0:T(8,128)(2,1)S(1)}, bf16[192,768]{1,0:T(8,128)(2,1)S(1)}, u32[]{:S(2)}, u32[]{:S(2)}) collective-permute-start(bf16[192,768]{1,0:T(8,128)(2,1)S(1)} %get-tuple-element.53.refs_5_), channel_id=1, source_target_pairs={{0,16},{1,9},{2,18},{3,11},{4,20},{5,13},{6,22},{7,15},{8,24},{9,1... | collective-permute-start | bytes 884744 | tf_op jit(solution)/shard_map/ppermute | solution.py:440
  59.6 1.6 %collective-permute-start.14 = (bf16[192,640]{1,0:T(8,128)(2,1)S(1)}, bf16[192,640]{1,0:T(8,128)(2,1)S(1)}, u32[]{:S(2)}, u32[]{:S(2)}) collective-permute-start(bf16[192,640]{1,0:T(8,128)(2,1)S(1)} %get-tuple-element.70), channel_id=1, source_target_pairs={{0,16},{1,9},{2,18},{3,11},{4,20},{5,13},{6,22},{7,15},{8,24},{9,1... | collective-permute-start | bytes 737288 | tf_op jit(solution)/shard_map/ppermute | solution.py:440
  61.2 7.6 %collective-permute-done.11.arrived_ref = bf16[384,640]{1,0:T(8,128)(2,1)S(1)} collective-permute-done((bf16[384,640]{1,0:T(8,128)(2,1)S(1)}, bf16[384,640]{1,0:T(8,128)(2,1)S(1)}, u32[]{:S(2)}, u32[]{:S(2)}) %collective-permute-start.11) | collective-permute-done | bytes 491552 | tf_op jit(solution)/shard_map/ppermute | solution.py:440
  68.9 1.6 %collective-permute-start.15 = (bf16[192,640]{1,0:T(8,128)(2,1)S(1)}, bf16[192,640]{1,0:T(8,128)(2,1)S(1)}, u32[]{:S(2)}, u32[]{:S(2)}) collective-permute-start(bf16[192,640]{1,0:T(8,128)(2,1)S(1)} %get-tuple-element.71), channel_id=1, source_target_pairs={{0,16},{1,9},{2,18},{3,11},{4,20},{5,13},{6,22},{7,15},{8,24},{9,1... | collective-permute-start | bytes 737288 | tf_op jit(solution)/shard_map/ppermute | solution.py:440
  70.7 3.4 %collective-permute-done.16 = f32[16,128]{1,0:T(8,128)S(1)} collective-permute-done((f32[16,128]{1,0:T(8,128)S(1)}, f32[16,128]{1,0:T(8,128)S(1)}, u32[]{:S(2)}, u32[]{:S(2)}) %collective-permute-start.16) | collective-permute-done | bytes 8224 | tf_op jit(solution)/shard_map/ppermute | solution.py:430
  74.1 1.2 %collective-permute-start.17 = (f32[32,128]{1,0:T(8,128)S(1)}, f32[32,128]{1,0:T(8,128)S(1)}, u32[]{:S(2)}, u32[]{:S(2)}) collective-permute-start(f32[32,128]{1,0:T(8,128)S(1)} %constant_dynamic-update-slice_fusion.2.near_ref), channel_id=1, source_target_pairs={{0,4},{1,5},{2,6},{3,7},{4,0},{5,1},{6,2},{7,3},{8,12},{9,13},{10,... | collective-permute-start | bytes 49160 | tf_op jit(solution)/shard_map/ppermute | solution.py:430
  75.4 3.4 %collective-permute-done.17.far_ref = f32[32,128]{1,0:T(8,128)S(1)} collective-permute-done((f32[32,128]{1,0:T(8,128)S(1)}, f32[32,128]{1,0:T(8,128)S(1)}, u32[]{:S(2)}, u32[]{:S(2)}) %collective-permute-start.17) | collective-permute-done | bytes 16416 | tf_op jit(solution)/shard_map/ppermute | solution.py:430
  78.8 0.8 %shard_map.110 = f32[2,128]{1,0:T(2,128)} custom-call(bf16[16,128]{1,0:T(8,128)(2,1)S(1)} %get-tuple-element.39.refs_0_.meta_ref, f32[32,128]{1,0:T(8,128)S(1)} %constant_dynamic-update-slice_fusion.2.near_ref, f32[32,128]{1,0:T(8,128)S(1)} %collective-permute-done.17.far_ref), custom_call_target="tpu_custom_call" | custom-call | flops 15625 | bytes 1562 | tf_op jit(solution)/shard_map/pallas_call | solution.py:402
  79.6 1.2 %shard_map.109 = f32[192,2048]{1,0:T(8,128)} custom-call(f32[192,768]{1,0:T(8,128)S(1)} %get-tuple-element.60.refs_0_, f32[192,640]{1,0:T(8,128)S(1)} %get-tuple-element.64.refs_1_, f32[192,640]{1,0:T(8,128)S(1)} %get-tuple-element.69.refs_2_, bf16[192,768]{1,0:T(8,128)(2,1)S(1)} %collective-permute-done.13.refs_3_, ...), custom_call_target="tpu_custom_call" | custom-call | flops 12288 | bytes 61440 | tf_op jit(solution)/shard_map/pallas_call | solution.py:261
  (39 shorter events, 3.0 us)
Async XLA Ops:
  0.6 8.0 %collective-permute-start.1 = (bf16[128,2048]{1,0:T(8,128)(2,1)}, bf16[128,2048]{1,0:T(8,128)(2,1)S(1)}, u32[]{:S(2)}, u32[]{:S(2)}) collective-permute-start(bf16[128,2048]{1,0:T(8,128)(2,1)} %refs_2_.1), channel_id=1, source_target_pairs={{0,1},{1,0},{2,3},{3,2},{4,5},{5,4},{6,7},{7,6},{8,9},{9,8},{10,11... | collective-permute-start | bytes 1572872 | tf_op jit(solution)/shard_map/ppermute | solution.py:430
  1.1 1.0 %copy-start.1 = (bf16[128,2048]{1,0:T(8,128)(2,1)S(1)}, bf16[128,2048]{1,0:T(8,128)(2,1)}, u32[]{:S(2)}) copy-start(bf16[128,2048]{1,0:T(8,128)(2,1)} %refs_2_.1) | copy-start | bytes 1572868
  2.2 0.7 copy-start.5
  2.9 0.7 copy-start.6
  3.8 14.6 %collective-permute-start.3 = (bf16[144,768]{1,0:T(8,128)(2,1)S(1)}, bf16[144,768]{1,0:T(8,128)(2,1)S(1)}, u32[]{:S(2)}, u32[]{:S(2)}) collective-permute-start(bf16[144,768]{1,0:T(8,128)(2,1)S(1)} %get-tuple-element.42), channel_id=1, source_target_pairs={{0,4},{1,5},{2,6},{3,7},{4,0},{5,1},{6,2},{7,3},{8,12},{9,13},{10,... | collective-permute-start | bytes 663560 | tf_op jit(solution)/shard_map/ppermute | solution.py:430
  7.4 1.2 %collective-permute-start = (bf16[16,128]{1,0:T(8,128)(2,1)S(1)}, bf16[16,128]{1,0:T(8,128)(2,1)S(1)}, u32[]{:S(2)}, u32[]{:S(2)}) collective-permute-start(bf16[16,128]{1,0:T(8,128)(2,1)S(1)} %get-tuple-element.39.refs_0_.meta_ref), channel_id=1, source_target_pairs={{0,1},{1,0},{2,3},{3,2},{4,5},{5,4},{6,7},{7,6},{8,9},{9,8},{10,11... | collective-permute-start | bytes 12296 | tf_op jit(solution)/shard_map/ppermute | solution.py:430
  8.6 1.0 %copy-start.2 = (bf16[128,2048]{1,0:T(8,128)(2,1)S(1)}, bf16[128,2048]{1,0:T(8,128)(2,1)}, u32[]{:S(2)}) copy-start(bf16[128,2048]{1,0:T(8,128)(2,1)} %refs_2_.1) | copy-start | bytes 1572868
  10.0 16.2 %copy-start.3 = (bf16[1,1,8,48,768]{4,3,2,1,0:T(8,128)(2,1)S(1)}, bf16[1,1,8,48,768]{4,3,2,1,0:T(8,128)(2,1)}, u32[]{:S(2)}) copy-start(bf16[1,1,8,48,768]{4,3,2,1,0:T(8,128)(2,1)} %param.9) | copy-start | bytes 1769476
  10.0 16.2 %copy-start.4 = (bf16[1,1,8,48,768]{4,3,2,1,0:T(8,128)(2,1)S(1)}, bf16[1,1,8,48,768]{4,3,2,1,0:T(8,128)(2,1)}, u32[]{:S(2)}) copy-start(bf16[1,1,8,48,768]{4,3,2,1,0:T(8,128)(2,1)} %param.10) | copy-start | bytes 1769476
  10.1 15.9 %collective-permute-start.2 = (bf16[96,2048]{1,0:T(8,128)(2,1)S(1)}, bf16[96,2048]{1,0:T(8,128)(2,1)S(1)}, u32[]{:S(2)}, u32[]{:S(2)}) collective-permute-start(bf16[96,2048]{1,0:T(8,128)(2,1)S(1)} %get-tuple-element.41.refs_1_), channel_id=1, source_target_pairs={{0,2},{1,3},{2,0},{3,1},{4,6},{5,7},{6,4},{7,5},{8,10},{9,11},{10,... | collective-permute-start | bytes 1179656 | tf_op jit(solution)/shard_map/ppermute | solution.py:430
  18.4 1.5 %collective-permute-start.4 = (bf16[144,768]{1,0:T(8,128)(2,1)S(1)}, bf16[144,768]{1,0:T(8,128)(2,1)S(1)}, u32[]{:S(2)}, u32[]{:S(2)}) collective-permute-start(bf16[144,768]{1,0:T(8,128)(2,1)S(1)} %shard_map.96.refs_0_.refs_2_), channel_id=1, source_target_pairs={{0,1},{1,0},{2,3},{3,2},{4,5},{5,4},{6,7},{7,6},{8,9},{9,8},{10,11... | collective-permute-start | bytes 663560 | tf_op jit(solution)/shard_map/ppermute | solution.py:430
  18.4 21.5 %collective-permute-start.6 = (bf16[128,1280]{1,0:T(8,128)(2,1)S(1)}, bf16[128,1280]{1,0:T(8,128)(2,1)S(1)}, u32[]{:S(2)}, u32[]{:S(2)}) collective-permute-start(bf16[128,1280]{1,0:T(8,128)(2,1)S(1)} %get-tuple-element.46), channel_id=1, source_target_pairs={{0,4},{1,5},{2,6},{3,7},{4,0},{5,1},{6,2},{7,3},{8,12},{9,13},{10,... | collective-permute-start | bytes 983048 | tf_op jit(solution)/shard_map/ppermute | solution.py:430
  26.2 11.2 %collective-permute-start.5 = (bf16[96,768]{1,0:T(8,128)(2,1)S(1)}, bf16[96,768]{1,0:T(8,128)(2,1)S(1)}, u32[]{:S(2)}, u32[]{:S(2)}) collective-permute-start(bf16[96,768]{1,0:T(8,128)(2,1)S(1)} %get-tuple-element.44.refs_1_), channel_id=1, source_target_pairs={{0,2},{1,3},{2,0},{3,1},{4,6},{5,7},{6,4},{7,5},{8,10},{9,11},{10,... | collective-permute-start | bytes 442376 | tf_op jit(solution)/shard_map/ppermute | solution.py:430
  37.4 4.4 %copy-start = (bf16[1,768,2048]{2,1,0:T(8,128)(2,1)S(1)}, bf16[1,768,2048]{2,1,0:T(8,128)(2,1)}, u32[]{:S(2)}) copy-start(bf16[1,768,2048]{2,1,0:T(8,128)(2,1)} %param.11) | copy-start | bytes 9437188
  38.2 14.2 %collective-permute-start.9 = (bf16[384,768]{1,0:T(8,128)(2,1)S(1)}, bf16[384,768]{1,0:T(8,128)(2,1)S(1)}, u32[]{:S(2)}, u32[]{:S(2)}) collective-permute-start(bf16[384,768]{1,0:T(8,128)(2,1)S(1)} %get-tuple-element.52), channel_id=1, source_target_pairs={{0,8},{1,17},{2,10},{3,19},{4,12},{5,21},{6,14},{7,23},{8,0},{9,25... | collective-permute-start | bytes 1769480 | tf_op jit(solution)/shard_map/ppermute | solution.py:440
  39.8 1.6 %collective-permute-start.7 = (bf16[128,1280]{1,0:T(8,128)(2,1)S(1)}, bf16[128,1280]{1,0:T(8,128)(2,1)S(1)}, u32[]{:S(2)}, u32[]{:S(2)}) collective-permute-start(bf16[128,1280]{1,0:T(8,128)(2,1)S(1)} %shard_map.100.refs_2_), channel_id=1, source_target_pairs={{0,1},{1,0},{2,3},{3,2},{4,5},{5,4},{6,7},{7,6},{8,9},{9,8},{10,11... | collective-permute-start | bytes 983048 | tf_op jit(solution)/shard_map/ppermute | solution.py:430
  41.8 8.1 %collective-permute-start.8 = (bf16[96,1280]{1,0:T(8,128)(2,1)S(1)}, bf16[96,1280]{1,0:T(8,128)(2,1)S(1)}, u32[]{:S(2)}, u32[]{:S(2)}) collective-permute-start(bf16[96,1280]{1,0:T(8,128)(2,1)S(1)} %get-tuple-element.48), channel_id=1, source_target_pairs={{0,2},{1,3},{2,0},{3,1},{4,6},{5,7},{6,4},{7,5},{8,10},{9,11},{10,... | collective-permute-start | bytes 737288 | tf_op jit(solution)/shard_map/ppermute | solution.py:430
  50.6 8.9 %collective-permute-start.10 = (bf16[384,640]{1,0:T(8,128)(2,1)S(1)}, bf16[384,640]{1,0:T(8,128)(2,1)S(1)}, u32[]{:S(2)}, u32[]{:S(2)}) collective-permute-start(bf16[384,640]{1,0:T(8,128)(2,1)S(1)} %get-tuple-element.63), channel_id=1, source_target_pairs={{0,8},{1,17},{2,10},{3,19},{4,12},{5,21},{6,14},{7,23},{8,0},{9,25... | collective-permute-start | bytes 1474568 | tf_op jit(solution)/shard_map/ppermute | solution.py:440
  53.4 15.4 %collective-permute-start.11 = (bf16[384,640]{1,0:T(8,128)(2,1)S(1)}, bf16[384,640]{1,0:T(8,128)(2,1)S(1)}, u32[]{:S(2)}, u32[]{:S(2)}) collective-permute-start(bf16[384,640]{1,0:T(8,128)(2,1)S(1)} %get-tuple-element.67), channel_id=1, source_target_pairs={{0,8},{1,17},{2,10},{3,19},{4,12},{5,21},{6,14},{7,23},{8,0},{9,25... | collective-permute-start | bytes 1474568 | tf_op jit(solution)/shard_map/ppermute | solution.py:440
  57.6 1.6 %collective-permute-start.12 = (f32[8,128]{1,0:T(8,128)S(1)}, f32[8,128]{1,0:T(8,128)S(1)}, u32[]{:S(2)}, u32[]{:S(2)}) collective-permute-start(f32[8,128]{1,0:T(8,128)S(1)} %get-tuple-element.68), channel_id=1, source_target_pairs={{0,1},{1,0},{2,3},{3,2},{4,5},{5,4},{6,7},{7,6},{8,9},{9,8},{10,11... | collective-permute-start | bytes 12296 | tf_op jit(solution)/shard_map/ppermute | solution.py:430
  57.6 22.0 %collective-permute-start.13 = (bf16[192,768]{1,0:T(8,128)(2,1)S(1)}, bf16[192,768]{1,0:T(8,128)(2,1)S(1)}, u32[]{:S(2)}, u32[]{:S(2)}) collective-permute-start(bf16[192,768]{1,0:T(8,128)(2,1)S(1)} %get-tuple-element.53.refs_5_), channel_id=1, source_target_pairs={{0,16},{1,9},{2,18},{3,11},{4,20},{5,13},{6,22},{7,15},{8,24},{9,1... | collective-permute-start | bytes 884744 | tf_op jit(solution)/shard_map/ppermute | solution.py:440
  59.6 20.0 %collective-permute-start.14 = (bf16[192,640]{1,0:T(8,128)(2,1)S(1)}, bf16[192,640]{1,0:T(8,128)(2,1)S(1)}, u32[]{:S(2)}, u32[]{:S(2)}) collective-permute-start(bf16[192,640]{1,0:T(8,128)(2,1)S(1)} %get-tuple-element.70), channel_id=1, source_target_pairs={{0,16},{1,9},{2,18},{3,11},{4,20},{5,13},{6,22},{7,15},{8,24},{9,1... | collective-permute-start | bytes 737288 | tf_op jit(solution)/shard_map/ppermute | solution.py:440
  68.9 10.7 %collective-permute-start.15 = (bf16[192,640]{1,0:T(8,128)(2,1)S(1)}, bf16[192,640]{1,0:T(8,128)(2,1)S(1)}, u32[]{:S(2)}, u32[]{:S(2)}) collective-permute-start(bf16[192,640]{1,0:T(8,128)(2,1)S(1)} %get-tuple-element.71), channel_id=1, source_target_pairs={{0,16},{1,9},{2,18},{3,11},{4,20},{5,13},{6,22},{7,15},{8,24},{9,1... | collective-permute-start | bytes 737288 | tf_op jit(solution)/shard_map/ppermute | solution.py:440
  70.5 3.7 %collective-permute-start.16 = (f32[16,128]{1,0:T(8,128)S(1)}, f32[16,128]{1,0:T(8,128)S(1)}, u32[]{:S(2)}, u32[]{:S(2)}) collective-permute-start(f32[16,128]{1,0:T(8,128)S(1)} %get-tuple-element.73.refs_0_), channel_id=1, source_target_pairs={{0,2},{1,3},{2,0},{3,1},{4,6},{5,7},{6,4},{7,5},{8,10},{9,11},{10,... | collective-permute-start | bytes 24584 | tf_op jit(solution)/shard_map/ppermute | solution.py:430
  74.1 4.6 %collective-permute-start.17 = (f32[32,128]{1,0:T(8,128)S(1)}, f32[32,128]{1,0:T(8,128)S(1)}, u32[]{:S(2)}, u32[]{:S(2)}) collective-permute-start(f32[32,128]{1,0:T(8,128)S(1)} %constant_dynamic-update-slice_fusion.2.near_ref), channel_id=1, source_target_pairs={{0,4},{1,5},{2,6},{3,7},{4,0},{5,1},{6,2},{7,3},{8,12},{9,13},{10,... | collective-permute-start | bytes 49160 | tf_op jit(solution)/shard_map/ppermute | solution.py:430

commit v5 on v4

--- a/solution.py
+++ b/solution.py
@@ -9,7 +9,7 @@
 
 LANES = 128
 META = 16
-PARTS = ((768,), (640, 640))
+PARTS = ((896,), (640, 512))
 VMEM_LIMIT = 10 * 1024 * 1024
 VMEM = pl.BlockSpec(memory_space=pltpu.VMEM)
 ANY = pl.BlockSpec(memory_space=pl.ANY)
@@ -238,7 +238,7 @@
 
 def total_kernel(count, *refs):
     own_refs, arrived_refs = refs[:count], refs[count : 2 * count]
-    total_ref, *sum_refs, semaphores = refs[2 * count :]
+    total_ref, *sum_refs, semaphores = refs[-2 - count :]
     copies = []
     start = 0
     for place, (own_ref, arrived_ref) in enumerate(zip(own_refs, arrived_refs)):
@@ -255,19 +255,19 @@
         copy.wait()
 
 
-def total(owns, arrived):
+def total(owns, arrived, earlier):
     share = owns[0].shape[0]
     size = share * sum(own.shape[1] for own in owns)
     return pl.pallas_call(
         functools.partial(total_kernel, len(owns)),
-        in_specs=[VMEM] * (2 * len(owns)),
+        in_specs=[VMEM] * (2 * len(owns)) + [ANY] * len(earlier),
         out_specs=HBM,
         out_shape=jax.ShapeDtypeStruct((share, size // share), jnp.float32),
         scratch_shapes=[pltpu.VMEM(own.shape, jnp.float32) for own in owns]
         + [pltpu.SemaphoreType.DMA((len(owns),))],
         compiler_params=params(),
         cost_estimate=cost(2 * size, 10 * size),
-    )(*owns, *arrived)
+    )(*owns, *arrived, *earlier)
 
 
 def rows_times_weight(start, rows_ref, weight_ref):
@@ -451,53 +451,57 @@
     meta, *parts = token_parts(routes.T, probs.T, grad_out, expert_count)
     parts = [swap(part, 4) for part in parts]
     metas = [meta, swap(meta, 1)]
-    local, sent = dispatch(
-        metas, [grad_out, swap(grad_out, 1)], capacity, top_count, 0, model_width
-    )
-    near = swap(sent, 2)
+    near_rows = [grad_out, swap(grad_out, 1)]
     weight = w_down[0]
     turned, hidden, up_scale, gate_scale = hidden_parts(
         saved_gate.reshape(row_count, hidden_width), saved_up.reshape(row_count, hidden_width)
     )
-    held, start = None, 0
-    halves, owns, arrived = [], [], []
+    held, start, far_sent = None, 0, None
+    owns, arrived = [], []
     for part, widths in enumerate(PARTS):
-        part_start, part_width = start, sum(widths)
-        parts[part] = after(parts[part], sent)
+        part_width = sum(widths)
+        local, sent = dispatch(
+            metas,
+            near_rows,
+            capacity,
+            top_count,
+            start,
+            part_width,
+            [] if far_sent is None else [far_sent],
+        )
+        near = swap(sent, 2)
+        parts[part] = after(parts[part], near)
         other_part = swap(parts[part], 1)
         far_metas = [parts[0], other_part] if part == 0 else far_metas
-        far_local, sent = dispatch(
+        far_local, far_sent = dispatch(
             far_metas,
             [parts[part], other_part],
             capacity,
             top_count,
             0,
             part_width,
-            [near] if part == 0 else [],
         )
-        far_near = swap(sent, 2)
+        far_near = swap(far_sent, 2)
+        column = 0
         for width in widths:
-            blocks = [(local, start), (near, start)]
-            blocks += [(far_local, start - part_start), (far_near, start - part_start)]
-            earlier = ([] if held is None else [held]) + halves[:-1]
+            blocks = [(block, column) for block in (local, near, far_local, far_near)]
+            earlier = [] if held is None else [held]
             rows, own, later, half = panel_parts(turned, blocks, capacity, width, earlier)
-            earlier = []
+            own, half = halve(own, later, swap_groups(half, False), arrived[-1:])
+            owns.append(own)
+            arrived.append(swap_groups(half, True))
             if start + width < model_width:
                 held = grad_hidden_step(held, rows, weight, start)
             else:
                 grad_gate, grad_up, lines = grad_hidden_last(
                     held, rows, weight, start, hidden, up_scale, gate_scale, capacity
                 )
-                lines = jnp.concatenate([lines, swap(lines, 1)], axis=0)
-                earlier = [lines]
-            own, half = halve(own, later, swap_groups(half, False), earlier)
-            halves.append(half)
-            owns.append(own)
-            arrived.append(swap_groups(half, True))
             start += width
-    lines = jnp.concatenate([lines, swap(lines, 2)], axis=0)
-    panel = total(owns, arrived)
+            column += width
+    for offset in (1, 2):
+        lines = jnp.concatenate([lines, swap(lines, offset)], axis=0)
     route_grad = route_back(meta, lines, swap(lines, 4), expert_count, top_count, capacity)
+    panel = total(owns, arrived, [route_grad])
     return (
         grad_gate.reshape(saved_gate.shape),
         grad_up.reshape(saved_up.shape),

time: 81 us -> 81.7 us (level)
  waiting for transfers between devices: 48.4 us -> 47.5 us
    ppermute x12 -> x13, starting transfers between devices: 7.71 us -> 9.95 us  [swap(): lax.ppermute(value, 'expert', [(place, place ^ offset) for place in range...]
    ppermute x6, starting transfers between devices: 8.46 us -> 6.96 us  [swap_groups(): return lax.ppermute(value, ('dp', 'expert'), pairs)]
    ppermute x12 -> x13, waiting for transfers between devices: 40.5 us -> 39.2 us  [swap(): lax.ppermute(value, 'expert', [(place, place ^ offset) for place in range...]
    unnamed x16 -> x20, local copies, waits for them, and re-layouts: 3.44 us -> 4.11 us
  transfers between devices with their start and end apart: 18 -> 19, of which waited for: 11 -> 13; matrix products, arithmetic and copies ran while one was open for 0% -> 0% of each run, Pallas kernels for 13% -> 13%
where the time goes in v5:
time: 81.7 us; the launch traced here: 81.5 us
  waiting for transfers between devices  47.5 us (58%)
  starting transfers between devices  16.9 us (21%)
  Pallas kernels  12.1 us (15%)
  local copies, waits for them, and re-layouts  4.12 us (5%)
    ppermute x13, waiting for transfers between devices, swap(): lax.ppermute(value, 'expert', [(place, place ^ offset) for place in range...  39.2 us
    ppermute x13, starting transfers between devices, swap(): lax.ppermute(value, 'expert', [(place, place ^ offset) for place in range...  9.95 us
    ppermute x6, waiting for transfers between devices, swap_groups(): return lax.ppermute(value, ('dp', 'expert'), pairs)  8.31 us
    ppermute x6, starting transfers between devices, swap_groups(): return lax.ppermute(value, ('dp', 'expert'), pairs)  6.96 us
    unnamed x20, local copies, waits for them, and re-layouts  4.11 us
    pallas_call x1, Pallas kernels, grad_hidden_last(): pl.pallas_call(functools.partial(last_kernel, capacity, start), grid=(hid...  2.56 us
    pallas_call x2, Pallas kernels, grad_hidden_step(): pl.pallas_call(functools.partial(first_kernel if held is None else middle...  2.55 us
    pallas_call x3, Pallas kernels, panel_parts(): pl.pallas_call(functools.partial(panel_kernel, capacity, [column for _, c...  2.42 us
  transfers between devices with their start and end apart: 19, of which 13 were waited for; matrix products, arithmetic and copies ran while one was open for 0% of the time, Pallas kernels for 13%

profile of v5, /device:TPU:0, one launch (start us, length us, event | category | flops | bytes accessed | tf_op | source)
XLA Modules:
  0.0 81.5 jit_solution(5193734423035809332)
XLA Ops:
  1.2 1.0 %copy-done.1 = bf16[128,2048]{1,0:T(8,128)(2,1)S(1)} copy-done((bf16[128,2048]{1,0:T(8,128)(2,1)S(1)}, bf16[128,2048]{1,0:T(8,128)(2,1)}, u32[]{:S(2)}) %copy-start.1) | copy-done | bytes 524312
  2.2 0.7 copy-done.7
  3.8 3.7 %collective-permute-start.3 = (bf16[144,896]{1,0:T(8,128)(2,1)S(1)}, bf16[144,896]{1,0:T(8,128)(2,1)S(1)}, u32[]{:S(2)}, u32[]{:S(2)}) collective-permute-start(bf16[144,896]{1,0:T(8,128)(2,1)S(1)} %get-tuple-element.44), channel_id=1, source_target_pairs={{0,4},{1,5},{2,6},{3,7},{4,0},{5,1},{6,2},{7,3},{8,12},{9,13},{10,... | collective-permute-start | bytes 774152 | tf_op jit(solution)/shard_map/ppermute | solution.py:430
  7.7 1.0 %collective-permute-done.refs_1_ = bf16[16,128]{1,0:T(8,128)(2,1)S(1)} collective-permute-done((bf16[16,128]{1,0:T(8,128)(2,1)S(1)}, bf16[16,128]{1,0:T(8,128)(2,1)S(1)}, u32[]{:S(2)}, u32[]{:S(2)}) %collective-permute-start) | collective-permute-done | bytes 4128 | tf_op jit(solution)/shard_map/ppermute | solution.py:430
  8.6 1.0 %copy-done.2 = bf16[128,2048]{1,0:T(8,128)(2,1)S(1)} copy-done((bf16[128,2048]{1,0:T(8,128)(2,1)S(1)}, bf16[128,2048]{1,0:T(8,128)(2,1)}, u32[]{:S(2)}) %copy-start.2) | copy-done | bytes 524312
  9.9 1.6 %collective-permute-start.2 = (bf16[96,896]{1,0:T(8,128)(2,1)S(1)}, bf16[96,896]{1,0:T(8,128)(2,1)S(1)}, u32[]{:S(2)}, u32[]{:S(2)}) collective-permute-start(bf16[96,896]{1,0:T(8,128)(2,1)S(1)} %get-tuple-element.43), channel_id=1, source_target_pairs={{0,2},{1,3},{2,0},{3,1},{4,6},{5,7},{6,4},{7,5},{8,10},{9,11},{10,... | collective-permute-start | bytes 516104 | tf_op jit(solution)/shard_map/ppermute | solution.py:430
  11.6 8.4 %collective-permute-done.3.refs_0_ = bf16[144,896]{1,0:T(8,128)(2,1)S(1)} collective-permute-done((bf16[144,896]{1,0:T(8,128)(2,1)S(1)}, bf16[144,896]{1,0:T(8,128)(2,1)S(1)}, u32[]{:S(2)}, u32[]{:S(2)}) %collective-permute-start.3) | collective-permute-done | bytes 258080 | tf_op jit(solution)/shard_map/ppermute | solution.py:430
  20.0 0.9 %collective-permute-done.2.refs_1_ = bf16[96,896]{1,0:T(8,128)(2,1)S(1)} collective-permute-done((bf16[96,896]{1,0:T(8,128)(2,1)S(1)}, bf16[96,896]{1,0:T(8,128)(2,1)S(1)}, u32[]{:S(2)}, u32[]{:S(2)}) %collective-permute-start.2) | collective-permute-done | bytes 172064 | tf_op jit(solution)/shard_map/ppermute | solution.py:430
  20.9 1.4 %collective-permute-done.4.refs_1_.refs_3_ = bf16[144,896]{1,0:T(8,128)(2,1)S(1)} collective-permute-done((bf16[144,896]{1,0:T(8,128)(2,1)S(1)}, bf16[144,896]{1,0:T(8,128)(2,1)S(1)}, u32[]{:S(2)}, u32[]{:S(2)}) %collective-permute-start.4) | collective-permute-done | bytes 258080 | tf_op jit(solution)/shard_map/ppermute | solution.py:430
  22.9 1.8 %collective-permute-start.6 = (bf16[96,1152]{1,0:T(8,128)(2,1)S(1)}, bf16[96,1152]{1,0:T(8,128)(2,1)S(1)}, u32[]{:S(2)}, u32[]{:S(2)}) collective-permute-start(bf16[96,1152]{1,0:T(8,128)(2,1)S(1)} %get-tuple-element.49), channel_id=1, source_target_pairs={{0,2},{1,3},{2,0},{3,1},{4,6},{5,7},{6,4},{7,5},{8,10},{9,11},{10,... | collective-permute-start | bytes 663560 | tf_op jit(solution)/shard_map/ppermute | solution.py:430
  25.0 1.0 %shard_map.93 = (bf16[768,384]{1,0:T(8,128)(2,1)S(1)}, bf16[384,768]{1,0:T(8,128)(2,1)S(1)}, f32[384,768]{1,0:T(8,128)S(1)}, f32[384,768]{1,0:T(8,128)S(1)}) custom-call(bf16[384,768]{1,0:T(8,128)(2,1)S(1)} %bitcast.12, bf16[384,768]{1,0:T(8,128)(2,1)S(1)} %bitcast.13), custom_call_target="tpu_custom_call" | custom-call | flops 92160 | bytes 73728 | tf_op jit(solution)/shard_map/pallas_call | solution.py:157
  26.0 14.4 %collective-permute-done.5.refs_3_ = bf16[96,896]{1,0:T(8,128)(2,1)S(1)} collective-permute-done((bf16[96,896]{1,0:T(8,128)(2,1)S(1)}, bf16[96,896]{1,0:T(8,128)(2,1)S(1)}, u32[]{:S(2)}, u32[]{:S(2)}) %collective-permute-start.5) | collective-permute-done | bytes 172064 | tf_op jit(solution)/shard_map/ppermute | solution.py:430
  40.4 1.0 %shard_map.98 = (bf16[384,896]{1,0:T(8,128)(2,1)S(1)}, f32[192,896]{1,0:T(8,128)S(1)}, f32[192,896]{1,0:T(8,128)S(1)}, bf16[384,896]{1,0:T(8,128)(2,1)S(1)}) custom-call(bf16[768,384]{1,0:T(8,128)(2,1)S(1)} %get-tuple-element.40.turned_ref, bf16[96,896]{1,0:T(8,128)(2,1)S(1)} %get-tuple-element.42.refs_0_, ...), custom_call_target="tpu_custom_call" | custom-call | flops 8257536 | bytes 30720 | tf_op jit(solution)/shard_map/pallas_call | solution.py:201
  41.4 1.6 %collective-permute-start.10 = (bf16[384,896]{1,0:T(8,128)(2,1)S(1)}, bf16[384,896]{1,0:T(8,128)(2,1)S(1)}, u32[]{:S(2)}, u32[]{:S(2)}) collective-permute-start(bf16[384,896]{1,0:T(8,128)(2,1)S(1)} %get-tuple-element.62), channel_id=1, source_target_pairs={{0,8},{1,17},{2,10},{3,19},{4,12},{5,21},{6,14},{7,23},{8,0},{9,25... | collective-permute-start | bytes 2064392 | tf_op jit(solution)/shard_map/ppermute | solution.py:440
  43.0 1.6 %collective-permute-done.8.refs_3_ = bf16[128,1152]{1,0:T(8,128)(2,1)S(1)} collective-permute-done((bf16[128,1152]{1,0:T(8,128)(2,1)S(1)}, bf16[128,1152]{1,0:T(8,128)(2,1)S(1)}, u32[]{:S(2)}, u32[]{:S(2)}) %collective-permute-start.8) | collective-permute-done | bytes 294944 | tf_op jit(solution)/shard_map/ppermute | solution.py:430
  45.0 1.3 %shard_map.99.refs_4_.held_ref = f32[384,768]{1,0:T(8,128)S(1)} custom-call(bf16[384,896]{1,0:T(8,128)(2,1)S(1)} %get-tuple-element.47.rows_ref, bf16[768,2048]{1,0:T(8,128)(2,1)S(1)} %bitcast.9), custom_call_target="tpu_custom_call" | custom-call | flops 8257536 | bytes 36864 | tf_op jit(solution)/shard_map/pallas_call | solution.py:299
  46.3 6.1 %collective-permute-done.9.refs_3_ = bf16[96,1152]{1,0:T(8,128)(2,1)S(1)} collective-permute-done((bf16[96,1152]{1,0:T(8,128)(2,1)S(1)}, bf16[96,1152]{1,0:T(8,128)(2,1)S(1)}, u32[]{:S(2)}, u32[]{:S(2)}) %collective-permute-start.9) | collective-permute-done | bytes 221216 | tf_op jit(solution)/shard_map/ppermute | solution.py:430
  52.4 0.8 shard_map.103
  53.9 1.6 %collective-permute-start.12 = (bf16[192,896]{1,0:T(8,128)(2,1)S(1)}, bf16[192,896]{1,0:T(8,128)(2,1)S(1)}, u32[]{:S(2)}, u32[]{:S(2)}) collective-permute-start(bf16[192,896]{1,0:T(8,128)(2,1)S(1)} %get-tuple-element.67), channel_id=1, source_target_pairs={{0,16},{1,9},{2,18},{3,11},{4,20},{5,13},{6,22},{7,15},{8,24},{9,1... | collective-permute-start | bytes 1032200 | tf_op jit(solution)/shard_map/ppermute | solution.py:440
  55.6 1.3 %shard_map.104.refs_4_.held_ref = f32[384,768]{1,0:T(8,128)S(1)} custom-call(f32[384,768]{1,0:T(8,128)S(1)} %shard_map.99.refs_4_.held_ref, bf16[384,640]{1,0:T(8,128)(2,1)S(1)} %get-tuple-element.53.rows_ref, bf16[768,2048]{1,0:T(8,128)(2,1)S(1)} %bitcast.10), custom_call_target="tpu_custom_call" | custom-call | flops 5898240 | bytes 36864 | tf_op jit(solution)/shard_map/pallas_call | solution.py:299
  57.4 1.6 %collective-permute-start.13 = (bf16[384,512]{1,0:T(8,128)(2,1)S(1)}, bf16[384,512]{1,0:T(8,128)(2,1)S(1)}, u32[]{:S(2)}, u32[]{:S(2)}) collective-permute-start(bf16[384,512]{1,0:T(8,128)(2,1)S(1)} %get-tuple-element.71), channel_id=1, source_target_pairs={{0,8},{1,17},{2,10},{3,19},{4,12},{5,21},{6,14},{7,23},{8,0},{9,25... | collective-permute-start | bytes 1179656 | tf_op jit(solution)/shard_map/ppermute | solution.py:440
  59.0 6.0 %collective-permute-done.12.refs_0_.refs_3_ = bf16[192,896]{1,0:T(8,128)(2,1)S(1)} collective-permute-done((bf16[192,896]{1,0:T(8,128)(2,1)S(1)}, bf16[192,896]{1,0:T(8,128)(2,1)S(1)}, u32[]{:S(2)}, u32[]{:S(2)}) %collective-permute-start.12) | collective-permute-done | bytes 344096 | tf_op jit(solution)/shard_map/ppermute | solution.py:440
  65.7 1.0 %collective-permute-start.14 = (bf16[192,640]{1,0:T(8,128)(2,1)S(1)}, bf16[192,640]{1,0:T(8,128)(2,1)S(1)}, u32[]{:S(2)}, u32[]{:S(2)}) collective-permute-start(bf16[192,640]{1,0:T(8,128)(2,1)S(1)} %get-tuple-element.72), channel_id=1, source_target_pairs={{0,16},{1,9},{2,18},{3,11},{4,20},{5,13},{6,22},{7,15},{8,24},{9,1... | collective-permute-start | bytes 737288 | tf_op jit(solution)/shard_map/ppermute | solution.py:440
  66.7 2.6 %shard_map.106 = (bf16[384,768]{1,0:T(8,128)(2,1)}, bf16[384,768]{1,0:T(8,128)(2,1)}, f32[8,128]{1,0:T(8,128)S(1)}) custom-call(f32[384,768]{1,0:T(8,128)S(1)} %shard_map.104.refs_4_.held_ref, bf16[384,512]{1,0:T(8,128)(2,1)S(1)} %get-tuple-element.54.rows_ref, bf16[768,2048]{1,0:T(8,128)(2,1)S(1)} %bitcast.11, ...), custom_call_target="tpu_custom_call" | custom-call | flops 4718592 | bytes 55296 | tf_op jit(solution)/shard_map/pallas_call | solution.py:357
  69.3 1.2 %collective-permute-done.16 = f32[8,128]{1,0:T(8,128)S(1)} collective-permute-done((f32[8,128]{1,0:T(8,128)S(1)}, f32[8,128]{1,0:T(8,128)S(1)}, u32[]{:S(2)}, u32[]{:S(2)}) %collective-permute-start.16) | collective-permute-done | bytes 4128 | tf_op jit(solution)/shard_map/ppermute | solution.py:430
  70.7 1.7 %collective-permute-done.13.arrived_ref = bf16[384,512]{1,0:T(8,128)(2,1)S(1)} collective-permute-done((bf16[384,512]{1,0:T(8,128)(2,1)S(1)}, bf16[384,512]{1,0:T(8,128)(2,1)S(1)}, u32[]{:S(2)}, u32[]{:S(2)}) %collective-permute-start.13) | collective-permute-done | bytes 393248 | tf_op jit(solution)/shard_map/ppermute | solution.py:440
  73.1 1.0 %collective-permute-done.17 = f32[16,128]{1,0:T(8,128)S(1)} collective-permute-done((f32[16,128]{1,0:T(8,128)S(1)}, f32[16,128]{1,0:T(8,128)S(1)}, u32[]{:S(2)}, u32[]{:S(2)}) %collective-permute-start.17) | collective-permute-done | bytes 8224 | tf_op jit(solution)/shard_map/ppermute | solution.py:430
  74.1 1.4 %collective-permute-start.18 = (f32[32,128]{1,0:T(8,128)S(1)}, f32[32,128]{1,0:T(8,128)S(1)}, u32[]{:S(2)}, u32[]{:S(2)}) collective-permute-start(f32[32,128]{1,0:T(8,128)S(1)} %constant_dynamic-update-slice_fusion.near_ref), channel_id=1, source_target_pairs={{0,4},{1,5},{2,6},{3,7},{4,0},{5,1},{6,2},{7,3},{8,12},{9,13},{10,... | collective-permute-start | bytes 49160 | tf_op jit(solution)/shard_map/ppermute | solution.py:430
  75.5 3.2 %collective-permute-done.18.far_ref = f32[32,128]{1,0:T(8,128)S(1)} collective-permute-done((f32[32,128]{1,0:T(8,128)S(1)}, f32[32,128]{1,0:T(8,128)S(1)}, u32[]{:S(2)}, u32[]{:S(2)}) %collective-permute-start.18) | collective-permute-done | bytes 16416 | tf_op jit(solution)/shard_map/ppermute | solution.py:430
  78.7 0.8 shard_map.110.refs_6_
  79.6 0.7 copy-done.6
  80.2 1.2 %shard_map.111 = f32[192,2048]{1,0:T(8,128)} custom-call(f32[192,896]{1,0:T(8,128)S(1)} %get-tuple-element.63.refs_0_, f32[192,640]{1,0:T(8,128)S(1)} %get-tuple-element.68.refs_1_, f32[192,512]{1,0:T(8,128)S(1)} %get-tuple-element.73.refs_2_, bf16[192,896]{1,0:T(8,128)(2,1)S(1)} %collective-permute-done.12.refs_0_.refs_3_, ...), custom_call_target="tpu_custom_call" | custom-call | flops 12288 | bytes 61440 | tf_op jit(solution)/shard_map/pallas_call | solution.py:261
  (47 shorter events, 6.1 us)
Async XLA Ops:
  0.6 8.0 %collective-permute-start.1 = (bf16[128,2048]{1,0:T(8,128)(2,1)}, bf16[128,2048]{1,0:T(8,128)(2,1)S(1)}, u32[]{:S(2)}, u32[]{:S(2)}) collective-permute-start(bf16[128,2048]{1,0:T(8,128)(2,1)} %refs_2_.3), channel_id=1, source_target_pairs={{0,1},{1,0},{2,3},{3,2},{4,5},{5,4},{6,7},{7,6},{8,9},{9,8},{10,11... | collective-permute-start | bytes 1572872 | tf_op jit(solution)/shard_map/ppermute | solution.py:430
  1.1 1.0 %copy-start.1 = (bf16[128,2048]{1,0:T(8,128)(2,1)S(1)}, bf16[128,2048]{1,0:T(8,128)(2,1)}, u32[]{:S(2)}) copy-start(bf16[128,2048]{1,0:T(8,128)(2,1)} %refs_2_.3) | copy-start | bytes 1572868
  2.2 0.7 copy-start.7
  2.9 0.7 copy-start.8
  3.8 16.2 %collective-permute-start.3 = (bf16[144,896]{1,0:T(8,128)(2,1)S(1)}, bf16[144,896]{1,0:T(8,128)(2,1)S(1)}, u32[]{:S(2)}, u32[]{:S(2)}) collective-permute-start(bf16[144,896]{1,0:T(8,128)(2,1)S(1)} %get-tuple-element.44), channel_id=1, source_target_pairs={{0,4},{1,5},{2,6},{3,7},{4,0},{5,1},{6,2},{7,3},{8,12},{9,13},{10,... | collective-permute-start | bytes 774152 | tf_op jit(solution)/shard_map/ppermute | solution.py:430
  7.4 1.2 %collective-permute-start = (bf16[16,128]{1,0:T(8,128)(2,1)S(1)}, bf16[16,128]{1,0:T(8,128)(2,1)S(1)}, u32[]{:S(2)}, u32[]{:S(2)}) collective-permute-start(bf16[16,128]{1,0:T(8,128)(2,1)S(1)} %get-tuple-element.41.refs_0_.meta_ref), channel_id=1, source_target_pairs={{0,1},{1,0},{2,3},{3,2},{4,5},{5,4},{6,7},{7,6},{8,9},{9,8},{10,11... | collective-permute-start | bytes 12296 | tf_op jit(solution)/shard_map/ppermute | solution.py:430
  8.6 1.0 %copy-start.2 = (bf16[128,2048]{1,0:T(8,128)(2,1)S(1)}, bf16[128,2048]{1,0:T(8,128)(2,1)}, u32[]{:S(2)}) copy-start(bf16[128,2048]{1,0:T(8,128)(2,1)} %refs_2_.3) | copy-start | bytes 1572868
  9.7 13.0 %copy-start.3 = (bf16[128,2048]{1,0:T(8,128)(2,1)S(1)}, bf16[128,2048]{1,0:T(8,128)(2,1)}, u32[]{:S(2)}) copy-start(bf16[128,2048]{1,0:T(8,128)(2,1)} %refs_2_.3) | copy-start | bytes 1572868
  9.9 10.9 %collective-permute-start.2 = (bf16[96,896]{1,0:T(8,128)(2,1)S(1)}, bf16[96,896]{1,0:T(8,128)(2,1)S(1)}, u32[]{:S(2)}, u32[]{:S(2)}) collective-permute-start(bf16[96,896]{1,0:T(8,128)(2,1)S(1)} %get-tuple-element.43), channel_id=1, source_target_pairs={{0,2},{1,3},{2,0},{3,1},{4,6},{5,7},{6,4},{7,5},{8,10},{9,11},{10,... | collective-permute-start | bytes 516104 | tf_op jit(solution)/shard_map/ppermute | solution.py:430
  20.8 4.2 %copy-start.4 = (bf16[1,1,8,48,768]{4,3,2,1,0:T(8,128)(2,1)S(1)}, bf16[1,1,8,48,768]{4,3,2,1,0:T(8,128)(2,1)}, u32[]{:S(2)}) copy-start(bf16[1,1,8,48,768]{4,3,2,1,0:T(8,128)(2,1)} %param.9) | copy-start | bytes 1769476
  20.8 4.2 %copy-start.5 = (bf16[1,1,8,48,768]{4,3,2,1,0:T(8,128)(2,1)S(1)}, bf16[1,1,8,48,768]{4,3,2,1,0:T(8,128)(2,1)}, u32[]{:S(2)}) copy-start(bf16[1,1,8,48,768]{4,3,2,1,0:T(8,128)(2,1)} %param.10) | copy-start | bytes 1769476
  20.8 1.5 %collective-permute-start.4 = (bf16[144,896]{1,0:T(8,128)(2,1)S(1)}, bf16[144,896]{1,0:T(8,128)(2,1)S(1)}, u32[]{:S(2)}, u32[]{:S(2)}) collective-permute-start(bf16[144,896]{1,0:T(8,128)(2,1)S(1)} %shard_map.96.refs_0_.refs_2_), channel_id=1, source_target_pairs={{0,1},{1,0},{2,3},{3,2},{4,5},{5,4},{6,7},{7,6},{8,9},{9,8},{10,11... | collective-permute-start | bytes 774152 | tf_op jit(solution)/shard_map/ppermute | solution.py:430
  20.9 22.2 %collective-permute-start.7 = (bf16[128,1152]{1,0:T(8,128)(2,1)S(1)}, bf16[128,1152]{1,0:T(8,128)(2,1)S(1)}, u32[]{:S(2)}, u32[]{:S(2)}) collective-permute-start(bf16[128,1152]{1,0:T(8,128)(2,1)S(1)} %get-tuple-element.50), channel_id=1, source_target_pairs={{0,4},{1,5},{2,6},{3,7},{4,0},{5,1},{6,2},{7,3},{8,12},{9,13},{10,... | collective-permute-start | bytes 884744 | tf_op jit(solution)/shard_map/ppermute | solution.py:430
  22.9 20.1 %collective-permute-start.6 = (bf16[96,1152]{1,0:T(8,128)(2,1)S(1)}, bf16[96,1152]{1,0:T(8,128)(2,1)S(1)}, u32[]{:S(2)}, u32[]{:S(2)}) collective-permute-start(bf16[96,1152]{1,0:T(8,128)(2,1)S(1)} %get-tuple-element.49), channel_id=1, source_target_pairs={{0,2},{1,3},{2,0},{3,1},{4,6},{5,7},{6,4},{7,5},{8,10},{9,11},{10,... | collective-permute-start | bytes 663560 | tf_op jit(solution)/shard_map/ppermute | solution.py:430
  24.7 15.7 %collective-permute-start.5 = (bf16[96,896]{1,0:T(8,128)(2,1)S(1)}, bf16[96,896]{1,0:T(8,128)(2,1)S(1)}, u32[]{:S(2)}, u32[]{:S(2)}) collective-permute-start(bf16[96,896]{1,0:T(8,128)(2,1)S(1)} %get-tuple-element.46.refs_4_), channel_id=1, source_target_pairs={{0,2},{1,3},{2,0},{3,1},{4,6},{5,7},{6,4},{7,5},{8,10},{9,11},{10,... | collective-permute-start | bytes 516104 | tf_op jit(solution)/shard_map/ppermute | solution.py:430
  40.4 4.6 %copy-start = (bf16[1,768,2048]{2,1,0:T(8,128)(2,1)S(1)}, bf16[1,768,2048]{2,1,0:T(8,128)(2,1)}, u32[]{:S(2)}) copy-start(bf16[1,768,2048]{2,1,0:T(8,128)(2,1)} %param.11) | copy-start | bytes 9437188
  41.4 12.4 %collective-permute-start.10 = (bf16[384,896]{1,0:T(8,128)(2,1)S(1)}, bf16[384,896]{1,0:T(8,128)(2,1)S(1)}, u32[]{:S(2)}, u32[]{:S(2)}) collective-permute-start(bf16[384,896]{1,0:T(8,128)(2,1)S(1)} %get-tuple-element.62), channel_id=1, source_target_pairs={{0,8},{1,17},{2,10},{3,19},{4,12},{5,21},{6,14},{7,23},{8,0},{9,25... | collective-permute-start | bytes 2064392 | tf_op jit(solution)/shard_map/ppermute | solution.py:440
  43.0 1.6 %collective-permute-start.8 = (bf16[128,1152]{1,0:T(8,128)(2,1)S(1)}, bf16[128,1152]{1,0:T(8,128)(2,1)S(1)}, u32[]{:S(2)}, u32[]{:S(2)}) collective-permute-start(bf16[128,1152]{1,0:T(8,128)(2,1)S(1)} %shard_map.101.refs_2_), channel_id=1, source_target_pairs={{0,1},{1,0},{2,3},{3,2},{4,5},{5,4},{6,7},{7,6},{8,9},{9,8},{10,11... | collective-permute-start | bytes 884744 | tf_op jit(solution)/shard_map/ppermute | solution.py:430
  44.9 7.5 %collective-permute-start.9 = (bf16[96,1152]{1,0:T(8,128)(2,1)S(1)}, bf16[96,1152]{1,0:T(8,128)(2,1)S(1)}, u32[]{:S(2)}, u32[]{:S(2)}) collective-permute-start(bf16[96,1152]{1,0:T(8,128)(2,1)S(1)} %get-tuple-element.52), channel_id=1, source_target_pairs={{0,2},{1,3},{2,0},{3,1},{4,6},{5,7},{6,4},{7,5},{8,10},{9,11},{10,... | collective-permute-start | bytes 663560 | tf_op jit(solution)/shard_map/ppermute | solution.py:430
  53.2 12.4 %collective-permute-start.11 = (bf16[384,640]{1,0:T(8,128)(2,1)S(1)}, bf16[384,640]{1,0:T(8,128)(2,1)S(1)}, u32[]{:S(2)}, u32[]{:S(2)}) collective-permute-start(bf16[384,640]{1,0:T(8,128)(2,1)S(1)} %get-tuple-element.66), channel_id=1, source_target_pairs={{0,8},{1,17},{2,10},{3,19},{4,12},{5,21},{6,14},{7,23},{8,0},{9,25... | collective-permute-start | bytes 1474568 | tf_op jit(solution)/shard_map/ppermute | solution.py:440
  53.9 11.1 %collective-permute-start.12 = (bf16[192,896]{1,0:T(8,128)(2,1)S(1)}, bf16[192,896]{1,0:T(8,128)(2,1)S(1)}, u32[]{:S(2)}, u32[]{:S(2)}) collective-permute-start(bf16[192,896]{1,0:T(8,128)(2,1)S(1)} %get-tuple-element.67), channel_id=1, source_target_pairs={{0,16},{1,9},{2,18},{3,11},{4,20},{5,13},{6,22},{7,15},{8,24},{9,1... | collective-permute-start | bytes 1032200 | tf_op jit(solution)/shard_map/ppermute | solution.py:440
  57.4 15.0 %collective-permute-start.13 = (bf16[384,512]{1,0:T(8,128)(2,1)S(1)}, bf16[384,512]{1,0:T(8,128)(2,1)S(1)}, u32[]{:S(2)}, u32[]{:S(2)}) collective-permute-start(bf16[384,512]{1,0:T(8,128)(2,1)S(1)} %get-tuple-element.71), channel_id=1, source_target_pairs={{0,8},{1,17},{2,10},{3,19},{4,12},{5,21},{6,14},{7,23},{8,0},{9,25... | collective-permute-start | bytes 1179656 | tf_op jit(solution)/shard_map/ppermute | solution.py:440
  65.7 6.8 %collective-permute-start.14 = (bf16[192,640]{1,0:T(8,128)(2,1)S(1)}, bf16[192,640]{1,0:T(8,128)(2,1)S(1)}, u32[]{:S(2)}, u32[]{:S(2)}) collective-permute-start(bf16[192,640]{1,0:T(8,128)(2,1)S(1)} %get-tuple-element.72), channel_id=1, source_target_pairs={{0,16},{1,9},{2,18},{3,11},{4,20},{5,13},{6,22},{7,15},{8,24},{9,1... | collective-permute-start | bytes 737288 | tf_op jit(solution)/shard_map/ppermute | solution.py:440
  69.3 1.2 %collective-permute-start.16 = (f32[8,128]{1,0:T(8,128)S(1)}, f32[8,128]{1,0:T(8,128)S(1)}, u32[]{:S(2)}, u32[]{:S(2)}) collective-permute-start(f32[8,128]{1,0:T(8,128)S(1)} %get-tuple-element.75), channel_id=1, source_target_pairs={{0,1},{1,0},{2,3},{3,2},{4,5},{5,4},{6,7},{7,6},{8,9},{9,8},{10,11... | collective-permute-start | bytes 12296 | tf_op jit(solution)/shard_map/ppermute | solution.py:430
  70.5 3.7 %collective-permute-start.17 = (f32[16,128]{1,0:T(8,128)S(1)}, f32[16,128]{1,0:T(8,128)S(1)}, u32[]{:S(2)}, u32[]{:S(2)}) collective-permute-start(f32[16,128]{1,0:T(8,128)S(1)} %pad_maximum_fusion), channel_id=1, source_target_pairs={{0,2},{1,3},{2,0},{3,1},{4,6},{5,7},{6,4},{7,5},{8,10},{9,11},{10,... | collective-permute-start | bytes 24584 | tf_op jit(solution)/shard_map/ppermute | solution.py:430
  72.5 7.0 %collective-permute-start.15 = (bf16[192,512]{1,0:T(8,128)(2,1)S(1)}, bf16[192,512]{1,0:T(8,128)(2,1)S(1)}, u32[]{:S(2)}, u32[]{:S(2)}) collective-permute-start(bf16[192,512]{1,0:T(8,128)(2,1)S(1)} %get-tuple-element.74), channel_id=1, source_target_pairs={{0,16},{1,9},{2,18},{3,11},{4,20},{5,13},{6,22},{7,15},{8,24},{9,1... | collective-permute-start | bytes 589832 | tf_op jit(solution)/shard_map/ppermute | solution.py:440
  74.1 4.6 %collective-permute-start.18 = (f32[32,128]{1,0:T(8,128)S(1)}, f32[32,128]{1,0:T(8,128)S(1)}, u32[]{:S(2)}, u32[]{:S(2)}) collective-permute-start(f32[32,128]{1,0:T(8,128)S(1)} %constant_dynamic-update-slice_fusion.near_ref), channel_id=1, source_target_pairs={{0,4},{1,5},{2,6},{3,7},{4,0},{5,1},{6,2},{7,3},{8,12},{9,13},{10,... | collective-permute-start | bytes 49160 | tf_op jit(solution)/shard_map/ppermute | solution.py:430
  79.6 0.7 copy-start.6

commit v6 on v5

--- a/solution.py
+++ b/solution.py
@@ -9,11 +9,10 @@
 
 LANES = 128
 META = 16
-PARTS = ((896,), (640, 512))
+WIDTHS = (768, 1280)
 VMEM_LIMIT = 10 * 1024 * 1024
 VMEM = pl.BlockSpec(memory_space=pltpu.VMEM)
 ANY = pl.BlockSpec(memory_space=pl.ANY)
-HBM = pl.BlockSpec(memory_space=pltpu.HBM)
 
 
 def params():
@@ -29,29 +28,8 @@
     return (gate_value * sigmoid, sigmoid * (1.0 + gate_value * (1.0 - sigmoid)))
 
 
-def tokens_kernel(expert_count, routes_hbm, probs_hbm, rows_hbm, meta_ref, *refs):
-    part_refs, (routes_ref, probs_ref, semaphores) = refs[:-3], refs[-3:]
-    token_count = rows_hbm.shape[0]
-    top_count = routes_ref.shape[0]
-    copies = [
-        pltpu.make_async_copy(routes_hbm, routes_ref, semaphores.at[0]),
-        pltpu.make_async_copy(probs_hbm, probs_ref, semaphores.at[1]),
-    ]
-    start = 0
-    for part, part_ref in enumerate(part_refs):
-        width = part_ref.shape[1]
-        copies.append(
-            pltpu.make_async_copy(
-                rows_hbm.at[:, start : start + width],
-                part_ref.at[:token_count, :],
-                semaphores.at[2 + part],
-            )
-        )
-        start += width
-    for copy in copies:
-        copy.start()
-    for copy in copies[:2]:
-        copy.wait()
+def tokens_kernel(expert_count, routes_ref, probs_ref, meta_ref):
+    top_count, token_count = routes_ref.shape
     names = [routes_ref[k : k + 1, :] for k in range(top_count)]
     experts = lax.broadcasted_iota(jnp.int32, (expert_count, token_count), 0)
     onehots = [(experts == name).astype(jnp.float32) for name in names]
@@ -69,40 +47,29 @@
     for k in range(top_count):
         lines.append(probs_ref[k : k + 1, :].astype(jnp.float32))
     lines.append(jnp.zeros((META - len(lines), token_count), jnp.float32))
-    meta = jnp.concatenate(lines, axis=0).astype(jnp.bfloat16)
-    meta_ref[...] = meta
-    lead_ref = part_refs[0]
-    lead_ref[token_count:, :] = jnp.zeros((META, lead_ref.shape[1]), jnp.bfloat16)
-    lead_ref[token_count:, :token_count] = meta
-    for copy in copies[2:]:
-        copy.wait()
-
-
-def token_parts(routes, probs, grad_out, expert_count):
+    meta_ref[...] = jnp.concatenate(lines, axis=0).astype(jnp.bfloat16)
+
+
+def token_lines(routes, probs, expert_count):
     token_count = routes.shape[1]
     return pl.pallas_call(
         functools.partial(tokens_kernel, expert_count),
-        in_specs=[HBM] * 3,
-        out_shape=[jax.ShapeDtypeStruct((META, token_count), jnp.bfloat16)]
-        + [
-            jax.ShapeDtypeStruct((token_count + (0 if part else META), width), jnp.bfloat16)
-            for part, width in enumerate(map(sum, PARTS))
-        ],
-        scratch_shapes=[
-            pltpu.VMEM(routes.shape, routes.dtype),
-            pltpu.VMEM(probs.shape, probs.dtype),
-            pltpu.SemaphoreType.DMA((2 + len(PARTS),)),
-        ],
-        compiler_params=params(),
-        cost_estimate=cost(100 * token_count * token_count, 4 * grad_out.size),
-    )(routes, probs, grad_out)
+        in_specs=[VMEM] * 2,
+        out_shape=jax.ShapeDtypeStruct((META, token_count), jnp.bfloat16),
+        compiler_params=params(),
+        cost_estimate=cost(100 * token_count * token_count, 4 * token_count * META),
+    )(routes, probs)
+
+
+def far_offset():
+    return 4 + 2 * lax.bitwise_and(lax.axis_index("expert"), 1)
 
 
 def chosen_rows(meta, top_count, capacity):
     token_count = meta.shape[1]
     slots = lax.broadcasted_iota(jnp.int32, (capacity, token_count), 0).astype(jnp.float32)
     parts = []
-    for offset in (0, 2):
+    for offset in (0, 2, far_offset(), far_offset() + 1):
         target = lax.bitwise_xor(lax.axis_index("expert"), offset).astype(jnp.float32)
         part = jnp.zeros((capacity, token_count), jnp.float32)
         for k in range(top_count):
@@ -114,29 +81,30 @@
 
 
 def dispatch_kernel(capacity, top_count, start, *refs):
-    meta_refs, row_refs, (local_ref, sent_ref) = refs[:2], refs[2:4], refs[-2:]
-    token_count = meta_refs[0].shape[1] if meta_refs[0].shape[0] == META else LANES
+    meta_refs, row_refs, (local_ref, near_ref, far_ref) = refs[:2], refs[2:4], refs[-3:]
     width = local_ref.shape[1]
     for source in range(2):
-        first = meta_refs[source].shape[0] - META
-        meta = meta_refs[source][first:, :token_count].astype(jnp.float32)
         rows = jnp.dot(
-            chosen_rows(meta, top_count, capacity),
-            row_refs[source][:token_count, start : start + width],
+            chosen_rows(meta_refs[source][...].astype(jnp.float32), top_count, capacity),
+            row_refs[source][:, start : start + width],
             preferred_element_type=jnp.float32,
         ).astype(jnp.bfloat16)
-        local_ref[source * capacity : (source + 1) * capacity, :] = rows[:capacity, :]
-        sent_ref[source * capacity : (source + 1) * capacity, :] = rows[capacity:, :]
-
-
-def dispatch(metas, rows, capacity, top_count, start, width, earlier=()):
-    block = jax.ShapeDtypeStruct((2 * capacity, width), jnp.bfloat16)
+        places = [(local_ref, source), (near_ref, source), (far_ref, source), (far_ref, source + 2)]
+        for step, (block_ref, place) in enumerate(places):
+            block_ref[place * capacity : (place + 1) * capacity, :] = rows[
+                step * capacity : (step + 1) * capacity, :
+            ]
+
+
+def dispatch(metas, rows, capacity, top_count, start, width, earlier):
     return pl.pallas_call(
         functools.partial(dispatch_kernel, capacity, top_count, start),
         in_specs=[VMEM] * 4 + [ANY] * len(earlier),
-        out_shape=[block, block],
-        compiler_params=params(),
-        cost_estimate=cost(8 * capacity * LANES * width, 8 * capacity * width),
+        out_shape=[
+            jax.ShapeDtypeStruct((count * capacity, width), jnp.bfloat16) for count in (2, 2, 4)
+        ],
+        compiler_params=params(),
+        cost_estimate=cost(16 * capacity * LANES * width, 16 * capacity * width),
     )(*metas, *rows, *earlier)
 
 
@@ -170,16 +138,19 @@
     )(gate, up)
 
 
-def panel_kernel(capacity, columns, turned_ref, *refs):
+def panel_kernel(capacity, turned_ref, *refs):
     block_refs, (rows_ref, own_ref, later_ref, sent_ref) = refs[:4], refs[-4:]
-    share, width = own_ref.shape
+    share = own_ref.shape[0]
     device = lax.axis_index("expert")
-    for block, (block_ref, column) in enumerate(zip(block_refs, columns)):
+    far = far_offset()
+    offsets = ((0, 1), (2, 3), (far, far + 1), (11 - far, 10 - far))
+    for block, block_ref in enumerate(block_refs):
+        first = 2 * capacity if block == 3 else 0
         for half in range(2):
-            place = lax.bitwise_xor(device, 2 * block + half)
+            place = lax.bitwise_xor(device, offsets[block][half])
             row = pl.multiple_of(place * capacity, capacity)
             rows_ref[pl.ds(row, capacity), :] = block_ref[
-                half * capacity : (half + 1) * capacity, column : column + width
+                first + half * capacity : first + (half + 1) * capacity, :
             ]
     rows = rows_ref[...]
 
@@ -195,11 +166,12 @@
     own_ref[...] = part(0)
 
 
-def panel_parts(turned, blocks, capacity, width, earlier):
+def panel_parts(turned, blocks, capacity, earlier):
     hidden_width, row_count = turned.shape
+    width = blocks[0].shape[1]
     share = hidden_width // 4
     return pl.pallas_call(
-        functools.partial(panel_kernel, capacity, [column for _, column in blocks]),
+        functools.partial(panel_kernel, capacity),
         in_specs=[VMEM] * 5 + [ANY] * len(earlier),
         out_shape=[
             jax.ShapeDtypeStruct((row_count, width), jnp.bfloat16),
@@ -211,7 +183,7 @@
         cost_estimate=cost(
             2 * hidden_width * row_count * width, 2 * hidden_width * (row_count + width)
         ),
-    )(turned, *[block for block, _ in blocks], *earlier)
+    )(turned, *blocks, *earlier)
 
 
 def halve_kernel(own_ref, later_ref, arrived_ref, *refs):
@@ -261,7 +233,7 @@
     return pl.pallas_call(
         functools.partial(total_kernel, len(owns)),
         in_specs=[VMEM] * (2 * len(owns)) + [ANY] * len(earlier),
-        out_specs=HBM,
+        out_specs=ANY,
         out_shape=jax.ShapeDtypeStruct((share, size // share), jnp.float32),
         scratch_shapes=[pltpu.VMEM(own.shape, jnp.float32) for own in owns]
         + [pltpu.SemaphoreType.DMA((len(owns),))],
@@ -430,6 +402,12 @@
     return lax.ppermute(value, "expert", [(place, place ^ offset) for place in range(size)])
 
 
+def swap_far(value):
+    size = lax.axis_size("expert")
+    pairs = [(place, place ^ (4 + 2 * (place & 1))) for place in range(size)]
+    return lax.ppermute(value, "expert", pairs)
+
+
 def swap_groups(value, later):
     groups, places = lax.axis_size("dp"), lax.axis_size("expert")
     pairs = []
@@ -448,60 +426,39 @@
     top_count = routes.shape[1]
     row_count = expert_count * capacity
 
-    meta, *parts = token_parts(routes.T, probs.T, grad_out, expert_count)
-    parts = [swap(part, 4) for part in parts]
+    meta = token_lines(routes.T, probs.T, expert_count)
     metas = [meta, swap(meta, 1)]
     near_rows = [grad_out, swap(grad_out, 1)]
     weight = w_down[0]
     turned, hidden, up_scale, gate_scale = hidden_parts(
         saved_gate.reshape(row_count, hidden_width), saved_up.reshape(row_count, hidden_width)
     )
-    held, start, far_sent = None, 0, None
-    owns, arrived = [], []
-    for part, widths in enumerate(PARTS):
-        part_width = sum(widths)
-        local, sent = dispatch(
-            metas,
-            near_rows,
-            capacity,
-            top_count,
-            start,
-            part_width,
-            [] if far_sent is None else [far_sent],
-        )
-        near = swap(sent, 2)
-        parts[part] = after(parts[part], near)
-        other_part = swap(parts[part], 1)
-        far_metas = [parts[0], other_part] if part == 0 else far_metas
-        far_local, far_sent = dispatch(
-            far_metas,
-            [parts[part], other_part],
-            capacity,
-            top_count,
-            0,
-            part_width,
-        )
-        far_near = swap(far_sent, 2)
-        column = 0
-        for width in widths:
-            blocks = [(block, column) for block in (local, near, far_local, far_near)]
-            earlier = [] if held is None else [held]
-            rows, own, later, half = panel_parts(turned, blocks, capacity, width, earlier)
-            own, half = halve(own, later, swap_groups(half, False), arrived[-1:])
-            owns.append(own)
-            arrived.append(swap_groups(half, True))
-            if start + width < model_width:
-                held = grad_hidden_step(held, rows, weight, start)
-            else:
-                grad_gate, grad_up, lines = grad_hidden_last(
-                    held, rows, weight, start, hidden, up_scale, gate_scale, capacity
-                )
-            start += width
-            column += width
+    held, start = None, 0
+    all_rows, owns, arrived = [], [], []
+    for chunk, width in enumerate(WIDTHS):
+        earlier = all_rows[chunk - 2 : chunk - 1] if chunk > 1 else []
+        local, near, far = dispatch(metas, near_rows, capacity, top_count, start, width, earlier)
+        near = swap(near, 2)
+        far = after(swap_far(far), near, *all_rows[-1:])
+        blocks = [local, near, far, swap(far, 1)]
+        earlier = [] if held is None else [held, own]
+        rows, own, later, half = panel_parts(turned, blocks, capacity, earlier)
+        all_rows.append(rows)
+        own, half = halve(own, later, swap_groups(half, False), arrived[-1:])
+        owns.append(own)
+        arrived.append(swap_groups(half, True))
+        if chunk + 1 < len(WIDTHS):
+            held = grad_hidden_step(held, rows, weight, start)
+        else:
+            grad_gate, grad_up, lines = grad_hidden_last(
+                held, rows, weight, start, hidden, up_scale, gate_scale, capacity
+            )
+        start += width
     for offset in (1, 2):
         lines = jnp.concatenate([lines, swap(lines, offset)], axis=0)
-    route_grad = route_back(meta, lines, swap(lines, 4), expert_count, top_count, capacity)
-    panel = total(owns, arrived, [route_grad])
+    far_lines = swap(lines, 4)
+    panel = total(owns, arrived, [far_lines])
+    route_grad = route_back(meta, lines, far_lines, expert_count, top_count, capacity)
     return (
         grad_gate.reshape(saved_gate.shape),
         grad_up.reshape(saved_up.shape),
@@ -571,7 +528,7 @@
         and capacity <= LANES
         and hidden_width % (16 * group_count) == 0
         and routes.shape[0] == LANES
-        and grad_out.shape[1] == sum(map(sum, PARTS))
+        and grad_out.shape[1] == sum(WIDTHS)
     )
     run = line_shards if aligned else plain_shards
     return run(grad_out, probs, routes, saved_gate, saved_up, w_down)

time: 81.7 us -> 82.1 us (level)
  waiting for transfers between devices: 47.5 us -> 52.5 us
  local copies, waits for them, and re-layouts: 4.12 us -> 2.39 us
  Pallas kernels: 12.1 us -> 10.4 us
  starting transfers between devices: 16.9 us -> 16 us
    ppermute x13 -> x9, waiting for transfers between devices: 39.2 us -> 24.1 us  [swap(): lax.ppermute(value, 'expert', [(place, place ^ offset) for place in range...]
    ppermute x0 -> x2, waiting for transfers between devices: none -> 14.4 us  [swap_far(): return lax.ppermute(value, 'expert', pairs)]
    ppermute x6 -> x4, waiting for transfers between devices: 8.31 us -> 14 us  [swap_groups(): return lax.ppermute(value, ('dp', 'expert'), pairs)]
    ppermute x0 -> x2, starting transfers between devices: none -> 4.21 us  [swap_far(): return lax.ppermute(value, 'expert', pairs)]
    ppermute x13 -> x9, starting transfers between devices: 9.95 us -> 5.77 us  [swap(): lax.ppermute(value, 'expert', [(place, place ^ offset) for place in range...]
    unnamed x20 -> x14, local copies, waits for them, and re-layouts: 4.11 us -> 2.39 us
    pallas_call x2 -> x1, Pallas kernels: 2.55 us -> 1.2 us  [grad_hidden_step(): pl.pallas_call(functools.partial(first_kernel if held is None else middle...]
    ppermute x6 -> x4, starting transfers between devices: 6.96 us -> 5.99 us  [swap_groups(): return lax.ppermute(value, ('dp', 'expert'), pairs)]
  transfers between devices with their start and end apart: 19 -> 15, of which waited for: 13 -> 10; matrix products, arithmetic and copies ran while one was open for 0% -> 0% of each run, Pallas kernels for 13% -> 9%
where the time goes in v6:
time: 82.1 us; the launch traced here: 82 us
  waiting for transfers between devices  52.5 us (64%)
  starting transfers between devices  16 us (19%)
  Pallas kernels  10.4 us (13%)
  local copies, waits for them, and re-layouts  2.39 us (3%)
    ppermute x9, waiting for transfers between devices, swap(): lax.ppermute(value, 'expert', [(place, place ^ offset) for place in range...  24.1 us
    ppermute x2, waiting for transfers between devices, swap_far(): return lax.ppermute(value, 'expert', pairs)  14.4 us
    ppermute x4, waiting for transfers between devices, swap_groups(): return lax.ppermute(value, ('dp', 'expert'), pairs)  14 us
    ppermute x4, starting transfers between devices, swap_groups(): return lax.ppermute(value, ('dp', 'expert'), pairs)  5.99 us
    ppermute x9, starting transfers between devices, swap(): lax.ppermute(value, 'expert', [(place, place ^ offset) for place in range...  5.77 us
    ppermute x2, starting transfers between devices, swap_far(): return lax.ppermute(value, 'expert', pairs)  4.21 us
    pallas_call x1, Pallas kernels, grad_hidden_last(): pl.pallas_call(functools.partial(last_kernel, capacity, start), grid=(hid...  2.97 us
    unnamed x14, local copies, waits for them, and re-layouts  2.39 us
  transfers between devices with their start and end apart: 15, of which 10 were waited for; matrix products, arithmetic and copies ran while one was open for 0% of the time, Pallas kernels for 9%

profile of v6, /device:TPU:0, one launch (start us, length us, event | category | flops | bytes accessed | tf_op | source)
XLA Modules:
  0.0 82.0 jit_solution(13567296304497153123)
XLA Ops:
  0.6 0.5 collective-permute-start.1
  1.2 0.7 copy-done.4
  1.8 0.7 copy-done.5
  2.7 1.1 %collective-permute-done.refs_1_ = bf16[16,128]{1,0:T(8,128)(2,1)S(1)} collective-permute-done((bf16[16,128]{1,0:T(8,128)(2,1)S(1)}, bf16[16,128]{1,0:T(8,128)(2,1)S(1)}, u32[]{:S(2)}, u32[]{:S(2)}) %collective-permute-start) | collective-permute-done | bytes 4128 | tf_op jit(solution)/shard_map/ppermute | solution.py:402
  3.8 1.0 %copy-done.1 = bf16[128,2048]{1,0:T(8,128)(2,1)S(1)} copy-done((bf16[128,2048]{1,0:T(8,128)(2,1)S(1)}, bf16[128,2048]{1,0:T(8,128)(2,1)}, u32[]{:S(2)}) %copy-start.1) | copy-done | bytes 524312
  4.8 0.3 shard_map.95
  5.2 3.8 %collective-permute-start.3 = (bf16[192,768]{1,0:T(8,128)(2,1)S(1)}, bf16[192,768]{1,0:T(8,128)(2,1)S(1)}, u32[]{:S(2)}, u32[]{:S(2)}) collective-permute-start(bf16[192,768]{1,0:T(8,128)(2,1)S(1)} %get-tuple-element.32), channel_id=1, source_target_pairs={{0,4},{1,7},{2,6},{3,5},{4,0},{5,3},{6,2},{7,1},{8,12},{9,15},{10,... | collective-permute-start | bytes 884744 | tf_op jit(solution)/shard_map/ppermute | solution.py:408
  9.0 1.6 %collective-permute-start.2 = (bf16[96,768]{1,0:T(8,128)(2,1)S(1)}, bf16[96,768]{1,0:T(8,128)(2,1)S(1)}, u32[]{:S(2)}, u32[]{:S(2)}) collective-permute-start(bf16[96,768]{1,0:T(8,128)(2,1)S(1)} %get-tuple-element.31), channel_id=1, source_target_pairs={{0,2},{1,3},{2,0},{3,1},{4,6},{5,7},{6,4},{7,5},{8,10},{9,11},{10,... | collective-permute-start | bytes 442376 | tf_op jit(solution)/shard_map/ppermute | solution.py:402
  10.6 0.4 shard_map.99
  11.0 0.4 collective-permute-start.6
  11.4 7.9 %collective-permute-done.2.refs_1_ = bf16[96,768]{1,0:T(8,128)(2,1)S(1)} collective-permute-done((bf16[96,768]{1,0:T(8,128)(2,1)S(1)}, bf16[96,768]{1,0:T(8,128)(2,1)S(1)}, u32[]{:S(2)}, u32[]{:S(2)}) %collective-permute-start.2) | collective-permute-done | bytes 147488 | tf_op jit(solution)/shard_map/ppermute | solution.py:402
  19.3 14.4 %collective-permute-done.3.refs_0_ = bf16[192,768]{1,0:T(8,128)(2,1)S(1)} collective-permute-done((bf16[192,768]{1,0:T(8,128)(2,1)S(1)}, bf16[192,768]{1,0:T(8,128)(2,1)S(1)}, u32[]{:S(2)}, u32[]{:S(2)}) %collective-permute-start.3) | collective-permute-done | bytes 294944 | tf_op jit(solution)/shard_map/ppermute | solution.py:408
  33.7 1.2 %collective-permute-start.5 = (bf16[96,1280]{1,0:T(8,128)(2,1)S(1)}, bf16[96,1280]{1,0:T(8,128)(2,1)S(1)}, u32[]{:S(2)}, u32[]{:S(2)}) collective-permute-start(bf16[96,1280]{1,0:T(8,128)(2,1)S(1)} %get-tuple-element.35), channel_id=1, source_target_pairs={{0,2},{1,3},{2,0},{3,1},{4,6},{5,7},{6,4},{7,5},{8,10},{9,11},{10,... | collective-permute-start | bytes 737288 | tf_op jit(solution)/shard_map/ppermute | solution.py:402
  34.9 1.0 %shard_map.93 = (bf16[768,384]{1,0:T(8,128)(2,1)S(1)}, bf16[384,768]{1,0:T(8,128)(2,1)S(1)}, f32[384,768]{1,0:T(8,128)S(1)}, f32[384,768]{1,0:T(8,128)S(1)}) custom-call(bf16[384,768]{1,0:T(8,128)(2,1)S(1)} %bitcast.11, bf16[384,768]{1,0:T(8,128)(2,1)S(1)} %bitcast.12), custom_call_target="tpu_custom_call" | custom-call | flops 92160 | bytes 73728 | tf_op jit(solution)/shard_map/pallas_call | solution.py:125
  35.9 0.8 %shard_map.97 = (bf16[384,768]{1,0:T(8,128)(2,1)S(1)}, f32[192,768]{1,0:T(8,128)S(1)}, f32[192,768]{1,0:T(8,128)S(1)}, bf16[384,768]{1,0:T(8,128)(2,1)S(1)}) custom-call(bf16[768,384]{1,0:T(8,128)(2,1)S(1)} %get-tuple-element.29.turned_ref, bf16[96,768]{1,0:T(8,128)(2,1)S(1)} %get-tuple-element.30.refs_0_, ...), custom_call_target="tpu_custom_call" | custom-call | flops 7077888 | bytes 27648 | tf_op jit(solution)/shard_map/pallas_call | solution.py:173
  36.7 1.6 %collective-permute-start.8 = (bf16[384,768]{1,0:T(8,128)(2,1)S(1)}, bf16[384,768]{1,0:T(8,128)(2,1)S(1)}, u32[]{:S(2)}, u32[]{:S(2)}) collective-permute-start(bf16[384,768]{1,0:T(8,128)(2,1)S(1)} %get-tuple-element.39), channel_id=1, source_target_pairs={{0,8},{1,17},{2,10},{3,19},{4,12},{5,21},{6,14},{7,23},{8,0},{9,25... | collective-permute-start | bytes 1769480 | tf_op jit(solution)/shard_map/ppermute | solution.py:418
  38.3 7.5 %collective-permute-done.5.refs_1_ = bf16[96,1280]{1,0:T(8,128)(2,1)S(1)} collective-permute-done((bf16[96,1280]{1,0:T(8,128)(2,1)S(1)}, bf16[96,1280]{1,0:T(8,128)(2,1)S(1)}, u32[]{:S(2)}, u32[]{:S(2)}) %collective-permute-start.5) | collective-permute-done | bytes 245792 | tf_op jit(solution)/shard_map/ppermute | solution.py:402
  45.8 1.2 %shard_map.98.refs_4_.held_ref = f32[384,768]{1,0:T(8,128)S(1)} custom-call(bf16[384,768]{1,0:T(8,128)(2,1)S(1)} %get-tuple-element.33.rows_ref.refs_2_, bf16[768,2048]{1,0:T(8,128)(2,1)S(1)} %bitcast.9), custom_call_target="tpu_custom_call" | custom-call | flops 7077888 | bytes 36864 | tf_op jit(solution)/shard_map/pallas_call | solution.py:271
  47.1 0.5 collective-permute-done.7.refs_3_
  47.6 1.3 %shard_map.102 = (bf16[384,1280]{1,0:T(8,128)(2,1)S(1)}, f32[192,1280]{1,0:T(8,128)S(1)}, f32[192,1280]{1,0:T(8,128)S(1)}, bf16[384,1280]{1,0:T(8,128)(2,1)S(1)}) custom-call(bf16[768,384]{1,0:T(8,128)(2,1)S(1)} %get-tuple-element.29.turned_ref, bf16[96,1280]{1,0:T(8,128)(2,1)S(1)} %get-tuple-element.34.refs_0_, ...), custom_call_target="tpu_custom_call" | custom-call | flops 11796480 | bytes 39936 | tf_op jit(solution)/shard_map/pallas_call | solution.py:173
  48.9 1.8 %collective-permute-start.9 = (bf16[384,1280]{1,0:T(8,128)(2,1)S(1)}, bf16[384,1280]{1,0:T(8,128)(2,1)S(1)}, u32[]{:S(2)}, u32[]{:S(2)}) collective-permute-start(bf16[384,1280]{1,0:T(8,128)(2,1)S(1)} %get-tuple-element.49), channel_id=1, source_target_pairs={{0,8},{1,17},{2,10},{3,19},{4,12},{5,21},{6,14},{7,23},{8,0},{9,25... | collective-permute-start | bytes 2949128 | tf_op jit(solution)/shard_map/ppermute | solution.py:418
  50.7 1.5 %collective-permute-start.10 = (bf16[192,768]{1,0:T(8,128)(2,1)S(1)}, bf16[192,768]{1,0:T(8,128)(2,1)S(1)}, u32[]{:S(2)}, u32[]{:S(2)}) collective-permute-start(bf16[192,768]{1,0:T(8,128)(2,1)S(1)} %get-tuple-element.50), channel_id=1, source_target_pairs={{0,16},{1,9},{2,18},{3,11},{4,20},{5,13},{6,22},{7,15},{8,24},{9,1... | collective-permute-start | bytes 884744 | tf_op jit(solution)/shard_map/ppermute | solution.py:418
  52.3 8.4 %collective-permute-done.10.refs_0_.refs_2_ = bf16[192,768]{1,0:T(8,128)(2,1)S(1)} collective-permute-done((bf16[192,768]{1,0:T(8,128)(2,1)S(1)}, bf16[192,768]{1,0:T(8,128)(2,1)S(1)}, u32[]{:S(2)}, u32[]{:S(2)}) %collective-permute-start.10) | collective-permute-done | bytes 294944 | tf_op jit(solution)/shard_map/ppermute | solution.py:418
  60.7 5.6 %collective-permute-done.9.arrived_ref = bf16[384,1280]{1,0:T(8,128)(2,1)S(1)} collective-permute-done((bf16[384,1280]{1,0:T(8,128)(2,1)S(1)}, bf16[384,1280]{1,0:T(8,128)(2,1)S(1)}, u32[]{:S(2)}, u32[]{:S(2)}) %collective-permute-start.9) | collective-permute-done | bytes 983072 | tf_op jit(solution)/shard_map/ppermute | solution.py:418
  66.4 1.1 %collective-permute-start.11 = (bf16[192,1280]{1,0:T(8,128)(2,1)S(1)}, bf16[192,1280]{1,0:T(8,128)(2,1)S(1)}, u32[]{:S(2)}, u32[]{:S(2)}) collective-permute-start(bf16[192,1280]{1,0:T(8,128)(2,1)S(1)} %get-tuple-element.52), channel_id=1, source_target_pairs={{0,16},{1,9},{2,18},{3,11},{4,20},{5,13},{6,22},{7,15},{8,24},{9,1... | collective-permute-start | bytes 1474568 | tf_op jit(solution)/shard_map/ppermute | solution.py:418
  67.5 3.0 %shard_map.103 = (bf16[384,768]{1,0:T(8,128)(2,1)}, bf16[384,768]{1,0:T(8,128)(2,1)}, f32[8,128]{1,0:T(8,128)S(1)}) custom-call(f32[384,768]{1,0:T(8,128)S(1)} %shard_map.98.refs_4_.held_ref, bf16[384,1280]{1,0:T(8,128)(2,1)S(1)} %get-tuple-element.41.rows_ref, bf16[768,2048]{1,0:T(8,128)(2,1)S(1)} %bitcast.10, ...), custom_call_target="tpu_custom_call" | custom-call | flops 11796480 | bytes 55296 | tf_op jit(solution)/shard_map/pallas_call | solution.py:329
  70.5 1.2 %collective-permute-done.12 = f32[8,128]{1,0:T(8,128)S(1)} collective-permute-done((f32[8,128]{1,0:T(8,128)S(1)}, f32[8,128]{1,0:T(8,128)S(1)}, u32[]{:S(2)}, u32[]{:S(2)}) %collective-permute-start.12) | collective-permute-done | bytes 4128 | tf_op jit(solution)/shard_map/ppermute | solution.py:402
  71.6 3.6 %collective-permute-done.13 = f32[16,128]{1,0:T(8,128)S(1)} collective-permute-done((f32[16,128]{1,0:T(8,128)S(1)}, f32[16,128]{1,0:T(8,128)S(1)}, u32[]{:S(2)}, u32[]{:S(2)}) %collective-permute-start.13) | collective-permute-done | bytes 8224 | tf_op jit(solution)/shard_map/ppermute | solution.py:402
  75.3 2.4 %collective-permute-start.14 = (f32[32,128]{1,0:T(8,128)S(1)}, f32[32,128]{1,0:T(8,128)S(1)}, u32[]{:S(2)}, u32[]{:S(2)}) collective-permute-start(f32[32,128]{1,0:T(8,128)S(1)} %constant_dynamic-update-slice_fusion.near_ref), channel_id=1, source_target_pairs={{0,4},{1,5},{2,6},{3,7},{4,0},{5,1},{6,2},{7,3},{8,12},{9,13},{10,... | collective-permute-start | bytes 49160 | tf_op jit(solution)/shard_map/ppermute | solution.py:402
  77.7 2.2 %collective-permute-done.14.refs_4_.far_ref = f32[32,128]{1,0:T(8,128)S(1)} collective-permute-done((f32[32,128]{1,0:T(8,128)S(1)}, f32[32,128]{1,0:T(8,128)S(1)}, u32[]{:S(2)}, u32[]{:S(2)}) %collective-permute-start.14) | collective-permute-done | bytes 16416 | tf_op jit(solution)/shard_map/ppermute | solution.py:402
  79.9 0.8 shard_map.106
  80.7 1.2 %shard_map.105 = f32[192,2048]{1,0:T(8,128)} custom-call(f32[192,768]{1,0:T(8,128)S(1)} %get-tuple-element.40.refs_5_.refs_0_, f32[192,1280]{1,0:T(8,128)S(1)} %get-tuple-element.51.refs_1_, bf16[192,768]{1,0:T(8,128)(2,1)S(1)} %collective-permute-done.10.refs_0_.refs_2_, bf16[192,1280]{1,0:T(8,128)(2,1)S(1)} %collective-permute-done.11.refs_3_, ...), custom_call_target="tpu_custom_call" | custom-call | flops 12288 | bytes 61440 | tf_op jit(solution)/shard_map/pallas_call | solution.py:233
  (28 shorter events, 0.5 us)
Async XLA Ops:
  0.6 3.2 %collective-permute-start.1 = (bf16[128,2048]{1,0:T(8,128)(2,1)}, bf16[128,2048]{1,0:T(8,128)(2,1)S(1)}, u32[]{:S(2)}, u32[]{:S(2)}) collective-permute-start(bf16[128,2048]{1,0:T(8,128)(2,1)} %refs_2_.3), channel_id=1, source_target_pairs={{0,1},{1,0},{2,3},{3,2},{4,5},{5,4},{6,7},{7,6},{8,9},{9,8},{10,11... | collective-permute-start | bytes 1572872 | tf_op jit(solution)/shard_map/ppermute | solution.py:402
  1.1 0.7 copy-start.4
  1.8 0.7 copy-start.5
  2.6 1.2 %collective-permute-start = (bf16[16,128]{1,0:T(8,128)(2,1)S(1)}, bf16[16,128]{1,0:T(8,128)(2,1)S(1)}, u32[]{:S(2)}, u32[]{:S(2)}) collective-permute-start(bf16[16,128]{1,0:T(8,128)(2,1)S(1)} %shard_map.94.refs_0_.meta_ref), channel_id=1, source_target_pairs={{0,1},{1,0},{2,3},{3,2},{4,5},{5,4},{6,7},{7,6},{8,9},{9,8},{10,11... | collective-permute-start | bytes 12296 | tf_op jit(solution)/shard_map/ppermute | solution.py:402
  3.8 1.0 %copy-start.1 = (bf16[128,2048]{1,0:T(8,128)(2,1)S(1)}, bf16[128,2048]{1,0:T(8,128)(2,1)}, u32[]{:S(2)}) copy-start(bf16[128,2048]{1,0:T(8,128)(2,1)} %refs_2_.3) | copy-start | bytes 1572868
  4.8 30.0 %copy-start.2 = (bf16[1,1,8,48,768]{4,3,2,1,0:T(8,128)(2,1)S(1)}, bf16[1,1,8,48,768]{4,3,2,1,0:T(8,128)(2,1)}, u32[]{:S(2)}) copy-start(bf16[1,1,8,48,768]{4,3,2,1,0:T(8,128)(2,1)} %param.9) | copy-start | bytes 1769476
  4.8 30.0 %copy-start.3 = (bf16[1,1,8,48,768]{4,3,2,1,0:T(8,128)(2,1)S(1)}, bf16[1,1,8,48,768]{4,3,2,1,0:T(8,128)(2,1)}, u32[]{:S(2)}) copy-start(bf16[1,1,8,48,768]{4,3,2,1,0:T(8,128)(2,1)} %param.10) | copy-start | bytes 1769476
  5.2 28.5 %collective-permute-start.3 = (bf16[192,768]{1,0:T(8,128)(2,1)S(1)}, bf16[192,768]{1,0:T(8,128)(2,1)S(1)}, u32[]{:S(2)}, u32[]{:S(2)}) collective-permute-start(bf16[192,768]{1,0:T(8,128)(2,1)S(1)} %get-tuple-element.32), channel_id=1, source_target_pairs={{0,4},{1,7},{2,6},{3,5},{4,0},{5,3},{6,2},{7,1},{8,12},{9,15},{10,... | collective-permute-start | bytes 884744 | tf_op jit(solution)/shard_map/ppermute | solution.py:408
  9.0 10.3 %collective-permute-start.2 = (bf16[96,768]{1,0:T(8,128)(2,1)S(1)}, bf16[96,768]{1,0:T(8,128)(2,1)S(1)}, u32[]{:S(2)}, u32[]{:S(2)}) collective-permute-start(bf16[96,768]{1,0:T(8,128)(2,1)S(1)} %get-tuple-element.31), channel_id=1, source_target_pairs={{0,2},{1,3},{2,0},{3,1},{4,6},{5,7},{6,4},{7,5},{8,10},{9,11},{10,... | collective-permute-start | bytes 442376 | tf_op jit(solution)/shard_map/ppermute | solution.py:402
  11.0 34.8 %collective-permute-start.6 = (bf16[192,1280]{1,0:T(8,128)(2,1)S(1)}, bf16[192,1280]{1,0:T(8,128)(2,1)S(1)}, u32[]{:S(2)}, u32[]{:S(2)}) collective-permute-start(bf16[192,1280]{1,0:T(8,128)(2,1)S(1)} %get-tuple-element.36), channel_id=1, source_target_pairs={{0,4},{1,7},{2,6},{3,5},{4,0},{5,3},{6,2},{7,1},{8,12},{9,15},{10,... | collective-permute-start | bytes 1474568 | tf_op jit(solution)/shard_map/ppermute | solution.py:408
  33.7 2.2 %collective-permute-start.4 = (bf16[192,768]{1,0:T(8,128)(2,1)S(1)}, bf16[192,768]{1,0:T(8,128)(2,1)S(1)}, u32[]{:S(2)}, u32[]{:S(2)}) collective-permute-start(bf16[192,768]{1,0:T(8,128)(2,1)S(1)} %shard_map.96.refs_2_), channel_id=1, source_target_pairs={{0,1},{1,0},{2,3},{3,2},{4,5},{5,4},{6,7},{7,6},{8,9},{9,8},{10,11... | collective-permute-start | bytes 884744 | tf_op jit(solution)/shard_map/ppermute | solution.py:402
  33.7 12.1 %collective-permute-start.5 = (bf16[96,1280]{1,0:T(8,128)(2,1)S(1)}, bf16[96,1280]{1,0:T(8,128)(2,1)S(1)}, u32[]{:S(2)}, u32[]{:S(2)}) collective-permute-start(bf16[96,1280]{1,0:T(8,128)(2,1)S(1)} %get-tuple-element.35), channel_id=1, source_target_pairs={{0,2},{1,3},{2,0},{3,1},{4,6},{5,7},{6,4},{7,5},{8,10},{9,11},{10,... | collective-permute-start | bytes 737288 | tf_op jit(solution)/shard_map/ppermute | solution.py:402
  35.9 9.9 %copy-start = (bf16[1,768,2048]{2,1,0:T(8,128)(2,1)S(1)}, bf16[1,768,2048]{2,1,0:T(8,128)(2,1)}, u32[]{:S(2)}) copy-start(bf16[1,768,2048]{2,1,0:T(8,128)(2,1)} %param.11) | copy-start | bytes 9437188
  36.7 10.3 %collective-permute-start.8 = (bf16[384,768]{1,0:T(8,128)(2,1)S(1)}, bf16[384,768]{1,0:T(8,128)(2,1)S(1)}, u32[]{:S(2)}, u32[]{:S(2)}) collective-permute-start(bf16[384,768]{1,0:T(8,128)(2,1)S(1)} %get-tuple-element.39), channel_id=1, source_target_pairs={{0,8},{1,17},{2,10},{3,19},{4,12},{5,21},{6,14},{7,23},{8,0},{9,25... | collective-permute-start | bytes 1769480 | tf_op jit(solution)/shard_map/ppermute | solution.py:418
  45.8 1.9 %collective-permute-start.7 = (bf16[192,1280]{1,0:T(8,128)(2,1)S(1)}, bf16[192,1280]{1,0:T(8,128)(2,1)S(1)}, u32[]{:S(2)}, u32[]{:S(2)}) collective-permute-start(bf16[192,1280]{1,0:T(8,128)(2,1)S(1)} %shard_map.100.refs_2_), channel_id=1, source_target_pairs={{0,1},{1,0},{2,3},{3,2},{4,5},{5,4},{6,7},{7,6},{8,9},{9,8},{10,11... | collective-permute-start | bytes 1474568 | tf_op jit(solution)/shard_map/ppermute | solution.py:402
  48.9 17.3 %collective-permute-start.9 = (bf16[384,1280]{1,0:T(8,128)(2,1)S(1)}, bf16[384,1280]{1,0:T(8,128)(2,1)S(1)}, u32[]{:S(2)}, u32[]{:S(2)}) collective-permute-start(bf16[384,1280]{1,0:T(8,128)(2,1)S(1)} %get-tuple-element.49), channel_id=1, source_target_pairs={{0,8},{1,17},{2,10},{3,19},{4,12},{5,21},{6,14},{7,23},{8,0},{9,25... | collective-permute-start | bytes 2949128 | tf_op jit(solution)/shard_map/ppermute | solution.py:418
  50.7 9.9 %collective-permute-start.10 = (bf16[192,768]{1,0:T(8,128)(2,1)S(1)}, bf16[192,768]{1,0:T(8,128)(2,1)S(1)}, u32[]{:S(2)}, u32[]{:S(2)}) collective-permute-start(bf16[192,768]{1,0:T(8,128)(2,1)S(1)} %get-tuple-element.50), channel_id=1, source_target_pairs={{0,16},{1,9},{2,18},{3,11},{4,20},{5,13},{6,22},{7,15},{8,24},{9,1... | collective-permute-start | bytes 884744 | tf_op jit(solution)/shard_map/ppermute | solution.py:418
  66.4 14.3 %collective-permute-start.11 = (bf16[192,1280]{1,0:T(8,128)(2,1)S(1)}, bf16[192,1280]{1,0:T(8,128)(2,1)S(1)}, u32[]{:S(2)}, u32[]{:S(2)}) collective-permute-start(bf16[192,1280]{1,0:T(8,128)(2,1)S(1)} %get-tuple-element.52), channel_id=1, source_target_pairs={{0,16},{1,9},{2,18},{3,11},{4,20},{5,13},{6,22},{7,15},{8,24},{9,1... | collective-permute-start | bytes 1474568 | tf_op jit(solution)/shard_map/ppermute | solution.py:418
  70.5 1.2 %collective-permute-start.12 = (f32[8,128]{1,0:T(8,128)S(1)}, f32[8,128]{1,0:T(8,128)S(1)}, u32[]{:S(2)}, u32[]{:S(2)}) collective-permute-start(f32[8,128]{1,0:T(8,128)S(1)} %get-tuple-element.53), channel_id=1, source_target_pairs={{0,1},{1,0},{2,3},{3,2},{4,5},{5,4},{6,7},{7,6},{8,9},{9,8},{10,11... | collective-permute-start | bytes 12296 | tf_op jit(solution)/shard_map/ppermute | solution.py:402
  71.6 3.7 %collective-permute-start.13 = (f32[16,128]{1,0:T(8,128)S(1)}, f32[16,128]{1,0:T(8,128)S(1)}, u32[]{:S(2)}, u32[]{:S(2)}) collective-permute-start(f32[16,128]{1,0:T(8,128)S(1)} %pad_maximum_fusion), channel_id=1, source_target_pairs={{0,2},{1,3},{2,0},{3,1},{4,6},{5,7},{6,4},{7,5},{8,10},{9,11},{10,... | collective-permute-start | bytes 24584 | tf_op jit(solution)/shard_map/ppermute | solution.py:402
  75.3 4.6 %collective-permute-start.14 = (f32[32,128]{1,0:T(8,128)S(1)}, f32[32,128]{1,0:T(8,128)S(1)}, u32[]{:S(2)}, u32[]{:S(2)}) collective-permute-start(f32[32,128]{1,0:T(8,128)S(1)} %constant_dynamic-update-slice_fusion.near_ref), channel_id=1, source_target_pairs={{0,4},{1,5},{2,6},{3,7},{4,0},{5,1},{6,2},{7,3},{8,12},{9,13},{10,... | collective-permute-start | bytes 49160 | tf_op jit(solution)/shard_map/ppermute | solution.py:402

commit v7 on v6

--- a/solution.py
+++ b/solution.py
@@ -9,7 +9,7 @@
 
 LANES = 128
 META = 16
-WIDTHS = (768, 1280)
+WIDTHS = (1280, 768)
 VMEM_LIMIT = 10 * 1024 * 1024
 VMEM = pl.BlockSpec(memory_space=pltpu.VMEM)
 ANY = pl.BlockSpec(memory_space=pl.ANY)
@@ -436,26 +436,28 @@
     held, start = None, 0
     all_rows, owns, arrived = [], [], []
     for chunk, width in enumerate(WIDTHS):
-        earlier = all_rows[chunk - 2 : chunk - 1] if chunk > 1 else []
+        earlier = all_rows[: max(0, chunk - 1)]
         local, near, far = dispatch(metas, near_rows, capacity, top_count, start, width, earlier)
         near = swap(near, 2)
-        far = after(swap_far(far), near, *all_rows[-1:])
+        far = after(swap_far(far), near, *owns[-1:])
         blocks = [local, near, far, swap(far, 1)]
-        earlier = [] if held is None else [held, own]
+        earlier = [] if held is None else [held, *arrived]
         rows, own, later, half = panel_parts(turned, blocks, capacity, earlier)
         all_rows.append(rows)
-        own, half = halve(own, later, swap_groups(half, False), arrived[-1:])
-        owns.append(own)
-        arrived.append(swap_groups(half, True))
+        earlier = arrived[-1:]
         if chunk + 1 < len(WIDTHS):
             held = grad_hidden_step(held, rows, weight, start)
         else:
             grad_gate, grad_up, lines = grad_hidden_last(
                 held, rows, weight, start, hidden, up_scale, gate_scale, capacity
             )
+            for offset in (1, 2):
+                lines = jnp.concatenate([lines, swap(lines, offset)], axis=0)
+            earlier = earlier + [lines]
+        own, half = halve(own, later, swap_groups(half, False), earlier)
+        owns.append(own)
+        arrived.append(swap_groups(half, True))
         start += width
-    for offset in (1, 2):
-        lines = jnp.concatenate([lines, swap(lines, offset)], axis=0)
     far_lines = swap(lines, 4)
     panel = total(owns, arrived, [far_lines])
     route_grad = route_back(meta, lines, far_lines, expert_count, top_count, capacity)

time: 82.1 us -> 77.2 us (0.940)
  starting transfers between devices: 16 us -> 12.6 us
  waiting for transfers between devices: 52.5 us -> 50.7 us
    ppermute x2, waiting for transfers between devices: 14.4 us -> 5.8 us  [swap_far(): return lax.ppermute(value, 'expert', pairs)]
    ppermute x9, waiting for transfers between devices: 24.1 us -> 31.3 us  [swap(): lax.ppermute(value, 'expert', [(place, place ^ offset) for place in range...]
    ppermute x9, starting transfers between devices: 5.77 us -> 2.47 us  [swap(): lax.ppermute(value, 'expert', [(place, place ^ offset) for place in range...]
    unnamed x14 -> x16, local copies, waits for them, and re-layouts: 2.39 us -> 2.4 us
  transfers between devices with their start and end apart: 15 -> 15, of which waited for: 10 -> 12; matrix products, arithmetic and copies ran while one was open for 0% -> 0% of each run, Pallas kernels for 9% -> 9%
where the time goes in v7:
time: 77.2 us; the launch traced here: 77 us
  waiting for transfers between devices  50.7 us (66%)
  starting transfers between devices  12.6 us (16%)
  Pallas kernels  10.5 us (14%)
  local copies, waits for them, and re-layouts  2.4 us (3%)
    ppermute x9, waiting for transfers between devices, swap(): lax.ppermute(value, 'expert', [(place, place ^ offset) for place in range...  31.3 us
    ppermute x4, waiting for transfers between devices, swap_groups(): return lax.ppermute(value, ('dp', 'expert'), pairs)  13.6 us
    ppermute x4, starting transfers between devices, swap_groups(): return lax.ppermute(value, ('dp', 'expert'), pairs)  6.28 us
    ppermute x2, waiting for transfers between devices, swap_far(): return lax.ppermute(value, 'expert', pairs)  5.8 us
    ppermute x2, starting transfers between devices, swap_far(): return lax.ppermute(value, 'expert', pairs)  3.89 us
    pallas_call x1, Pallas kernels, grad_hidden_last(): pl.pallas_call(functools.partial(last_kernel, capacity, start), grid=(hid...  2.78 us
    ppermute x9, starting transfers between devices, swap(): lax.ppermute(value, 'expert', [(place, place ^ offset) for place in range...  2.47 us
    unnamed x16, local copies, waits for them, and re-layouts  2.4 us
  transfers between devices with their start and end apart: 15, of which 12 were waited for; matrix products, arithmetic and copies ran while one was open for 0% of the time, Pallas kernels for 9%

profile of v7, /device:TPU:0, one launch (start us, length us, event | category | flops | bytes accessed | tf_op | source)
XLA Modules:
  0.0 77.0 jit_solution(7787323961412305260)
XLA Ops:
  0.6 0.5 collective-permute-start.1
  1.2 0.7 copy-done.5
  1.8 0.7 copy-done.6
  2.7 1.1 %collective-permute-done.refs_1_ = bf16[16,128]{1,0:T(8,128)(2,1)S(1)} collective-permute-done((bf16[16,128]{1,0:T(8,128)(2,1)S(1)}, bf16[16,128]{1,0:T(8,128)(2,1)S(1)}, u32[]{:S(2)}, u32[]{:S(2)}) %collective-permute-start) | collective-permute-done | bytes 4128 | tf_op jit(solution)/shard_map/ppermute | solution.py:402
  3.8 1.0 %copy-done.1 = bf16[128,2048]{1,0:T(8,128)(2,1)S(1)} copy-done((bf16[128,2048]{1,0:T(8,128)(2,1)S(1)}, bf16[128,2048]{1,0:T(8,128)(2,1)}, u32[]{:S(2)}) %copy-start.1) | copy-done | bytes 524312
  4.8 0.4 shard_map.95
  5.3 3.8 %collective-permute-start.3 = (bf16[192,1280]{1,0:T(8,128)(2,1)S(1)}, bf16[192,1280]{1,0:T(8,128)(2,1)S(1)}, u32[]{:S(2)}, u32[]{:S(2)}) collective-permute-start(bf16[192,1280]{1,0:T(8,128)(2,1)S(1)} %get-tuple-element.32), channel_id=1, source_target_pairs={{0,4},{1,7},{2,6},{3,5},{4,0},{5,3},{6,2},{7,1},{8,12},{9,15},{10,... | collective-permute-start | bytes 1474568 | tf_op jit(solution)/shard_map/ppermute | solution.py:408
  9.1 1.6 %collective-permute-start.2 = (bf16[96,1280]{1,0:T(8,128)(2,1)S(1)}, bf16[96,1280]{1,0:T(8,128)(2,1)S(1)}, u32[]{:S(2)}, u32[]{:S(2)}) collective-permute-start(bf16[96,1280]{1,0:T(8,128)(2,1)S(1)} %get-tuple-element.31), channel_id=1, source_target_pairs={{0,2},{1,3},{2,0},{3,1},{4,6},{5,7},{6,4},{7,5},{8,10},{9,11},{10,... | collective-permute-start | bytes 737288 | tf_op jit(solution)/shard_map/ppermute | solution.py:402
  10.6 15.1 %collective-permute-done.2.refs_1_ = bf16[96,1280]{1,0:T(8,128)(2,1)S(1)} collective-permute-done((bf16[96,1280]{1,0:T(8,128)(2,1)S(1)}, bf16[96,1280]{1,0:T(8,128)(2,1)S(1)}, u32[]{:S(2)}, u32[]{:S(2)}) %collective-permute-start.2) | collective-permute-done | bytes 245792 | tf_op jit(solution)/shard_map/ppermute | solution.py:402
  25.7 5.8 %collective-permute-done.3.refs_0_ = bf16[192,1280]{1,0:T(8,128)(2,1)S(1)} collective-permute-done((bf16[192,1280]{1,0:T(8,128)(2,1)S(1)}, bf16[192,1280]{1,0:T(8,128)(2,1)S(1)}, u32[]{:S(2)}, u32[]{:S(2)}) %collective-permute-start.3) | collective-permute-done | bytes 491552 | tf_op jit(solution)/shard_map/ppermute | solution.py:408
  31.5 1.0 %shard_map.93 = (bf16[768,384]{1,0:T(8,128)(2,1)S(1)}, bf16[384,768]{1,0:T(8,128)(2,1)S(1)}, f32[384,768]{1,0:T(8,128)S(1)}, f32[384,768]{1,0:T(8,128)S(1)}) custom-call(bf16[384,768]{1,0:T(8,128)(2,1)S(1)} %bitcast.11, bf16[384,768]{1,0:T(8,128)(2,1)S(1)} %bitcast.12), custom_call_target="tpu_custom_call" | custom-call | flops 92160 | bytes 73728 | tf_op jit(solution)/shard_map/pallas_call | solution.py:125
  32.5 0.8 %collective-permute-done.4.refs_3_ = bf16[192,1280]{1,0:T(8,128)(2,1)S(1)} collective-permute-done((bf16[192,1280]{1,0:T(8,128)(2,1)S(1)}, bf16[192,1280]{1,0:T(8,128)(2,1)S(1)}, u32[]{:S(2)}, u32[]{:S(2)}) %collective-permute-start.4) | collective-permute-done | bytes 491552 | tf_op jit(solution)/shard_map/ppermute | solution.py:402
  33.4 1.3 %shard_map.97 = (bf16[384,1280]{1,0:T(8,128)(2,1)S(1)}, f32[192,1280]{1,0:T(8,128)S(1)}, f32[192,1280]{1,0:T(8,128)S(1)}, bf16[384,1280]{1,0:T(8,128)(2,1)S(1)}) custom-call(bf16[768,384]{1,0:T(8,128)(2,1)S(1)} %get-tuple-element.29.turned_ref, bf16[96,1280]{1,0:T(8,128)(2,1)S(1)} %get-tuple-element.30.refs_0_, ...), custom_call_target="tpu_custom_call" | custom-call | flops 11796480 | bytes 39936 | tf_op jit(solution)/shard_map/pallas_call | solution.py:173
  34.6 1.6 %collective-permute-start.7 = (bf16[384,1280]{1,0:T(8,128)(2,1)S(1)}, bf16[384,1280]{1,0:T(8,128)(2,1)S(1)}, u32[]{:S(2)}, u32[]{:S(2)}) collective-permute-start(bf16[384,1280]{1,0:T(8,128)(2,1)S(1)} %get-tuple-element.39), channel_id=1, source_target_pairs={{0,8},{1,17},{2,10},{3,19},{4,12},{5,21},{6,14},{7,23},{8,0},{9,25... | collective-permute-start | bytes 2949128 | tf_op jit(solution)/shard_map/ppermute | solution.py:418
  36.2 0.3 shard_map.99
  36.6 12.2 %collective-permute-done.7.arrived_ref = bf16[384,1280]{1,0:T(8,128)(2,1)S(1)} collective-permute-done((bf16[384,1280]{1,0:T(8,128)(2,1)S(1)}, bf16[384,1280]{1,0:T(8,128)(2,1)S(1)}, u32[]{:S(2)}, u32[]{:S(2)}) %collective-permute-start.7) | collective-permute-done | bytes 983072 | tf_op jit(solution)/shard_map/ppermute | solution.py:418
  48.8 0.2 shard_map.100
  49.0 1.6 %collective-permute-start.9 = (bf16[192,1280]{1,0:T(8,128)(2,1)S(1)}, bf16[192,1280]{1,0:T(8,128)(2,1)S(1)}, u32[]{:S(2)}, u32[]{:S(2)}) collective-permute-start(bf16[192,1280]{1,0:T(8,128)(2,1)S(1)} %get-tuple-element.41), channel_id=1, source_target_pairs={{0,16},{1,9},{2,18},{3,11},{4,20},{5,13},{6,22},{7,15},{8,24},{9,1... | collective-permute-start | bytes 1474568 | tf_op jit(solution)/shard_map/ppermute | solution.py:418
  50.6 5.1 %collective-permute-done.5.refs_1_ = bf16[96,768]{1,0:T(8,128)(2,1)S(1)} collective-permute-done((bf16[96,768]{1,0:T(8,128)(2,1)S(1)}, bf16[96,768]{1,0:T(8,128)(2,1)S(1)}, u32[]{:S(2)}, u32[]{:S(2)}) %collective-permute-start.5) | collective-permute-done | bytes 147488 | tf_op jit(solution)/shard_map/ppermute | solution.py:402
  55.7 1.5 %shard_map.98.refs_4_.held_ref = f32[384,768]{1,0:T(8,128)S(1)} custom-call(bf16[384,1280]{1,0:T(8,128)(2,1)S(1)} %get-tuple-element.33.rows_ref, bf16[768,2048]{1,0:T(8,128)(2,1)S(1)} %bitcast.9), custom_call_target="tpu_custom_call" | custom-call | flops 11796480 | bytes 36864 | tf_op jit(solution)/shard_map/pallas_call | solution.py:271
  57.3 0.6 collective-permute-done.9.refs_5_.refs_0_.refs_2_
  57.9 0.8 %shard_map.102 = (bf16[384,768]{1,0:T(8,128)(2,1)S(1)}, f32[192,768]{1,0:T(8,128)S(1)}, f32[192,768]{1,0:T(8,128)S(1)}, bf16[384,768]{1,0:T(8,128)(2,1)S(1)}) custom-call(bf16[768,384]{1,0:T(8,128)(2,1)S(1)} %get-tuple-element.29.turned_ref, bf16[96,768]{1,0:T(8,128)(2,1)S(1)} %get-tuple-element.34.refs_0_, ...), custom_call_target="tpu_custom_call" | custom-call | flops 7077888 | bytes 27648 | tf_op jit(solution)/shard_map/pallas_call | solution.py:173
  58.7 1.6 %collective-permute-start.10 = (bf16[384,768]{1,0:T(8,128)(2,1)S(1)}, bf16[384,768]{1,0:T(8,128)(2,1)S(1)}, u32[]{:S(2)}, u32[]{:S(2)}) collective-permute-start(bf16[384,768]{1,0:T(8,128)(2,1)S(1)} %get-tuple-element.50), channel_id=1, source_target_pairs={{0,8},{1,17},{2,10},{3,19},{4,12},{5,21},{6,14},{7,23},{8,0},{9,25... | collective-permute-start | bytes 1769480 | tf_op jit(solution)/shard_map/ppermute | solution.py:418
  60.3 2.8 %shard_map.103 = (bf16[384,768]{1,0:T(8,128)(2,1)}, bf16[384,768]{1,0:T(8,128)(2,1)}, f32[8,128]{1,0:T(8,128)S(1)}) custom-call(f32[384,768]{1,0:T(8,128)S(1)} %shard_map.98.refs_4_.held_ref, bf16[384,768]{1,0:T(8,128)(2,1)S(1)} %get-tuple-element.42.rows_ref, bf16[768,2048]{1,0:T(8,128)(2,1)S(1)} %bitcast.10, ...), custom_call_target="tpu_custom_call" | custom-call | flops 7077888 | bytes 55296 | tf_op jit(solution)/shard_map/pallas_call | solution.py:329
  63.0 1.2 %collective-permute-done.11 = f32[8,128]{1,0:T(8,128)S(1)} collective-permute-done((f32[8,128]{1,0:T(8,128)S(1)}, f32[8,128]{1,0:T(8,128)S(1)}, u32[]{:S(2)}, u32[]{:S(2)}) %collective-permute-start.11) | collective-permute-done | bytes 4128 | tf_op jit(solution)/shard_map/ppermute | solution.py:402
  64.2 3.6 %collective-permute-done.12 = f32[16,128]{1,0:T(8,128)S(1)} collective-permute-done((f32[16,128]{1,0:T(8,128)S(1)}, f32[16,128]{1,0:T(8,128)S(1)}, u32[]{:S(2)}, u32[]{:S(2)}) %collective-permute-start.12) | collective-permute-done | bytes 8224 | tf_op jit(solution)/shard_map/ppermute | solution.py:402
  67.9 0.8 %collective-permute-done.10.arrived_ref = bf16[384,768]{1,0:T(8,128)(2,1)S(1)} collective-permute-done((bf16[384,768]{1,0:T(8,128)(2,1)S(1)}, bf16[384,768]{1,0:T(8,128)(2,1)S(1)}, u32[]{:S(2)}, u32[]{:S(2)}) %collective-permute-start.10) | collective-permute-done | bytes 589856 | tf_op jit(solution)/shard_map/ppermute | solution.py:418
  68.8 1.6 %collective-permute-start.13 = (bf16[192,768]{1,0:T(8,128)(2,1)S(1)}, bf16[192,768]{1,0:T(8,128)(2,1)S(1)}, u32[]{:S(2)}, u32[]{:S(2)}) collective-permute-start(bf16[192,768]{1,0:T(8,128)(2,1)S(1)} %get-tuple-element.53), channel_id=1, source_target_pairs={{0,16},{1,9},{2,18},{3,11},{4,20},{5,13},{6,22},{7,15},{8,24},{9,1... | collective-permute-start | bytes 884744 | tf_op jit(solution)/shard_map/ppermute | solution.py:418
  70.3 0.3 collective-permute-start.14
  70.6 4.3 %collective-permute-done.14.refs_4_.far_ref = f32[32,128]{1,0:T(8,128)S(1)} collective-permute-done((f32[32,128]{1,0:T(8,128)S(1)}, f32[32,128]{1,0:T(8,128)S(1)}, u32[]{:S(2)}, u32[]{:S(2)}) %collective-permute-start.14) | collective-permute-done | bytes 16416 | tf_op jit(solution)/shard_map/ppermute | solution.py:402
  75.0 0.8 %shard_map.106 = f32[2,128]{1,0:T(2,128)} custom-call(bf16[16,128]{1,0:T(8,128)(2,1)S(1)} %shard_map.94.refs_0_.meta_ref, f32[32,128]{1,0:T(8,128)S(1)} %constant_dynamic-update-slice_fusion.refs_1_.near_ref, f32[32,128]{1,0:T(8,128)S(1)} %collective-permute-done.14.refs_4_.far_ref), custom_call_target="tpu_custom_call" | custom-call | flops 15625 | bytes 1562 | tf_op jit(solution)/shard_map/pallas_call | solution.py:374
  75.8 1.2 %shard_map.105 = f32[192,2048]{1,0:T(8,128)} custom-call(f32[192,1280]{1,0:T(8,128)S(1)} %get-tuple-element.40.refs_2_.refs_0_, f32[192,768]{1,0:T(8,128)S(1)} %get-tuple-element.52.refs_1_, bf16[192,1280]{1,0:T(8,128)(2,1)S(1)} %collective-permute-done.9.refs_5_.refs_0_.refs_2_, bf16[192,768]{1,0:T(8,128)(2,1)S(1)} %collective-permute-done.13.refs_3_, ...), custom_call_target="tpu_custom_call" | custom-call | flops 12288 | bytes 61440 | tf_op jit(solution)/shard_map/pallas_call | solution.py:233
  (30 shorter events, 0.5 us)
Async XLA Ops:
  0.6 3.2 %collective-permute-start.1 = (bf16[128,2048]{1,0:T(8,128)(2,1)}, bf16[128,2048]{1,0:T(8,128)(2,1)S(1)}, u32[]{:S(2)}, u32[]{:S(2)}) collective-permute-start(bf16[128,2048]{1,0:T(8,128)(2,1)} %refs_2_.3), channel_id=1, source_target_pairs={{0,1},{1,0},{2,3},{3,2},{4,5},{5,4},{6,7},{7,6},{8,9},{9,8},{10,11... | collective-permute-start | bytes 1572872 | tf_op jit(solution)/shard_map/ppermute | solution.py:402
  1.1 0.7 copy-start.5
  1.8 0.7 copy-start.6
  2.6 1.2 %collective-permute-start = (bf16[16,128]{1,0:T(8,128)(2,1)S(1)}, bf16[16,128]{1,0:T(8,128)(2,1)S(1)}, u32[]{:S(2)}, u32[]{:S(2)}) collective-permute-start(bf16[16,128]{1,0:T(8,128)(2,1)S(1)} %shard_map.94.refs_0_.meta_ref), channel_id=1, source_target_pairs={{0,1},{1,0},{2,3},{3,2},{4,5},{5,4},{6,7},{7,6},{8,9},{9,8},{10,11... | collective-permute-start | bytes 12296 | tf_op jit(solution)/shard_map/ppermute | solution.py:402
  3.8 1.0 %copy-start.1 = (bf16[128,2048]{1,0:T(8,128)(2,1)S(1)}, bf16[128,2048]{1,0:T(8,128)(2,1)}, u32[]{:S(2)}) copy-start(bf16[128,2048]{1,0:T(8,128)(2,1)} %refs_2_.3) | copy-start | bytes 1572868
  4.8 26.7 %copy-start.3 = (bf16[1,1,8,48,768]{4,3,2,1,0:T(8,128)(2,1)S(1)}, bf16[1,1,8,48,768]{4,3,2,1,0:T(8,128)(2,1)}, u32[]{:S(2)}) copy-start(bf16[1,1,8,48,768]{4,3,2,1,0:T(8,128)(2,1)} %param.9) | copy-start | bytes 1769476
  4.8 26.7 %copy-start.4 = (bf16[1,1,8,48,768]{4,3,2,1,0:T(8,128)(2,1)S(1)}, bf16[1,1,8,48,768]{4,3,2,1,0:T(8,128)(2,1)}, u32[]{:S(2)}) copy-start(bf16[1,1,8,48,768]{4,3,2,1,0:T(8,128)(2,1)} %param.10) | copy-start | bytes 1769476
  5.3 26.2 %collective-permute-start.3 = (bf16[192,1280]{1,0:T(8,128)(2,1)S(1)}, bf16[192,1280]{1,0:T(8,128)(2,1)S(1)}, u32[]{:S(2)}, u32[]{:S(2)}) collective-permute-start(bf16[192,1280]{1,0:T(8,128)(2,1)S(1)} %get-tuple-element.32), channel_id=1, source_target_pairs={{0,4},{1,7},{2,6},{3,5},{4,0},{5,3},{6,2},{7,1},{8,12},{9,15},{10,... | collective-permute-start | bytes 1474568 | tf_op jit(solution)/shard_map/ppermute | solution.py:408
  9.1 16.6 %collective-permute-start.2 = (bf16[96,1280]{1,0:T(8,128)(2,1)S(1)}, bf16[96,1280]{1,0:T(8,128)(2,1)S(1)}, u32[]{:S(2)}, u32[]{:S(2)}) collective-permute-start(bf16[96,1280]{1,0:T(8,128)(2,1)S(1)} %get-tuple-element.31), channel_id=1, source_target_pairs={{0,2},{1,3},{2,0},{3,1},{4,6},{5,7},{6,4},{7,5},{8,10},{9,11},{10,... | collective-permute-start | bytes 737288 | tf_op jit(solution)/shard_map/ppermute | solution.py:402
  31.5 1.9 %collective-permute-start.4 = (bf16[192,1280]{1,0:T(8,128)(2,1)S(1)}, bf16[192,1280]{1,0:T(8,128)(2,1)S(1)}, u32[]{:S(2)}, u32[]{:S(2)}) collective-permute-start(bf16[192,1280]{1,0:T(8,128)(2,1)S(1)} %shard_map.96.refs_2_), channel_id=1, source_target_pairs={{0,1},{1,0},{2,3},{3,2},{4,5},{5,4},{6,7},{7,6},{8,9},{9,8},{10,11... | collective-permute-start | bytes 1474568 | tf_op jit(solution)/shard_map/ppermute | solution.py:402
  32.5 3.7 %copy-start.2 = (bf16[128,2048]{1,0:T(8,128)(2,1)S(1)}, bf16[128,2048]{1,0:T(8,128)(2,1)}, u32[]{:S(2)}) copy-start(bf16[128,2048]{1,0:T(8,128)(2,1)} %refs_2_.3) | copy-start | bytes 1572868
  34.6 14.2 %collective-permute-start.7 = (bf16[384,1280]{1,0:T(8,128)(2,1)S(1)}, bf16[384,1280]{1,0:T(8,128)(2,1)S(1)}, u32[]{:S(2)}, u32[]{:S(2)}) collective-permute-start(bf16[384,1280]{1,0:T(8,128)(2,1)S(1)} %get-tuple-element.39), channel_id=1, source_target_pairs={{0,8},{1,17},{2,10},{3,19},{4,12},{5,21},{6,14},{7,23},{8,0},{9,25... | collective-permute-start | bytes 2949128 | tf_op jit(solution)/shard_map/ppermute | solution.py:418
  36.5 19.2 %collective-permute-start.6 = (bf16[192,768]{1,0:T(8,128)(2,1)S(1)}, bf16[192,768]{1,0:T(8,128)(2,1)S(1)}, u32[]{:S(2)}, u32[]{:S(2)}) collective-permute-start(bf16[192,768]{1,0:T(8,128)(2,1)S(1)} %get-tuple-element.36), channel_id=1, source_target_pairs={{0,4},{1,7},{2,6},{3,5},{4,0},{5,3},{6,2},{7,1},{8,12},{9,15},{10,... | collective-permute-start | bytes 884744 | tf_op jit(solution)/shard_map/ppermute | solution.py:408
  48.8 6.9 %copy-start = (bf16[1,768,2048]{2,1,0:T(8,128)(2,1)S(1)}, bf16[1,768,2048]{2,1,0:T(8,128)(2,1)}, u32[]{:S(2)}) copy-start(bf16[1,768,2048]{2,1,0:T(8,128)(2,1)} %param.11) | copy-start | bytes 9437188
  49.0 8.9 %collective-permute-start.9 = (bf16[192,1280]{1,0:T(8,128)(2,1)S(1)}, bf16[192,1280]{1,0:T(8,128)(2,1)S(1)}, u32[]{:S(2)}, u32[]{:S(2)}) collective-permute-start(bf16[192,1280]{1,0:T(8,128)(2,1)S(1)} %get-tuple-element.41), channel_id=1, source_target_pairs={{0,16},{1,9},{2,18},{3,11},{4,20},{5,13},{6,22},{7,15},{8,24},{9,1... | collective-permute-start | bytes 1474568 | tf_op jit(solution)/shard_map/ppermute | solution.py:418
  50.6 5.1 %collective-permute-start.5 = (bf16[96,768]{1,0:T(8,128)(2,1)S(1)}, bf16[96,768]{1,0:T(8,128)(2,1)S(1)}, u32[]{:S(2)}, u32[]{:S(2)}) collective-permute-start(bf16[96,768]{1,0:T(8,128)(2,1)S(1)} %get-tuple-element.35), channel_id=1, source_target_pairs={{0,2},{1,3},{2,0},{3,1},{4,6},{5,7},{6,4},{7,5},{8,10},{9,11},{10,... | collective-permute-start | bytes 442376 | tf_op jit(solution)/shard_map/ppermute | solution.py:402
  55.7 1.6 %collective-permute-start.8 = (bf16[192,768]{1,0:T(8,128)(2,1)S(1)}, bf16[192,768]{1,0:T(8,128)(2,1)S(1)}, u32[]{:S(2)}, u32[]{:S(2)}) collective-permute-start(bf16[192,768]{1,0:T(8,128)(2,1)S(1)} %shard_map.101.refs_2_), channel_id=1, source_target_pairs={{0,1},{1,0},{2,3},{3,2},{4,5},{5,4},{6,7},{7,6},{8,9},{9,8},{10,11... | collective-permute-start | bytes 884744 | tf_op jit(solution)/shard_map/ppermute | solution.py:402
  58.7 9.9 %collective-permute-start.10 = (bf16[384,768]{1,0:T(8,128)(2,1)S(1)}, bf16[384,768]{1,0:T(8,128)(2,1)S(1)}, u32[]{:S(2)}, u32[]{:S(2)}) collective-permute-start(bf16[384,768]{1,0:T(8,128)(2,1)S(1)} %get-tuple-element.50), channel_id=1, source_target_pairs={{0,8},{1,17},{2,10},{3,19},{4,12},{5,21},{6,14},{7,23},{8,0},{9,25... | collective-permute-start | bytes 1769480 | tf_op jit(solution)/shard_map/ppermute | solution.py:418
  63.0 1.2 %collective-permute-start.11 = (f32[8,128]{1,0:T(8,128)S(1)}, f32[8,128]{1,0:T(8,128)S(1)}, u32[]{:S(2)}, u32[]{:S(2)}) collective-permute-start(f32[8,128]{1,0:T(8,128)S(1)} %get-tuple-element.51), channel_id=1, source_target_pairs={{0,1},{1,0},{2,3},{3,2},{4,5},{5,4},{6,7},{7,6},{8,9},{9,8},{10,11... | collective-permute-start | bytes 12296 | tf_op jit(solution)/shard_map/ppermute | solution.py:402
  64.2 3.7 %collective-permute-start.12 = (f32[16,128]{1,0:T(8,128)S(1)}, f32[16,128]{1,0:T(8,128)S(1)}, u32[]{:S(2)}, u32[]{:S(2)}) collective-permute-start(f32[16,128]{1,0:T(8,128)S(1)} %pad_maximum_fusion), channel_id=1, source_target_pairs={{0,2},{1,3},{2,0},{3,1},{4,6},{5,7},{6,4},{7,5},{8,10},{9,11},{10,... | collective-permute-start | bytes 24584 | tf_op jit(solution)/shard_map/ppermute | solution.py:402
  68.8 7.0 %collective-permute-start.13 = (bf16[192,768]{1,0:T(8,128)(2,1)S(1)}, bf16[192,768]{1,0:T(8,128)(2,1)S(1)}, u32[]{:S(2)}, u32[]{:S(2)}) collective-permute-start(bf16[192,768]{1,0:T(8,128)(2,1)S(1)} %get-tuple-element.53), channel_id=1, source_target_pairs={{0,16},{1,9},{2,18},{3,11},{4,20},{5,13},{6,22},{7,15},{8,24},{9,1... | collective-permute-start | bytes 884744 | tf_op jit(solution)/shard_map/ppermute | solution.py:418
  70.3 4.6 %collective-permute-start.14 = (f32[32,128]{1,0:T(8,128)S(1)}, f32[32,128]{1,0:T(8,128)S(1)}, u32[]{:S(2)}, u32[]{:S(2)}) collective-permute-start(f32[32,128]{1,0:T(8,128)S(1)} %constant_dynamic-update-slice_fusion.refs_1_.near_ref), channel_id=1, source_target_pairs={{0,4},{1,5},{2,6},{3,7},{4,0},{5,1},{6,2},{7,3},{8,12},{9,13},{10,... | collective-permute-start | bytes 49160 | tf_op jit(solution)/shard_map/ppermute | solution.py:402

commit v8 on v7

--- a/solution.py
+++ b/solution.py
@@ -65,11 +65,11 @@
     return 4 + 2 * lax.bitwise_and(lax.axis_index("expert"), 1)
 
 
-def chosen_rows(meta, top_count, capacity):
+def chosen_rows(meta, top_count, capacity, offsets):
     token_count = meta.shape[1]
     slots = lax.broadcasted_iota(jnp.int32, (capacity, token_count), 0).astype(jnp.float32)
     parts = []
-    for offset in (0, 2, far_offset(), far_offset() + 1):
+    for offset in offsets:
         target = lax.bitwise_xor(lax.axis_index("expert"), offset).astype(jnp.float32)
         part = jnp.zeros((capacity, token_count), jnp.float32)
         for k in range(top_count):
@@ -80,32 +80,40 @@
     return jnp.concatenate(parts, axis=0).astype(jnp.bfloat16)
 
 
-def dispatch_kernel(capacity, top_count, start, *refs):
-    meta_refs, row_refs, (local_ref, near_ref, far_ref) = refs[:2], refs[2:4], refs[-3:]
-    width = local_ref.shape[1]
+def dispatch_kernel(capacity, top_count, start, far, *refs):
+    meta_refs, row_refs, block_refs = refs[:2], refs[2:4], refs[4:]
+    if far:
+        offsets = (far_offset(), far_offset() + 1)
+        block_refs = refs[-1:] * 2
+    else:
+        offsets = (0, 2)
+        block_refs = refs[-2:]
+    width = block_refs[0].shape[1]
     for source in range(2):
+        meta = meta_refs[source][...].astype(jnp.float32)
         rows = jnp.dot(
-            chosen_rows(meta_refs[source][...].astype(jnp.float32), top_count, capacity),
+            chosen_rows(meta, top_count, capacity, offsets),
             row_refs[source][:, start : start + width],
             preferred_element_type=jnp.float32,
         ).astype(jnp.bfloat16)
-        places = [(local_ref, source), (near_ref, source), (far_ref, source), (far_ref, source + 2)]
-        for step, (block_ref, place) in enumerate(places):
+        for step, block_ref in enumerate(block_refs):
+            place = source + (2 * step if far else 0)
             block_ref[place * capacity : (place + 1) * capacity, :] = rows[
                 step * capacity : (step + 1) * capacity, :
             ]
 
 
-def dispatch(metas, rows, capacity, top_count, start, width, earlier):
-    return pl.pallas_call(
-        functools.partial(dispatch_kernel, capacity, top_count, start),
-        in_specs=[VMEM] * 4 + [ANY] * len(earlier),
+def dispatch(metas, rows, capacity, top_count, start, width, far):
+    counts = (4,) if far else (2, 2)
+    return pl.pallas_call(
+        functools.partial(dispatch_kernel, capacity, top_count, start, far),
+        in_specs=[VMEM] * 4,
         out_shape=[
-            jax.ShapeDtypeStruct((count * capacity, width), jnp.bfloat16) for count in (2, 2, 4)
+            jax.ShapeDtypeStruct((count * capacity, width), jnp.bfloat16) for count in counts
         ],
         compiler_params=params(),
-        cost_estimate=cost(16 * capacity * LANES * width, 16 * capacity * width),
-    )(*metas, *rows, *earlier)
+        cost_estimate=cost(8 * capacity * LANES * width, 8 * capacity * width),
+    )(*metas, *rows)
 
 
 def hidden_kernel(gate_ref, up_ref, turned_ref, hidden_ref, up_scale_ref, gate_scale_ref):
@@ -138,19 +146,20 @@
     )(gate, up)
 
 
-def panel_kernel(capacity, turned_ref, *refs):
+def panel_kernel(capacity, start, turned_ref, *refs):
     block_refs, (rows_ref, own_ref, later_ref, sent_ref) = refs[:4], refs[-4:]
-    share = own_ref.shape[0]
+    share, width = own_ref.shape
     device = lax.axis_index("expert")
     far = far_offset()
     offsets = ((0, 1), (2, 3), (far, far + 1), (11 - far, 10 - far))
     for block, block_ref in enumerate(block_refs):
         first = 2 * capacity if block == 3 else 0
+        column = start if block < 2 else 0
         for half in range(2):
             place = lax.bitwise_xor(device, offsets[block][half])
             row = pl.multiple_of(place * capacity, capacity)
             rows_ref[pl.ds(row, capacity), :] = block_ref[
-                first + half * capacity : first + (half + 1) * capacity, :
+                first + half * capacity : first + (half + 1) * capacity, column : column + width
             ]
     rows = rows_ref[...]
 
@@ -166,12 +175,12 @@
     own_ref[...] = part(0)
 
 
-def panel_parts(turned, blocks, capacity, earlier):
+def panel_parts(turned, blocks, capacity, start, earlier):
     hidden_width, row_count = turned.shape
-    width = blocks[0].shape[1]
+    width = blocks[-1].shape[1]
     share = hidden_width // 4
     return pl.pallas_call(
-        functools.partial(panel_kernel, capacity),
+        functools.partial(panel_kernel, capacity, start),
         in_specs=[VMEM] * 5 + [ANY] * len(earlier),
         out_shape=[
             jax.ShapeDtypeStruct((row_count, width), jnp.bfloat16),
@@ -280,23 +289,11 @@
 
 
 def last_kernel(
-    capacity,
-    start,
-    held_ref,
-    rows_ref,
-    weight_ref,
-    hidden_ref,
-    up_scale_ref,
-    gate_scale_ref,
-    grad_gate_ref,
-    grad_up_ref,
-    slot_ref,
-    sum_ref,
+    capacity, start, held_ref, rows_ref, weight_ref, hidden_ref, grad_ref, slot_ref, sum_ref
 ):
     grid_place = pl.program_id(0)
     grad_hidden = held_ref[...] + rows_times_weight(start, rows_ref, weight_ref)
-    grad_up_ref[...] = (grad_hidden * up_scale_ref[...]).astype(jnp.bfloat16)
-    grad_gate_ref[...] = (grad_hidden * gate_scale_ref[...]).astype(jnp.bfloat16)
+    grad_ref[...] = grad_hidden
     product = hidden_ref[...].astype(jnp.float32) * grad_hidden
     folded = product[:, :LANES]
     for column in range(LANES, product.shape[1], LANES):
@@ -320,7 +317,7 @@
             ]
 
 
-def grad_hidden_last(held, rows, weight, start, hidden, up_scale, gate_scale, capacity):
+def grad_hidden_last(held, rows, weight, start, hidden, capacity):
     row_count, width = rows.shape
     hidden_width = weight.shape[0]
     step = 2 * LANES
@@ -334,16 +331,37 @@
             pl.BlockSpec((row_count, width), lambda i: (0, 0)),
             pl.BlockSpec((step, weight.shape[1]), lambda i: (i, 0)),
             block,
-            block,
-            block,
         ],
-        out_specs=[block, block, pl.BlockSpec((expert_count, LANES), lambda i: (0, 0))],
-        out_shape=[jax.ShapeDtypeStruct((row_count, hidden_width), jnp.bfloat16)] * 2
-        + [jax.ShapeDtypeStruct((expert_count, LANES), jnp.float32)],
+        out_specs=[block, pl.BlockSpec((expert_count, LANES), lambda i: (0, 0))],
+        out_shape=[
+            jax.ShapeDtypeStruct((row_count, hidden_width), jnp.float32),
+            jax.ShapeDtypeStruct((expert_count, LANES), jnp.float32),
+        ],
         scratch_shapes=[pltpu.VMEM((row_count, LANES), jnp.float32)],
         compiler_params=params(),
         cost_estimate=cost(2 * row_count * hidden_width * width, 12 * row_count * hidden_width),
-    )(held, rows, weight, hidden, up_scale, gate_scale)
+    )(held, rows, weight, hidden)
+
+
+def scale_kernel(grad_ref, up_scale_ref, gate_scale_ref, *refs):
+    grad_gate_ref, grad_up_ref = refs[-2:]
+    grad_up_ref[...] = (grad_ref[...] * up_scale_ref[...]).astype(jnp.bfloat16)
+    grad_gate_ref[...] = (grad_ref[...] * gate_scale_ref[...]).astype(jnp.bfloat16)
+
+
+def scaled_grads(grad_hidden, up_scale, gate_scale, earlier):
+    row_count, hidden_width = grad_hidden.shape
+    step = 2 * LANES
+    block = pl.BlockSpec((row_count, step), lambda i: (0, i))
+    return pl.pallas_call(
+        scale_kernel,
+        grid=(hidden_width // step,),
+        in_specs=[block] * 3 + [ANY] * len(earlier),
+        out_specs=[block, block],
+        out_shape=[jax.ShapeDtypeStruct((row_count, hidden_width), jnp.bfloat16)] * 2,
+        compiler_params=params(),
+        cost_estimate=cost(2 * row_count * hidden_width, 16 * row_count * hidden_width),
+    )(grad_hidden, up_scale, gate_scale, *earlier)
 
 
 def route_kernel(capacity, meta_ref, near_ref, far_ref, out_ref, table_ref):
@@ -434,25 +452,25 @@
         saved_gate.reshape(row_count, hidden_width), saved_up.reshape(row_count, hidden_width)
     )
     held, start = None, 0
-    all_rows, owns, arrived = [], [], []
+    owns, arrived = [], []
     for chunk, width in enumerate(WIDTHS):
-        earlier = all_rows[: max(0, chunk - 1)]
-        local, near, far = dispatch(metas, near_rows, capacity, top_count, start, width, earlier)
-        near = swap(near, 2)
-        far = after(swap_far(far), near, *owns[-1:])
-        blocks = [local, near, far, swap(far, 1)]
-        earlier = [] if held is None else [held, *arrived]
-        rows, own, later, half = panel_parts(turned, blocks, capacity, earlier)
-        all_rows.append(rows)
+        far = swap_far(dispatch(metas, near_rows, capacity, top_count, start, width, True)[0])
+        if chunk == 0:
+            local, near = dispatch(metas, near_rows, capacity, top_count, 0, model_width, False)
+            near = swap(near, 2)
+        far = after(far, near, *owns)
+        earlier = [] if held is None else [held]
+        rows, own, later, half = panel_parts(
+            turned, [local, near, far, swap(far, 1)], capacity, start, earlier
+        )
         earlier = arrived[-1:]
         if chunk + 1 < len(WIDTHS):
             held = grad_hidden_step(held, rows, weight, start)
         else:
-            grad_gate, grad_up, lines = grad_hidden_last(
-                held, rows, weight, start, hidden, up_scale, gate_scale, capacity
-            )
-            for offset in (1, 2):
-                lines = jnp.concatenate([lines, swap(lines, offset)], axis=0)
+            grad_hidden, lines = grad_hidden_last(held, rows, weight, start, hidden, capacity)
+            lines = jnp.concatenate([lines, swap(lines, 1)], axis=0)
+            grad_gate, grad_up = scaled_grads(grad_hidden, up_scale, gate_scale, [lines])
+            lines = jnp.concatenate([lines, swap(lines, 2)], axis=0)
             earlier = earlier + [lines]
         own, half = halve(own, later, swap_groups(half, False), earlier)
         owns.append(own)

time: 77.2 us -> 76.7 us (level)
  Pallas kernels: 10.5 us -> 11.4 us
    ppermute x4, waiting for transfers between devices: 13.6 us -> 18.1 us  [swap_groups(): return lax.ppermute(value, ('dp', 'expert'), pairs)]
    ppermute x9 -> x8, waiting for transfers between devices: 31.3 us -> 27.8 us  [swap(): lax.ppermute(value, 'expert', [(place, place ^ offset) for place in range...]
    pallas_call x2 -> x3, Pallas kernels: 2.09 us -> 3.88 us  [the longest x2 2.09 us: panel_parts(): pl.pallas_call(functools.partial(panel_kernel, capacity, start), in_specs...]
    ppermute x2, waiting for transfers between devices: 5.8 us -> 4.19 us  [swap_far(): return lax.ppermute(value, 'expert', pairs)]
    pallas_call x1, Pallas kernels: 2.78 us -> 1.64 us  [grad_hidden_last(): pl.pallas_call(functools.partial(last_kernel, capacity, start), grid=(hid...]
    ppermute x9 -> x8, starting transfers between devices: 2.47 us -> 2.31 us  [swap(): lax.ppermute(value, 'expert', [(place, place ^ offset) for place in range...]
  transfers between devices with their start and end apart: 15 -> 14, of which waited for: 12 -> 12; matrix products, arithmetic and copies ran while one was open for 0% -> 0% of each run, Pallas kernels for 9% -> 10%
where the time goes in v8:
time: 76.7 us; the launch traced here: 76.5 us
  waiting for transfers between devices  50.1 us (65%)
  starting transfers between devices  11.9 us (16%)
  Pallas kernels  11.4 us (15%)
  local copies, waits for them, and re-layouts  2.4 us (3%)
    ppermute x8, waiting for transfers between devices, swap(): lax.ppermute(value, 'expert', [(place, place ^ offset) for place in range...  27.8 us
    ppermute x4, waiting for transfers between devices, swap_groups(): return lax.ppermute(value, ('dp', 'expert'), pairs)  18.1 us
    ppermute x4, starting transfers between devices, swap_groups(): return lax.ppermute(value, ('dp', 'expert'), pairs)  5.7 us
    ppermute x2, waiting for transfers between devices, swap_far(): return lax.ppermute(value, 'expert', pairs)  4.19 us
    ppermute x2, starting transfers between devices, swap_far(): return lax.ppermute(value, 'expert', pairs)  3.89 us
    unnamed x16, local copies, waits for them, and re-layouts  2.4 us
    ppermute x8, starting transfers between devices, swap(): lax.ppermute(value, 'expert', [(place, place ^ offset) for place in range...  2.31 us
    pallas_call x2, Pallas kernels, panel_parts(): pl.pallas_call(functools.partial(panel_kernel, capacity, start), in_specs...  2.09 us
  transfers between devices with their start and end apart: 14, of which 12 were waited for; matrix products, arithmetic and copies ran while one was open for 0% of the time, Pallas kernels for 10%

profile of v8, /device:TPU:0, one launch (start us, length us, event | category | flops | bytes accessed | tf_op | source)
XLA Modules:
  0.0 76.5 jit_solution(236614326930633186)
XLA Ops:
  0.6 0.5 collective-permute-start.1
  1.2 0.7 copy-done.5
  1.8 0.7 copy-done.6
  2.7 1.1 %collective-permute-done.refs_1_ = bf16[16,128]{1,0:T(8,128)(2,1)S(1)} collective-permute-done((bf16[16,128]{1,0:T(8,128)(2,1)S(1)}, bf16[16,128]{1,0:T(8,128)(2,1)S(1)}, u32[]{:S(2)}, u32[]{:S(2)}) %collective-permute-start) | collective-permute-done | bytes 4128 | tf_op jit(solution)/shard_map/ppermute | solution.py:420
  3.8 1.0 %copy-done.1 = bf16[128,2048]{1,0:T(8,128)(2,1)S(1)} copy-done((bf16[128,2048]{1,0:T(8,128)(2,1)S(1)}, bf16[128,2048]{1,0:T(8,128)(2,1)}, u32[]{:S(2)}) %copy-start.1) | copy-done | bytes 524312
  4.8 0.3 shard_map.96
  5.2 3.8 %collective-permute-start.3 = (bf16[192,1280]{1,0:T(8,128)(2,1)S(1)}, bf16[192,1280]{1,0:T(8,128)(2,1)S(1)}, u32[]{:S(2)}, u32[]{:S(2)}) collective-permute-start(bf16[192,1280]{1,0:T(8,128)(2,1)S(1)} %shard_map.96), channel_id=1, source_target_pairs={{0,4},{1,7},{2,6},{3,5},{4,0},{5,3},{6,2},{7,1},{8,12},{9,15},{10,... | collective-permute-start | bytes 1474568 | tf_op jit(solution)/shard_map/ppermute | solution.py:426
  9.0 0.4 shard_map.95
  9.4 1.6 %collective-permute-start.2 = (bf16[96,2048]{1,0:T(8,128)(2,1)S(1)}, bf16[96,2048]{1,0:T(8,128)(2,1)S(1)}, u32[]{:S(2)}, u32[]{:S(2)}) collective-permute-start(bf16[96,2048]{1,0:T(8,128)(2,1)S(1)} %get-tuple-element.28), channel_id=1, source_target_pairs={{0,2},{1,3},{2,0},{3,1},{4,6},{5,7},{6,4},{7,5},{8,10},{9,11},{10,... | collective-permute-start | bytes 1179656 | tf_op jit(solution)/shard_map/ppermute | solution.py:420
  11.0 18.1 %collective-permute-done.2.refs_1_ = bf16[96,2048]{1,0:T(8,128)(2,1)S(1)} collective-permute-done((bf16[96,2048]{1,0:T(8,128)(2,1)S(1)}, bf16[96,2048]{1,0:T(8,128)(2,1)S(1)}, u32[]{:S(2)}, u32[]{:S(2)}) %collective-permute-start.2) | collective-permute-done | bytes 393248 | tf_op jit(solution)/shard_map/ppermute | solution.py:420
  29.1 2.3 %collective-permute-done.3.refs_0_ = bf16[192,1280]{1,0:T(8,128)(2,1)S(1)} collective-permute-done((bf16[192,1280]{1,0:T(8,128)(2,1)S(1)}, bf16[192,1280]{1,0:T(8,128)(2,1)S(1)}, u32[]{:S(2)}, u32[]{:S(2)}) %collective-permute-start.3) | collective-permute-done | bytes 491552 | tf_op jit(solution)/shard_map/ppermute | solution.py:426
  31.4 1.0 %shard_map.93 = (bf16[768,384]{1,0:T(8,128)(2,1)S(1)}, bf16[384,768]{1,0:T(8,128)(2,1)S(1)}, f32[384,768]{1,0:T(8,128)S(1)}, f32[384,768]{1,0:T(8,128)S(1)}) custom-call(bf16[384,768]{1,0:T(8,128)(2,1)S(1)} %bitcast.11, bf16[384,768]{1,0:T(8,128)(2,1)S(1)} %bitcast.12), custom_call_target="tpu_custom_call" | custom-call | flops 92160 | bytes 73728 | tf_op jit(solution)/shard_map/pallas_call | solution.py:133
  32.4 0.8 %collective-permute-done.4.refs_3_ = bf16[192,1280]{1,0:T(8,128)(2,1)S(1)} collective-permute-done((bf16[192,1280]{1,0:T(8,128)(2,1)S(1)}, bf16[192,1280]{1,0:T(8,128)(2,1)S(1)}, u32[]{:S(2)}, u32[]{:S(2)}) %collective-permute-start.4) | collective-permute-done | bytes 491552 | tf_op jit(solution)/shard_map/ppermute | solution.py:420
  33.3 1.3 %shard_map.98 = (bf16[384,1280]{1,0:T(8,128)(2,1)S(1)}, f32[192,1280]{1,0:T(8,128)S(1)}, f32[192,1280]{1,0:T(8,128)S(1)}, bf16[384,1280]{1,0:T(8,128)(2,1)S(1)}) custom-call(bf16[768,384]{1,0:T(8,128)(2,1)S(1)} %get-tuple-element.26.turned_ref, bf16[96,2048]{1,0:T(8,128)(2,1)S(1)} %get-tuple-element.27.refs_0_, ...), custom_call_target="tpu_custom_call" | custom-call | flops 11796480 | bytes 39936 | tf_op jit(solution)/shard_map/pallas_call | solution.py:182
  34.5 1.6 %collective-permute-start.6 = (bf16[384,1280]{1,0:T(8,128)(2,1)S(1)}, bf16[384,1280]{1,0:T(8,128)(2,1)S(1)}, u32[]{:S(2)}, u32[]{:S(2)}) collective-permute-start(bf16[384,1280]{1,0:T(8,128)(2,1)S(1)} %get-tuple-element.32), channel_id=1, source_target_pairs={{0,8},{1,17},{2,10},{3,19},{4,12},{5,21},{6,14},{7,23},{8,0},{9,25... | collective-permute-start | bytes 2949128 | tf_op jit(solution)/shard_map/ppermute | solution.py:436
  36.1 0.2 shard_map.100
  36.4 12.3 %collective-permute-done.6.arrived_ref = bf16[384,1280]{1,0:T(8,128)(2,1)S(1)} collective-permute-done((bf16[384,1280]{1,0:T(8,128)(2,1)S(1)}, bf16[384,1280]{1,0:T(8,128)(2,1)S(1)}, u32[]{:S(2)}, u32[]{:S(2)}) %collective-permute-start.6) | collective-permute-done | bytes 983072 | tf_op jit(solution)/shard_map/ppermute | solution.py:436
  48.9 1.9 %collective-permute-done.5.refs_0_ = bf16[192,768]{1,0:T(8,128)(2,1)S(1)} collective-permute-done((bf16[192,768]{1,0:T(8,128)(2,1)S(1)}, bf16[192,768]{1,0:T(8,128)(2,1)S(1)}, u32[]{:S(2)}, u32[]{:S(2)}) %collective-permute-start.5) | collective-permute-done | bytes 294944 | tf_op jit(solution)/shard_map/ppermute | solution.py:426
  50.8 1.5 %shard_map.99.refs_4_.held_ref = f32[384,768]{1,0:T(8,128)S(1)} custom-call(bf16[384,1280]{1,0:T(8,128)(2,1)S(1)} %get-tuple-element.29.rows_ref, bf16[768,2048]{1,0:T(8,128)(2,1)S(1)} %bitcast.9), custom_call_target="tpu_custom_call" | custom-call | flops 11796480 | bytes 36864 | tf_op jit(solution)/shard_map/pallas_call | solution.py:280
  52.4 0.8 %shard_map.103 = (bf16[384,768]{1,0:T(8,128)(2,1)S(1)}, f32[192,768]{1,0:T(8,128)S(1)}, f32[192,768]{1,0:T(8,128)S(1)}, bf16[384,768]{1,0:T(8,128)(2,1)S(1)}) custom-call(bf16[768,384]{1,0:T(8,128)(2,1)S(1)} %get-tuple-element.26.turned_ref, bf16[96,2048]{1,0:T(8,128)(2,1)S(1)} %get-tuple-element.27.refs_0_, ...), custom_call_target="tpu_custom_call" | custom-call | flops 7077888 | bytes 27648 | tf_op jit(solution)/shard_map/pallas_call | solution.py:182
  53.2 1.6 %collective-permute-start.9 = (bf16[384,768]{1,0:T(8,128)(2,1)S(1)}, bf16[384,768]{1,0:T(8,128)(2,1)S(1)}, u32[]{:S(2)}, u32[]{:S(2)}) collective-permute-start(bf16[384,768]{1,0:T(8,128)(2,1)S(1)} %get-tuple-element.44), channel_id=1, source_target_pairs={{0,8},{1,17},{2,10},{3,19},{4,12},{5,21},{6,14},{7,23},{8,0},{9,25... | collective-permute-start | bytes 1769480 | tf_op jit(solution)/shard_map/ppermute | solution.py:436
  54.8 1.2 %collective-permute-start.10 = (bf16[192,1280]{1,0:T(8,128)(2,1)S(1)}, bf16[192,1280]{1,0:T(8,128)(2,1)S(1)}, u32[]{:S(2)}, u32[]{:S(2)}) collective-permute-start(bf16[192,1280]{1,0:T(8,128)(2,1)S(1)} %get-tuple-element.45), channel_id=1, source_target_pairs={{0,16},{1,9},{2,18},{3,11},{4,20},{5,13},{6,22},{7,15},{8,24},{9,1... | collective-permute-start | bytes 1474568 | tf_op jit(solution)/shard_map/ppermute | solution.py:436
  56.0 1.6 %shard_map.104 = (f32[384,768]{1,0:T(8,128)S(1)}, f32[8,128]{1,0:T(8,128)S(1)}) custom-call(f32[384,768]{1,0:T(8,128)S(1)} %shard_map.99.refs_4_.held_ref, bf16[384,768]{1,0:T(8,128)(2,1)S(1)} %get-tuple-element.34.rows_ref, bf16[768,2048]{1,0:T(8,128)(2,1)S(1)} %bitcast.10, bf16[384,768]{1,0:T(8,128)(2,1)S(1)} %get-tuple-element.35.hidden_ref), custom_call_target="tpu_custom_call" | custom-call | flops 7077888 | bytes 55296 | tf_op jit(solution)/shard_map/pallas_call | solution.py:326
  57.7 1.1 %collective-permute-done.8 = f32[8,128]{1,0:T(8,128)S(1)} collective-permute-done((f32[8,128]{1,0:T(8,128)S(1)}, f32[8,128]{1,0:T(8,128)S(1)}, u32[]{:S(2)}, u32[]{:S(2)}) %collective-permute-start.8) | collective-permute-done | bytes 4128 | tf_op jit(solution)/shard_map/ppermute | solution.py:420
  58.9 3.6 %collective-permute-done.11 = f32[16,128]{1,0:T(8,128)S(1)} collective-permute-done((f32[16,128]{1,0:T(8,128)S(1)}, f32[16,128]{1,0:T(8,128)S(1)}, u32[]{:S(2)}, u32[]{:S(2)}) %collective-permute-start.11) | collective-permute-done | bytes 8224 | tf_op jit(solution)/shard_map/ppermute | solution.py:420
  62.5 5.3 %collective-permute-done.10.refs_0_.refs_2_ = bf16[192,1280]{1,0:T(8,128)(2,1)S(1)} collective-permute-done((bf16[192,1280]{1,0:T(8,128)(2,1)S(1)}, bf16[192,1280]{1,0:T(8,128)(2,1)S(1)}, u32[]{:S(2)}, u32[]{:S(2)}) %collective-permute-start.10) | collective-permute-done | bytes 491552 | tf_op jit(solution)/shard_map/ppermute | solution.py:436
  67.9 0.5 collective-permute-done.9.arrived_ref
  68.4 1.4 %collective-permute-start.12 = (bf16[192,768]{1,0:T(8,128)(2,1)S(1)}, bf16[192,768]{1,0:T(8,128)(2,1)S(1)}, u32[]{:S(2)}, u32[]{:S(2)}) collective-permute-start(bf16[192,768]{1,0:T(8,128)(2,1)S(1)} %get-tuple-element.47), channel_id=1, source_target_pairs={{0,16},{1,9},{2,18},{3,11},{4,20},{5,13},{6,22},{7,15},{8,24},{9,1... | collective-permute-start | bytes 884744 | tf_op jit(solution)/shard_map/ppermute | solution.py:436
  69.8 1.8 %shard_map.105 = (bf16[384,768]{1,0:T(8,128)(2,1)}, bf16[384,768]{1,0:T(8,128)(2,1)}) custom-call(f32[384,768]{1,0:T(8,128)S(1)} %get-tuple-element.36.grad_ref, f32[384,768]{1,0:T(8,128)S(1)} %get-tuple-element.37.up_scale_ref, f32[384,768]{1,0:T(8,128)S(1)} %get-tuple-element.38.gate_scale_ref, f32[16,128]{1,0:T(8,128)S(1)} %get-tuple-element.49.refs_0_), custom_call_target="tpu_custom_call" | custom-call | flops 9216 | bytes 73728 | tf_op jit(solution)/shard_map/pallas_call | solution.py:356
  71.6 2.8 %collective-permute-done.13.refs_4_.far_ref = f32[32,128]{1,0:T(8,128)S(1)} collective-permute-done((f32[32,128]{1,0:T(8,128)S(1)}, f32[32,128]{1,0:T(8,128)S(1)}, u32[]{:S(2)}, u32[]{:S(2)}) %collective-permute-start.13) | collective-permute-done | bytes 16416 | tf_op jit(solution)/shard_map/ppermute | solution.py:420
  74.4 0.8 %shard_map.108 = f32[2,128]{1,0:T(2,128)} custom-call(bf16[16,128]{1,0:T(8,128)(2,1)S(1)} %shard_map.94.refs_0_.meta_ref, f32[32,128]{1,0:T(8,128)S(1)} %constant_dynamic-update-slice_fusion.2.refs_1_.near_ref, f32[32,128]{1,0:T(8,128)S(1)} %collective-permute-done.13.refs_4_.far_ref), custom_call_target="tpu_custom_call" | custom-call | flops 15625 | bytes 1562 | tf_op jit(solution)/shard_map/pallas_call | solution.py:392
  75.2 1.2 %shard_map.107 = f32[192,2048]{1,0:T(8,128)} custom-call(f32[192,1280]{1,0:T(8,128)S(1)} %get-tuple-element.33.refs_2_.refs_0_, f32[192,768]{1,0:T(8,128)S(1)} %get-tuple-element.46.refs_1_, bf16[192,1280]{1,0:T(8,128)(2,1)S(1)} %collective-permute-done.10.refs_0_.refs_2_, bf16[192,768]{1,0:T(8,128)(2,1)S(1)} %collective-permute-done.12.refs_3_, ...), custom_call_target="tpu_custom_call" | custom-call | flops 12288 | bytes 61440 | tf_op jit(solution)/shard_map/pallas_call | solution.py:242
  (29 shorter events, 0.8 us)
Async XLA Ops:
  0.6 3.2 %collective-permute-start.1 = (bf16[128,2048]{1,0:T(8,128)(2,1)}, bf16[128,2048]{1,0:T(8,128)(2,1)S(1)}, u32[]{:S(2)}, u32[]{:S(2)}) collective-permute-start(bf16[128,2048]{1,0:T(8,128)(2,1)} %refs_2_.5), channel_id=1, source_target_pairs={{0,1},{1,0},{2,3},{3,2},{4,5},{5,4},{6,7},{7,6},{8,9},{9,8},{10,11... | collective-permute-start | bytes 1572872 | tf_op jit(solution)/shard_map/ppermute | solution.py:420
  1.1 0.7 copy-start.5
  1.8 0.7 copy-start.6
  2.6 1.2 %collective-permute-start = (bf16[16,128]{1,0:T(8,128)(2,1)S(1)}, bf16[16,128]{1,0:T(8,128)(2,1)S(1)}, u32[]{:S(2)}, u32[]{:S(2)}) collective-permute-start(bf16[16,128]{1,0:T(8,128)(2,1)S(1)} %shard_map.94.refs_0_.meta_ref), channel_id=1, source_target_pairs={{0,1},{1,0},{2,3},{3,2},{4,5},{5,4},{6,7},{7,6},{8,9},{9,8},{10,11... | collective-permute-start | bytes 12296 | tf_op jit(solution)/shard_map/ppermute | solution.py:420
  3.8 1.0 %copy-start.1 = (bf16[128,2048]{1,0:T(8,128)(2,1)S(1)}, bf16[128,2048]{1,0:T(8,128)(2,1)}, u32[]{:S(2)}) copy-start(bf16[128,2048]{1,0:T(8,128)(2,1)} %refs_2_.5) | copy-start | bytes 1572868
  5.1 26.3 %copy-start.3 = (bf16[1,1,8,48,768]{4,3,2,1,0:T(8,128)(2,1)S(1)}, bf16[1,1,8,48,768]{4,3,2,1,0:T(8,128)(2,1)}, u32[]{:S(2)}) copy-start(bf16[1,1,8,48,768]{4,3,2,1,0:T(8,128)(2,1)} %param.9) | copy-start | bytes 1769476
  5.1 26.3 %copy-start.4 = (bf16[1,1,8,48,768]{4,3,2,1,0:T(8,128)(2,1)S(1)}, bf16[1,1,8,48,768]{4,3,2,1,0:T(8,128)(2,1)}, u32[]{:S(2)}) copy-start(bf16[1,1,8,48,768]{4,3,2,1,0:T(8,128)(2,1)} %param.10) | copy-start | bytes 1769476
  5.2 26.2 %collective-permute-start.3 = (bf16[192,1280]{1,0:T(8,128)(2,1)S(1)}, bf16[192,1280]{1,0:T(8,128)(2,1)S(1)}, u32[]{:S(2)}, u32[]{:S(2)}) collective-permute-start(bf16[192,1280]{1,0:T(8,128)(2,1)S(1)} %shard_map.96), channel_id=1, source_target_pairs={{0,4},{1,7},{2,6},{3,5},{4,0},{5,3},{6,2},{7,1},{8,12},{9,15},{10,... | collective-permute-start | bytes 1474568 | tf_op jit(solution)/shard_map/ppermute | solution.py:426
  9.4 19.8 %collective-permute-start.2 = (bf16[96,2048]{1,0:T(8,128)(2,1)S(1)}, bf16[96,2048]{1,0:T(8,128)(2,1)S(1)}, u32[]{:S(2)}, u32[]{:S(2)}) collective-permute-start(bf16[96,2048]{1,0:T(8,128)(2,1)S(1)} %get-tuple-element.28), channel_id=1, source_target_pairs={{0,2},{1,3},{2,0},{3,1},{4,6},{5,7},{6,4},{7,5},{8,10},{9,11},{10,... | collective-permute-start | bytes 1179656 | tf_op jit(solution)/shard_map/ppermute | solution.py:420
  31.4 1.9 %collective-permute-start.4 = (bf16[192,1280]{1,0:T(8,128)(2,1)S(1)}, bf16[192,1280]{1,0:T(8,128)(2,1)S(1)}, u32[]{:S(2)}, u32[]{:S(2)}) collective-permute-start(bf16[192,1280]{1,0:T(8,128)(2,1)S(1)} %shard_map.97.refs_2_), channel_id=1, source_target_pairs={{0,1},{1,0},{2,3},{3,2},{4,5},{5,4},{6,7},{7,6},{8,9},{9,8},{10,11... | collective-permute-start | bytes 1474568 | tf_op jit(solution)/shard_map/ppermute | solution.py:420
  33.3 2.8 %copy-start.2 = (bf16[128,2048]{1,0:T(8,128)(2,1)S(1)}, bf16[128,2048]{1,0:T(8,128)(2,1)}, u32[]{:S(2)}) copy-start(bf16[128,2048]{1,0:T(8,128)(2,1)} %refs_2_.5) | copy-start | bytes 1572868
  34.5 14.2 %collective-permute-start.6 = (bf16[384,1280]{1,0:T(8,128)(2,1)S(1)}, bf16[384,1280]{1,0:T(8,128)(2,1)S(1)}, u32[]{:S(2)}, u32[]{:S(2)}) collective-permute-start(bf16[384,1280]{1,0:T(8,128)(2,1)S(1)} %get-tuple-element.32), channel_id=1, source_target_pairs={{0,8},{1,17},{2,10},{3,19},{4,12},{5,21},{6,14},{7,23},{8,0},{9,25... | collective-permute-start | bytes 2949128 | tf_op jit(solution)/shard_map/ppermute | solution.py:436
  36.3 14.5 %collective-permute-start.5 = (bf16[192,768]{1,0:T(8,128)(2,1)S(1)}, bf16[192,768]{1,0:T(8,128)(2,1)S(1)}, u32[]{:S(2)}, u32[]{:S(2)}) collective-permute-start(bf16[192,768]{1,0:T(8,128)(2,1)S(1)} %shard_map.100), channel_id=1, source_target_pairs={{0,4},{1,7},{2,6},{3,5},{4,0},{5,3},{6,2},{7,1},{8,12},{9,15},{10,... | collective-permute-start | bytes 884744 | tf_op jit(solution)/shard_map/ppermute | solution.py:426
  48.7 2.1 %copy-start = (bf16[1,768,2048]{2,1,0:T(8,128)(2,1)S(1)}, bf16[1,768,2048]{2,1,0:T(8,128)(2,1)}, u32[]{:S(2)}) copy-start(bf16[1,768,2048]{2,1,0:T(8,128)(2,1)} %param.11) | copy-start | bytes 9437188
  50.8 1.6 %collective-permute-start.7 = (bf16[192,768]{1,0:T(8,128)(2,1)S(1)}, bf16[192,768]{1,0:T(8,128)(2,1)S(1)}, u32[]{:S(2)}, u32[]{:S(2)}) collective-permute-start(bf16[192,768]{1,0:T(8,128)(2,1)S(1)} %shard_map.102.refs_2_), channel_id=1, source_target_pairs={{0,1},{1,0},{2,3},{3,2},{4,5},{5,4},{6,7},{7,6},{8,9},{9,8},{10,11... | collective-permute-start | bytes 884744 | tf_op jit(solution)/shard_map/ppermute | solution.py:420
  53.2 15.1 %collective-permute-start.9 = (bf16[384,768]{1,0:T(8,128)(2,1)S(1)}, bf16[384,768]{1,0:T(8,128)(2,1)S(1)}, u32[]{:S(2)}, u32[]{:S(2)}) collective-permute-start(bf16[384,768]{1,0:T(8,128)(2,1)S(1)} %get-tuple-element.44), channel_id=1, source_target_pairs={{0,8},{1,17},{2,10},{3,19},{4,12},{5,21},{6,14},{7,23},{8,0},{9,25... | collective-permute-start | bytes 1769480 | tf_op jit(solution)/shard_map/ppermute | solution.py:436
  54.8 13.1 %collective-permute-start.10 = (bf16[192,1280]{1,0:T(8,128)(2,1)S(1)}, bf16[192,1280]{1,0:T(8,128)(2,1)S(1)}, u32[]{:S(2)}, u32[]{:S(2)}) collective-permute-start(bf16[192,1280]{1,0:T(8,128)(2,1)S(1)} %get-tuple-element.45), channel_id=1, source_target_pairs={{0,16},{1,9},{2,18},{3,11},{4,20},{5,13},{6,22},{7,15},{8,24},{9,1... | collective-permute-start | bytes 1474568 | tf_op jit(solution)/shard_map/ppermute | solution.py:436
  57.6 1.2 %collective-permute-start.8 = (f32[8,128]{1,0:T(8,128)S(1)}, f32[8,128]{1,0:T(8,128)S(1)}, u32[]{:S(2)}, u32[]{:S(2)}) collective-permute-start(f32[8,128]{1,0:T(8,128)S(1)} %get-tuple-element.39), channel_id=1, source_target_pairs={{0,1},{1,0},{2,3},{3,2},{4,5},{5,4},{6,7},{7,6},{8,9},{9,8},{10,11... | collective-permute-start | bytes 12296 | tf_op jit(solution)/shard_map/ppermute | solution.py:420
  58.9 3.7 %collective-permute-start.11 = (f32[16,128]{1,0:T(8,128)S(1)}, f32[16,128]{1,0:T(8,128)S(1)}, u32[]{:S(2)}, u32[]{:S(2)}) collective-permute-start(f32[16,128]{1,0:T(8,128)S(1)} %get-tuple-element.49.refs_0_), channel_id=1, source_target_pairs={{0,2},{1,3},{2,0},{3,1},{4,6},{5,7},{6,4},{7,5},{8,10},{9,11},{10,... | collective-permute-start | bytes 24584 | tf_op jit(solution)/shard_map/ppermute | solution.py:420
  68.4 6.8 %collective-permute-start.12 = (bf16[192,768]{1,0:T(8,128)(2,1)S(1)}, bf16[192,768]{1,0:T(8,128)(2,1)S(1)}, u32[]{:S(2)}, u32[]{:S(2)}) collective-permute-start(bf16[192,768]{1,0:T(8,128)(2,1)S(1)} %get-tuple-element.47), channel_id=1, source_target_pairs={{0,16},{1,9},{2,18},{3,11},{4,20},{5,13},{6,22},{7,15},{8,24},{9,1... | collective-permute-start | bytes 884744 | tf_op jit(solution)/shard_map/ppermute | solution.py:436
  69.8 4.6 %collective-permute-start.13 = (f32[32,128]{1,0:T(8,128)S(1)}, f32[32,128]{1,0:T(8,128)S(1)}, u32[]{:S(2)}, u32[]{:S(2)}) collective-permute-start(f32[32,128]{1,0:T(8,128)S(1)} %constant_dynamic-update-slice_fusion.2.refs_1_.near_ref), channel_id=1, source_target_pairs={{0,4},{1,5},{2,6},{3,7},{4,0},{5,1},{6,2},{7,3},{8,12},{9,13},{10,... | collective-permute-start | bytes 49160 | tf_op jit(solution)/shard_map/ppermute | solution.py:420

commit v9 on v8

--- a/solution.py
+++ b/solution.py
@@ -9,7 +9,7 @@
 
 LANES = 128
 META = 16
-WIDTHS = (1280, 768)
+WIDTHS = (1152, 896)
 VMEM_LIMIT = 10 * 1024 * 1024
 VMEM = pl.BlockSpec(memory_space=pltpu.VMEM)
 ANY = pl.BlockSpec(memory_space=pl.ANY)
@@ -459,7 +459,7 @@
             local, near = dispatch(metas, near_rows, capacity, top_count, 0, model_width, False)
             near = swap(near, 2)
         far = after(far, near, *owns)
-        earlier = [] if held is None else [held]
+        earlier = [] if held is None else [held, *arrived]
         rows, own, later, half = panel_parts(
             turned, [local, near, far, swap(far, 1)], capacity, start, earlier
         )

time: 76.7 us -> 74.9 us (0.977)
  waiting for transfers between devices: 50.1 us -> 45.9 us
  starting transfers between devices: 11.9 us -> 14 us
    ppermute x4, waiting for transfers between devices: 18.1 us -> 14.5 us  [swap_groups(): return lax.ppermute(value, ('dp', 'expert'), pairs)]
    ppermute x8, starting transfers between devices: 2.31 us -> 3.36 us  [swap(): lax.ppermute(value, 'expert', [(place, place ^ offset) for place in range...]
    ppermute x8, waiting for transfers between devices: 27.8 us -> 26.7 us  [swap(): lax.ppermute(value, 'expert', [(place, place ^ offset) for place in range...]
    ppermute x4, starting transfers between devices: 5.7 us -> 6.52 us  [swap_groups(): return lax.ppermute(value, ('dp', 'expert'), pairs)]
  transfers between devices with their start and end apart: 14 -> 14, of which waited for: 12 -> 13; matrix products, arithmetic and copies ran while one was open for 0% -> 0% of each run, Pallas kernels for 10% -> 10%
where the time goes in v9:
time: 74.9 us; the launch traced here: 74.7 us
  waiting for transfers between devices  45.9 us (61%)
  starting transfers between devices  14 us (19%)
  Pallas kernels  11.6 us (15%)
  local copies, waits for them, and re-layouts  2.4 us (3%)
  between operations  0.76 us (1%)
    ppermute x8, waiting for transfers between devices, swap(): lax.ppermute(value, 'expert', [(place, place ^ offset) for place in range...  26.7 us
    ppermute x4, waiting for transfers between devices, swap_groups(): return lax.ppermute(value, ('dp', 'expert'), pairs)  14.5 us
    ppermute x4, starting transfers between devices, swap_groups(): return lax.ppermute(value, ('dp', 'expert'), pairs)  6.52 us
    ppermute x2, waiting for transfers between devices, swap_far(): return lax.ppermute(value, 'expert', pairs)  4.69 us
    ppermute x2, starting transfers between devices, swap_far(): return lax.ppermute(value, 'expert', pairs)  4.16 us
    ppermute x8, starting transfers between devices, swap(): lax.ppermute(value, 'expert', [(place, place ^ offset) for place in range...  3.36 us
    unnamed x16, local copies, waits for them, and re-layouts  2.4 us
    pallas_call x2, Pallas kernels, panel_parts(): pl.pallas_call(functools.partial(panel_kernel, capacity, start), in_specs...  2.25 us
  transfers between devices with their start and end apart: 14, of which 13 were waited for; matrix products, arithmetic and copies ran while one was open for 0% of the time, Pallas kernels for 10%

profile of v9, /device:TPU:0, one launch (start us, length us, event | category | flops | bytes accessed | tf_op | source)
XLA Modules:
  0.0 74.7 jit_solution(8715240389520189115)
XLA Ops:
  0.6 0.5 collective-permute-start.1
  1.2 0.7 copy-done.5
  1.8 0.7 copy-done.6
  2.7 1.1 %collective-permute-done.refs_1_ = bf16[16,128]{1,0:T(8,128)(2,1)S(1)} collective-permute-done((bf16[16,128]{1,0:T(8,128)(2,1)S(1)}, bf16[16,128]{1,0:T(8,128)(2,1)S(1)}, u32[]{:S(2)}, u32[]{:S(2)}) %collective-permute-start) | collective-permute-done | bytes 4128 | tf_op jit(solution)/shard_map/ppermute | solution.py:420
  3.8 1.0 %copy-done.1 = bf16[128,2048]{1,0:T(8,128)(2,1)S(1)} copy-done((bf16[128,2048]{1,0:T(8,128)(2,1)S(1)}, bf16[128,2048]{1,0:T(8,128)(2,1)}, u32[]{:S(2)}) %copy-start.1) | copy-done | bytes 524312
  5.1 3.8 %collective-permute-start.3 = (bf16[192,1152]{1,0:T(8,128)(2,1)S(1)}, bf16[192,1152]{1,0:T(8,128)(2,1)S(1)}, u32[]{:S(2)}, u32[]{:S(2)}) collective-permute-start(bf16[192,1152]{1,0:T(8,128)(2,1)S(1)} %shard_map.96), channel_id=1, source_target_pairs={{0,4},{1,7},{2,6},{3,5},{4,0},{5,3},{6,2},{7,1},{8,12},{9,15},{10,... | collective-permute-start | bytes 1327112 | tf_op jit(solution)/shard_map/ppermute | solution.py:426
  9.0 0.4 shard_map.95
  9.4 1.6 %collective-permute-start.2 = (bf16[96,2048]{1,0:T(8,128)(2,1)S(1)}, bf16[96,2048]{1,0:T(8,128)(2,1)S(1)}, u32[]{:S(2)}, u32[]{:S(2)}) collective-permute-start(bf16[96,2048]{1,0:T(8,128)(2,1)S(1)} %get-tuple-element.28), channel_id=1, source_target_pairs={{0,2},{1,3},{2,0},{3,1},{4,6},{5,7},{6,4},{7,5},{8,10},{9,11},{10,... | collective-permute-start | bytes 1179656 | tf_op jit(solution)/shard_map/ppermute | solution.py:420
  11.0 18.1 %collective-permute-done.2.refs_1_ = bf16[96,2048]{1,0:T(8,128)(2,1)S(1)} collective-permute-done((bf16[96,2048]{1,0:T(8,128)(2,1)S(1)}, bf16[96,2048]{1,0:T(8,128)(2,1)S(1)}, u32[]{:S(2)}, u32[]{:S(2)}) %collective-permute-start.2) | collective-permute-done | bytes 393248 | tf_op jit(solution)/shard_map/ppermute | solution.py:420
  29.4 1.0 %shard_map.93 = (bf16[768,384]{1,0:T(8,128)(2,1)S(1)}, bf16[384,768]{1,0:T(8,128)(2,1)S(1)}, f32[384,768]{1,0:T(8,128)S(1)}, f32[384,768]{1,0:T(8,128)S(1)}) custom-call(bf16[384,768]{1,0:T(8,128)(2,1)S(1)} %bitcast.11, bf16[384,768]{1,0:T(8,128)(2,1)S(1)} %bitcast.12), custom_call_target="tpu_custom_call" | custom-call | flops 92160 | bytes 73728 | tf_op jit(solution)/shard_map/pallas_call | solution.py:133
  30.4 0.7 %collective-permute-done.4.refs_3_ = bf16[192,1152]{1,0:T(8,128)(2,1)S(1)} collective-permute-done((bf16[192,1152]{1,0:T(8,128)(2,1)S(1)}, bf16[192,1152]{1,0:T(8,128)(2,1)S(1)}, u32[]{:S(2)}, u32[]{:S(2)}) %collective-permute-start.4) | collective-permute-done | bytes 442400 | tf_op jit(solution)/shard_map/ppermute | solution.py:420
  31.1 1.2 %shard_map.98 = (bf16[384,1152]{1,0:T(8,128)(2,1)S(1)}, f32[192,1152]{1,0:T(8,128)S(1)}, f32[192,1152]{1,0:T(8,128)S(1)}, bf16[384,1152]{1,0:T(8,128)(2,1)S(1)}) custom-call(bf16[768,384]{1,0:T(8,128)(2,1)S(1)} %get-tuple-element.26.turned_ref, bf16[96,2048]{1,0:T(8,128)(2,1)S(1)} %get-tuple-element.27.refs_0_, ...), custom_call_target="tpu_custom_call" | custom-call | flops 10616832 | bytes 36864 | tf_op jit(solution)/shard_map/pallas_call | solution.py:182
  32.4 1.6 %collective-permute-start.6 = (bf16[384,1152]{1,0:T(8,128)(2,1)S(1)}, bf16[384,1152]{1,0:T(8,128)(2,1)S(1)}, u32[]{:S(2)}, u32[]{:S(2)}) collective-permute-start(bf16[384,1152]{1,0:T(8,128)(2,1)S(1)} %get-tuple-element.32), channel_id=1, source_target_pairs={{0,8},{1,17},{2,10},{3,19},{4,12},{5,21},{6,14},{7,23},{8,0},{9,25... | collective-permute-start | bytes 2654216 | tf_op jit(solution)/shard_map/ppermute | solution.py:436
  34.2 0.3 collective-permute-start.5
  34.6 10.9 %collective-permute-done.6.arrived_ref = bf16[384,1152]{1,0:T(8,128)(2,1)S(1)} collective-permute-done((bf16[384,1152]{1,0:T(8,128)(2,1)S(1)}, bf16[384,1152]{1,0:T(8,128)(2,1)S(1)}, u32[]{:S(2)}, u32[]{:S(2)}) %collective-permute-start.6) | collective-permute-done | bytes 884768 | tf_op jit(solution)/shard_map/ppermute | solution.py:436
  45.6 1.6 %collective-permute-start.8 = (bf16[192,1152]{1,0:T(8,128)(2,1)S(1)}, bf16[192,1152]{1,0:T(8,128)(2,1)S(1)}, u32[]{:S(2)}, u32[]{:S(2)}) collective-permute-start(bf16[192,1152]{1,0:T(8,128)(2,1)S(1)} %get-tuple-element.34), channel_id=1, source_target_pairs={{0,16},{1,9},{2,18},{3,11},{4,20},{5,13},{6,22},{7,15},{8,24},{9,1... | collective-permute-start | bytes 1327112 | tf_op jit(solution)/shard_map/ppermute | solution.py:436
  47.3 4.5 %collective-permute-done.5.refs_0_ = bf16[192,896]{1,0:T(8,128)(2,1)S(1)} collective-permute-done((bf16[192,896]{1,0:T(8,128)(2,1)S(1)}, bf16[192,896]{1,0:T(8,128)(2,1)S(1)}, u32[]{:S(2)}, u32[]{:S(2)}) %collective-permute-start.5) | collective-permute-done | bytes 344096 | tf_op jit(solution)/shard_map/ppermute | solution.py:426
  51.8 1.5 %shard_map.99.refs_4_.held_ref = f32[384,768]{1,0:T(8,128)S(1)} custom-call(bf16[384,1152]{1,0:T(8,128)(2,1)S(1)} %get-tuple-element.29.rows_ref, bf16[768,2048]{1,0:T(8,128)(2,1)S(1)} %bitcast.9), custom_call_target="tpu_custom_call" | custom-call | flops 10616832 | bytes 36864 | tf_op jit(solution)/shard_map/pallas_call | solution.py:280
  53.4 0.6 collective-permute-done.8.refs_5_.refs_0_.refs_2_
  54.0 1.0 %shard_map.103 = (bf16[384,896]{1,0:T(8,128)(2,1)S(1)}, f32[192,896]{1,0:T(8,128)S(1)}, f32[192,896]{1,0:T(8,128)S(1)}, bf16[384,896]{1,0:T(8,128)(2,1)S(1)}) custom-call(bf16[768,384]{1,0:T(8,128)(2,1)S(1)} %get-tuple-element.26.turned_ref, bf16[96,2048]{1,0:T(8,128)(2,1)S(1)} %get-tuple-element.27.refs_0_, ...), custom_call_target="tpu_custom_call" | custom-call | flops 8257536 | bytes 30720 | tf_op jit(solution)/shard_map/pallas_call | solution.py:182
  55.0 1.6 %collective-permute-start.10 = (bf16[384,896]{1,0:T(8,128)(2,1)S(1)}, bf16[384,896]{1,0:T(8,128)(2,1)S(1)}, u32[]{:S(2)}, u32[]{:S(2)}) collective-permute-start(bf16[384,896]{1,0:T(8,128)(2,1)S(1)} %get-tuple-element.45), channel_id=1, source_target_pairs={{0,8},{1,17},{2,10},{3,19},{4,12},{5,21},{6,14},{7,23},{8,0},{9,25... | collective-permute-start | bytes 2064392 | tf_op jit(solution)/shard_map/ppermute | solution.py:436
  56.6 1.7 %shard_map.104 = (f32[384,768]{1,0:T(8,128)S(1)}, f32[8,128]{1,0:T(8,128)S(1)}) custom-call(f32[384,768]{1,0:T(8,128)S(1)} %shard_map.99.refs_4_.held_ref, bf16[384,896]{1,0:T(8,128)(2,1)S(1)} %get-tuple-element.35.rows_ref, bf16[768,2048]{1,0:T(8,128)(2,1)S(1)} %bitcast.10, bf16[384,768]{1,0:T(8,128)(2,1)S(1)} %get-tuple-element.36.hidden_ref), custom_call_target="tpu_custom_call" | custom-call | flops 8257536 | bytes 55296 | tf_op jit(solution)/shard_map/pallas_call | solution.py:326
  58.5 1.1 %collective-permute-done.9 = f32[8,128]{1,0:T(8,128)S(1)} collective-permute-done((f32[8,128]{1,0:T(8,128)S(1)}, f32[8,128]{1,0:T(8,128)S(1)}, u32[]{:S(2)}, u32[]{:S(2)}) %collective-permute-start.9) | collective-permute-done | bytes 4128 | tf_op jit(solution)/shard_map/ppermute | solution.py:420
  59.6 0.8 %collective-permute-start.11 = (f32[16,128]{1,0:T(8,128)S(1)}, f32[16,128]{1,0:T(8,128)S(1)}, u32[]{:S(2)}, u32[]{:S(2)}) collective-permute-start(f32[16,128]{1,0:T(8,128)S(1)} %get-tuple-element.49.refs_0_), channel_id=1, source_target_pairs={{0,2},{1,3},{2,0},{3,1},{4,6},{5,7},{6,4},{7,5},{8,10},{9,11},{10,... | collective-permute-start | bytes 24584 | tf_op jit(solution)/shard_map/ppermute | solution.py:420
  60.4 2.9 %collective-permute-done.11 = f32[16,128]{1,0:T(8,128)S(1)} collective-permute-done((f32[16,128]{1,0:T(8,128)S(1)}, f32[16,128]{1,0:T(8,128)S(1)}, u32[]{:S(2)}, u32[]{:S(2)}) %collective-permute-start.11) | collective-permute-done | bytes 8224 | tf_op jit(solution)/shard_map/ppermute | solution.py:420
  63.3 2.7 %collective-permute-done.10.arrived_ref = bf16[384,896]{1,0:T(8,128)(2,1)S(1)} collective-permute-done((bf16[384,896]{1,0:T(8,128)(2,1)S(1)}, bf16[384,896]{1,0:T(8,128)(2,1)S(1)}, u32[]{:S(2)}, u32[]{:S(2)}) %collective-permute-start.10) | collective-permute-done | bytes 688160 | tf_op jit(solution)/shard_map/ppermute | solution.py:436
  66.1 1.6 %collective-permute-start.12 = (bf16[192,896]{1,0:T(8,128)(2,1)S(1)}, bf16[192,896]{1,0:T(8,128)(2,1)S(1)}, u32[]{:S(2)}, u32[]{:S(2)}) collective-permute-start(bf16[192,896]{1,0:T(8,128)(2,1)S(1)} %get-tuple-element.47), channel_id=1, source_target_pairs={{0,16},{1,9},{2,18},{3,11},{4,20},{5,13},{6,22},{7,15},{8,24},{9,1... | collective-permute-start | bytes 1032200 | tf_op jit(solution)/shard_map/ppermute | solution.py:436
  67.8 0.3 collective-permute-start.13
  68.1 1.8 %shard_map.105 = (bf16[384,768]{1,0:T(8,128)(2,1)}, bf16[384,768]{1,0:T(8,128)(2,1)}) custom-call(f32[384,768]{1,0:T(8,128)S(1)} %get-tuple-element.37.grad_ref, f32[384,768]{1,0:T(8,128)S(1)} %get-tuple-element.38.up_scale_ref, f32[384,768]{1,0:T(8,128)S(1)} %get-tuple-element.39.gate_scale_ref, f32[16,128]{1,0:T(8,128)S(1)} %get-tuple-element.49.refs_0_), custom_call_target="tpu_custom_call" | custom-call | flops 9216 | bytes 73728 | tf_op jit(solution)/shard_map/pallas_call | solution.py:356
  69.9 2.6 %collective-permute-done.13.refs_4_.far_ref = f32[32,128]{1,0:T(8,128)S(1)} collective-permute-done((f32[32,128]{1,0:T(8,128)S(1)}, f32[32,128]{1,0:T(8,128)S(1)}, u32[]{:S(2)}, u32[]{:S(2)}) %collective-permute-start.13) | collective-permute-done | bytes 16416 | tf_op jit(solution)/shard_map/ppermute | solution.py:420
  72.4 0.8 %shard_map.108 = f32[2,128]{1,0:T(2,128)} custom-call(bf16[16,128]{1,0:T(8,128)(2,1)S(1)} %shard_map.94.refs_0_.meta_ref, f32[32,128]{1,0:T(8,128)S(1)} %constant_dynamic-update-slice_fusion.2.refs_1_.near_ref, f32[32,128]{1,0:T(8,128)S(1)} %collective-permute-done.13.refs_4_.far_ref), custom_call_target="tpu_custom_call" | custom-call | flops 15625 | bytes 1562 | tf_op jit(solution)/shard_map/pallas_call | solution.py:392
  73.5 1.2 %shard_map.107 = f32[192,2048]{1,0:T(8,128)} custom-call(f32[192,1152]{1,0:T(8,128)S(1)} %get-tuple-element.33.refs_2_.refs_0_, f32[192,896]{1,0:T(8,128)S(1)} %get-tuple-element.46.refs_1_, bf16[192,1152]{1,0:T(8,128)(2,1)S(1)} %collective-permute-done.8.refs_5_.refs_0_.refs_2_, bf16[192,896]{1,0:T(8,128)(2,1)S(1)} %collective-permute-done.12.refs_3_, ...), custom_call_target="tpu_custom_call" | custom-call | flops 12288 | bytes 61440 | tf_op jit(solution)/shard_map/pallas_call | solution.py:242
  (29 shorter events, 1.7 us)
Async XLA Ops:
  0.6 3.2 %collective-permute-start.1 = (bf16[128,2048]{1,0:T(8,128)(2,1)}, bf16[128,2048]{1,0:T(8,128)(2,1)S(1)}, u32[]{:S(2)}, u32[]{:S(2)}) collective-permute-start(bf16[128,2048]{1,0:T(8,128)(2,1)} %refs_2_.5), channel_id=1, source_target_pairs={{0,1},{1,0},{2,3},{3,2},{4,5},{5,4},{6,7},{7,6},{8,9},{9,8},{10,11... | collective-permute-start | bytes 1572872 | tf_op jit(solution)/shard_map/ppermute | solution.py:420
  1.1 0.7 copy-start.5
  1.8 0.7 copy-start.6
  2.6 1.2 %collective-permute-start = (bf16[16,128]{1,0:T(8,128)(2,1)S(1)}, bf16[16,128]{1,0:T(8,128)(2,1)S(1)}, u32[]{:S(2)}, u32[]{:S(2)}) collective-permute-start(bf16[16,128]{1,0:T(8,128)(2,1)S(1)} %shard_map.94.refs_0_.meta_ref), channel_id=1, source_target_pairs={{0,1},{1,0},{2,3},{3,2},{4,5},{5,4},{6,7},{7,6},{8,9},{9,8},{10,11... | collective-permute-start | bytes 12296 | tf_op jit(solution)/shard_map/ppermute | solution.py:420
  3.8 1.0 %copy-start.1 = (bf16[128,2048]{1,0:T(8,128)(2,1)S(1)}, bf16[128,2048]{1,0:T(8,128)(2,1)}, u32[]{:S(2)}) copy-start(bf16[128,2048]{1,0:T(8,128)(2,1)} %refs_2_.5) | copy-start | bytes 1572868
  5.1 24.2 %copy-start.3 = (bf16[1,1,8,48,768]{4,3,2,1,0:T(8,128)(2,1)S(1)}, bf16[1,1,8,48,768]{4,3,2,1,0:T(8,128)(2,1)}, u32[]{:S(2)}) copy-start(bf16[1,1,8,48,768]{4,3,2,1,0:T(8,128)(2,1)} %param.9) | copy-start | bytes 1769476
  5.1 24.2 %copy-start.4 = (bf16[1,1,8,48,768]{4,3,2,1,0:T(8,128)(2,1)S(1)}, bf16[1,1,8,48,768]{4,3,2,1,0:T(8,128)(2,1)}, u32[]{:S(2)}) copy-start(bf16[1,1,8,48,768]{4,3,2,1,0:T(8,128)(2,1)} %param.10) | copy-start | bytes 1769476
  5.1 24.2 %collective-permute-start.3 = (bf16[192,1152]{1,0:T(8,128)(2,1)S(1)}, bf16[192,1152]{1,0:T(8,128)(2,1)S(1)}, u32[]{:S(2)}, u32[]{:S(2)}) collective-permute-start(bf16[192,1152]{1,0:T(8,128)(2,1)S(1)} %shard_map.96), channel_id=1, source_target_pairs={{0,4},{1,7},{2,6},{3,5},{4,0},{5,3},{6,2},{7,1},{8,12},{9,15},{10,... | collective-permute-start | bytes 1327112 | tf_op jit(solution)/shard_map/ppermute | solution.py:426
  9.4 19.8 %collective-permute-start.2 = (bf16[96,2048]{1,0:T(8,128)(2,1)S(1)}, bf16[96,2048]{1,0:T(8,128)(2,1)S(1)}, u32[]{:S(2)}, u32[]{:S(2)}) collective-permute-start(bf16[96,2048]{1,0:T(8,128)(2,1)S(1)} %get-tuple-element.28), channel_id=1, source_target_pairs={{0,2},{1,3},{2,0},{3,1},{4,6},{5,7},{6,4},{7,5},{8,10},{9,11},{10,... | collective-permute-start | bytes 1179656 | tf_op jit(solution)/shard_map/ppermute | solution.py:420
  29.3 1.8 %collective-permute-start.4 = (bf16[192,1152]{1,0:T(8,128)(2,1)S(1)}, bf16[192,1152]{1,0:T(8,128)(2,1)S(1)}, u32[]{:S(2)}, u32[]{:S(2)}) collective-permute-start(bf16[192,1152]{1,0:T(8,128)(2,1)S(1)} %shard_map.97.refs_2_), channel_id=1, source_target_pairs={{0,1},{1,0},{2,3},{3,2},{4,5},{5,4},{6,7},{7,6},{8,9},{9,8},{10,11... | collective-permute-start | bytes 1327112 | tf_op jit(solution)/shard_map/ppermute | solution.py:420
  30.4 3.6 %copy-start.2 = (bf16[128,2048]{1,0:T(8,128)(2,1)S(1)}, bf16[128,2048]{1,0:T(8,128)(2,1)}, u32[]{:S(2)}) copy-start(bf16[128,2048]{1,0:T(8,128)(2,1)} %refs_2_.5) | copy-start | bytes 1572868
  32.4 13.1 %collective-permute-start.6 = (bf16[384,1152]{1,0:T(8,128)(2,1)S(1)}, bf16[384,1152]{1,0:T(8,128)(2,1)S(1)}, u32[]{:S(2)}, u32[]{:S(2)}) collective-permute-start(bf16[384,1152]{1,0:T(8,128)(2,1)S(1)} %get-tuple-element.32), channel_id=1, source_target_pairs={{0,8},{1,17},{2,10},{3,19},{4,12},{5,21},{6,14},{7,23},{8,0},{9,25... | collective-permute-start | bytes 2654216 | tf_op jit(solution)/shard_map/ppermute | solution.py:436
  34.2 17.5 %collective-permute-start.5 = (bf16[192,896]{1,0:T(8,128)(2,1)S(1)}, bf16[192,896]{1,0:T(8,128)(2,1)S(1)}, u32[]{:S(2)}, u32[]{:S(2)}) collective-permute-start(bf16[192,896]{1,0:T(8,128)(2,1)S(1)} %shard_map.100), channel_id=1, source_target_pairs={{0,4},{1,7},{2,6},{3,5},{4,0},{5,3},{6,2},{7,1},{8,12},{9,15},{10,... | collective-permute-start | bytes 1032200 | tf_op jit(solution)/shard_map/ppermute | solution.py:426
  45.5 6.3 %copy-start = (bf16[1,768,2048]{2,1,0:T(8,128)(2,1)S(1)}, bf16[1,768,2048]{2,1,0:T(8,128)(2,1)}, u32[]{:S(2)}) copy-start(bf16[1,768,2048]{2,1,0:T(8,128)(2,1)} %param.11) | copy-start | bytes 9437188
  45.6 8.4 %collective-permute-start.8 = (bf16[192,1152]{1,0:T(8,128)(2,1)S(1)}, bf16[192,1152]{1,0:T(8,128)(2,1)S(1)}, u32[]{:S(2)}, u32[]{:S(2)}) collective-permute-start(bf16[192,1152]{1,0:T(8,128)(2,1)S(1)} %get-tuple-element.34), channel_id=1, source_target_pairs={{0,16},{1,9},{2,18},{3,11},{4,20},{5,13},{6,22},{7,15},{8,24},{9,1... | collective-permute-start | bytes 1327112 | tf_op jit(solution)/shard_map/ppermute | solution.py:436
  51.7 1.7 %collective-permute-start.7 = (bf16[192,896]{1,0:T(8,128)(2,1)S(1)}, bf16[192,896]{1,0:T(8,128)(2,1)S(1)}, u32[]{:S(2)}, u32[]{:S(2)}) collective-permute-start(bf16[192,896]{1,0:T(8,128)(2,1)S(1)} %shard_map.102.refs_2_), channel_id=1, source_target_pairs={{0,1},{1,0},{2,3},{3,2},{4,5},{5,4},{6,7},{7,6},{8,9},{9,8},{10,11... | collective-permute-start | bytes 1032200 | tf_op jit(solution)/shard_map/ppermute | solution.py:420
  55.0 11.0 %collective-permute-start.10 = (bf16[384,896]{1,0:T(8,128)(2,1)S(1)}, bf16[384,896]{1,0:T(8,128)(2,1)S(1)}, u32[]{:S(2)}, u32[]{:S(2)}) collective-permute-start(bf16[384,896]{1,0:T(8,128)(2,1)S(1)} %get-tuple-element.45), channel_id=1, source_target_pairs={{0,8},{1,17},{2,10},{3,19},{4,12},{5,21},{6,14},{7,23},{8,0},{9,25... | collective-permute-start | bytes 2064392 | tf_op jit(solution)/shard_map/ppermute | solution.py:436
  58.4 1.2 %collective-permute-start.9 = (f32[8,128]{1,0:T(8,128)S(1)}, f32[8,128]{1,0:T(8,128)S(1)}, u32[]{:S(2)}, u32[]{:S(2)}) collective-permute-start(f32[8,128]{1,0:T(8,128)S(1)} %get-tuple-element.40), channel_id=1, source_target_pairs={{0,1},{1,0},{2,3},{3,2},{4,5},{5,4},{6,7},{7,6},{8,9},{9,8},{10,11... | collective-permute-start | bytes 12296 | tf_op jit(solution)/shard_map/ppermute | solution.py:420
  59.6 3.7 %collective-permute-start.11 = (f32[16,128]{1,0:T(8,128)S(1)}, f32[16,128]{1,0:T(8,128)S(1)}, u32[]{:S(2)}, u32[]{:S(2)}) collective-permute-start(f32[16,128]{1,0:T(8,128)S(1)} %get-tuple-element.49.refs_0_), channel_id=1, source_target_pairs={{0,2},{1,3},{2,0},{3,1},{4,6},{5,7},{6,4},{7,5},{8,10},{9,11},{10,... | collective-permute-start | bytes 24584 | tf_op jit(solution)/shard_map/ppermute | solution.py:420
  66.1 7.3 %collective-permute-start.12 = (bf16[192,896]{1,0:T(8,128)(2,1)S(1)}, bf16[192,896]{1,0:T(8,128)(2,1)S(1)}, u32[]{:S(2)}, u32[]{:S(2)}) collective-permute-start(bf16[192,896]{1,0:T(8,128)(2,1)S(1)} %get-tuple-element.47), channel_id=1, source_target_pairs={{0,16},{1,9},{2,18},{3,11},{4,20},{5,13},{6,22},{7,15},{8,24},{9,1... | collective-permute-start | bytes 1032200 | tf_op jit(solution)/shard_map/ppermute | solution.py:436
  67.8 4.6 %collective-permute-start.13 = (f32[32,128]{1,0:T(8,128)S(1)}, f32[32,128]{1,0:T(8,128)S(1)}, u32[]{:S(2)}, u32[]{:S(2)}) collective-permute-start(f32[32,128]{1,0:T(8,128)S(1)} %constant_dynamic-update-slice_fusion.2.refs_1_.near_ref), channel_id=1, source_target_pairs={{0,4},{1,5},{2,6},{3,7},{4,0},{5,1},{6,2},{7,3},{8,12},{9,13},{10,... | collective-permute-start | bytes 49160 | tf_op jit(solution)/shard_map/ppermute | solution.py:420

commit v10 on v9

--- a/solution.py
+++ b/solution.py
@@ -444,9 +444,10 @@
     top_count = routes.shape[1]
     row_count = expert_count * capacity
 
-    meta = token_lines(routes.T, probs.T, expert_count)
-    metas = [meta, swap(meta, 1)]
     near_rows = [grad_out, swap(grad_out, 1)]
+    routes, probs = routes.T, probs.T
+    meta = token_lines(routes, probs, expert_count)
+    metas = [meta, token_lines(swap(routes, 1), swap(probs, 1), expert_count)]
     weight = w_down[0]
     turned, hidden, up_scale, gate_scale = hidden_parts(
         saved_gate.reshape(row_count, hidden_width), saved_up.reshape(row_count, hidden_width)

time: 74.9 us -> 74.3 us (level)
  waiting for transfers between devices: 45.9 us -> 44.8 us
    ppermute x8 -> x9, waiting for transfers between devices: 26.7 us -> 25.7 us  [swap(): lax.ppermute(value, 'expert', [(place, place ^ offset) for place in range...]
    ppermute x8 -> x9, starting transfers between devices: 3.36 us -> 3.75 us  [swap(): lax.ppermute(value, 'expert', [(place, place ^ offset) for place in range...]
  transfers between devices with their start and end apart: 14 -> 15, of which waited for: 13 -> 12; matrix products, arithmetic and copies ran while one was open for 0% -> 0% of each run, Pallas kernels for 10% -> 11%
where the time goes in v10:
time: 74.3 us; the launch traced here: 74.2 us
  waiting for transfers between devices  44.8 us (60%)
  starting transfers between devices  14.5 us (20%)
  Pallas kernels  11.7 us (16%)
  local copies, waits for them, and re-layouts  2.4 us (3%)
  between operations  0.79 us (1%)
    ppermute x9, waiting for transfers between devices, swap(): lax.ppermute(value, 'expert', [(place, place ^ offset) for place in range...  25.7 us
    ppermute x4, waiting for transfers between devices, swap_groups(): return lax.ppermute(value, ('dp', 'expert'), pairs)  14.4 us
    ppermute x4, starting transfers between devices, swap_groups(): return lax.ppermute(value, ('dp', 'expert'), pairs)  6.6 us
    ppermute x2, waiting for transfers between devices, swap_far(): return lax.ppermute(value, 'expert', pairs)  4.7 us
    ppermute x2, starting transfers between devices, swap_far(): return lax.ppermute(value, 'expert', pairs)  4.13 us
    ppermute x9, starting transfers between devices, swap(): lax.ppermute(value, 'expert', [(place, place ^ offset) for place in range...  3.75 us
    unnamed x16, local copies, waits for them, and re-layouts  2.4 us
    pallas_call x2, Pallas kernels, panel_parts(): pl.pallas_call(functools.partial(panel_kernel, capacity, start), in_specs...  2.24 us
  transfers between devices with their start and end apart: 15, of which 12 were waited for; matrix products, arithmetic and copies ran while one was open for 0% of the time, Pallas kernels for 11%

profile of v10, /device:TPU:0, one launch (start us, length us, event | category | flops | bytes accessed | tf_op | source)
XLA Modules:
  0.0 74.2 jit_solution(9171908677996191319)
XLA Ops:
  0.6 0.5 collective-permute-start.2
  1.2 0.4 collective-permute-start.1
  1.7 0.7 copy-done.5
  2.3 0.7 copy-done.6
  3.3 1.0 %copy-done.1 = bf16[128,2048]{1,0:T(8,128)(2,1)S(1)} copy-done((bf16[128,2048]{1,0:T(8,128)(2,1)S(1)}, bf16[128,2048]{1,0:T(8,128)(2,1)}, u32[]{:S(2)}) %copy-start.1) | copy-done | bytes 524312
  4.7 3.8 %collective-permute-start.4 = (bf16[192,1152]{1,0:T(8,128)(2,1)S(1)}, bf16[192,1152]{1,0:T(8,128)(2,1)S(1)}, u32[]{:S(2)}, u32[]{:S(2)}) collective-permute-start(bf16[192,1152]{1,0:T(8,128)(2,1)S(1)} %shard_map.97), channel_id=1, source_target_pairs={{0,4},{1,7},{2,6},{3,5},{4,0},{5,3},{6,2},{7,1},{8,12},{9,15},{10,... | collective-permute-start | bytes 1327112 | tf_op jit(solution)/shard_map/ppermute | solution.py:426
  8.4 0.4 shard_map.96
  8.8 1.6 %collective-permute-start.3 = (bf16[96,2048]{1,0:T(8,128)(2,1)S(1)}, bf16[96,2048]{1,0:T(8,128)(2,1)S(1)}, u32[]{:S(2)}, u32[]{:S(2)}) collective-permute-start(bf16[96,2048]{1,0:T(8,128)(2,1)S(1)} %get-tuple-element.28), channel_id=1, source_target_pairs={{0,2},{1,3},{2,0},{3,1},{4,6},{5,7},{6,4},{7,5},{8,10},{9,11},{10,... | collective-permute-start | bytes 1179656 | tf_op jit(solution)/shard_map/ppermute | solution.py:420
  10.4 18.1 %collective-permute-done.3.refs_1_ = bf16[96,2048]{1,0:T(8,128)(2,1)S(1)} collective-permute-done((bf16[96,2048]{1,0:T(8,128)(2,1)S(1)}, bf16[96,2048]{1,0:T(8,128)(2,1)S(1)}, u32[]{:S(2)}, u32[]{:S(2)}) %collective-permute-start.3) | collective-permute-done | bytes 393248 | tf_op jit(solution)/shard_map/ppermute | solution.py:420
  28.8 1.0 %shard_map.93 = (bf16[768,384]{1,0:T(8,128)(2,1)S(1)}, bf16[384,768]{1,0:T(8,128)(2,1)S(1)}, f32[384,768]{1,0:T(8,128)S(1)}, f32[384,768]{1,0:T(8,128)S(1)}) custom-call(bf16[384,768]{1,0:T(8,128)(2,1)S(1)} %bitcast.11, bf16[384,768]{1,0:T(8,128)(2,1)S(1)} %bitcast.12), custom_call_target="tpu_custom_call" | custom-call | flops 92160 | bytes 73728 | tf_op jit(solution)/shard_map/pallas_call | solution.py:133
  29.9 0.7 %collective-permute-done.5.refs_3_ = bf16[192,1152]{1,0:T(8,128)(2,1)S(1)} collective-permute-done((bf16[192,1152]{1,0:T(8,128)(2,1)S(1)}, bf16[192,1152]{1,0:T(8,128)(2,1)S(1)}, u32[]{:S(2)}, u32[]{:S(2)}) %collective-permute-start.5) | collective-permute-done | bytes 442400 | tf_op jit(solution)/shard_map/ppermute | solution.py:420
  30.6 1.2 %shard_map.99 = (bf16[384,1152]{1,0:T(8,128)(2,1)S(1)}, f32[192,1152]{1,0:T(8,128)S(1)}, f32[192,1152]{1,0:T(8,128)S(1)}, bf16[384,1152]{1,0:T(8,128)(2,1)S(1)}) custom-call(bf16[768,384]{1,0:T(8,128)(2,1)S(1)} %get-tuple-element.26.turned_ref, bf16[96,2048]{1,0:T(8,128)(2,1)S(1)} %get-tuple-element.27.refs_0_, ...), custom_call_target="tpu_custom_call" | custom-call | flops 10616832 | bytes 36864 | tf_op jit(solution)/shard_map/pallas_call | solution.py:182
  31.8 1.6 %collective-permute-start.7 = (bf16[384,1152]{1,0:T(8,128)(2,1)S(1)}, bf16[384,1152]{1,0:T(8,128)(2,1)S(1)}, u32[]{:S(2)}, u32[]{:S(2)}) collective-permute-start(bf16[384,1152]{1,0:T(8,128)(2,1)S(1)} %get-tuple-element.32), channel_id=1, source_target_pairs={{0,8},{1,17},{2,10},{3,19},{4,12},{5,21},{6,14},{7,23},{8,0},{9,25... | collective-permute-start | bytes 2654216 | tf_op jit(solution)/shard_map/ppermute | solution.py:436
  33.7 0.4 collective-permute-start.6
  34.1 10.9 %collective-permute-done.7.arrived_ref = bf16[384,1152]{1,0:T(8,128)(2,1)S(1)} collective-permute-done((bf16[384,1152]{1,0:T(8,128)(2,1)S(1)}, bf16[384,1152]{1,0:T(8,128)(2,1)S(1)}, u32[]{:S(2)}, u32[]{:S(2)}) %collective-permute-start.7) | collective-permute-done | bytes 884768 | tf_op jit(solution)/shard_map/ppermute | solution.py:436
  45.1 1.7 %collective-permute-start.9 = (bf16[192,1152]{1,0:T(8,128)(2,1)S(1)}, bf16[192,1152]{1,0:T(8,128)(2,1)S(1)}, u32[]{:S(2)}, u32[]{:S(2)}) collective-permute-start(bf16[192,1152]{1,0:T(8,128)(2,1)S(1)} %get-tuple-element.34), channel_id=1, source_target_pairs={{0,16},{1,9},{2,18},{3,11},{4,20},{5,13},{6,22},{7,15},{8,24},{9,1... | collective-permute-start | bytes 1327112 | tf_op jit(solution)/shard_map/ppermute | solution.py:436
  46.8 4.4 %collective-permute-done.6.refs_0_ = bf16[192,896]{1,0:T(8,128)(2,1)S(1)} collective-permute-done((bf16[192,896]{1,0:T(8,128)(2,1)S(1)}, bf16[192,896]{1,0:T(8,128)(2,1)S(1)}, u32[]{:S(2)}, u32[]{:S(2)}) %collective-permute-start.6) | collective-permute-done | bytes 344096 | tf_op jit(solution)/shard_map/ppermute | solution.py:426
  51.2 1.5 %shard_map.100.refs_4_.held_ref = f32[384,768]{1,0:T(8,128)S(1)} custom-call(bf16[384,1152]{1,0:T(8,128)(2,1)S(1)} %get-tuple-element.29.rows_ref, bf16[768,2048]{1,0:T(8,128)(2,1)S(1)} %bitcast.9), custom_call_target="tpu_custom_call" | custom-call | flops 10616832 | bytes 36864 | tf_op jit(solution)/shard_map/pallas_call | solution.py:280
  52.8 0.6 collective-permute-done.9.refs_5_.refs_0_.refs_2_
  53.5 1.0 %shard_map.104 = (bf16[384,896]{1,0:T(8,128)(2,1)S(1)}, f32[192,896]{1,0:T(8,128)S(1)}, f32[192,896]{1,0:T(8,128)S(1)}, bf16[384,896]{1,0:T(8,128)(2,1)S(1)}) custom-call(bf16[768,384]{1,0:T(8,128)(2,1)S(1)} %get-tuple-element.26.turned_ref, bf16[96,2048]{1,0:T(8,128)(2,1)S(1)} %get-tuple-element.27.refs_0_, ...), custom_call_target="tpu_custom_call" | custom-call | flops 8257536 | bytes 30720 | tf_op jit(solution)/shard_map/pallas_call | solution.py:182
  54.5 1.6 %collective-permute-start.11 = (bf16[384,896]{1,0:T(8,128)(2,1)S(1)}, bf16[384,896]{1,0:T(8,128)(2,1)S(1)}, u32[]{:S(2)}, u32[]{:S(2)}) collective-permute-start(bf16[384,896]{1,0:T(8,128)(2,1)S(1)} %get-tuple-element.45), channel_id=1, source_target_pairs={{0,8},{1,17},{2,10},{3,19},{4,12},{5,21},{6,14},{7,23},{8,0},{9,25... | collective-permute-start | bytes 2064392 | tf_op jit(solution)/shard_map/ppermute | solution.py:436
  56.1 1.7 %shard_map.105 = (f32[384,768]{1,0:T(8,128)S(1)}, f32[8,128]{1,0:T(8,128)S(1)}) custom-call(f32[384,768]{1,0:T(8,128)S(1)} %shard_map.100.refs_4_.held_ref, bf16[384,896]{1,0:T(8,128)(2,1)S(1)} %get-tuple-element.35.rows_ref, bf16[768,2048]{1,0:T(8,128)(2,1)S(1)} %bitcast.10, bf16[384,768]{1,0:T(8,128)(2,1)S(1)} %get-tuple-element.36.hidden_ref), custom_call_target="tpu_custom_call" | custom-call | flops 8257536 | bytes 55296 | tf_op jit(solution)/shard_map/pallas_call | solution.py:326
  58.0 1.1 %collective-permute-done.10 = f32[8,128]{1,0:T(8,128)S(1)} collective-permute-done((f32[8,128]{1,0:T(8,128)S(1)}, f32[8,128]{1,0:T(8,128)S(1)}, u32[]{:S(2)}, u32[]{:S(2)}) %collective-permute-start.10) | collective-permute-done | bytes 4128 | tf_op jit(solution)/shard_map/ppermute | solution.py:420
  59.1 0.7 collective-permute-start.12
  59.8 3.0 %collective-permute-done.12 = f32[16,128]{1,0:T(8,128)S(1)} collective-permute-done((f32[16,128]{1,0:T(8,128)S(1)}, f32[16,128]{1,0:T(8,128)S(1)}, u32[]{:S(2)}, u32[]{:S(2)}) %collective-permute-start.12) | collective-permute-done | bytes 8224 | tf_op jit(solution)/shard_map/ppermute | solution.py:420
  62.8 2.7 %collective-permute-done.11.arrived_ref = bf16[384,896]{1,0:T(8,128)(2,1)S(1)} collective-permute-done((bf16[384,896]{1,0:T(8,128)(2,1)S(1)}, bf16[384,896]{1,0:T(8,128)(2,1)S(1)}, u32[]{:S(2)}, u32[]{:S(2)}) %collective-permute-start.11) | collective-permute-done | bytes 688160 | tf_op jit(solution)/shard_map/ppermute | solution.py:436
  65.6 1.7 %collective-permute-start.13 = (bf16[192,896]{1,0:T(8,128)(2,1)S(1)}, bf16[192,896]{1,0:T(8,128)(2,1)S(1)}, u32[]{:S(2)}, u32[]{:S(2)}) collective-permute-start(bf16[192,896]{1,0:T(8,128)(2,1)S(1)} %get-tuple-element.47), channel_id=1, source_target_pairs={{0,16},{1,9},{2,18},{3,11},{4,20},{5,13},{6,22},{7,15},{8,24},{9,1... | collective-permute-start | bytes 1032200 | tf_op jit(solution)/shard_map/ppermute | solution.py:436
  67.3 0.3 collective-permute-start.14
  67.6 1.8 %shard_map.106 = (bf16[384,768]{1,0:T(8,128)(2,1)}, bf16[384,768]{1,0:T(8,128)(2,1)}) custom-call(f32[384,768]{1,0:T(8,128)S(1)} %get-tuple-element.37.grad_ref, f32[384,768]{1,0:T(8,128)S(1)} %get-tuple-element.38.up_scale_ref, f32[384,768]{1,0:T(8,128)S(1)} %get-tuple-element.39.gate_scale_ref, f32[16,128]{1,0:T(8,128)S(1)} %get-tuple-element.49.refs_0_), custom_call_target="tpu_custom_call" | custom-call | flops 9216 | bytes 73728 | tf_op jit(solution)/shard_map/pallas_call | solution.py:356
  69.4 2.6 %collective-permute-done.14.refs_4_.far_ref = f32[32,128]{1,0:T(8,128)S(1)} collective-permute-done((f32[32,128]{1,0:T(8,128)S(1)}, f32[32,128]{1,0:T(8,128)S(1)}, u32[]{:S(2)}, u32[]{:S(2)}) %collective-permute-start.14) | collective-permute-done | bytes 16416 | tf_op jit(solution)/shard_map/ppermute | solution.py:420
  71.9 0.8 %shard_map.109 = f32[2,128]{1,0:T(2,128)} custom-call(bf16[16,128]{1,0:T(8,128)(2,1)S(1)} %shard_map.94.refs_0_.meta_ref, f32[32,128]{1,0:T(8,128)S(1)} %constant_dynamic-update-slice_fusion.2.refs_1_.near_ref, f32[32,128]{1,0:T(8,128)S(1)} %collective-permute-done.14.refs_4_.far_ref), custom_call_target="tpu_custom_call" | custom-call | flops 15625 | bytes 1562 | tf_op jit(solution)/shard_map/pallas_call | solution.py:392
  72.9 1.2 %shard_map.108 = f32[192,2048]{1,0:T(8,128)} custom-call(f32[192,1152]{1,0:T(8,128)S(1)} %get-tuple-element.33.refs_2_.refs_0_, f32[192,896]{1,0:T(8,128)S(1)} %get-tuple-element.46.refs_1_, bf16[192,1152]{1,0:T(8,128)(2,1)S(1)} %collective-permute-done.9.refs_5_.refs_0_.refs_2_, bf16[192,896]{1,0:T(8,128)(2,1)S(1)} %collective-permute-done.13.refs_3_, ...), custom_call_target="tpu_custom_call" | custom-call | flops 12288 | bytes 61440 | tf_op jit(solution)/shard_map/pallas_call | solution.py:242
  (32 shorter events, 1.9 us)
Async XLA Ops:
  0.6 2.7 %collective-permute-start.2 = (bf16[128,2048]{1,0:T(8,128)(2,1)}, bf16[128,2048]{1,0:T(8,128)(2,1)S(1)}, u32[]{:S(2)}, u32[]{:S(2)}) collective-permute-start(bf16[128,2048]{1,0:T(8,128)(2,1)} %refs_2_.5), channel_id=1, source_target_pairs={{0,1},{1,0},{2,3},{3,2},{4,5},{5,4},{6,7},{7,6},{8,9},{9,8},{10,11... | collective-permute-start | bytes 1572872 | tf_op jit(solution)/shard_map/ppermute | solution.py:420
  1.1 2.0 %collective-permute-start = (s32[2,128]{1,0:T(2,128)}, s32[2,128]{1,0:T(2,128)S(1)}, u32[]{:S(2)}, u32[]{:S(2)}) collective-permute-start(s32[2,128]{1,0:T(2,128)} %bitcast.13), channel_id=1, source_target_pairs={{0,1},{1,0},{2,3},{3,2},{4,5},{5,4},{6,7},{7,6},{8,9},{9,8},{10,11... | collective-permute-start | bytes 3080 | tf_op jit(solution)/shard_map/ppermute | solution.py:420
  1.2 1.9 %collective-permute-start.1 = (bf16[2,128]{1,0:T(2,128)(2,1)}, bf16[2,128]{1,0:T(2,128)(2,1)S(1)}, u32[]{:S(2)}, u32[]{:S(2)}) collective-permute-start(bf16[2,128]{1,0:T(2,128)(2,1)} %bitcast.15), channel_id=1, source_target_pairs={{0,1},{1,0},{2,3},{3,2},{4,5},{5,4},{6,7},{7,6},{8,9},{9,8},{10,11... | collective-permute-start | bytes 1544 | tf_op jit(solution)/shard_map/ppermute | solution.py:420
  1.7 0.7 copy-start.5
  2.3 0.7 copy-start.6
  3.3 1.0 %copy-start.1 = (bf16[128,2048]{1,0:T(8,128)(2,1)S(1)}, bf16[128,2048]{1,0:T(8,128)(2,1)}, u32[]{:S(2)}) copy-start(bf16[128,2048]{1,0:T(8,128)(2,1)} %refs_2_.5) | copy-start | bytes 1572868
  4.6 24.2 %copy-start.3 = (bf16[1,1,8,48,768]{4,3,2,1,0:T(8,128)(2,1)S(1)}, bf16[1,1,8,48,768]{4,3,2,1,0:T(8,128)(2,1)}, u32[]{:S(2)}) copy-start(bf16[1,1,8,48,768]{4,3,2,1,0:T(8,128)(2,1)} %param.9) | copy-start | bytes 1769476
  4.6 24.2 %copy-start.4 = (bf16[1,1,8,48,768]{4,3,2,1,0:T(8,128)(2,1)S(1)}, bf16[1,1,8,48,768]{4,3,2,1,0:T(8,128)(2,1)}, u32[]{:S(2)}) copy-start(bf16[1,1,8,48,768]{4,3,2,1,0:T(8,128)(2,1)} %param.10) | copy-start | bytes 1769476
  4.7 24.2 %collective-permute-start.4 = (bf16[192,1152]{1,0:T(8,128)(2,1)S(1)}, bf16[192,1152]{1,0:T(8,128)(2,1)S(1)}, u32[]{:S(2)}, u32[]{:S(2)}) collective-permute-start(bf16[192,1152]{1,0:T(8,128)(2,1)S(1)} %shard_map.97), channel_id=1, source_target_pairs={{0,4},{1,7},{2,6},{3,5},{4,0},{5,3},{6,2},{7,1},{8,12},{9,15},{10,... | collective-permute-start | bytes 1327112 | tf_op jit(solution)/shard_map/ppermute | solution.py:426
  8.8 19.7 %collective-permute-start.3 = (bf16[96,2048]{1,0:T(8,128)(2,1)S(1)}, bf16[96,2048]{1,0:T(8,128)(2,1)S(1)}, u32[]{:S(2)}, u32[]{:S(2)}) collective-permute-start(bf16[96,2048]{1,0:T(8,128)(2,1)S(1)} %get-tuple-element.28), channel_id=1, source_target_pairs={{0,2},{1,3},{2,0},{3,1},{4,6},{5,7},{6,4},{7,5},{8,10},{9,11},{10,... | collective-permute-start | bytes 1179656 | tf_op jit(solution)/shard_map/ppermute | solution.py:420
  28.8 1.8 %collective-permute-start.5 = (bf16[192,1152]{1,0:T(8,128)(2,1)S(1)}, bf16[192,1152]{1,0:T(8,128)(2,1)S(1)}, u32[]{:S(2)}, u32[]{:S(2)}) collective-permute-start(bf16[192,1152]{1,0:T(8,128)(2,1)S(1)} %shard_map.98.refs_2_), channel_id=1, source_target_pairs={{0,1},{1,0},{2,3},{3,2},{4,5},{5,4},{6,7},{7,6},{8,9},{9,8},{10,11... | collective-permute-start | bytes 1327112 | tf_op jit(solution)/shard_map/ppermute | solution.py:420
  29.8 3.6 %copy-start.2 = (bf16[128,2048]{1,0:T(8,128)(2,1)S(1)}, bf16[128,2048]{1,0:T(8,128)(2,1)}, u32[]{:S(2)}) copy-start(bf16[128,2048]{1,0:T(8,128)(2,1)} %refs_2_.5) | copy-start | bytes 1572868
  31.8 13.1 %collective-permute-start.7 = (bf16[384,1152]{1,0:T(8,128)(2,1)S(1)}, bf16[384,1152]{1,0:T(8,128)(2,1)S(1)}, u32[]{:S(2)}, u32[]{:S(2)}) collective-permute-start(bf16[384,1152]{1,0:T(8,128)(2,1)S(1)} %get-tuple-element.32), channel_id=1, source_target_pairs={{0,8},{1,17},{2,10},{3,19},{4,12},{5,21},{6,14},{7,23},{8,0},{9,25... | collective-permute-start | bytes 2654216 | tf_op jit(solution)/shard_map/ppermute | solution.py:436
  33.7 17.5 %collective-permute-start.6 = (bf16[192,896]{1,0:T(8,128)(2,1)S(1)}, bf16[192,896]{1,0:T(8,128)(2,1)S(1)}, u32[]{:S(2)}, u32[]{:S(2)}) collective-permute-start(bf16[192,896]{1,0:T(8,128)(2,1)S(1)} %shard_map.101), channel_id=1, source_target_pairs={{0,4},{1,7},{2,6},{3,5},{4,0},{5,3},{6,2},{7,1},{8,12},{9,15},{10,... | collective-permute-start | bytes 1032200 | tf_op jit(solution)/shard_map/ppermute | solution.py:426
  44.9 6.2 %copy-start = (bf16[1,768,2048]{2,1,0:T(8,128)(2,1)S(1)}, bf16[1,768,2048]{2,1,0:T(8,128)(2,1)}, u32[]{:S(2)}) copy-start(bf16[1,768,2048]{2,1,0:T(8,128)(2,1)} %param.11) | copy-start | bytes 9437188
  45.1 8.4 %collective-permute-start.9 = (bf16[192,1152]{1,0:T(8,128)(2,1)S(1)}, bf16[192,1152]{1,0:T(8,128)(2,1)S(1)}, u32[]{:S(2)}, u32[]{:S(2)}) collective-permute-start(bf16[192,1152]{1,0:T(8,128)(2,1)S(1)} %get-tuple-element.34), channel_id=1, source_target_pairs={{0,16},{1,9},{2,18},{3,11},{4,20},{5,13},{6,22},{7,15},{8,24},{9,1... | collective-permute-start | bytes 1327112 | tf_op jit(solution)/shard_map/ppermute | solution.py:436
  51.2 1.7 %collective-permute-start.8 = (bf16[192,896]{1,0:T(8,128)(2,1)S(1)}, bf16[192,896]{1,0:T(8,128)(2,1)S(1)}, u32[]{:S(2)}, u32[]{:S(2)}) collective-permute-start(bf16[192,896]{1,0:T(8,128)(2,1)S(1)} %shard_map.103.refs_2_), channel_id=1, source_target_pairs={{0,1},{1,0},{2,3},{3,2},{4,5},{5,4},{6,7},{7,6},{8,9},{9,8},{10,11... | collective-permute-start | bytes 1032200 | tf_op jit(solution)/shard_map/ppermute | solution.py:420
  54.5 11.0 %collective-permute-start.11 = (bf16[384,896]{1,0:T(8,128)(2,1)S(1)}, bf16[384,896]{1,0:T(8,128)(2,1)S(1)}, u32[]{:S(2)}, u32[]{:S(2)}) collective-permute-start(bf16[384,896]{1,0:T(8,128)(2,1)S(1)} %get-tuple-element.45), channel_id=1, source_target_pairs={{0,8},{1,17},{2,10},{3,19},{4,12},{5,21},{6,14},{7,23},{8,0},{9,25... | collective-permute-start | bytes 2064392 | tf_op jit(solution)/shard_map/ppermute | solution.py:436
  57.9 1.2 %collective-permute-start.10 = (f32[8,128]{1,0:T(8,128)S(1)}, f32[8,128]{1,0:T(8,128)S(1)}, u32[]{:S(2)}, u32[]{:S(2)}) collective-permute-start(f32[8,128]{1,0:T(8,128)S(1)} %get-tuple-element.40), channel_id=1, source_target_pairs={{0,1},{1,0},{2,3},{3,2},{4,5},{5,4},{6,7},{7,6},{8,9},{9,8},{10,11... | collective-permute-start | bytes 12296 | tf_op jit(solution)/shard_map/ppermute | solution.py:420
  59.1 3.7 %collective-permute-start.12 = (f32[16,128]{1,0:T(8,128)S(1)}, f32[16,128]{1,0:T(8,128)S(1)}, u32[]{:S(2)}, u32[]{:S(2)}) collective-permute-start(f32[16,128]{1,0:T(8,128)S(1)} %get-tuple-element.49.refs_0_), channel_id=1, source_target_pairs={{0,2},{1,3},{2,0},{3,1},{4,6},{5,7},{6,4},{7,5},{8,10},{9,11},{10,... | collective-permute-start | bytes 24584 | tf_op jit(solution)/shard_map/ppermute | solution.py:420
  65.6 7.3 %collective-permute-start.13 = (bf16[192,896]{1,0:T(8,128)(2,1)S(1)}, bf16[192,896]{1,0:T(8,128)(2,1)S(1)}, u32[]{:S(2)}, u32[]{:S(2)}) collective-permute-start(bf16[192,896]{1,0:T(8,128)(2,1)S(1)} %get-tuple-element.47), channel_id=1, source_target_pairs={{0,16},{1,9},{2,18},{3,11},{4,20},{5,13},{6,22},{7,15},{8,24},{9,1... | collective-permute-start | bytes 1032200 | tf_op jit(solution)/shard_map/ppermute | solution.py:436
  67.3 4.6 %collective-permute-start.14 = (f32[32,128]{1,0:T(8,128)S(1)}, f32[32,128]{1,0:T(8,128)S(1)}, u32[]{:S(2)}, u32[]{:S(2)}) collective-permute-start(f32[32,128]{1,0:T(8,128)S(1)} %constant_dynamic-update-slice_fusion.2.refs_1_.near_ref), channel_id=1, source_target_pairs={{0,4},{1,5},{2,6},{3,7},{4,0},{5,1},{6,2},{7,3},{8,12},{9,13},{10,... | collective-permute-start | bytes 49160 | tf_op jit(solution)/shard_map/ppermute | solution.py:420

commit v11 on v10

--- a/solution.py
+++ b/solution.py
@@ -217,38 +217,30 @@
     )(own, later, arrived, *earlier)
 
 
-def total_kernel(count, *refs):
-    own_refs, arrived_refs = refs[:count], refs[count : 2 * count]
-    total_ref, *sum_refs, semaphores = refs[-2 - count :]
-    copies = []
-    start = 0
-    for place, (own_ref, arrived_ref) in enumerate(zip(own_refs, arrived_refs)):
-        width = own_ref.shape[1]
-        sum_refs[place][...] = own_ref[...] + arrived_ref[...].astype(jnp.float32)
-        copies.append(
-            pltpu.make_async_copy(
-                sum_refs[place], total_ref.at[:, start : start + width], semaphores.at[place]
-            )
-        )
-        copies[-1].start()
-        start += width
-    for copy in copies:
-        copy.wait()
-
-
-def total(owns, arrived, earlier):
-    share = owns[0].shape[0]
-    size = share * sum(own.shape[1] for own in owns)
-    return pl.pallas_call(
-        functools.partial(total_kernel, len(owns)),
-        in_specs=[VMEM] * (2 * len(owns)) + [ANY] * len(earlier),
+def total_kernel(start, *refs):
+    own_ref, arrived_ref = refs[:2]
+    total_ref, sum_ref, semaphore = refs[-3:]
+    sum_ref[...] = own_ref[...] + arrived_ref[...].astype(jnp.float32)
+    copy = pltpu.make_async_copy(
+        sum_ref, total_ref.at[:, start : start + sum_ref.shape[1]], semaphore
+    )
+    copy.start()
+    copy.wait()
+
+
+def total(held, own, arrived, start, model_width, earlier):
+    share, width = own.shape
+    extra = ([] if held is None else [held]) + list(earlier)
+    return pl.pallas_call(
+        functools.partial(total_kernel, start),
+        in_specs=[VMEM] * 2 + [ANY] * len(extra),
         out_specs=ANY,
-        out_shape=jax.ShapeDtypeStruct((share, size // share), jnp.float32),
-        scratch_shapes=[pltpu.VMEM(own.shape, jnp.float32) for own in owns]
-        + [pltpu.SemaphoreType.DMA((len(owns),))],
-        compiler_params=params(),
-        cost_estimate=cost(2 * size, 10 * size),
-    )(*owns, *arrived, *earlier)
+        out_shape=jax.ShapeDtypeStruct((share, model_width), jnp.float32),
+        scratch_shapes=[pltpu.VMEM((share, width), jnp.float32), pltpu.SemaphoreType.DMA],
+        input_output_aliases={} if held is None else {2: 0},
+        compiler_params=params(),
+        cost_estimate=cost(2 * share * width, 10 * share * width),
+    )(own, arrived, *extra)
 
 
 def rows_times_weight(start, rows_ref, weight_ref):
@@ -478,7 +470,11 @@
         arrived.append(swap_groups(half, True))
         start += width
     far_lines = swap(lines, 4)
-    panel = total(owns, arrived, [far_lines])
+    panel, start = None, 0
+    for own, half in zip(owns, arrived):
+        last = start + own.shape[1] == model_width
+        panel = total(panel, own, half, start, model_width, [far_lines] if last else [])
+        start += own.shape[1]
     route_grad = route_back(meta, lines, far_lines, expert_count, top_count, capacity)
     return (
         grad_gate.reshape(saved_gate.shape),

time: 74.3 us -> 74 us (level)
  waiting for transfers between devices: 44.8 us -> 43.8 us
    ppermute x9, waiting for transfers between devices: 25.7 us -> 24.7 us  [swap(): lax.ppermute(value, 'expert', [(place, place ^ offset) for place in range...]
    pallas_call x1 -> x2, Pallas kernels: 1.23 us -> 1.92 us  [total(): pl.pallas_call(functools.partial(total_kernel, start), in_specs=[VMEM] *...]
  transfers between devices with their start and end apart: 15 -> 15, of which waited for: 12 -> 12; matrix products, arithmetic and copies ran while one was open for 0% -> 0% of each run, Pallas kernels for 11% -> 12%
where the time goes in v11:
time: 74 us; the launch traced here: 73.8 us
  waiting for transfers between devices  43.8 us (59%)
  starting transfers between devices  14.5 us (20%)
  Pallas kernels  12.4 us (17%)
  local copies, waits for them, and re-layouts  2.4 us (3%)
  between operations  0.8 us (1%)
    ppermute x9, waiting for transfers between devices, swap(): lax.ppermute(value, 'expert', [(place, place ^ offset) for place in range...  24.7 us
    ppermute x4, waiting for transfers between devices, swap_groups(): return lax.ppermute(value, ('dp', 'expert'), pairs)  14.4 us
    ppermute x4, starting transfers between devices, swap_groups(): return lax.ppermute(value, ('dp', 'expert'), pairs)  6.6 us
    ppermute x2, waiting for transfers between devices, swap_far(): return lax.ppermute(value, 'expert', pairs)  4.7 us
    ppermute x2, starting transfers between devices, swap_far(): return lax.ppermute(value, 'expert', pairs)  4.13 us
    ppermute x9, starting transfers between devices, swap(): lax.ppermute(value, 'expert', [(place, place ^ offset) for place in range...  3.75 us
    unnamed x16, local copies, waits for them, and re-layouts  2.4 us
    pallas_call x2, Pallas kernels, panel_parts(): pl.pallas_call(functools.partial(panel_kernel, capacity, start), in_specs...  2.24 us
  transfers between devices with their start and end apart: 15, of which 12 were waited for; matrix products, arithmetic and copies ran while one was open for 0% of the time, Pallas kernels for 12%

profile of v11, /device:TPU:0, one launch (start us, length us, event | category | flops | bytes accessed | tf_op | source)
XLA Modules:
  0.0 73.8 jit_solution(15673816773668452737)
XLA Ops:
  0.6 0.5 collective-permute-start.2
  1.2 0.4 collective-permute-start.1
  1.7 0.7 copy-done.5
  2.3 0.7 copy-done.6
  3.3 1.0 %copy-done.1 = bf16[128,2048]{1,0:T(8,128)(2,1)S(1)} copy-done((bf16[128,2048]{1,0:T(8,128)(2,1)S(1)}, bf16[128,2048]{1,0:T(8,128)(2,1)}, u32[]{:S(2)}) %copy-start.1) | copy-done | bytes 524312
  4.7 3.8 %collective-permute-start.4 = (bf16[192,1152]{1,0:T(8,128)(2,1)S(1)}, bf16[192,1152]{1,0:T(8,128)(2,1)S(1)}, u32[]{:S(2)}, u32[]{:S(2)}) collective-permute-start(bf16[192,1152]{1,0:T(8,128)(2,1)S(1)} %shard_map.97), channel_id=1, source_target_pairs={{0,4},{1,7},{2,6},{3,5},{4,0},{5,3},{6,2},{7,1},{8,12},{9,15},{10,... | collective-permute-start | bytes 1327112 | tf_op jit(solution)/shard_map/ppermute | solution.py:418
  8.4 0.4 shard_map.96
  8.8 1.6 %collective-permute-start.3 = (bf16[96,2048]{1,0:T(8,128)(2,1)S(1)}, bf16[96,2048]{1,0:T(8,128)(2,1)S(1)}, u32[]{:S(2)}, u32[]{:S(2)}) collective-permute-start(bf16[96,2048]{1,0:T(8,128)(2,1)S(1)} %get-tuple-element.28), channel_id=1, source_target_pairs={{0,2},{1,3},{2,0},{3,1},{4,6},{5,7},{6,4},{7,5},{8,10},{9,11},{10,... | collective-permute-start | bytes 1179656 | tf_op jit(solution)/shard_map/ppermute | solution.py:412
  10.4 18.1 %collective-permute-done.3.refs_1_ = bf16[96,2048]{1,0:T(8,128)(2,1)S(1)} collective-permute-done((bf16[96,2048]{1,0:T(8,128)(2,1)S(1)}, bf16[96,2048]{1,0:T(8,128)(2,1)S(1)}, u32[]{:S(2)}, u32[]{:S(2)}) %collective-permute-start.3) | collective-permute-done | bytes 393248 | tf_op jit(solution)/shard_map/ppermute | solution.py:412
  28.8 1.0 %shard_map.93 = (bf16[768,384]{1,0:T(8,128)(2,1)S(1)}, bf16[384,768]{1,0:T(8,128)(2,1)S(1)}, f32[384,768]{1,0:T(8,128)S(1)}, f32[384,768]{1,0:T(8,128)S(1)}) custom-call(bf16[384,768]{1,0:T(8,128)(2,1)S(1)} %bitcast.11, bf16[384,768]{1,0:T(8,128)(2,1)S(1)} %bitcast.12), custom_call_target="tpu_custom_call" | custom-call | flops 92160 | bytes 73728 | tf_op jit(solution)/shard_map/pallas_call | solution.py:133
  29.9 0.7 %collective-permute-done.5.refs_3_ = bf16[192,1152]{1,0:T(8,128)(2,1)S(1)} collective-permute-done((bf16[192,1152]{1,0:T(8,128)(2,1)S(1)}, bf16[192,1152]{1,0:T(8,128)(2,1)S(1)}, u32[]{:S(2)}, u32[]{:S(2)}) %collective-permute-start.5) | collective-permute-done | bytes 442400 | tf_op jit(solution)/shard_map/ppermute | solution.py:412
  30.6 1.2 %shard_map.99 = (bf16[384,1152]{1,0:T(8,128)(2,1)S(1)}, f32[192,1152]{1,0:T(8,128)S(1)}, f32[192,1152]{1,0:T(8,128)S(1)}, bf16[384,1152]{1,0:T(8,128)(2,1)S(1)}) custom-call(bf16[768,384]{1,0:T(8,128)(2,1)S(1)} %get-tuple-element.26.turned_ref, bf16[96,2048]{1,0:T(8,128)(2,1)S(1)} %get-tuple-element.27.refs_0_, ...), custom_call_target="tpu_custom_call" | custom-call | flops 10616832 | bytes 36864 | tf_op jit(solution)/shard_map/pallas_call | solution.py:182
  31.8 1.6 %collective-permute-start.7 = (bf16[384,1152]{1,0:T(8,128)(2,1)S(1)}, bf16[384,1152]{1,0:T(8,128)(2,1)S(1)}, u32[]{:S(2)}, u32[]{:S(2)}) collective-permute-start(bf16[384,1152]{1,0:T(8,128)(2,1)S(1)} %get-tuple-element.32), channel_id=1, source_target_pairs={{0,8},{1,17},{2,10},{3,19},{4,12},{5,21},{6,14},{7,23},{8,0},{9,25... | collective-permute-start | bytes 2654216 | tf_op jit(solution)/shard_map/ppermute | solution.py:428
  33.7 0.4 collective-permute-start.6
  34.1 10.9 %collective-permute-done.7.arrived_ref = bf16[384,1152]{1,0:T(8,128)(2,1)S(1)} collective-permute-done((bf16[384,1152]{1,0:T(8,128)(2,1)S(1)}, bf16[384,1152]{1,0:T(8,128)(2,1)S(1)}, u32[]{:S(2)}, u32[]{:S(2)}) %collective-permute-start.7) | collective-permute-done | bytes 884768 | tf_op jit(solution)/shard_map/ppermute | solution.py:428
  45.1 1.7 %collective-permute-start.9 = (bf16[192,1152]{1,0:T(8,128)(2,1)S(1)}, bf16[192,1152]{1,0:T(8,128)(2,1)S(1)}, u32[]{:S(2)}, u32[]{:S(2)}) collective-permute-start(bf16[192,1152]{1,0:T(8,128)(2,1)S(1)} %get-tuple-element.34), channel_id=1, source_target_pairs={{0,16},{1,9},{2,18},{3,11},{4,20},{5,13},{6,22},{7,15},{8,24},{9,1... | collective-permute-start | bytes 1327112 | tf_op jit(solution)/shard_map/ppermute | solution.py:428
  46.8 4.4 %collective-permute-done.6.refs_0_ = bf16[192,896]{1,0:T(8,128)(2,1)S(1)} collective-permute-done((bf16[192,896]{1,0:T(8,128)(2,1)S(1)}, bf16[192,896]{1,0:T(8,128)(2,1)S(1)}, u32[]{:S(2)}, u32[]{:S(2)}) %collective-permute-start.6) | collective-permute-done | bytes 344096 | tf_op jit(solution)/shard_map/ppermute | solution.py:418
  51.2 1.5 %shard_map.100.refs_4_.held_ref = f32[384,768]{1,0:T(8,128)S(1)} custom-call(bf16[384,1152]{1,0:T(8,128)(2,1)S(1)} %get-tuple-element.29.rows_ref, bf16[768,2048]{1,0:T(8,128)(2,1)S(1)} %bitcast.9), custom_call_target="tpu_custom_call" | custom-call | flops 10616832 | bytes 36864 | tf_op jit(solution)/shard_map/pallas_call | solution.py:272
  52.8 0.6 collective-permute-done.9.refs_5_.refs_0_.refs_1_
  53.5 1.0 %shard_map.104 = (bf16[384,896]{1,0:T(8,128)(2,1)S(1)}, f32[192,896]{1,0:T(8,128)S(1)}, f32[192,896]{1,0:T(8,128)S(1)}, bf16[384,896]{1,0:T(8,128)(2,1)S(1)}) custom-call(bf16[768,384]{1,0:T(8,128)(2,1)S(1)} %get-tuple-element.26.turned_ref, bf16[96,2048]{1,0:T(8,128)(2,1)S(1)} %get-tuple-element.27.refs_0_, ...), custom_call_target="tpu_custom_call" | custom-call | flops 8257536 | bytes 30720 | tf_op jit(solution)/shard_map/pallas_call | solution.py:182
  54.5 1.6 %collective-permute-start.11 = (bf16[384,896]{1,0:T(8,128)(2,1)S(1)}, bf16[384,896]{1,0:T(8,128)(2,1)S(1)}, u32[]{:S(2)}, u32[]{:S(2)}) collective-permute-start(bf16[384,896]{1,0:T(8,128)(2,1)S(1)} %get-tuple-element.45), channel_id=1, source_target_pairs={{0,8},{1,17},{2,10},{3,19},{4,12},{5,21},{6,14},{7,23},{8,0},{9,25... | collective-permute-start | bytes 2064392 | tf_op jit(solution)/shard_map/ppermute | solution.py:428
  56.1 1.7 %shard_map.105 = (f32[384,768]{1,0:T(8,128)S(1)}, f32[8,128]{1,0:T(8,128)S(1)}) custom-call(f32[384,768]{1,0:T(8,128)S(1)} %shard_map.100.refs_4_.held_ref, bf16[384,896]{1,0:T(8,128)(2,1)S(1)} %get-tuple-element.35.rows_ref, bf16[768,2048]{1,0:T(8,128)(2,1)S(1)} %bitcast.10, bf16[384,768]{1,0:T(8,128)(2,1)S(1)} %get-tuple-element.36.hidden_ref), custom_call_target="tpu_custom_call" | custom-call | flops 8257536 | bytes 55296 | tf_op jit(solution)/shard_map/pallas_call | solution.py:318
  58.0 1.1 %collective-permute-done.10 = f32[8,128]{1,0:T(8,128)S(1)} collective-permute-done((f32[8,128]{1,0:T(8,128)S(1)}, f32[8,128]{1,0:T(8,128)S(1)}, u32[]{:S(2)}, u32[]{:S(2)}) %collective-permute-start.10) | collective-permute-done | bytes 4128 | tf_op jit(solution)/shard_map/ppermute | solution.py:412
  59.1 0.7 collective-permute-start.12
  59.8 3.0 %collective-permute-done.12 = f32[16,128]{1,0:T(8,128)S(1)} collective-permute-done((f32[16,128]{1,0:T(8,128)S(1)}, f32[16,128]{1,0:T(8,128)S(1)}, u32[]{:S(2)}, u32[]{:S(2)}) %collective-permute-start.12) | collective-permute-done | bytes 8224 | tf_op jit(solution)/shard_map/ppermute | solution.py:412
  62.8 2.7 %collective-permute-done.11.arrived_ref = bf16[384,896]{1,0:T(8,128)(2,1)S(1)} collective-permute-done((bf16[384,896]{1,0:T(8,128)(2,1)S(1)}, bf16[384,896]{1,0:T(8,128)(2,1)S(1)}, u32[]{:S(2)}, u32[]{:S(2)}) %collective-permute-start.11) | collective-permute-done | bytes 688160 | tf_op jit(solution)/shard_map/ppermute | solution.py:428
  65.6 1.7 %collective-permute-start.13 = (bf16[192,896]{1,0:T(8,128)(2,1)S(1)}, bf16[192,896]{1,0:T(8,128)(2,1)S(1)}, u32[]{:S(2)}, u32[]{:S(2)}) collective-permute-start(bf16[192,896]{1,0:T(8,128)(2,1)S(1)} %get-tuple-element.47), channel_id=1, source_target_pairs={{0,16},{1,9},{2,18},{3,11},{4,20},{5,13},{6,22},{7,15},{8,24},{9,1... | collective-permute-start | bytes 1032200 | tf_op jit(solution)/shard_map/ppermute | solution.py:428
  67.6 1.0 %shard_map.108.refs_2_ = f32[192,2048]{1,0:T(8,128)} custom-call(f32[192,1152]{1,0:T(8,128)S(1)} %get-tuple-element.33.refs_2_.refs_0_, bf16[192,1152]{1,0:T(8,128)(2,1)S(1)} %collective-permute-done.9.refs_5_.refs_0_.refs_1_), custom_call_target="tpu_custom_call" | custom-call | flops 6912 | bytes 34560 | tf_op jit(solution)/shard_map/pallas_call | solution.py:234
  68.6 1.8 %shard_map.106 = (bf16[384,768]{1,0:T(8,128)(2,1)}, bf16[384,768]{1,0:T(8,128)(2,1)}) custom-call(f32[384,768]{1,0:T(8,128)S(1)} %get-tuple-element.37.grad_ref, f32[384,768]{1,0:T(8,128)S(1)} %get-tuple-element.38.up_scale_ref, f32[384,768]{1,0:T(8,128)S(1)} %get-tuple-element.39.gate_scale_ref, f32[16,128]{1,0:T(8,128)S(1)} %get-tuple-element.49.refs_0_), custom_call_target="tpu_custom_call" | custom-call | flops 9216 | bytes 73728 | tf_op jit(solution)/shard_map/pallas_call | solution.py:348
  70.4 1.5 %collective-permute-done.14.refs_3_.far_ref = f32[32,128]{1,0:T(8,128)S(1)} collective-permute-done((f32[32,128]{1,0:T(8,128)S(1)}, f32[32,128]{1,0:T(8,128)S(1)}, u32[]{:S(2)}, u32[]{:S(2)}) %collective-permute-start.14) | collective-permute-done | bytes 16416 | tf_op jit(solution)/shard_map/ppermute | solution.py:412
  71.9 0.8 %shard_map.110 = f32[2,128]{1,0:T(2,128)} custom-call(bf16[16,128]{1,0:T(8,128)(2,1)S(1)} %shard_map.94.refs_0_.meta_ref, f32[32,128]{1,0:T(8,128)S(1)} %constant_dynamic-update-slice_fusion.2.refs_1_.near_ref, f32[32,128]{1,0:T(8,128)S(1)} %collective-permute-done.14.refs_3_.far_ref), custom_call_target="tpu_custom_call" | custom-call | flops 15625 | bytes 1562 | tf_op jit(solution)/shard_map/pallas_call | solution.py:384
  72.9 0.9 %shard_map.109 = f32[192,2048]{1,0:T(8,128)} custom-call(f32[192,896]{1,0:T(8,128)S(1)} %get-tuple-element.46.refs_0_, bf16[192,896]{1,0:T(8,128)(2,1)S(1)} %collective-permute-done.13.refs_1_, f32[192,2048]{1,0:T(8,128)} %shard_map.108.refs_2_, f32[32,128]{1,0:T(8,128)S(1)} %collective-permute-done.14.refs_3_.far_ref), custom_call_target="tpu_custom_call", output_to_operand_aliasing={{}: (2, {})} | custom-call | flops 5376 | bytes 26880 | tf_op jit(solution)/shard_map/pallas_call | solution.py:234
  (33 shorter events, 2.2 us)
Async XLA Ops:
  0.6 2.7 %collective-permute-start.2 = (bf16[128,2048]{1,0:T(8,128)(2,1)}, bf16[128,2048]{1,0:T(8,128)(2,1)S(1)}, u32[]{:S(2)}, u32[]{:S(2)}) collective-permute-start(bf16[128,2048]{1,0:T(8,128)(2,1)} %refs_2_.5), channel_id=1, source_target_pairs={{0,1},{1,0},{2,3},{3,2},{4,5},{5,4},{6,7},{7,6},{8,9},{9,8},{10,11... | collective-permute-start | bytes 1572872 | tf_op jit(solution)/shard_map/ppermute | solution.py:412
  1.1 2.0 %collective-permute-start = (s32[2,128]{1,0:T(2,128)}, s32[2,128]{1,0:T(2,128)S(1)}, u32[]{:S(2)}, u32[]{:S(2)}) collective-permute-start(s32[2,128]{1,0:T(2,128)} %bitcast.13), channel_id=1, source_target_pairs={{0,1},{1,0},{2,3},{3,2},{4,5},{5,4},{6,7},{7,6},{8,9},{9,8},{10,11... | collective-permute-start | bytes 3080 | tf_op jit(solution)/shard_map/ppermute | solution.py:412
  1.2 1.9 %collective-permute-start.1 = (bf16[2,128]{1,0:T(2,128)(2,1)}, bf16[2,128]{1,0:T(2,128)(2,1)S(1)}, u32[]{:S(2)}, u32[]{:S(2)}) collective-permute-start(bf16[2,128]{1,0:T(2,128)(2,1)} %bitcast.15), channel_id=1, source_target_pairs={{0,1},{1,0},{2,3},{3,2},{4,5},{5,4},{6,7},{7,6},{8,9},{9,8},{10,11... | collective-permute-start | bytes 1544 | tf_op jit(solution)/shard_map/ppermute | solution.py:412
  1.7 0.7 copy-start.5
  2.3 0.7 copy-start.6
  3.3 1.0 %copy-start.1 = (bf16[128,2048]{1,0:T(8,128)(2,1)S(1)}, bf16[128,2048]{1,0:T(8,128)(2,1)}, u32[]{:S(2)}) copy-start(bf16[128,2048]{1,0:T(8,128)(2,1)} %refs_2_.5) | copy-start | bytes 1572868
  4.6 24.2 %copy-start.3 = (bf16[1,1,8,48,768]{4,3,2,1,0:T(8,128)(2,1)S(1)}, bf16[1,1,8,48,768]{4,3,2,1,0:T(8,128)(2,1)}, u32[]{:S(2)}) copy-start(bf16[1,1,8,48,768]{4,3,2,1,0:T(8,128)(2,1)} %param.9) | copy-start | bytes 1769476
  4.6 24.2 %copy-start.4 = (bf16[1,1,8,48,768]{4,3,2,1,0:T(8,128)(2,1)S(1)}, bf16[1,1,8,48,768]{4,3,2,1,0:T(8,128)(2,1)}, u32[]{:S(2)}) copy-start(bf16[1,1,8,48,768]{4,3,2,1,0:T(8,128)(2,1)} %param.10) | copy-start | bytes 1769476
  4.7 24.2 %collective-permute-start.4 = (bf16[192,1152]{1,0:T(8,128)(2,1)S(1)}, bf16[192,1152]{1,0:T(8,128)(2,1)S(1)}, u32[]{:S(2)}, u32[]{:S(2)}) collective-permute-start(bf16[192,1152]{1,0:T(8,128)(2,1)S(1)} %shard_map.97), channel_id=1, source_target_pairs={{0,4},{1,7},{2,6},{3,5},{4,0},{5,3},{6,2},{7,1},{8,12},{9,15},{10,... | collective-permute-start | bytes 1327112 | tf_op jit(solution)/shard_map/ppermute | solution.py:418
  8.8 19.7 %collective-permute-start.3 = (bf16[96,2048]{1,0:T(8,128)(2,1)S(1)}, bf16[96,2048]{1,0:T(8,128)(2,1)S(1)}, u32[]{:S(2)}, u32[]{:S(2)}) collective-permute-start(bf16[96,2048]{1,0:T(8,128)(2,1)S(1)} %get-tuple-element.28), channel_id=1, source_target_pairs={{0,2},{1,3},{2,0},{3,1},{4,6},{5,7},{6,4},{7,5},{8,10},{9,11},{10,... | collective-permute-start | bytes 1179656 | tf_op jit(solution)/shard_map/ppermute | solution.py:412
  28.8 1.8 %collective-permute-start.5 = (bf16[192,1152]{1,0:T(8,128)(2,1)S(1)}, bf16[192,1152]{1,0:T(8,128)(2,1)S(1)}, u32[]{:S(2)}, u32[]{:S(2)}) collective-permute-start(bf16[192,1152]{1,0:T(8,128)(2,1)S(1)} %shard_map.98.refs_2_), channel_id=1, source_target_pairs={{0,1},{1,0},{2,3},{3,2},{4,5},{5,4},{6,7},{7,6},{8,9},{9,8},{10,11... | collective-permute-start | bytes 1327112 | tf_op jit(solution)/shard_map/ppermute | solution.py:412
  29.8 3.6 %copy-start.2 = (bf16[128,2048]{1,0:T(8,128)(2,1)S(1)}, bf16[128,2048]{1,0:T(8,128)(2,1)}, u32[]{:S(2)}) copy-start(bf16[128,2048]{1,0:T(8,128)(2,1)} %refs_2_.5) | copy-start | bytes 1572868
  31.8 13.1 %collective-permute-start.7 = (bf16[384,1152]{1,0:T(8,128)(2,1)S(1)}, bf16[384,1152]{1,0:T(8,128)(2,1)S(1)}, u32[]{:S(2)}, u32[]{:S(2)}) collective-permute-start(bf16[384,1152]{1,0:T(8,128)(2,1)S(1)} %get-tuple-element.32), channel_id=1, source_target_pairs={{0,8},{1,17},{2,10},{3,19},{4,12},{5,21},{6,14},{7,23},{8,0},{9,25... | collective-permute-start | bytes 2654216 | tf_op jit(solution)/shard_map/ppermute | solution.py:428
  33.7 17.5 %collective-permute-start.6 = (bf16[192,896]{1,0:T(8,128)(2,1)S(1)}, bf16[192,896]{1,0:T(8,128)(2,1)S(1)}, u32[]{:S(2)}, u32[]{:S(2)}) collective-permute-start(bf16[192,896]{1,0:T(8,128)(2,1)S(1)} %shard_map.101), channel_id=1, source_target_pairs={{0,4},{1,7},{2,6},{3,5},{4,0},{5,3},{6,2},{7,1},{8,12},{9,15},{10,... | collective-permute-start | bytes 1032200 | tf_op jit(solution)/shard_map/ppermute | solution.py:418
  44.9 6.2 %copy-start = (bf16[1,768,2048]{2,1,0:T(8,128)(2,1)S(1)}, bf16[1,768,2048]{2,1,0:T(8,128)(2,1)}, u32[]{:S(2)}) copy-start(bf16[1,768,2048]{2,1,0:T(8,128)(2,1)} %param.11) | copy-start | bytes 9437188
  45.1 8.4 %collective-permute-start.9 = (bf16[192,1152]{1,0:T(8,128)(2,1)S(1)}, bf16[192,1152]{1,0:T(8,128)(2,1)S(1)}, u32[]{:S(2)}, u32[]{:S(2)}) collective-permute-start(bf16[192,1152]{1,0:T(8,128)(2,1)S(1)} %get-tuple-element.34), channel_id=1, source_target_pairs={{0,16},{1,9},{2,18},{3,11},{4,20},{5,13},{6,22},{7,15},{8,24},{9,1... | collective-permute-start | bytes 1327112 | tf_op jit(solution)/shard_map/ppermute | solution.py:428
  51.2 1.7 %collective-permute-start.8 = (bf16[192,896]{1,0:T(8,128)(2,1)S(1)}, bf16[192,896]{1,0:T(8,128)(2,1)S(1)}, u32[]{:S(2)}, u32[]{:S(2)}) collective-permute-start(bf16[192,896]{1,0:T(8,128)(2,1)S(1)} %shard_map.103.refs_2_), channel_id=1, source_target_pairs={{0,1},{1,0},{2,3},{3,2},{4,5},{5,4},{6,7},{7,6},{8,9},{9,8},{10,11... | collective-permute-start | bytes 1032200 | tf_op jit(solution)/shard_map/ppermute | solution.py:412
  54.5 11.0 %collective-permute-start.11 = (bf16[384,896]{1,0:T(8,128)(2,1)S(1)}, bf16[384,896]{1,0:T(8,128)(2,1)S(1)}, u32[]{:S(2)}, u32[]{:S(2)}) collective-permute-start(bf16[384,896]{1,0:T(8,128)(2,1)S(1)} %get-tuple-element.45), channel_id=1, source_target_pairs={{0,8},{1,17},{2,10},{3,19},{4,12},{5,21},{6,14},{7,23},{8,0},{9,25... | collective-permute-start | bytes 2064392 | tf_op jit(solution)/shard_map/ppermute | solution.py:428
  57.9 1.2 %collective-permute-start.10 = (f32[8,128]{1,0:T(8,128)S(1)}, f32[8,128]{1,0:T(8,128)S(1)}, u32[]{:S(2)}, u32[]{:S(2)}) collective-permute-start(f32[8,128]{1,0:T(8,128)S(1)} %get-tuple-element.40), channel_id=1, source_target_pairs={{0,1},{1,0},{2,3},{3,2},{4,5},{5,4},{6,7},{7,6},{8,9},{9,8},{10,11... | collective-permute-start | bytes 12296 | tf_op jit(solution)/shard_map/ppermute | solution.py:412
  59.1 3.7 %collective-permute-start.12 = (f32[16,128]{1,0:T(8,128)S(1)}, f32[16,128]{1,0:T(8,128)S(1)}, u32[]{:S(2)}, u32[]{:S(2)}) collective-permute-start(f32[16,128]{1,0:T(8,128)S(1)} %get-tuple-element.49.refs_0_), channel_id=1, source_target_pairs={{0,2},{1,3},{2,0},{3,1},{4,6},{5,7},{6,4},{7,5},{8,10},{9,11},{10,... | collective-permute-start | bytes 24584 | tf_op jit(solution)/shard_map/ppermute | solution.py:412
  65.6 7.3 %collective-permute-start.13 = (bf16[192,896]{1,0:T(8,128)(2,1)S(1)}, bf16[192,896]{1,0:T(8,128)(2,1)S(1)}, u32[]{:S(2)}, u32[]{:S(2)}) collective-permute-start(bf16[192,896]{1,0:T(8,128)(2,1)S(1)} %get-tuple-element.47), channel_id=1, source_target_pairs={{0,16},{1,9},{2,18},{3,11},{4,20},{5,13},{6,22},{7,15},{8,24},{9,1... | collective-permute-start | bytes 1032200 | tf_op jit(solution)/shard_map/ppermute | solution.py:428
  67.3 4.6 %collective-permute-start.14 = (f32[32,128]{1,0:T(8,128)S(1)}, f32[32,128]{1,0:T(8,128)S(1)}, u32[]{:S(2)}, u32[]{:S(2)}) collective-permute-start(f32[32,128]{1,0:T(8,128)S(1)} %constant_dynamic-update-slice_fusion.2.refs_1_.near_ref), channel_id=1, source_target_pairs={{0,4},{1,5},{2,6},{3,7},{4,0},{5,1},{6,2},{7,3},{8,12},{9,13},{10,... | collective-permute-start | bytes 49160 | tf_op jit(solution)/shard_map/ppermute | solution.py:412
